TPU v7x, 32 devices: a whole 2x2x4 slice. The times are simulated.
32 devices in a mesh: section: 4 (over y, x), tile: 8 (over z, core).
Axes of the slice: x: 2, y: 2, z: 4, core: 2. Of those that a mesh axis runs over, the one named last changes fastest.
Arguments:
- bricks: bfloat16 [128, 39304], P('tile'), may hold values from -6 to 6
- sends: int32 [4, 8, 8, 2], P('section', 'tile'), may hold values from 0 to 15
- cells: int32 [4, 8, 3, 40960], P('section', 'tile'), may hold values from 0 to 32
- fracs: float32 [4, 8, 3, 40960], P('section', 'tile'), may hold values from 0 to 1
- sample_order: int32 [4, 8, 160, 256], P('section', 'tile'), may hold values from 0 to 255, each once within a row
- pending: bfloat16 [4, 4, 64, 256], P('section', None, 'tile'), may hold values from -6 to 6
- w_in: bfloat16 [9, 32, 4], replicated, may hold values from -1 to 1
- w_mid: bfloat16 [9, 32, 32], replicated, may hold values from -0.375 to 0.375
- w_down: bfloat16 [9, 112, 32], replicated, may hold values from -0.375 to 0.375
- w_deep: bfloat16 [9, 112, 112], replicated, may hold values from -0.1875 to 0.1875
- w_up: bfloat16 [9, 32, 144], replicated, may hold values from -0.15625 to 0.15625
- w_out: bfloat16 [9, 3, 32], replicated, may hold values from -0.375 to 0.375
Outputs:
- handoff: bfloat16 [4, 4, 64, 256], P('section', None, 'tile')
- denoised: bfloat16 [4, 3, 64, 256], P('section', None, 'tile')
Inputs may be any that keep to these rules, and one draw needn't show every extreme that they name: `sample_order`: each block of 256 names every number below 256 once.
All inputs are finite; a program needn't handle non-finite values.
Results may differ from a plain program's by a relative error of at most 0.012.
Values may be sent and summed in bfloat16 or wider, within the bound.
No kernel may reach another device: no remote copies, remote signals or barrier semaphores. Data moves between devices by JAX's collectives and lax.ppermute only.
A program may use at most 128 MiB of HBM per device.

v0:
```python
import jax
import jax.numpy as jnp
from jax import lax
from jax.sharding import PartitionSpec as P

EDGE = 34
NSP = 4
NRAY = 8
NOS = 2


SHARP = 2.0


def passed_along(value, axis, steps):
    count = lax.axis_size(axis)
    pairs = [(source, (source + steps) % count) for source in range(count)]
    return lax.ppermute(value, axis, pairs)


def with_halo(block, sides, width):
    for axis, dim in sides:
        count = lax.axis_size(axis)
        forward = [(i, i + 1) for i in range(count - 1)]
        backward = [(target, source) for source, target in forward]
        low = lax.ppermute(
            lax.slice_in_dim(block, block.shape[dim] - width, None, axis=dim), axis, forward
        )
        high = lax.ppermute(lax.slice_in_dim(block, 0, width, axis=dim), axis, backward)
        block = jnp.concatenate([low, block, high], axis=dim)
    return block


def axis_weights(index, frac):
    places = jnp.arange(EDGE, dtype=jnp.int32)
    lower = (places == index[..., None]).astype(jnp.float32)
    upper = (places == index[..., None] + 1).astype(jnp.float32)
    return lower * (1.0 - frac[..., None]) + upper * frac[..., None]


def spread_weights(index, frac, places):
    lower = (places == index[..., None]).astype(jnp.float32)
    upper = (places == index[..., None] + 1).astype(jnp.float32)
    return lower * (1.0 - frac[..., None]) + upper * frac[..., None]


def trilinear(slabs, cell_part, frac_part):
    groups = cell_part.shape[1]
    flat_places = jnp.arange(EDGE * EDGE, dtype=jnp.int32)
    row_place = flat_places // EDGE
    col_place = flat_places % EDGE
    weight_x = spread_weights(cell_part[0], frac_part[0], row_place)
    weight_y = spread_weights(cell_part[1], frac_part[1], col_place)
    weight_z = axis_weights(cell_part[2], frac_part[2])
    plane = (weight_x * weight_y).astype(jnp.bfloat16)
    cube = slabs.reshape(groups, EDGE, EDGE * EDGE)
    rows_out = jnp.einsum("gsq,gzq->gsz", plane, cube, preferred_element_type=jnp.float32)
    return jnp.sum(rows_out * weight_z, axis=-1)


def group_size(slots, per_slot):
    width = min(slots, max(1, 4096 // per_slot))
    while slots % width:
        width -= 1
    return width


def sample_values(received, cell_all, frac_all):
    slots = received.shape[0]
    per_slot = cell_all.shape[1] // slots
    width = group_size(slots, per_slot)
    cell_grid = cell_all.reshape(3, slots, per_slot)
    frac_grid = frac_all.reshape(3, slots, per_slot)

    def one_group(number):
        start = number * width
        slabs = lax.dynamic_slice_in_dim(received, start, width, 0)
        cell_part = lax.dynamic_slice_in_dim(cell_grid, start, width, 1)
        frac_part = lax.dynamic_slice_in_dim(frac_grid, start, width, 1)
        return trilinear(slabs, cell_part, frac_part)

    found = lax.map(one_group, jnp.arange(slots // width, dtype=jnp.int32))
    return found.reshape(-1)


def gbuffer(values, order, height, width):
    base = jnp.arange(order.shape[0], dtype=jnp.int32)[:, None] * order.shape[1]
    flat_order = (order + base).reshape(-1)
    ray = jnp.take(values, flat_order).reshape(NSP + NRAY * NOS, height, width)
    alpha = jax.nn.sigmoid(SHARP * ray)
    remain = jnp.ones((height, width), jnp.float32)
    shade = jnp.zeros((height, width), jnp.float32)
    depth = jnp.zeros((height, width), jnp.float32)
    for step in range(NSP):
        weight = remain * alpha[step]
        shade = shade + weight * ray[step]
        depth = depth + weight * ((step + 1) / NSP)
        remain = remain * (1.0 - alpha[step])
    opacity = 1.0 - remain
    passing = (1.0 - alpha[NSP:]).reshape(NRAY, NOS, height, width)
    occlusion = jnp.mean(jnp.prod(passing, axis=1), axis=0)
    return jnp.stack([shade, opacity, depth, occlusion], axis=0).astype(jnp.bfloat16)


def conv_rows(padded, weight):
    height = padded.shape[1] - 2
    width = padded.shape[2]
    wide = jnp.pad(padded, ((0, 0), (0, 0), (1, 1)))
    total = jnp.zeros((weight.shape[1], height, width), jnp.float32)
    for row_tap in range(3):
        for col_tap in range(3):
            total = total + jnp.einsum(
                "oc,crw->orw",
                weight[3 * row_tap + col_tap],
                wide[:, row_tap : row_tap + height, col_tap : col_tap + width],
                preferred_element_type=jnp.float32,
            )
    return total


def pooling(field):
    chans, height, width = field.shape
    return (
        field.astype(jnp.float32)
        .reshape(chans, height // 2, 2, width // 2, 2)
        .mean(axis=(2, 4))
        .astype(jnp.bfloat16)
    )


def activate(field):
    return jax.nn.silu(field).astype(jnp.bfloat16)


def raise_up(field):
    return jnp.repeat(jnp.repeat(field, 2, axis=1), 2, axis=2)


def on_device(
    bricks, sends, cells, fracs, sample_order, pending, w_in, w_mid, w_down, w_deep, w_up, w_out
):
    n_tile = lax.axis_size("tile")
    cap = sends.shape[3]
    routes = sends[0, 0].reshape(-1)
    cell_all = cells[0, 0]
    frac_all = fracs[0, 0]
    height = pending.shape[2]
    width = pending.shape[3]
    outgoing = jnp.take(bricks, routes, axis=0).reshape(n_tile, cap, bricks.shape[1])
    arrived = lax.all_to_all(outgoing, "tile", split_axis=0, concat_axis=0, tiled=True)
    values = sample_values(arrived.reshape(n_tile * cap, bricks.shape[1]), cell_all, frac_all)
    rendered = gbuffer(values, sample_order[0, 0], height, width)
    handoff = passed_along(rendered[None], "section", 1)
    field = pending[0]

    def same_conv(source, weight):
        padded = with_halo(source, (("tile", 1),), 1)
        return conv_rows(padded, weight)

    first = activate(same_conv(field, w_in))
    second = activate(same_conv(first, w_mid))
    pooled = pooling(second)
    third = activate(same_conv(pooled, w_down))
    fourth = activate(same_conv(third, w_deep))
    joined = jnp.concatenate([second, raise_up(fourth)], axis=0)
    fifth = activate(same_conv(joined, w_up))
    result = same_conv(fifth, w_out).astype(jnp.bfloat16)
    return (handoff, result[None])


def solution(mesh):
    in_specs = (
        P("tile", None),
        P("section", "tile", None, None),
        P("section", "tile", None, None),
        P("section", "tile", None, None),
        P("section", "tile", None, None),
        P("section", None, "tile", None),
        P(),
        P(),
        P(),
        P(),
        P(),
        P(),
    )
    out_specs = (P("section", None, "tile", None), P("section", None, "tile", None))
    return jax.shard_map(
        on_device, mesh=mesh, in_specs=in_specs, out_specs=out_specs, check_vma=False
    )
```

profile of v0, /device:TPU:0, one launch (start us, length us, event | category | flops | bytes accessed | tf_op | source)
XLA Modules:
  0.0 519.5 jit_solution(13664635360891224303)
XLA Ops:
  13.0 8.4 %all-to-all-start = ((bf16[8,2,39304]{2,1,0:T(2,128)(2,1)}), bf16[8,2,39304]{2,1,0:T(2,128)(2,1)S(1)}, u32[]{:S(2)}, u32[]{:S(2)}) async-start(bf16[8,2,39304]{2,1,0:T(2,128)(2,1)} %broadcast_select_fusion), calls=%async_computation | async-start | bytes 2523136 | tf_op jit(solution)/shard_map/all_to_all | solution.py:150
  35.8 14.6 %collective-permute-start.5 = (bf16[32,1,128]{2,0,1:T(8,128)(2,1)S(1)}, bf16[32,1,128]{2,0,1:T(8,128)(2,1)S(1)}, u32[]{:S(2)}, u32[]{:S(2)}) collective-permute-start(bf16[32,1,128]{2,0,1:T(8,128)(2,1)S(1)} %get-tuple-element.125), channel_id=1, source_target_pairs={{0,1},{1,2},{2,3},{3,4},{4,5},{5,6},{6,7},{8,9},{9,10},{10,11},{11... | collective-permute-start | bytes 24584 | tf_op jit(solution)/shard_map/ppermute | solution.py:26
  52.2 3.3 collective-permute-done.6
  59.9 10.2 %collective-permute-start.7 = (bf16[112,1,128]{2,0,1:T(8,128)(2,1)S(1)}, bf16[112,1,128]{2,0,1:T(8,128)(2,1)S(1)}, u32[]{:S(2)}, u32[]{:S(2)}) collective-permute-start(bf16[112,1,128]{2,0,1:T(8,128)(2,1)S(1)} %get-tuple-element.123), channel_id=1, source_target_pairs={{0,1},{1,2},{2,3},{3,4},{4,5},{5,6},{6,7},{8,9},{9,10},{10,11},{11... | collective-permute-start | bytes 86024 | tf_op jit(solution)/shard_map/ppermute | solution.py:26
  77.9 4.8 collective-permute-start.9
  89.6 4.4 collective-permute-start.11
  106.4 181.8 %while.12 = (s32[]{:T(128)}, f32[16,1,2560]{2,1,0:T(1,128)S(1)}, s32[16]{0:T(128)S(1)}, s32[3,16,2560]{2,1,0:T(8,128)}, f32[3,16,2560]{2,1,0:T(8,128)}, /*index=...) while((s32[]{:T(128)}, f32[16,1,2560]{2,1,0:T(1,128)S(1)}, ...), condition=%wide.region_2.3_spmd, body=%wide.region_0.0_spmd.sunk | while | flops 237384752 | bytes 813155 | solution.py:82
  112.9 4.8 fusion.281
  124.2 4.8 fusion.281
  135.6 4.8 fusion.281
  147.0 4.8 fusion.281
  158.3 4.8 fusion.281
  169.7 4.8 fusion.281
  181.1 4.8 fusion.281
  192.4 4.8 fusion.281
  203.8 4.8 fusion.281
  215.1 4.8 fusion.281
  226.5 4.8 fusion.281
  237.9 4.8 fusion.281
  249.2 4.8 fusion.281
  260.6 4.8 fusion.281
  272.0 4.8 fusion.281
  283.3 4.8 fusion.281
  288.2 225.5 %gather_fusion.1 = f32[40960]{0:T(1024)S(1)} fusion(f32[40960]{0:T(1024)S(1)} %bitcast.357, s32[40960]{0:T(1024)S(1)} %copy-done.5), kind=kCustom, calls=%fused_computation.1 | custom fusion | bytes 491520 | tf_op jit(solution)/shard_map/jit(_take)/gather | solution.py:89
  (335 shorter events, 137.5 us)
Async XLA Ops:
  0.6 6.1 %copy-start = (bf16[16,39304]{1,0:T(8,128)(2,1)S(1)}, bf16[16,39304]{1,0:T(8,128)(2,1)}, u32[]{:S(2)}) copy-start(bf16[16,39304]{1,0:T(8,128)(2,1)} %param.14) | copy-start | bytes 3773188
  1.5 19.9 %collective-permute-start.1 = (bf16[4,1,256]{2,0,1:T(4,128)(2,1)S(1)}, bf16[4,1,256]{2,0,1:T(4,128)(2,1)S(1)}, u32[]{:S(2)}, u32[]{:S(2)}) collective-permute-start(bf16[4,1,256]{2,0,1:T(4,128)(2,1)S(1)} %get-tuple-element.127), channel_id=1, source_target_pairs={{0,1},{1,2},{2,3},{3,4},{4,5},{5,6},{6,7},{8,9},{9,10},{10,11},{11... | collective-permute-start | bytes 6152 | tf_op jit(solution)/shard_map/ppermute | solution.py:26
  3.8 17.6 %collective-permute-start.2 = (bf16[4,1,256]{2,0,1:T(4,128)(2,1)S(1)}, bf16[4,1,256]{2,0,1:T(4,128)(2,1)S(1)}, u32[]{:S(2)}, u32[]{:S(2)}) collective-permute-start(bf16[4,1,256]{2,0,1:T(4,128)(2,1)S(1)} %get-tuple-element.128), channel_id=1, source_target_pairs={{1,0},{2,1},{3,2},{4,3},{5,4},{6,5},{7,6},{9,8},{10,9},{11,10},{12... | collective-permute-start | bytes 6152 | tf_op jit(solution)/shard_map/ppermute | solution.py:29
  13.0 8.5 %copy-start.12 = (bf16[9,32,4]{1,2,0:T(4,128)(2,1)S(1)}, bf16[9,32,4]{1,2,0:T(4,128)(2,1)}, u32[]{:S(2)}) copy-start(bf16[9,32,4]{1,2,0:T(4,128)(2,1)} %param.20) | copy-start | bytes 6916
  13.0 91.6 %all-to-all-start = ((bf16[8,2,39304]{2,1,0:T(2,128)(2,1)}), bf16[8,2,39304]{2,1,0:T(2,128)(2,1)S(1)}, u32[]{:S(2)}, u32[]{:S(2)}) async-start(bf16[8,2,39304]{2,1,0:T(2,128)(2,1)} %broadcast_select_fusion), calls=%async_computation | async-start | bytes 2523136 | tf_op jit(solution)/shard_map/all_to_all | solution.py:150
  23.2 7.3 %copy-start.11 = (bf16[9,32,32]{2,1,0:T(8,128)(2,1)S(1)}, bf16[9,32,32]{2,1,0:T(8,128)(2,1)}, u32[]{:S(2)}) copy-start(bf16[9,32,32]{2,1,0:T(8,128)(2,1)} %param.21) | copy-start | bytes 55300
  23.8 3.7 collective-permute-start.3
  26.2 4.2 collective-permute-start.4
  33.5 18.5 %copy-start.1 = (s32[1,1,160,256]{3,2,1,0:T(8,128)S(1)}, s32[1,1,160,256]{3,2,1,0:T(8,128)}, u32[]{:S(2)}) copy-start(s32[1,1,160,256]{3,2,1,0:T(8,128)} %param.18) | copy-start | bytes 491524
  35.8 22.6 %copy-start.10 = (bf16[9,112,32]{1,2,0:T(8,128)(2,1)S(1)}, bf16[9,112,32]{1,2,0:T(8,128)(2,1)}, u32[]{:S(2)}) copy-start(bf16[9,112,32]{1,2,0:T(8,128)(2,1)} %param.22) | copy-start | bytes 193540
  35.8 16.4 %collective-permute-start.5 = (bf16[32,1,128]{2,0,1:T(8,128)(2,1)S(1)}, bf16[32,1,128]{2,0,1:T(8,128)(2,1)S(1)}, u32[]{:S(2)}, u32[]{:S(2)}) collective-permute-start(bf16[32,1,128]{2,0,1:T(8,128)(2,1)S(1)} %get-tuple-element.125), channel_id=1, source_target_pairs={{0,1},{1,2},{2,3},{3,4},{4,5},{5,6},{6,7},{8,9},{9,10},{10,11},{11... | collective-permute-start | bytes 24584 | tf_op jit(solution)/shard_map/ppermute | solution.py:26
  50.4 5.1 collective-permute-start.6
  59.6 13.8 %copy-start.7 = (bf16[9,112,112]{2,1,0:T(8,128)(2,1)S(1)}, bf16[9,112,112]{2,1,0:T(8,128)(2,1)}, u32[]{:S(2)}) copy-start(bf16[9,112,112]{2,1,0:T(8,128)(2,1)} %param.23) | copy-start | bytes 677380
  59.9 12.4 %collective-permute-start.7 = (bf16[112,1,128]{2,0,1:T(8,128)(2,1)S(1)}, bf16[112,1,128]{2,0,1:T(8,128)(2,1)S(1)}, u32[]{:S(2)}, u32[]{:S(2)}) collective-permute-start(bf16[112,1,128]{2,0,1:T(8,128)(2,1)S(1)} %get-tuple-element.123), channel_id=1, source_target_pairs={{0,1},{1,2},{2,3},{3,4},{4,5},{5,6},{6,7},{8,9},{9,10},{10,11},{11... | collective-permute-start | bytes 86024 | tf_op jit(solution)/shard_map/ppermute | solution.py:26
  70.1 3.1 collective-permute-start.8
  75.6 8.4 %copy-start.6 = (s32[40960,1]{0,1:T(1,128)S(1)}, s32[40960,1]{0,1:T(1,128)}, u32[]{:S(2)}) copy-start(s32[40960,1]{0,1:T(1,128)} %compare_select_fusion) | copy-start | bytes 491524
  77.8 8.6 %copy-start.8 = (bf16[9,32,144]{2,1,0:T(8,128)(2,1)S(1)}, bf16[9,32,144]{2,1,0:T(8,128)(2,1)}, u32[]{:S(2)}) copy-start(bf16[9,32,144]{2,1,0:T(8,128)(2,1)} %param.24) | copy-start | bytes 248836
  77.9 6.8 %collective-permute-start.9 = (bf16[144,1,256]{2,0,1:T(8,128)(2,1)S(1)}, bf16[144,1,256]{2,0,1:T(8,128)(2,1)S(1)}, u32[]{:S(2)}, u32[]{:S(2)}) collective-permute-start(bf16[144,1,256]{2,0,1:T(8,128)(2,1)S(1)} %get-tuple-element.115), channel_id=1, source_target_pairs={{0,1},{1,2},{2,3},{3,4},{4,5},{5,6},{6,7},{8,9},{9,10},{10,11},{11... | collective-permute-start | bytes 221192 | tf_op jit(solution)/shard_map/ppermute | solution.py:26
  82.7 3.2 collective-permute-start.10
  88.9 6.6 %copy-start.2 = (bf16[32,8,256]{2,0,1:T(8,128)(2,1)}, bf16[32,8,256]{2,0,1:T(8,128)(2,1)S(1)}, u32[]{:S(2)}) copy-start(bf16[32,8,256]{2,0,1:T(8,128)(2,1)S(1)} %multiply_convert_fusion.1) | copy-start | bytes 393220
  89.6 12.6 %collective-permute-start.11 = (bf16[32,1,256]{2,0,1:T(8,128)(2,1)}, bf16[32,1,256]{2,0,1:T(8,128)(2,1)S(1)}, u32[]{:S(2)}, u32[]{:S(2)}) collective-permute-start(bf16[32,1,256]{2,0,1:T(8,128)(2,1)} %get-tuple-element.119), channel_id=1, source_target_pairs={{0,1},{1,2},{2,3},{3,4},{4,5},{5,6},{6,7},{8,9},{9,10},{10,11},{11... | collective-permute-start | bytes 49160 | tf_op jit(solution)/shard_map/ppermute | solution.py:26
  94.0 8.2 %collective-permute-start.12 = (bf16[32,1,256]{2,0,1:T(8,128)(2,1)}, bf16[32,1,256]{2,0,1:T(8,128)(2,1)S(1)}, u32[]{:S(2)}, u32[]{:S(2)}) collective-permute-start(bf16[32,1,256]{2,0,1:T(8,128)(2,1)} %get-tuple-element.120), channel_id=1, source_target_pairs={{1,0},{2,1},{3,2},{4,3},{5,4},{6,5},{7,6},{9,8},{10,9},{11,10},{12... | collective-permute-start | bytes 49160 | tf_op jit(solution)/shard_map/ppermute | solution.py:29
  106.4 181.8 %copy-start.5 = (s32[40960]{0:T(1024)S(1)}, s32[40960]{0:T(1024)}, u32[]{:S(2)}) copy-start(s32[40960]{0:T(1024)} %broadcast_clamp_fusion) | copy-start | bytes 491524
  514.2 4.7 collective-permute-start
  (4 other events, 7.6 us)
where the time goes:
time: 523 us; the launch traced here: 520 us
  local copies, waits for them, and re-layouts  313 us (60%)
  matrix products  91.3 us (17%)
  starting transfers between devices  56.7 us (11%)
  loops' own time  32.3 us (6%)
  other arithmetic  14.3 us (3%)
  waiting for transfers between devices  10 us (2%)
    gather x3, local copies, waits for them, and re-layouts, gbuffer(): ray = jnp.take(values, flat_order).reshape(NSP + NRAY * NOS, height, width)  226 us
    dot_general x16, matrix products, trilinear(): jnp.einsum('gsq,gzq->gsz', plane, cube, preferred_element_type=jnp.float32)  76.9 us
    ppermute x6, starting transfers between devices, with_halo(): lax.ppermute(lax.slice_in_dim(block, block.shape[dim] - width, None, axis...  38.8 us
    slice x32, local copies, waits for them, and re-layouts, trilinear(): weight_z = axis_weights(cell_part[2], frac_part[2])  34 us
    another operation x1, loops' own time, sample_values(): found = lax.map(one_group, jnp.arange(slots // width, dtype=jnp.int32))  32.3 us
    dynamic_slice x16, local copies, waits for them, and re-layouts, one_group(): slabs = lax.dynamic_slice_in_dim(received, start, width, 0)  25 us
    dot_general x54, matrix products, conv_rows(): jnp.einsum('oc,crw->orw', weight[3 * row_tap + col_tap], wide[:, row_tap:...  14.4 us
  transfers between devices with their start and end apart: 14, of which 5 were waited for; matrix products, arithmetic and copies ran while one was open for 8% of the time, Pallas kernels for 0%

commit v1 on v0

v1 whole, which is shorter than its diff:
```python
import functools

import jax
import jax.numpy as jnp
from jax import lax
from jax.experimental import pallas as pl
from jax.experimental.pallas import tpu as pltpu
from jax.sharding import PartitionSpec as P

EDGE = 34
NSP = 4
NRAY = 8
NOS = 2
LANES = 128
BLOCK = 256
STRIDE = 6
WINDOWS = 6
MAIN = 32
TAIL = 16
BRICK_ROWS = WINDOWS * MAIN + TAIL
KDIM = 256

F32 = jnp.float32
BF16 = jnp.bfloat16
VMEM_LIMIT = 48 * 1024 * 1024


def params():
    return pltpu.CompilerParams(vmem_limit_bytes=VMEM_LIMIT)


def vmem():
    return pl.BlockSpec(memory_space=pltpu.VMEM)


def smem():
    return pl.BlockSpec(memory_space=pltpu.SMEM)


def positions_kernel(cells_ref, fracs_ref, out_ref):
    owners, rows, _ = out_ref.shape
    blocks = rows // 6
    span = blocks * BLOCK

    def one_owner(owner, carry):
        for block in range(blocks):
            start = pl.multiple_of(owner * span + block * BLOCK, BLOCK)
            place = (
                cells_ref[0, 0, :, pl.ds(start, BLOCK)].astype(F32)
                + fracs_ref[0, 0, :, pl.ds(start, BLOCK)]
            )
            for axis in range(3):
                for half in range(2):
                    row = axis * 2 * blocks + half * blocks + block
                    out_ref[owner, row : row + 1, :] = place[
                        axis : axis + 1, half * LANES : (half + 1) * LANES
                    ]
        return carry

    lax.fori_loop(0, owners, one_owner, 0)


def positions(cells, fracs, owners):
    samples = cells.shape[3]
    rows = 3 * samples // owners // LANES
    return pl.pallas_call(
        positions_kernel,
        out_shape=jax.ShapeDtypeStruct((owners, rows, LANES), F32),
        in_specs=[vmem(), vmem()],
        out_specs=vmem(),
        compiler_params=params(),
        cost_estimate=pl.CostEstimate(
            flops=3 * samples, bytes_accessed=36 * samples, transcendentals=0
        ),
        name="positions",
    )(cells, fracs)


def windows_kernel(cube_ref, out_ref, wide, tail):
    count = cube_ref.shape[0]
    plane = EDGE * EDGE
    wide[...] = jnp.zeros_like(wide)
    wide[:, :EDGE, :plane] = cube_ref[...]
    column = lax.broadcasted_iota(jnp.int32, (1, KDIM), 1)
    main = (column // MAIN) * EDGE + column % MAIN
    rest = column - 7 * MAIN
    last = (rest % 8) * EDGE + MAIN + rest // 8
    source = jnp.where(column < 7 * MAIN, main, last)
    unused = (column >= 7 * MAIN) & ((rest % 8 == 7) | (rest >= TAIL))
    source = jnp.where(unused, -(1 << 20), source)
    for window in range(WINDOWS):
        first = window * STRIDE * EDGE
        low = first // LANES * LANES
        length = min(3 * LANES, wide.shape[2] - low)
        place = lax.broadcasted_iota(jnp.int32, (length, KDIM), 0)
        pick = jnp.where(place == source + (first - low), 1.0, 0.0).astype(BF16)
        found = jnp.dot(
            wide[:, :, low : low + length].reshape(-1, length),
            pick,
            preferred_element_type=F32,
        )
        found = found.reshape(count, 48, KDIM)
        out_ref[:, window * MAIN : (window + 1) * MAIN, :] = found[:, :MAIN, :].astype(BF16)
        tail[:, window : window + 1, :] = found[:, MAIN : MAIN + 1, :]
        tail[:, 8 + window : 9 + window, :] = found[:, MAIN + 1 : MAIN + 2, :]
    for row in (6, 7, 14, 15):
        tail[:, row : row + 1, :] = jnp.zeros((count, 1, KDIM), F32)
    out_ref[:, WINDOWS * MAIN :, :] = tail[...].astype(BF16)


def windows_of(bricks):
    count = bricks.shape[0]
    cube = bricks.reshape(count, EDGE, EDGE * EDGE)
    return pl.pallas_call(
        windows_kernel,
        out_shape=jax.ShapeDtypeStruct((count, BRICK_ROWS, KDIM), BF16),
        in_specs=[vmem()],
        out_specs=vmem(),
        scratch_shapes=[
            pltpu.VMEM((count, 48, 10 * LANES), BF16),
            pltpu.VMEM((count, TAIL, KDIM), F32),
        ],
        compiler_params=params(),
        cost_estimate=pl.CostEstimate(
            flops=2 * count * 48 * 384 * KDIM * WINDOWS, bytes_accessed=4 * 1024 * 1024,
            transcendentals=0,
        ),
        name="brick_windows",
    )(cube)


def hat(distance):
    return jnp.maximum(1.0 - jnp.abs(distance), 0.0)


def blend(brick, px, py, pz):
    width = px.shape[1]
    places = lax.broadcasted_iota(jnp.int32, (MAIN, width), 0).astype(F32)
    eight = lax.broadcasted_iota(jnp.int32, (8, width), 0).astype(F32)
    weight_y = hat(places - py)
    weight_z = hat(places - pz)
    window = jnp.clip(jnp.floor(px * (1.0 / STRIDE)), 0.0, WINDOWS - 1.0)
    weight_x = hat(eight - (px - STRIDE * window))
    parts = [(weight_y * weight_x[i : i + 1]).astype(BF16) for i in range(STRIDE + 1)]
    parts.append((weight_x * hat(MAIN - py)).astype(BF16))
    parts.append((weight_x * hat(MAIN + 1 - py)).astype(BF16))
    parts.append(jnp.zeros((TAIL, width), BF16))
    plane = jnp.concatenate(parts, axis=0)
    found = jnp.dot(brick, plane, preferred_element_type=F32)
    chosen = found[:MAIN]
    for other in range(1, WINDOWS):
        chosen = jnp.where(
            window == float(other), found[other * MAIN : (other + 1) * MAIN], chosen
        )
    total = (chosen * weight_z).reshape(MAIN // 8, 8, width).sum(axis=0)
    base = WINDOWS * MAIN
    edges = found[base : base + 8] * hat(MAIN - pz) + found[base + 8 :] * hat(MAIN + 1 - pz)
    total = total + jnp.where(eight == window, edges, 0.0)
    return jnp.sum(total, axis=0, keepdims=True)


def samples_kernel(picks_ref, brick_ref, place_ref, out_ref):
    owners, rows, _ = place_ref.shape
    cap = picks_ref.shape[3]
    blocks = rows // 6
    per_slot = blocks // cap

    def one_slot(slot, carry):
        renderer = slot // cap
        piece = slot % cap
        brick = brick_ref[picks_ref[0, 0, renderer, piece]]
        for step in range(per_slot):
            row = piece * per_slot + step

            def line(axis):
                both = [
                    place_ref[renderer, pl.ds((2 * axis + half) * blocks + row, 1), :]
                    for half in range(2)
                ]
                return jnp.concatenate(both, axis=1)

            value = blend(brick, line(0), line(1), line(2))
            for half in range(2):
                out_ref[renderer, pl.ds(half * blocks + row, 1), :] = value[
                    :, half * LANES : (half + 1) * LANES
                ]
        return carry

    lax.fori_loop(0, owners * cap, one_slot, 0)


def sample_values(picks, windows, places):
    owners, rows, _ = places.shape
    samples = owners * rows * LANES // 3
    return pl.pallas_call(
        samples_kernel,
        out_shape=jax.ShapeDtypeStruct((owners, rows // 3, LANES), F32),
        in_specs=[smem(), vmem(), vmem()],
        out_specs=vmem(),
        compiler_params=params(),
        cost_estimate=pl.CostEstimate(
            flops=2 * samples * KDIM * BRICK_ROWS, bytes_accessed=3 * 1024 * 1024,
            transcendentals=0,
        ),
        name="sample_values",
    )(picks, windows, places)


def gbuffer_kernel(value_ref, order_ref, out_ref, low, high):
    groups, rows, _ = value_ref.shape
    blocks = rows // 2
    for group in range(groups):
        low[group * blocks : (group + 1) * blocks, :] = value_ref[group, :blocks, :]
        high[group * blocks : (group + 1) * blocks, :] = value_ref[group, blocks:, :]
    height = out_ref.shape[2]

    def ray_of(number):
        rows_now = slice(number * height, (number + 1) * height)
        first, second = low[rows_now, :], high[rows_now, :]
        parts = []
        for half in range(2):
            order = order_ref[0, 0, rows_now, half * LANES : (half + 1) * LANES]
            inner = order & (LANES - 1)
            parts.append(
                jnp.where(
                    order < LANES,
                    jnp.take_along_axis(first, inner, axis=1, mode="promise_in_bounds"),
                    jnp.take_along_axis(second, inner, axis=1, mode="promise_in_bounds"),
                )
            )
        return jnp.concatenate(parts, axis=1)

    remain = 1.0
    shade = 0.0
    depth = 0.0
    for step in range(NSP):
        ray = ray_of(step)
        half_tanh = 0.5 * jnp.tanh(ray)
        weight = remain * (0.5 + half_tanh)
        shade = shade + weight * ray
        depth = depth + weight * ((step + 1) / NSP)
        remain = remain * (0.5 - half_tanh)
    occlusion = 0.0
    for ray_number in range(NRAY):
        passing = 1.0
        for step in range(NOS):
            ray = ray_of(NSP + ray_number * NOS + step)
            passing = passing * (0.5 - 0.5 * jnp.tanh(ray))
        occlusion = occlusion + passing
    out_ref[0, 0] = shade.astype(BF16)
    out_ref[0, 1] = (1.0 - remain).astype(BF16)
    out_ref[0, 2] = depth.astype(BF16)
    out_ref[0, 3] = (occlusion * (1.0 / NRAY)).astype(BF16)


def gbuffer(values, order, height, width):
    total = order.shape[2]
    return pl.pallas_call(
        gbuffer_kernel,
        out_shape=jax.ShapeDtypeStruct((1, 4, height, width), BF16),
        in_specs=[vmem(), vmem()],
        out_specs=vmem(),
        scratch_shapes=[pltpu.VMEM((total, LANES), F32), pltpu.VMEM((total, LANES), F32)],
        compiler_params=params(),
        cost_estimate=pl.CostEstimate(
            flops=20 * total * BLOCK, bytes_accessed=8 * total * BLOCK, transcendentals=0
        ),
        name="gbuffer",
    )(values, order)


def silu(field):
    half = 0.5 * field
    return half + half * jnp.tanh(half)


def conv_line(source, row, weight_ref, out_chans):
    chans = weight_ref.shape[2]
    total = None
    for tap in range(3):
        weight = weight_ref[3 * tap : 3 * tap + 3].reshape(3 * out_chans, chans)
        part = jnp.dot(weight, source[row + tap], preferred_element_type=F32)
        total = part if total is None else total + part
    width = total.shape[1]
    left, middle, right = (total[i * out_chans : (i + 1) * out_chans] for i in range(3))
    lane = lax.broadcasted_iota(jnp.int32, (1, width), 1)
    from_left = jnp.where(lane == 0, 0.0, pltpu.roll(left, 1, 1))
    from_right = jnp.where(lane == width - 1, 0.0, pltpu.roll(right, width - 1, 1))
    return middle + from_left + from_right


def unet_kernel(
    where_ref, x_ref, w_in, w_mid, w_down, w_deep, w_up, w_out, out_ref,
    first, second, pooled, third, fourth, joined, fifth, final,
):
    height = out_ref.shape[2]
    half_height = height // 2
    width = out_ref.shape[3]
    above = jnp.where(where_ref[0] > 0, 1.0, 0.0)
    below = jnp.where(where_ref[0] < where_ref[1] - 1, 1.0, 0.0)

    def inside(row, low, high):
        return jnp.where(row < low, above, jnp.where(row >= high, below, 1.0))

    def layer(source, weight_ref, target, low, high):
        chans = target.shape[1]

        def step(row, carry):
            line = silu(conv_line(source, row, weight_ref, chans))
            target[row] = (line * inside(row, low, high)).astype(BF16)
            return carry

        lax.fori_loop(0, target.shape[0], step, 0, unroll=2)

    layer(x_ref, w_in, first, height - 1, 2 * height - 1)
    layer(first, w_mid, second, height - 2, 2 * height - 2)

    place = lax.broadcasted_iota(jnp.int32, (width, width // 2), 0) // 2
    target = lax.broadcasted_iota(jnp.int32, (width, width // 2), 1)
    shrink = jnp.where(place == target, 0.25, 0.0).astype(BF16)
    count, chans = second.shape[0], second.shape[1]
    pairs = jnp.dot(
        second[...].reshape(count * chans, width), shrink, preferred_element_type=F32
    ).reshape(count // 2, 2, chans, width // 2)
    pooled[...] = (pairs[:, 0] + pairs[:, 1]).astype(BF16)

    layer(pooled, w_down, third, half_height - 2, 2 * half_height - 2)
    layer(third, w_deep, fourth, half_height - 3, 2 * half_height - 3)

    place = lax.broadcasted_iota(jnp.int32, (width // 2, width), 0)
    target = lax.broadcasted_iota(jnp.int32, (width // 2, width), 1) // 2
    spread = jnp.where(place == target, 1.0, 0.0).astype(BF16)
    deep = fourth.shape[1]
    for row in range(fourth.shape[0]):
        wide = jnp.dot(fourth[row], spread, preferred_element_type=F32).astype(BF16)
        for half in range(2):
            joined[2 * row + half, chans:, :] = wide
            joined[2 * row + half, :chans, :] = second[2 * row + half + 4]

    layer(joined, w_up, fifth, 1, height + 1)

    colours = out_ref.shape[1]
    for row in range(height):
        line = conv_line(fifth, row, w_out, w_out.shape[1])
        for colour in range(colours):
            final[colour, row : row + 1, :] = line[colour : colour + 1, :]
    out_ref[0] = final[...].astype(BF16)


def unet(where, field, w_in, w_mid, w_down, w_deep, w_up, w_out, colours):
    height = field.shape[0] // 3
    half = height // 2
    width = field.shape[2]
    one, two = w_mid.shape[1], w_deep.shape[1]
    return pl.pallas_call(
        unet_kernel,
        out_shape=jax.ShapeDtypeStruct((1, colours, height, width), BF16),
        in_specs=[smem()] + [vmem()] * 7,
        out_specs=vmem(),
        scratch_shapes=[
            pltpu.VMEM((3 * height - 2, one, width), BF16),
            pltpu.VMEM((3 * height - 4, one, width), BF16),
            pltpu.VMEM((3 * half - 2, one, width // 2), BF16),
            pltpu.VMEM((3 * half - 4, two, width // 2), BF16),
            pltpu.VMEM((3 * half - 6, two, width // 2), BF16),
            pltpu.VMEM((height + 4, one + two, width), BF16),
            pltpu.VMEM((height + 2, one, width), BF16),
            pltpu.VMEM((colours, height, width), F32),
        ],
        compiler_params=params(),
        cost_estimate=pl.CostEstimate(
            flops=3_000_000_000, bytes_accessed=2 * 1024 * 1024, transcendentals=500_000
        ),
        name="unet",
    )(where, field, w_in, w_mid, w_down, w_deep, w_up, w_out)


def on_device(
    bricks, sends, cells, fracs, sample_order, pending, w_in, w_mid, w_down, w_deep, w_up, w_out
):
    n_tile = lax.axis_size("tile")
    tile = lax.axis_index("tile")
    n_section = lax.axis_size("section")
    cap = sends.shape[3]
    height = pending.shape[2]
    width = pending.shape[3]
    samples = cells.shape[3]
    slots = n_tile * cap
    per_slot = samples // slots
    padded = -(-per_slot // BLOCK) * BLOCK

    def fill(part):
        if padded == per_slot:
            return part
        part = part.reshape(1, 1, 3, slots, per_slot)
        part = jnp.pad(part, ((0, 0),) * 4 + ((0, padded - per_slot),))
        return part.reshape(1, 1, 3, slots * padded)

    def trim(found):
        if padded == per_slot:
            return found
        rows = found.shape[1] // 2
        flat = found.reshape(n_tile, 2, rows, LANES).transpose(0, 2, 1, 3)
        flat = flat.reshape(slots, padded)[:, :per_slot]
        flat = flat.reshape(1, samples // BLOCK, 2, LANES).transpose(0, 2, 1, 3)
        return flat.reshape(1, samples // LANES, LANES)

    down = [(i, i + 1) for i in range(n_tile - 1)]
    up = [(i + 1, i) for i in range(n_tile - 1)]
    over = lax.ppermute(pending, "tile", down)
    under = lax.ppermute(pending, "tile", up)
    places = positions(fill(cells), fill(fracs), n_tile)
    arrived = lax.all_to_all(places, "tile", split_axis=0, concat_axis=0, tiled=True)

    windows = windows_of(bricks)
    field = jnp.concatenate([over[0], pending[0], under[0]], axis=1).transpose(1, 0, 2)
    field = jnp.pad(field, ((0, 0), (0, 16 - field.shape[1]), (0, 0)))
    colours = w_out.shape[1]
    where = jnp.stack([tile, jnp.int32(n_tile)]).astype(jnp.int32)
    denoised = unet(
        where,
        field,
        jnp.pad(w_in, ((0, 0), (0, 0), (0, 16 - w_in.shape[2]))),
        w_mid,
        w_down,
        w_deep,
        w_up,
        jnp.pad(w_out, ((0, 0), (0, 16 - colours), (0, 0))),
        colours,
    )

    found = sample_values(sends, windows, arrived)
    values = lax.all_to_all(found, "tile", split_axis=0, concat_axis=0, tiled=True)
    rendered = gbuffer(trim(values), sample_order, height, width)
    ring = [(i, (i + 1) % n_section) for i in range(n_section)]
    handoff = lax.ppermute(rendered, "section", ring)
    return (handoff, denoised)


def solution(mesh):
    in_specs = (
        P("tile", None),
        P("section", "tile", None, None),
        P("section", "tile", None, None),
        P("section", "tile", None, None),
        P("section", "tile", None, None),
        P("section", None, "tile", None),
        P(),
        P(),
        P(),
        P(),
        P(),
        P(),
    )
    out_specs = (P("section", None, "tile", None), P("section", None, "tile", None))
    return jax.shard_map(
        on_device, mesh=mesh, in_specs=in_specs, out_specs=out_specs, check_vma=False
    )
```

time: 523 us -> 64.6 us (0.12)
  local copies, waits for them, and re-layouts: 313 us -> 8.87 us
  matrix products: 91.3 us -> 0 us
  starting transfers between devices: 56.7 us -> 15.7 us
  loops' own time: 32.3 us -> 0 us
  Pallas kernels: 0 us -> 27 us
  other arithmetic: 14.3 us -> 0.11 us
    gather x5 -> x0, local copies, waits for them, and re-layouts: 230 us -> none  [the longest x3 226 us: gbuffer(): ray = jnp.take(values, flat_order).reshape(NSP + NRAY * NOS, height, width)]
    dot_general x70 -> x0, matrix products: 91.3 us -> none  [the longest x16 76.9 us: trilinear(): jnp.einsum('gsq,gzq->gsz', plane, cube, preferred_element_type=jnp.float32)]
    ppermute x13 -> x3, starting transfers between devices: 48.3 us -> 5.85 us  [the longest x1 3.03 us: on_device(): over = lax.ppermute(pending, 'tile', down)]
    slice x37 -> x0, local copies, waits for them, and re-layouts: 34.7 us -> none  [the longest x32 34 us: trilinear(): weight_z = axis_weights(cell_part[2], frac_part[2])]
    dynamic_slice x32 -> x0, local copies, waits for them, and re-layouts: 34.4 us -> none  [the longest x16 25 us: one_group(): slabs = lax.dynamic_slice_in_dim(received, start, width, 0)]
    another operation x1 -> x0, loops' own time: 32.3 us -> none  [sample_values(): found = lax.map(one_group, jnp.arange(slots // width, dtype=jnp.int32))]
    pallas_call x0 -> x5, Pallas kernels: none -> 27 us  [the longest x1 13.3 us: unet(): pl.pallas_call(unet_kernel, out_shape=jax.ShapeDtypeStruct((1, colours, h...]
    all_to_all x1 -> x2, waiting for transfers between devices: 0.01 us -> 11.4 us  [the longest x1 9.48 us: on_device(): lax.all_to_all(places, 'tile', split_axis=0, concat_axis=0, tiled=True)]
  transfers between devices with their start and end apart: 14 -> 5, of which waited for: 5 -> 3; matrix products, arithmetic and copies ran while one was open for 8% -> 5% of each run, Pallas kernels for 0% -> 23%
where the time goes in v1:
time: 64.6 us; the launch traced here: 64.1 us
  Pallas kernels  27 us (42%)
  starting transfers between devices  15.7 us (24%)
  waiting for transfers between devices  11.7 us (18%)
  local copies, waits for them, and re-layouts  8.87 us (14%)
  between operations  0.79 us (1%)
    pallas_call x1, Pallas kernels, unet(): pl.pallas_call(unet_kernel, out_shape=jax.ShapeDtypeStruct((1, colours, h...  13.3 us
    pallas_call x1, Pallas kernels, sample_values(): pl.pallas_call(samples_kernel, out_shape=jax.ShapeDtypeStruct((owners, ro...  10.7 us
    all_to_all x1, waiting for transfers between devices, on_device(): lax.all_to_all(places, 'tile', split_axis=0, concat_axis=0, tiled=True)  9.48 us
    unnamed x31, local copies, waits for them, and re-layouts  6.49 us
    all_to_all x1, starting transfers between devices, on_device(): lax.all_to_all(places, 'tile', split_axis=0, concat_axis=0, tiled=True)  6.33 us
    all_to_all x1, starting transfers between devices, on_device(): lax.all_to_all(found, 'tile', split_axis=0, concat_axis=0, tiled=True)  3.51 us
    ppermute x1, starting transfers between devices, on_device(): over = lax.ppermute(pending, 'tile', down)  3.03 us
    reshape x1, local copies, waits for them, and re-layouts, windows_of(): cube = bricks.reshape(count, EDGE, EDGE * EDGE)  2.31 us
  transfers between devices with their start and end apart: 5, of which 3 were waited for; matrix products, arithmetic and copies ran while one was open for 5% of the time, Pallas kernels for 23%

profile of v1, /device:TPU:0, one launch (start us, length us, event | category | flops | bytes accessed | tf_op | source)
XLA Modules:
  0.0 64.1 jit_solution(7233556003243367900)
XLA Ops:
  0.6 1.4 %copy.22.cells_ref = s32[1,1,3,40960]{3,2,1,0:T(4,128)S(1)} copy(s32[1,1,3,40960]{3,1,2,0:T(1,128)} %param.14) | data formatting | bytes 983040 | tf_op args[2]
  2.0 1.4 %copy.23.fracs_ref = f32[1,1,3,40960]{3,2,1,0:T(4,128)S(1)} copy(f32[1,1,3,40960]{3,1,2,0:T(1,128)} %param.15) | data formatting | bytes 983040 | tf_op args[3]
  3.4 0.0 copy-start.11
  3.4 1.1 %positions.1 = f32[8,120,128]{2,1,0:T(8,128)} custom-call(s32[1,1,3,40960]{3,2,1,0:T(4,128)S(1)} %copy.22.cells_ref, f32[1,1,3,40960]{3,2,1,0:T(4,128)S(1)} %copy.23.fracs_ref), custom_call_target="tpu_custom_call" | custom-call | flops 122880 | bytes 1474560 | tf_op jit(solution)/shard_map/positions/pallas_call | solution.py:66
  4.5 6.3 %all-to-all-start = ((f32[8,120,128]{2,1,0:T(8,128)}), f32[8,120,128]{2,1,0:T(8,128)S(1)}, u32[]{:S(2)}, u32[]{:S(2)}) async-start(f32[8,120,128]{2,1,0:T(8,128)} %positions.1), calls=%async_computation | async-start | bytes 983040 | tf_op jit(solution)/shard_map/all_to_all | solution.py:413
  10.9 0.1 copy.24.picks_ref
  10.9 2.3 %reshape.7.cube_ref = bf16[16,34,1156]{2,1,0:T(8,128)(2,1)S(1)} reshape(bf16[16,39304]{1,0:T(8,128)(2,1)S(1)} %copy-done.6) | data formatting | bytes 2515456 | tf_op jit(solution)/shard_map/reshape | solution.py:113
  13.3 1.5 %brick_windows.1.brick_ref = bf16[16,208,256]{2,1,0:T(8,128)(2,1)S(1)} custom-call(bf16[16,34,1156]{2,1,0:T(8,128)(2,1)S(1)} %reshape.7.cube_ref), custom_call_target="tpu_custom_call" | custom-call | flops 905969664 | bytes 4194304 | tf_op jit(solution)/shard_map/brick_windows/pallas_call | solution.py:114
  14.8 1.2 %copy-done.4 = bf16[16,208,256]{2,1,0:T(8,128)(2,1)} copy-done((bf16[16,208,256]{2,1,0:T(8,128)(2,1)}, bf16[16,208,256]{2,1,0:T(8,128)(2,1)S(1)}, u32[]{:S(2)}) %copy-start.4) | copy-done | bytes 1703960
  16.0 9.5 %all-to-all-done.place_ref = f32[8,120,128]{2,1,0:T(8,128)S(1)} async-done(((f32[8,120,128]{2,1,0:T(8,128)}), f32[8,120,128]{2,1,0:T(8,128)S(1)}, u32[]{:S(2)}, u32[]{:S(2)}) %all-to-all-start) | async-done | bytes 491552 | tf_op jit(solution)/shard_map/all_to_all | solution.py:413
  25.5 1.5 %copy-done.5 = bf16[16,208,256]{2,1,0:T(8,128)(2,1)S(1)} copy-done((bf16[16,208,256]{2,1,0:T(8,128)(2,1)S(1)}, bf16[16,208,256]{2,1,0:T(8,128)(2,1)}, u32[]{:S(2)}) %copy-start.5) | copy-done | bytes 1703960
  27.0 10.7 %sample_values.1 = f32[8,40,128]{2,1,0:T(8,128)} custom-call(s32[1,1,8,2]{3,2,1,0:T(8,128)S(1)} %copy.24.picks_ref, bf16[16,208,256]{2,1,0:T(8,128)(2,1)S(1)} %copy-done.5, f32[8,120,128]{2,1,0:T(8,128)S(1)} %all-to-all-done.place_ref), custom_call_target="tpu_custom_call" | custom-call | flops 4362076160 | bytes 3145728 | tf_op jit(solution)/shard_map/sample_values/pallas_call | solution.py:195
  37.7 3.5 %all-to-all-start.1 = ((f32[8,40,128]{2,1,0:T(8,128)}), f32[8,40,128]{2,1,0:T(8,128)S(1)}, u32[]{:S(2)}, u32[]{:S(2)}) async-start(f32[8,40,128]{2,1,0:T(8,128)} %sample_values.1), calls=%async_computation.1 | async-start | bytes 327680 | tf_op jit(solution)/shard_map/all_to_all | solution.py:433
  41.2 1.3 %collective-permute-start.2 = (bf16[1,4,8,256]{3,1,2,0:T(4,128)(2,1)S(1)}, bf16[1,4,8,256]{3,1,2,0:T(4,128)(2,1)S(1)}, u32[]{:S(2)}, u32[]{:S(2)}) collective-permute-start(bf16[1,4,8,256]{3,1,2,0:T(4,128)(2,1)S(1)} %copy.32), channel_id=1, source_target_pairs={{1,0},{2,1},{3,2},{4,3},{5,4},{6,5},{7,6},{9,8},{10,9},{11,10},{12... | collective-permute-start | bytes 49160 | tf_op jit(solution)/shard_map/ppermute | solution.py:411
  42.5 3.0 %collective-permute-start.1 = (bf16[1,4,8,256]{3,1,2,0:T(4,128)(2,1)S(1)}, bf16[1,4,8,256]{3,1,2,0:T(4,128)(2,1)S(1)}, u32[]{:S(2)}, u32[]{:S(2)}) collective-permute-start(bf16[1,4,8,256]{3,1,2,0:T(4,128)(2,1)S(1)} %copy.32), channel_id=1, source_target_pairs={{0,1},{1,2},{2,3},{3,4},{4,5},{5,6},{6,7},{8,9},{9,10},{10,11},{11... | collective-permute-start | bytes 49160 | tf_op jit(solution)/shard_map/ppermute | solution.py:410
  45.6 0.1 pad_add_fusion.where_ref
  45.6 0.1 copy.28
  45.8 0.2 copy.29.w_down
  46.1 0.3 collective-permute-done.1
  46.4 1.9 %all-to-all-done.1.value_ref = f32[8,40,128]{2,1,0:T(8,128)S(1)} async-done(((f32[8,40,128]{2,1,0:T(8,128)}), f32[8,40,128]{2,1,0:T(8,128)S(1)}, u32[]{:S(2)}, u32[]{:S(2)}) %all-to-all-start.1) | async-done | bytes 163872 | tf_op jit(solution)/shard_map/all_to_all | solution.py:433
  48.4 0.3 gbuffer.1
  48.7 1.5 %collective-permute-start = (bf16[1,4,8,256]{3,2,1,0:T(8,128)(2,1)S(1)}, bf16[1,4,8,256]{3,2,1,0:T(8,128)(2,1)S(1)}, u32[]{:S(2)}, u32[]{:S(2)}) collective-permute-start(bf16[1,4,8,256]{3,2,1,0:T(8,128)(2,1)S(1)} %gbuffer.1), channel_id=1, source_target_pairs={{0,8},{8,16},{16,24},{24,0},{1,9},{9,17},{17,25},{25,1},{2,10},{10... | collective-permute-start | bytes 49160 | tf_op jit(solution)/shard_map/ppermute | solution.py:436
  50.2 13.3 %unet.1 = bf16[1,3,8,256]{3,2,1,0:T(8,128)(2,1)} custom-call(s32[2]{0:T(128)S(1)} %pad_add_fusion.where_ref, bf16[24,16,256]{2,1,0:T(8,128)(2,1)S(1)} %pad.12.x_ref, bf16[9,32,16]{2,1,0:T(8,128)(2,1)S(1)} %pad.13.w_in, bf16[9,32,32]{2,1,0:T(8,128)(2,1)S(1)} %copy-done.3, bf16[9,112,32]{2,1,0:T(8,128)(2,1)S(1)} %copy.29.w_down, ...), custom_call_target="tpu_custom_call" | custom-call | flops 3000000000 | bytes 2097152 | tf_op jit(solution)/shard_map/unet/pallas_call | solution.py:355
  63.5 0.6 copy.34
  (28 shorter events, 0.2 us)
Async XLA Ops:
  3.4 7.5 %copy-start.11 = (s32[1,1,8,2]{2,3,1,0:T(2,128)S(1)}, s32[1,1,8,2]{2,3,1,0:T(2,128)}, u32[]{:S(2)}) copy-start(s32[1,1,8,2]{2,3,1,0:T(2,128)} %param.13) | copy-start | bytes 196
  3.4 7.6 %copy-start.6 = (bf16[16,39304]{1,0:T(8,128)(2,1)S(1)}, bf16[16,39304]{1,0:T(8,128)(2,1)}, u32[]{:S(2)}) copy-start(bf16[16,39304]{1,0:T(8,128)(2,1)} %param.12) | copy-start | bytes 3773188
  4.5 21.0 %all-to-all-start = ((f32[8,120,128]{2,1,0:T(8,128)}), f32[8,120,128]{2,1,0:T(8,128)S(1)}, u32[]{:S(2)}, u32[]{:S(2)}) async-start(f32[8,120,128]{2,1,0:T(8,128)} %positions.1), calls=%async_computation | async-start | bytes 983040 | tf_op jit(solution)/shard_map/all_to_all | solution.py:413
  14.8 1.2 %copy-start.4 = (bf16[16,208,256]{2,1,0:T(8,128)(2,1)}, bf16[16,208,256]{2,1,0:T(8,128)(2,1)S(1)}, u32[]{:S(2)}) copy-start(bf16[16,208,256]{2,1,0:T(8,128)(2,1)S(1)} %brick_windows.1.brick_ref) | copy-start | bytes 5111812
  16.0 32.4 %copy-start = (s32[1,1,160,256]{3,2,1,0:T(8,128)S(1)}, s32[1,1,160,256]{3,2,1,0:T(8,128)}, u32[]{:S(2)}) copy-start(s32[1,1,160,256]{3,2,1,0:T(8,128)} %order_ref.1) | copy-start | bytes 491524
  25.5 1.5 %copy-start.5 = (bf16[16,208,256]{2,1,0:T(8,128)(2,1)S(1)}, bf16[16,208,256]{2,1,0:T(8,128)(2,1)}, u32[]{:S(2)}) copy-start(bf16[16,208,256]{2,1,0:T(8,128)(2,1)} %copy-done.4) | copy-start | bytes 5111812
  27.0 14.2 %copy-start.8 = (bf16[1,4,8,256]{3,2,1,0:T(8,128)(2,1)S(1)}, bf16[1,4,8,256]{3,2,1,0:T(8,128)(2,1)}, u32[]{:S(2)}) copy-start(bf16[1,4,8,256]{3,2,1,0:T(8,128)(2,1)} %param.17) | copy-start | bytes 49156
  27.0 18.7 %copy-start.9 = (bf16[9,32,4]{1,2,0:T(4,128)(2,1)S(1)}, bf16[9,32,4]{1,2,0:T(4,128)(2,1)}, u32[]{:S(2)}) copy-start(bf16[9,32,4]{1,2,0:T(4,128)(2,1)} %param.18) | copy-start | bytes 6916
  27.0 18.8 %copy-start.7 = (bf16[9,112,32]{1,2,0:T(8,128)(2,1)S(1)}, bf16[9,112,32]{1,2,0:T(8,128)(2,1)}, u32[]{:S(2)}) copy-start(bf16[9,112,32]{1,2,0:T(8,128)(2,1)} %param.20) | copy-start | bytes 193540
  27.0 19.0 %copy-start.10 = (bf16[9,3,32]{2,1,0:T(4,128)(2,1)S(1)}, bf16[9,3,32]{2,1,0:T(4,128)(2,1)}, u32[]{:S(2)}) copy-start(bf16[9,3,32]{2,1,0:T(4,128)(2,1)} %param.23) | copy-start | bytes 5188
  37.7 12.5 %copy-start.1 = (bf16[9,112,112]{2,1,0:T(8,128)(2,1)S(1)}, bf16[9,112,112]{2,1,0:T(8,128)(2,1)}, u32[]{:S(2)}) copy-start(bf16[9,112,112]{2,1,0:T(8,128)(2,1)} %w_deep.1) | copy-start | bytes 677380
  37.7 12.5 %copy-start.2 = (bf16[9,32,144]{2,1,0:T(8,128)(2,1)S(1)}, bf16[9,32,144]{2,1,0:T(8,128)(2,1)}, u32[]{:S(2)}) copy-start(bf16[9,32,144]{2,1,0:T(8,128)(2,1)} %w_up.1) | copy-start | bytes 248836
  37.7 12.5 %copy-start.3 = (bf16[9,32,32]{2,1,0:T(8,128)(2,1)S(1)}, bf16[9,32,32]{2,1,0:T(8,128)(2,1)}, u32[]{:S(2)}) copy-start(bf16[9,32,32]{2,1,0:T(8,128)(2,1)} %w_mid.1) | copy-start | bytes 55300
  37.7 10.7 %all-to-all-start.1 = ((f32[8,40,128]{2,1,0:T(8,128)}), f32[8,40,128]{2,1,0:T(8,128)S(1)}, u32[]{:S(2)}, u32[]{:S(2)}) async-start(f32[8,40,128]{2,1,0:T(8,128)} %sample_values.1), calls=%async_computation.1 | async-start | bytes 327680 | tf_op jit(solution)/shard_map/all_to_all | solution.py:433
  41.2 4.8 %collective-permute-start.2 = (bf16[1,4,8,256]{3,1,2,0:T(4,128)(2,1)S(1)}, bf16[1,4,8,256]{3,1,2,0:T(4,128)(2,1)S(1)}, u32[]{:S(2)}, u32[]{:S(2)}) collective-permute-start(bf16[1,4,8,256]{3,1,2,0:T(4,128)(2,1)S(1)} %copy.32), channel_id=1, source_target_pairs={{1,0},{2,1},{3,2},{4,3},{5,4},{6,5},{7,6},{9,8},{10,9},{11,10},{12... | collective-permute-start | bytes 49160 | tf_op jit(solution)/shard_map/ppermute | solution.py:411
  42.5 3.9 %collective-permute-start.1 = (bf16[1,4,8,256]{3,1,2,0:T(4,128)(2,1)S(1)}, bf16[1,4,8,256]{3,1,2,0:T(4,128)(2,1)S(1)}, u32[]{:S(2)}, u32[]{:S(2)}) collective-permute-start(bf16[1,4,8,256]{3,1,2,0:T(4,128)(2,1)S(1)} %copy.32), channel_id=1, source_target_pairs={{0,1},{1,2},{2,3},{3,4},{4,5},{5,6},{6,7},{8,9},{9,10},{10,11},{11... | collective-permute-start | bytes 49160 | tf_op jit(solution)/shard_map/ppermute | solution.py:410
  48.7 14.9 %collective-permute-start = (bf16[1,4,8,256]{3,2,1,0:T(8,128)(2,1)S(1)}, bf16[1,4,8,256]{3,2,1,0:T(8,128)(2,1)S(1)}, u32[]{:S(2)}, u32[]{:S(2)}) collective-permute-start(bf16[1,4,8,256]{3,2,1,0:T(8,128)(2,1)S(1)} %gbuffer.1), channel_id=1, source_target_pairs={{0,8},{8,16},{16,24},{24,0},{1,9},{9,17},{17,25},{25,1},{2,10},{10... | collective-permute-start | bytes 49160 | tf_op jit(solution)/shard_map/ppermute | solution.py:436

commit v2 on v1

--- a/solution.py
+++ b/solution.py
@@ -39,38 +39,22 @@
 
 def positions_kernel(cells_ref, fracs_ref, out_ref):
     owners, rows, _ = out_ref.shape
-    blocks = rows // 6
-    span = blocks * BLOCK
-
-    def one_owner(owner, carry):
-        for block in range(blocks):
-            start = pl.multiple_of(owner * span + block * BLOCK, BLOCK)
-            place = (
-                cells_ref[0, 0, :, pl.ds(start, BLOCK)].astype(F32)
-                + fracs_ref[0, 0, :, pl.ds(start, BLOCK)]
-            )
-            for axis in range(3):
-                for half in range(2):
-                    row = axis * 2 * blocks + half * blocks + block
-                    out_ref[owner, row : row + 1, :] = place[
-                        axis : axis + 1, half * LANES : (half + 1) * LANES
-                    ]
-        return carry
-
-    lax.fori_loop(0, owners, one_owner, 0)
+    lines = rows // 3
+    for axis in range(3):
+        place = cells_ref[axis].astype(F32) + fracs_ref[axis]
+        out_ref[:, axis * lines : (axis + 1) * lines, :] = place.reshape(owners, lines, LANES)
 
 
 def positions(cells, fracs, owners):
-    samples = cells.shape[3]
-    rows = 3 * samples // owners // LANES
+    lines = cells.shape[1]
     return pl.pallas_call(
         positions_kernel,
-        out_shape=jax.ShapeDtypeStruct((owners, rows, LANES), F32),
+        out_shape=jax.ShapeDtypeStruct((owners, 3 * lines // owners, LANES), F32),
         in_specs=[vmem(), vmem()],
         out_specs=vmem(),
         compiler_params=params(),
         cost_estimate=pl.CostEstimate(
-            flops=3 * samples, bytes_accessed=36 * samples, transcendentals=0
+            flops=3 * lines * LANES, bytes_accessed=36 * lines * LANES, transcendentals=0
         ),
         name="positions",
     )(cells, fracs)
@@ -159,64 +143,65 @@
     return jnp.sum(total, axis=0, keepdims=True)
 
 
-def samples_kernel(picks_ref, brick_ref, place_ref, out_ref):
+def samples_kernel(picks_ref, brick_ref, place_ref, after_ref, out_ref, values):
     owners, rows, _ = place_ref.shape
     cap = picks_ref.shape[3]
-    blocks = rows // 6
-    per_slot = blocks // cap
+    lines = rows // 3
+    per_slot = lines // 2 // cap
 
     def one_slot(slot, carry):
         renderer = slot // cap
         piece = slot % cap
         brick = brick_ref[picks_ref[0, 0, renderer, piece]]
         for step in range(per_slot):
-            row = piece * per_slot + step
+            row = 2 * (piece * per_slot + step)
 
             def line(axis):
                 both = [
-                    place_ref[renderer, pl.ds((2 * axis + half) * blocks + row, 1), :]
+                    place_ref[renderer, pl.ds(axis * lines + row + half, 1), :]
                     for half in range(2)
                 ]
                 return jnp.concatenate(both, axis=1)
 
             value = blend(brick, line(0), line(1), line(2))
             for half in range(2):
-                out_ref[renderer, pl.ds(half * blocks + row, 1), :] = value[
+                values[renderer, pl.ds(row + half, 1), :] = value[
                     :, half * LANES : (half + 1) * LANES
                 ]
         return carry
 
     lax.fori_loop(0, owners * cap, one_slot, 0)
-
-
-def sample_values(picks, windows, places):
+    out_ref[...] = values[...].astype(BF16)
+
+
+def sample_values(picks, windows, places, after):
     owners, rows, _ = places.shape
     samples = owners * rows * LANES // 3
+    shape = (owners, rows // 3, LANES)
     return pl.pallas_call(
         samples_kernel,
-        out_shape=jax.ShapeDtypeStruct((owners, rows // 3, LANES), F32),
-        in_specs=[smem(), vmem(), vmem()],
+        out_shape=jax.ShapeDtypeStruct(shape, BF16),
+        in_specs=[smem(), vmem(), vmem(), pl.BlockSpec(memory_space=pltpu.HBM)],
         out_specs=vmem(),
+        scratch_shapes=[pltpu.VMEM(shape, F32)],
         compiler_params=params(),
         cost_estimate=pl.CostEstimate(
             flops=2 * samples * KDIM * BRICK_ROWS, bytes_accessed=3 * 1024 * 1024,
             transcendentals=0,
         ),
         name="sample_values",
-    )(picks, windows, places)
-
-
-def gbuffer_kernel(value_ref, order_ref, out_ref, low, high):
-    groups, rows, _ = value_ref.shape
-    blocks = rows // 2
-    for group in range(groups):
-        low[group * blocks : (group + 1) * blocks, :] = value_ref[group, :blocks, :]
-        high[group * blocks : (group + 1) * blocks, :] = value_ref[group, blocks:, :]
+    )(picks, windows, places, after)
+
+
+def gbuffer_kernel(value_ref, order_ref, out_ref, values):
+    values[...] = value_ref[...].astype(F32).reshape(values.shape)
     height = out_ref.shape[2]
 
     def ray_of(number):
         rows_now = slice(number * height, (number + 1) * height)
-        first, second = low[rows_now, :], high[rows_now, :]
+        first, second = (
+            values[pl.ds(2 * number * height + half, height, stride=2), :] for half in range(2)
+        )
         parts = []
         for half in range(2):
             order = order_ref[0, 0, rows_now, half * LANES : (half + 1) * LANES]
@@ -260,7 +245,7 @@
         out_shape=jax.ShapeDtypeStruct((1, 4, height, width), BF16),
         in_specs=[vmem(), vmem()],
         out_specs=vmem(),
-        scratch_shapes=[pltpu.VMEM((total, LANES), F32), pltpu.VMEM((total, LANES), F32)],
+        scratch_shapes=[pltpu.VMEM((2 * total, LANES), F32)],
         compiler_params=params(),
         cost_estimate=pl.CostEstimate(
             flops=20 * total * BLOCK, bytes_accessed=8 * total * BLOCK, transcendentals=0
@@ -390,20 +375,15 @@
     padded = -(-per_slot // BLOCK) * BLOCK
 
     def fill(part):
-        if padded == per_slot:
-            return part
-        part = part.reshape(1, 1, 3, slots, per_slot)
-        part = jnp.pad(part, ((0, 0),) * 4 + ((0, padded - per_slot),))
-        return part.reshape(1, 1, 3, slots * padded)
+        if padded != per_slot:
+            part = part.reshape(3, slots, per_slot)
+            part = jnp.pad(part, ((0, 0), (0, 0), (0, padded - per_slot)))
+        return part.reshape(3, slots * padded // LANES, LANES)
 
     def trim(found):
         if padded == per_slot:
             return found
-        rows = found.shape[1] // 2
-        flat = found.reshape(n_tile, 2, rows, LANES).transpose(0, 2, 1, 3)
-        flat = flat.reshape(slots, padded)[:, :per_slot]
-        flat = flat.reshape(1, samples // BLOCK, 2, LANES).transpose(0, 2, 1, 3)
-        return flat.reshape(1, samples // LANES, LANES)
+        return found.reshape(slots, padded)[:, :per_slot].reshape(1, samples // LANES, LANES)
 
     down = [(i, i + 1) for i in range(n_tile - 1)]
     up = [(i + 1, i) for i in range(n_tile - 1)]
@@ -429,7 +409,7 @@
         colours,
     )
 
-    found = sample_values(sends, windows, arrived)
+    found = sample_values(sends, windows, arrived, denoised)
     values = lax.all_to_all(found, "tile", split_axis=0, concat_axis=0, tiled=True)
     rendered = gbuffer(trim(values), sample_order, height, width)
     ring = [(i, (i + 1) % n_section) for i in range(n_section)]

time: 64.6 us -> 63.8 us (0.988)
  blocking collectives: 0 us -> 12.3 us
  waiting for transfers between devices: 11.7 us -> 3.12 us
  starting transfers between devices: 15.7 us -> 12.2 us
  Pallas kernels: 27 us -> 25.8 us
    all_to_all x0 -> x1, blocking collectives: none -> 12.3 us  [on_device(): lax.all_to_all(found, 'tile', split_axis=0, concat_axis=0, tiled=True)]
    all_to_all x1, waiting for transfers between devices: 9.48 us -> 0.01 us  [on_device(): lax.all_to_all(places, 'tile', split_axis=0, concat_axis=0, tiled=True)]
    all_to_all x1 -> x0, starting transfers between devices: 3.51 us -> none  [on_device(): lax.all_to_all(found, 'tile', split_axis=0, concat_axis=0, tiled=True)]
    ppermute x1, waiting for transfers between devices: 0.01 us -> 3.11 us  [on_device(): handoff = lax.ppermute(rendered, 'section', ring)]
    all_to_all x1 -> x0, waiting for transfers between devices: 1.94 us -> none  [on_device(): lax.all_to_all(found, 'tile', split_axis=0, concat_axis=0, tiled=True)]
    pallas_call x1, Pallas kernels: 10.7 us -> 9.95 us  [sample_values(): pl.pallas_call(samples_kernel, out_shape=jax.ShapeDtypeStruct(shape, BF16...]
    unnamed x31 -> x35, local copies, waits for them, and re-layouts: 6.49 us -> 6.55 us
  transfers between devices with their start and end apart: 5 -> 4, of which waited for: 3 -> 1; matrix products, arithmetic and copies ran while one was open for 5% -> 5% of each run, Pallas kernels for 23% -> 23%
where the time goes in v2:
time: 63.8 us; the launch traced here: 63.3 us
  Pallas kernels  25.8 us (40%)
  blocking collectives  12.3 us (19%)
  starting transfers between devices  12.2 us (19%)
  local copies, waits for them, and re-layouts  8.93 us (14%)
  waiting for transfers between devices  3.12 us (5%)
  between operations  0.84 us (1%)
    pallas_call x1, Pallas kernels, unet(): pl.pallas_call(unet_kernel, out_shape=jax.ShapeDtypeStruct((1, colours, h...  13.3 us
    all_to_all x1, blocking collectives, on_device(): lax.all_to_all(found, 'tile', split_axis=0, concat_axis=0, tiled=True)  12.3 us
    pallas_call x1, Pallas kernels, sample_values(): pl.pallas_call(samples_kernel, out_shape=jax.ShapeDtypeStruct(shape, BF16...  9.95 us
    unnamed x35, local copies, waits for them, and re-layouts  6.55 us
    all_to_all x1, starting transfers between devices, on_device(): lax.all_to_all(places, 'tile', split_axis=0, concat_axis=0, tiled=True)  6.33 us
    ppermute x1, waiting for transfers between devices, on_device(): handoff = lax.ppermute(rendered, 'section', ring)  3.11 us
    ppermute x1, starting transfers between devices, on_device(): over = lax.ppermute(pending, 'tile', down)  3.03 us
    reshape x1, local copies, waits for them, and re-layouts, windows_of(): cube = bricks.reshape(count, EDGE, EDGE * EDGE)  2.33 us
  transfers between devices with their start and end apart: 4, of which 1 were waited for; matrix products, arithmetic and copies ran while one was open for 5% of the time, Pallas kernels for 23%

profile of v2, /device:TPU:0, one launch (start us, length us, event | category | flops | bytes accessed | tf_op | source)
XLA Modules:
  0.0 63.3 jit_solution(5283211032898607678)
XLA Ops:
  0.6 1.0 %copy-done = s32[1,1,3,40960]{3,1,2,0:T(1,128)S(1)} copy-done((s32[1,1,3,40960]{3,1,2,0:T(1,128)S(1)}, s32[1,1,3,40960]{3,1,2,0:T(1,128)}, u32[]{:S(2)}) %copy-start) | copy-done | bytes 491544
  1.7 1.0 %copy-done.1 = f32[1,1,3,40960]{3,1,2,0:T(1,128)S(1)} copy-done((f32[1,1,3,40960]{3,1,2,0:T(1,128)S(1)}, f32[1,1,3,40960]{3,1,2,0:T(1,128)}, u32[]{:S(2)}) %copy-start.1) | copy-done | bytes 491544
  2.7 0.8 %positions.1 = f32[8,120,128]{2,1,0:T(8,128)} custom-call(s32[3,320,128]{2,1,0:T(8,128)S(1)} %bitcast.10, f32[3,320,128]{2,1,0:T(8,128)S(1)} %bitcast.11), custom_call_target="tpu_custom_call" | custom-call | flops 122880 | bytes 1474560 | tf_op jit(solution)/shard_map/positions/pallas_call | solution.py:50
  3.5 6.3 %all-to-all-start = ((f32[8,120,128]{2,1,0:T(8,128)}), f32[8,120,128]{2,1,0:T(8,128)S(1)}, u32[]{:S(2)}, u32[]{:S(2)}) async-start(f32[8,120,128]{2,1,0:T(8,128)} %positions.1), calls=%async_computation | async-start | bytes 983040 | tf_op jit(solution)/shard_map/all_to_all | solution.py:393
  9.9 1.3 %collective-permute-start.1 = (bf16[1,4,8,256]{3,1,2,0:T(4,128)(2,1)S(1)}, bf16[1,4,8,256]{3,1,2,0:T(4,128)(2,1)S(1)}, u32[]{:S(2)}, u32[]{:S(2)}) collective-permute-start(bf16[1,4,8,256]{3,1,2,0:T(4,128)(2,1)S(1)} %copy.28), channel_id=1, source_target_pairs={{1,0},{2,1},{3,2},{4,3},{5,4},{6,5},{7,6},{9,8},{10,9},{11,10},{12... | collective-permute-start | bytes 49160 | tf_op jit(solution)/shard_map/ppermute | solution.py:391
  11.2 3.0 %collective-permute-start = (bf16[1,4,8,256]{3,1,2,0:T(4,128)(2,1)S(1)}, bf16[1,4,8,256]{3,1,2,0:T(4,128)(2,1)S(1)}, u32[]{:S(2)}, u32[]{:S(2)}) collective-permute-start(bf16[1,4,8,256]{3,1,2,0:T(4,128)(2,1)S(1)} %copy.28), channel_id=1, source_target_pairs={{0,1},{1,2},{2,3},{3,4},{4,5},{5,6},{6,7},{8,9},{9,10},{10,11},{11... | collective-permute-start | bytes 49160 | tf_op jit(solution)/shard_map/ppermute | solution.py:390
  14.2 2.3 %reshape.13.cube_ref = bf16[16,34,1156]{2,1,0:T(8,128)(2,1)S(1)} reshape(bf16[16,39304]{1,0:T(8,128)(2,1)S(1)} %copy-done.9) | data formatting | bytes 2515456 | tf_op jit(solution)/shard_map/reshape | solution.py:97
  16.6 0.1 pad_add_fusion.where_ref
  16.7 0.0 copy-start.3
  16.7 0.0 copy-start.4
  16.7 1.5 %brick_windows.1.brick_ref = bf16[16,208,256]{2,1,0:T(8,128)(2,1)S(1)} custom-call(bf16[16,34,1156]{2,1,0:T(8,128)(2,1)S(1)} %reshape.13.cube_ref), custom_call_target="tpu_custom_call" | custom-call | flops 905969664 | bytes 4194304 | tf_op jit(solution)/shard_map/brick_windows/pallas_call | solution.py:98
  18.2 1.2 %copy-done.6 = bf16[16,208,256]{2,1,0:T(8,128)(2,1)} copy-done((bf16[16,208,256]{2,1,0:T(8,128)(2,1)}, bf16[16,208,256]{2,1,0:T(8,128)(2,1)S(1)}, u32[]{:S(2)}) %copy-start.6) | copy-done | bytes 1703960
  19.5 0.1 copy.25.picks_ref
  19.5 0.1 copy.23
  19.7 0.2 copy.24.w_down
  20.1 13.3 %unet.1.after_ref = bf16[1,3,8,256]{3,2,1,0:T(8,128)(2,1)} custom-call(s32[2]{0:T(128)S(1)} %pad_add_fusion.where_ref, bf16[24,16,256]{2,1,0:T(8,128)(2,1)S(1)} %pad.12.x_ref, bf16[9,32,16]{2,1,0:T(8,128)(2,1)S(1)} %pad.13.w_in, bf16[9,32,32]{2,1,0:T(8,128)(2,1)S(1)} %copy-done.5, bf16[9,112,32]{2,1,0:T(8,128)(2,1)S(1)} %copy.24.w_down, ...), custom_call_target="tpu_custom_call" | custom-call | flops 3000000000 | bytes 2097152 | tf_op jit(solution)/shard_map/unet/pallas_call | solution.py:340
  33.4 1.5 %copy-done.7 = bf16[16,208,256]{2,1,0:T(8,128)(2,1)S(1)} copy-done((bf16[16,208,256]{2,1,0:T(8,128)(2,1)S(1)}, bf16[16,208,256]{2,1,0:T(8,128)(2,1)}, u32[]{:S(2)}) %copy-start.7) | copy-done | bytes 1703960
  34.9 0.7 %copy-done.8 = bf16[1,3,8,256]{3,2,1,0:T(8,128)(2,1)S(1)} copy-done((bf16[1,3,8,256]{3,2,1,0:T(8,128)(2,1)S(1)}, bf16[1,3,8,256]{3,2,1,0:T(8,128)(2,1)}, u32[]{:S(2)}) %copy-start.8) | copy-done | bytes 12312
  35.6 9.9 %sample_values.1 = bf16[8,40,128]{2,1,0:T(8,128)(2,1)S(1)} custom-call(s32[1,1,8,2]{3,2,1,0:T(8,128)S(1)} %copy.25.picks_ref, bf16[16,208,256]{2,1,0:T(8,128)(2,1)S(1)} %copy-done.7, f32[8,120,128]{2,1,0:T(8,128)S(1)} %all-to-all-done.place_ref, bf16[1,3,8,256]{3,2,1,0:T(8,128)(2,1)S(1)} %copy-done.8), custom_call_target="tpu_custom_call" | custom-call | flops 4362076160 | bytes 3145728 | tf_op jit(solution)/shard_map/sample_values/pallas_call | solution.py:181
  45.6 12.3 %all_to_all.10.value_ref = bf16[8,40,128]{2,1,0:T(8,128)(2,1)S(1)} all-to-all(bf16[8,40,128]{2,1,0:T(8,128)(2,1)S(1)} %sample_values.1), channel_id=1, replica_groups=mesh['section'=4,'tile'=8] {'tile'}, dimensions={0} | all-to-all | bytes 163840 | tf_op jit(solution)/shard_map/all_to_all | solution.py:413
  57.8 0.2 gbuffer.1
  58.0 1.6 %collective-permute-start.2 = (bf16[1,4,8,256]{3,2,1,0:T(8,128)(2,1)S(1)}, bf16[1,4,8,256]{3,2,1,0:T(8,128)(2,1)S(1)}, u32[]{:S(2)}, u32[]{:S(2)}) collective-permute-start(bf16[1,4,8,256]{3,2,1,0:T(8,128)(2,1)S(1)} %gbuffer.1), channel_id=1, source_target_pairs={{0,8},{8,16},{16,24},{24,0},{1,9},{9,17},{17,25},{25,1},{2,10},{10... | collective-permute-start | bytes 49160 | tf_op jit(solution)/shard_map/ppermute | solution.py:416
  59.6 3.1 %collective-permute-done.2 = bf16[1,4,8,256]{3,2,1,0:T(8,128)(2,1)S(1)} collective-permute-done((bf16[1,4,8,256]{3,2,1,0:T(8,128)(2,1)S(1)}, bf16[1,4,8,256]{3,2,1,0:T(8,128)(2,1)S(1)}, u32[]{:S(2)}, u32[]{:S(2)}) %collective-permute-start.2) | collective-permute-done | bytes 16416 | tf_op jit(solution)/shard_map/ppermute | solution.py:416
  62.7 0.6 copy.30
  (31 shorter events, 0.2 us)
Async XLA Ops:
  0.6 1.0 %copy-start = (s32[1,1,3,40960]{3,1,2,0:T(1,128)S(1)}, s32[1,1,3,40960]{3,1,2,0:T(1,128)}, u32[]{:S(2)}) copy-start(s32[1,1,3,40960]{3,1,2,0:T(1,128)} %param.14) | copy-start | bytes 1474564
  1.7 1.0 %copy-start.1 = (f32[1,1,3,40960]{3,1,2,0:T(1,128)S(1)}, f32[1,1,3,40960]{3,1,2,0:T(1,128)}, u32[]{:S(2)}) copy-start(f32[1,1,3,40960]{3,1,2,0:T(1,128)} %param.15) | copy-start | bytes 1474564
  2.7 7.2 %copy-start.11 = (bf16[1,4,8,256]{3,2,1,0:T(8,128)(2,1)S(1)}, bf16[1,4,8,256]{3,2,1,0:T(8,128)(2,1)}, u32[]{:S(2)}) copy-start(bf16[1,4,8,256]{3,2,1,0:T(8,128)(2,1)} %param.17) | copy-start | bytes 49156
  2.7 11.5 %copy-start.9 = (bf16[16,39304]{1,0:T(8,128)(2,1)S(1)}, bf16[16,39304]{1,0:T(8,128)(2,1)}, u32[]{:S(2)}) copy-start(bf16[16,39304]{1,0:T(8,128)(2,1)} %param.12) | copy-start | bytes 3773188
  3.5 29.9 %all-to-all-start = ((f32[8,120,128]{2,1,0:T(8,128)}), f32[8,120,128]{2,1,0:T(8,128)S(1)}, u32[]{:S(2)}, u32[]{:S(2)}) async-start(f32[8,120,128]{2,1,0:T(8,128)} %positions.1), calls=%async_computation | async-start | bytes 983040 | tf_op jit(solution)/shard_map/all_to_all | solution.py:393
  9.9 10.1 %collective-permute-start.1 = (bf16[1,4,8,256]{3,1,2,0:T(4,128)(2,1)S(1)}, bf16[1,4,8,256]{3,1,2,0:T(4,128)(2,1)S(1)}, u32[]{:S(2)}, u32[]{:S(2)}) collective-permute-start(bf16[1,4,8,256]{3,1,2,0:T(4,128)(2,1)S(1)} %copy.28), channel_id=1, source_target_pairs={{1,0},{2,1},{3,2},{4,3},{5,4},{6,5},{7,6},{9,8},{10,9},{11,10},{12... | collective-permute-start | bytes 49160 | tf_op jit(solution)/shard_map/ppermute | solution.py:391
  11.2 8.8 %collective-permute-start = (bf16[1,4,8,256]{3,1,2,0:T(4,128)(2,1)S(1)}, bf16[1,4,8,256]{3,1,2,0:T(4,128)(2,1)S(1)}, u32[]{:S(2)}, u32[]{:S(2)}) collective-permute-start(bf16[1,4,8,256]{3,1,2,0:T(4,128)(2,1)S(1)} %copy.28), channel_id=1, source_target_pairs={{0,1},{1,2},{2,3},{3,4},{4,5},{5,6},{6,7},{8,9},{9,10},{10,11},{11... | collective-permute-start | bytes 49160 | tf_op jit(solution)/shard_map/ppermute | solution.py:390
  16.6 2.8 %copy-start.14 = (s32[1,1,8,2]{2,3,1,0:T(2,128)S(1)}, s32[1,1,8,2]{2,3,1,0:T(2,128)}, u32[]{:S(2)}) copy-start(s32[1,1,8,2]{2,3,1,0:T(2,128)} %param.13) | copy-start | bytes 196
  16.7 2.9 %copy-start.12 = (bf16[9,32,4]{1,2,0:T(4,128)(2,1)S(1)}, bf16[9,32,4]{1,2,0:T(4,128)(2,1)}, u32[]{:S(2)}) copy-start(bf16[9,32,4]{1,2,0:T(4,128)(2,1)} %param.18) | copy-start | bytes 6916
  16.7 3.0 %copy-start.10 = (bf16[9,112,32]{1,2,0:T(8,128)(2,1)S(1)}, bf16[9,112,32]{1,2,0:T(8,128)(2,1)}, u32[]{:S(2)}) copy-start(bf16[9,112,32]{1,2,0:T(8,128)(2,1)} %param.20) | copy-start | bytes 193540
  16.7 3.3 %copy-start.13 = (bf16[9,3,32]{2,1,0:T(4,128)(2,1)S(1)}, bf16[9,3,32]{2,1,0:T(4,128)(2,1)}, u32[]{:S(2)}) copy-start(bf16[9,3,32]{2,1,0:T(4,128)(2,1)} %param.23) | copy-start | bytes 5188
  16.7 3.4 %copy-start.3 = (bf16[9,112,112]{2,1,0:T(8,128)(2,1)S(1)}, bf16[9,112,112]{2,1,0:T(8,128)(2,1)}, u32[]{:S(2)}) copy-start(bf16[9,112,112]{2,1,0:T(8,128)(2,1)} %w_deep.1) | copy-start | bytes 677380
  16.7 3.4 %copy-start.4 = (bf16[9,32,144]{2,1,0:T(8,128)(2,1)S(1)}, bf16[9,32,144]{2,1,0:T(8,128)(2,1)}, u32[]{:S(2)}) copy-start(bf16[9,32,144]{2,1,0:T(8,128)(2,1)} %w_up.1) | copy-start | bytes 248836
  16.7 3.4 %copy-start.5 = (bf16[9,32,32]{2,1,0:T(8,128)(2,1)S(1)}, bf16[9,32,32]{2,1,0:T(8,128)(2,1)}, u32[]{:S(2)}) copy-start(bf16[9,32,32]{2,1,0:T(8,128)(2,1)} %w_mid.1) | copy-start | bytes 55300
  18.2 1.2 %copy-start.6 = (bf16[16,208,256]{2,1,0:T(8,128)(2,1)}, bf16[16,208,256]{2,1,0:T(8,128)(2,1)S(1)}, u32[]{:S(2)}) copy-start(bf16[16,208,256]{2,1,0:T(8,128)(2,1)S(1)} %brick_windows.1.brick_ref) | copy-start | bytes 5111812
  33.4 24.4 %copy-start.2 = (s32[1,1,160,256]{3,2,1,0:T(8,128)S(1)}, s32[1,1,160,256]{3,2,1,0:T(8,128)}, u32[]{:S(2)}) copy-start(s32[1,1,160,256]{3,2,1,0:T(8,128)} %order_ref.1) | copy-start | bytes 491524
  33.4 1.5 %copy-start.7 = (bf16[16,208,256]{2,1,0:T(8,128)(2,1)S(1)}, bf16[16,208,256]{2,1,0:T(8,128)(2,1)}, u32[]{:S(2)}) copy-start(bf16[16,208,256]{2,1,0:T(8,128)(2,1)} %copy-done.6) | copy-start | bytes 5111812
  34.9 0.7 %copy-start.8 = (bf16[1,3,8,256]{3,2,1,0:T(8,128)(2,1)S(1)}, bf16[1,3,8,256]{3,2,1,0:T(8,128)(2,1)}, u32[]{:S(2)}) copy-start(bf16[1,3,8,256]{3,2,1,0:T(8,128)(2,1)} %unet.1.after_ref) | copy-start | bytes 36868
  58.0 4.7 %collective-permute-start.2 = (bf16[1,4,8,256]{3,2,1,0:T(8,128)(2,1)S(1)}, bf16[1,4,8,256]{3,2,1,0:T(8,128)(2,1)S(1)}, u32[]{:S(2)}, u32[]{:S(2)}) collective-permute-start(bf16[1,4,8,256]{3,2,1,0:T(8,128)(2,1)S(1)} %gbuffer.1), channel_id=1, source_target_pairs={{0,8},{8,16},{16,24},{24,0},{1,9},{9,17},{17,25},{25,1},{2,10},{10... | collective-permute-start | bytes 49160 | tf_op jit(solution)/shard_map/ppermute | solution.py:416

commit v3 on v2

--- a/solution.py
+++ b/solution.py
@@ -22,11 +22,11 @@
 
 F32 = jnp.float32
 BF16 = jnp.bfloat16
-VMEM_LIMIT = 48 * 1024 * 1024
-
-
-def params():
-    return pltpu.CompilerParams(vmem_limit_bytes=VMEM_LIMIT)
+MIB = 1024 * 1024
+
+
+def params(mib):
+    return pltpu.CompilerParams(vmem_limit_bytes=mib * MIB)
 
 
 def vmem():
@@ -37,11 +37,21 @@
     return pl.BlockSpec(memory_space=pltpu.SMEM)
 
 
-def positions_kernel(cells_ref, fracs_ref, out_ref):
+def positions_kernel(cells_ref, fracs_ref, out_ref, cells, fracs, arrivals):
     owners, rows, _ = out_ref.shape
     lines = rows // 3
+    copies = []
     for axis in range(3):
-        place = cells_ref[axis].astype(F32) + fracs_ref[axis]
+        for number, (source, target) in enumerate(((cells_ref, cells), (fracs_ref, fracs))):
+            copy = pltpu.make_async_copy(
+                source.at[axis], target.at[axis], arrivals.at[2 * axis + number]
+            )
+            copy.start()
+            copies.append(copy)
+    for axis in range(3):
+        copies[2 * axis].wait()
+        copies[2 * axis + 1].wait()
+        place = cells[axis].astype(F32) + fracs[axis]
         out_ref[:, axis * lines : (axis + 1) * lines, :] = place.reshape(owners, lines, LANES)
 
 
@@ -50,9 +60,14 @@
     return pl.pallas_call(
         positions_kernel,
         out_shape=jax.ShapeDtypeStruct((owners, 3 * lines // owners, LANES), F32),
-        in_specs=[vmem(), vmem()],
+        in_specs=[pl.BlockSpec(memory_space=pltpu.HBM)] * 2,
         out_specs=vmem(),
-        compiler_params=params(),
+        scratch_shapes=[
+            pltpu.VMEM(cells.shape, jnp.int32),
+            pltpu.VMEM(fracs.shape, F32),
+            pltpu.SemaphoreType.DMA((6,)),
+        ],
+        compiler_params=params(12),
         cost_estimate=pl.CostEstimate(
             flops=3 * lines * LANES, bytes_accessed=36 * lines * LANES, transcendentals=0
         ),
@@ -104,7 +119,7 @@
             pltpu.VMEM((count, 48, 10 * LANES), BF16),
             pltpu.VMEM((count, TAIL, KDIM), F32),
         ],
-        compiler_params=params(),
+        compiler_params=params(16),
         cost_estimate=pl.CostEstimate(
             flops=2 * count * 48 * 384 * KDIM * WINDOWS, bytes_accessed=4 * 1024 * 1024,
             transcendentals=0,
@@ -121,13 +136,34 @@
     width = px.shape[1]
     places = lax.broadcasted_iota(jnp.int32, (MAIN, width), 0).astype(F32)
     eight = lax.broadcasted_iota(jnp.int32, (8, width), 0).astype(F32)
-    weight_y = hat(places - py)
+    places_low = places.astype(BF16)
+
+    def tile(line):
+        return jnp.broadcast_to(line, (TAIL, width)).astype(BF16)
+
+    cell_y = jnp.floor(py)
+    frac_y = py - cell_y
+    both = MAIN // TAIL
+    lower = jnp.concatenate([tile(cell_y)] * both, axis=0)
+    low_share = jnp.concatenate([tile(1.0 - frac_y)] * both, axis=0)
+    high_share = jnp.concatenate([tile(frac_y)] * both, axis=0)
+    nothing = jnp.zeros((MAIN, width), BF16)
+    offset = places_low - lower
+    weight_y = jnp.where(
+        offset == 0, low_share, jnp.where(offset == 1, high_share, nothing)
+    )
     weight_z = hat(places - pz)
     window = jnp.clip(jnp.floor(px * (1.0 / STRIDE)), 0.0, WINDOWS - 1.0)
     weight_x = hat(eight - (px - STRIDE * window))
-    parts = [(weight_y * weight_x[i : i + 1]).astype(BF16) for i in range(STRIDE + 1)]
-    parts.append((weight_x * hat(MAIN - py)).astype(BF16))
-    parts.append((weight_x * hat(MAIN + 1 - py)).astype(BF16))
+    parts = []
+    for i in range(STRIDE + 1):
+        share = tile(weight_x[i : i + 1])
+        parts.append(weight_y * jnp.concatenate([share] * both, axis=0))
+    parts.append(
+        jnp.concatenate(
+            [weight_x * hat(MAIN - py), weight_x * hat(MAIN + 1 - py)], axis=0
+        ).astype(BF16)
+    )
     parts.append(jnp.zeros((TAIL, width), BF16))
     plane = jnp.concatenate(parts, axis=0)
     found = jnp.dot(brick, plane, preferred_element_type=F32)
@@ -181,10 +217,10 @@
     return pl.pallas_call(
         samples_kernel,
         out_shape=jax.ShapeDtypeStruct(shape, BF16),
-        in_specs=[smem(), vmem(), vmem(), pl.BlockSpec(memory_space=pltpu.HBM)],
+        in_specs=[smem(), vmem(), vmem(), vmem()],
         out_specs=vmem(),
         scratch_shapes=[pltpu.VMEM(shape, F32)],
-        compiler_params=params(),
+        compiler_params=params(16),
         cost_estimate=pl.CostEstimate(
             flops=2 * samples * KDIM * BRICK_ROWS, bytes_accessed=3 * 1024 * 1024,
             transcendentals=0,
@@ -246,7 +282,7 @@
         in_specs=[vmem(), vmem()],
         out_specs=vmem(),
         scratch_shapes=[pltpu.VMEM((2 * total, LANES), F32)],
-        compiler_params=params(),
+        compiler_params=params(16),
         cost_estimate=pl.CostEstimate(
             flops=20 * total * BLOCK, bytes_accessed=8 * total * BLOCK, transcendentals=0
         ),
@@ -259,74 +295,136 @@
     return half + half * jnp.tanh(half)
 
 
-def conv_line(source, row, weight_ref, out_chans):
-    chans = weight_ref.shape[2]
-    total = None
-    for tap in range(3):
-        weight = weight_ref[3 * tap : 3 * tap + 3].reshape(3 * out_chans, chans)
-        part = jnp.dot(weight, source[row + tap], preferred_element_type=F32)
-        total = part if total is None else total + part
-    width = total.shape[1]
-    left, middle, right = (total[i * out_chans : (i + 1) * out_chans] for i in range(3))
-    lane = lax.broadcasted_iota(jnp.int32, (1, width), 1)
-    from_left = jnp.where(lane == 0, 0.0, pltpu.roll(left, 1, 1))
-    from_right = jnp.where(lane == width - 1, 0.0, pltpu.roll(right, width - 1, 1))
-    return middle + from_left + from_right
+def shifted(rows, steps):
+    lane = lax.broadcasted_iota(jnp.int32, (1, LANES), 1)
+    edge = lane == (0 if steps == 1 else LANES - 1)
+    moved = []
+    for row in rows:
+        tiles = [row[:, i : i + LANES] for i in range(0, row.shape[1], LANES)]
+        tiles = [pltpu.roll(tile, steps % LANES, 1) for tile in tiles]
+        for i, tile in enumerate(tiles):
+            source = i - steps
+            fill = tiles[source] if 0 <= source < len(tiles) else 0.0
+            moved.append(jnp.where(edge, fill, tile))
+    return jnp.concatenate(moved, axis=1)
+
+
+def across(total, chans, row_width):
+    left, middle, right = (total[i * chans : (i + 1) * chans] for i in range(3))
+
+    def rows_of(part):
+        return [part[:, i : i + row_width] for i in range(0, part.shape[1], row_width)]
+
+    return middle + shifted(rows_of(left), 1) + shifted(rows_of(right), -1)
+
+
+def taps(weight_ref, tap):
+    _, out_chans, chans = weight_ref.shape
+    return weight_ref[3 * tap : 3 * tap + 3].reshape(3 * out_chans, chans)
+
+
+def beside(weight_ref):
+    return jnp.concatenate([taps(weight_ref, tap) for tap in range(3)], axis=1)
 
 
 def unet_kernel(
-    where_ref, x_ref, w_in, w_mid, w_down, w_deep, w_up, w_out, out_ref,
+    where_ref, x_ref, w_in, w_mid, w_down, w_deep, w_up, w_out, out_ref, token_ref,
     first, second, pooled, third, fourth, joined, fifth, final,
 ):
     height = out_ref.shape[2]
     half_height = height // 2
     width = out_ref.shape[3]
+    half_width = width // 2
+    token_ref[...] = jnp.zeros_like(token_ref)
     above = jnp.where(where_ref[0] > 0, 1.0, 0.0)
     below = jnp.where(where_ref[0] < where_ref[1] - 1, 1.0, 0.0)
 
     def inside(row, low, high):
         return jnp.where(row < low, above, jnp.where(row >= high, below, 1.0))
 
-    def layer(source, weight_ref, target, low, high):
+    def full_layer(weight, source, target, low, high, unroll):
         chans = target.shape[1]
+        depth = weight.shape[1]
 
         def step(row, carry):
-            line = silu(conv_line(source, row, weight_ref, chans))
-            target[row] = (line * inside(row, low, high)).astype(BF16)
+            lines = source[pl.ds(row, 3)].reshape(depth, width)
+            line = across(jnp.dot(weight, lines, preferred_element_type=F32), chans, width)
+            target[row] = (silu(line) * inside(row, low, high)).astype(BF16)
             return carry
 
-        lax.fori_loop(0, target.shape[0], step, 0, unroll=2)
-
-    layer(x_ref, w_in, first, height - 1, 2 * height - 1)
-    layer(first, w_mid, second, height - 2, 2 * height - 2)
-
-    place = lax.broadcasted_iota(jnp.int32, (width, width // 2), 0) // 2
-    target = lax.broadcasted_iota(jnp.int32, (width, width // 2), 1)
+        lax.fori_loop(0, target.shape[0], step, 0, unroll=unroll)
+
+    full_layer(beside(w_in), x_ref, first, height - 1, 2 * height - 1, first.shape[0] // 2)
+    full_layer(beside(w_mid), first, second, height - 2, 2 * height - 2, second.shape[0] // 2)
+
+    place = lax.broadcasted_iota(jnp.int32, (width, half_width), 0) // 2
+    target = lax.broadcasted_iota(jnp.int32, (width, half_width), 1)
     shrink = jnp.where(place == target, 0.25, 0.0).astype(BF16)
     count, chans = second.shape[0], second.shape[1]
     pairs = jnp.dot(
         second[...].reshape(count * chans, width), shrink, preferred_element_type=F32
-    ).reshape(count // 2, 2, chans, width // 2)
+    ).reshape(count // 2, 2, chans, half_width)
     pooled[...] = (pairs[:, 0] + pairs[:, 1]).astype(BF16)
 
-    layer(pooled, w_down, third, half_height - 2, 2 * half_height - 2)
-    layer(third, w_deep, fourth, half_height - 3, 2 * half_height - 3)
-
-    place = lax.broadcasted_iota(jnp.int32, (width // 2, width), 0)
-    target = lax.broadcasted_iota(jnp.int32, (width // 2, width), 1) // 2
+    def half_pair(source, row, tap):
+        return jnp.concatenate([source[row + tap], source[row + tap + 1]], axis=1)
+
+    def half_layer(product, target, low, high):
+        chans = target.shape[1]
+        for row in range(0, target.shape[0], 2):
+            both = silu(across(product(row), chans, half_width))
+            for now in range(2):
+                line = both[:, now * half_width : (now + 1) * half_width]
+                if row + now < low or row + now >= high:
+                    line = line * inside(row + now, low, high)
+                target[row + now] = line.astype(BF16)
+
+    weight_down = beside(w_down)
+
+    def down_product(row):
+        lines = jnp.concatenate([half_pair(pooled, row, tap) for tap in range(3)], axis=0)
+        return jnp.dot(weight_down, lines, preferred_element_type=F32)
+
+    def deep_product(row):
+        total = None
+        for tap in range(3):
+            part = jnp.dot(
+                taps(w_deep, tap), half_pair(third, row, tap), preferred_element_type=F32
+            )
+            total = part if total is None else total + part
+        return total
+
+    half_layer(down_product, third, half_height - 2, 2 * half_height - 2)
+    half_layer(deep_product, fourth, half_height - 3, 2 * half_height - 3)
+
+    place = lax.broadcasted_iota(jnp.int32, (half_width, width), 0)
+    target = lax.broadcasted_iota(jnp.int32, (half_width, width), 1) // 2
     spread = jnp.where(place == target, 1.0, 0.0).astype(BF16)
     deep = fourth.shape[1]
-    for row in range(fourth.shape[0]):
-        wide = jnp.dot(fourth[row], spread, preferred_element_type=F32).astype(BF16)
-        for half in range(2):
-            joined[2 * row + half, chans:, :] = wide
-            joined[2 * row + half, :chans, :] = second[2 * row + half + 4]
-
-    layer(joined, w_up, fifth, 1, height + 1)
+    wide = jnp.dot(
+        fourth[...].reshape(-1, half_width), spread, preferred_element_type=F32
+    ).astype(BF16).reshape(fourth.shape[0], deep, width)
+    for row in range(2 * fourth.shape[0]):
+        joined[row, chans:, :] = wide[row // 2]
+        joined[row, :chans, :] = second[row + 4]
+
+    def up_step(row, carry):
+        total = None
+        for tap in range(3):
+            part = jnp.dot(taps(w_up, tap), joined[row + tap], preferred_element_type=F32)
+            total = part if total is None else total + part
+        line = silu(across(total, chans, width))
+        fifth[row] = (line * inside(row, 1, height + 1)).astype(BF16)
+        return carry
+
+    lax.fori_loop(0, fifth.shape[0], up_step, 0, unroll=fifth.shape[0] // 2)
 
     colours = out_ref.shape[1]
+    weight_out = beside(w_out)
     for row in range(height):
-        line = conv_line(fifth, row, w_out, w_out.shape[1])
+        lines = fifth[row : row + 3].reshape(3 * chans, width)
+        total = jnp.dot(weight_out, lines, preferred_element_type=F32)
+        line = across(total, w_out.shape[1], width)
         for colour in range(colours):
             final[colour, row : row + 1, :] = line[colour : colour + 1, :]
     out_ref[0] = final[...].astype(BF16)
@@ -339,9 +437,12 @@
     one, two = w_mid.shape[1], w_deep.shape[1]
     return pl.pallas_call(
         unet_kernel,
-        out_shape=jax.ShapeDtypeStruct((1, colours, height, width), BF16),
+        out_shape=(
+            jax.ShapeDtypeStruct((1, colours, height, width), BF16),
+            jax.ShapeDtypeStruct((8, LANES), F32),
+        ),
         in_specs=[smem()] + [vmem()] * 7,
-        out_specs=vmem(),
+        out_specs=(vmem(), vmem()),
         scratch_shapes=[
             pltpu.VMEM((3 * height - 2, one, width), BF16),
             pltpu.VMEM((3 * height - 4, one, width), BF16),
@@ -352,7 +453,7 @@
             pltpu.VMEM((height + 2, one, width), BF16),
             pltpu.VMEM((colours, height, width), F32),
         ],
-        compiler_params=params(),
+        compiler_params=params(20),
         cost_estimate=pl.CostEstimate(
             flops=3_000_000_000, bytes_accessed=2 * 1024 * 1024, transcendentals=500_000
         ),
@@ -397,7 +498,7 @@
     field = jnp.pad(field, ((0, 0), (0, 16 - field.shape[1]), (0, 0)))
     colours = w_out.shape[1]
     where = jnp.stack([tile, jnp.int32(n_tile)]).astype(jnp.int32)
-    denoised = unet(
+    denoised, token = unet(
         where,
         field,
         jnp.pad(w_in, ((0, 0), (0, 0), (0, 16 - w_in.shape[2]))),
@@ -409,7 +510,7 @@
         colours,
     )
 
-    found = sample_values(sends, windows, arrived, denoised)
+    found = sample_values(sends, windows, arrived, token)
     values = lax.all_to_all(found, "tile", split_axis=0, concat_axis=0, tiled=True)
     rendered = gbuffer(trim(values), sample_order, height, width)
     ring = [(i, (i + 1) % n_section) for i in range(n_section)]

time: 63.8 us -> 55.9 us (0.88)
  Pallas kernels: 25.8 us -> 18.6 us
  local copies, waits for them, and re-layouts: 8.93 us -> 8.19 us
    pallas_call x1, Pallas kernels: 13.3 us -> 5.74 us  [unet(): pl.pallas_call(unet_kernel, out_shape=(jax.ShapeDtypeStruct((1, colours,...]
    pallas_call x1, Pallas kernels: 0.84 us -> 2.15 us  [positions(): pl.pallas_call(positions_kernel, out_shape=jax.ShapeDtypeStruct((owners,...]
    pallas_call x1, Pallas kernels: 9.95 us -> 9 us  [sample_values(): pl.pallas_call(samples_kernel, out_shape=jax.ShapeDtypeStruct(shape, BF16...]
    unnamed x35 -> x33, local copies, waits for them, and re-layouts: 6.55 us -> 5.8 us
  transfers between devices with their start and end apart: 4 -> 4, of which waited for: 1 -> 1; matrix products, arithmetic and copies ran while one was open for 5% -> 5% of each run, Pallas kernels for 23% -> 13%
where the time goes in v3:
time: 55.9 us; the launch traced here: 55.5 us
  Pallas kernels  18.6 us (33%)
  blocking collectives  12.4 us (22%)
  starting transfers between devices  12.2 us (22%)
  local copies, waits for them, and re-layouts  8.19 us (15%)
  waiting for transfers between devices  3.14 us (6%)
  between operations  0.84 us (2%)
    all_to_all x1, blocking collectives, on_device(): lax.all_to_all(found, 'tile', split_axis=0, concat_axis=0, tiled=True)  12.4 us
    pallas_call x1, Pallas kernels, sample_values(): pl.pallas_call(samples_kernel, out_shape=jax.ShapeDtypeStruct(shape, BF16...  9 us
    all_to_all x1, starting transfers between devices, on_device(): lax.all_to_all(places, 'tile', split_axis=0, concat_axis=0, tiled=True)  6.34 us
    unnamed x33, local copies, waits for them, and re-layouts  5.8 us
    pallas_call x1, Pallas kernels, unet(): pl.pallas_call(unet_kernel, out_shape=(jax.ShapeDtypeStruct((1, colours,...  5.74 us
    ppermute x1, waiting for transfers between devices, on_device(): handoff = lax.ppermute(rendered, 'section', ring)  3.13 us
    ppermute x1, starting transfers between devices, on_device(): over = lax.ppermute(pending, 'tile', down)  3.03 us
    reshape x1, local copies, waits for them, and re-layouts, windows_of(): cube = bricks.reshape(count, EDGE, EDGE * EDGE)  2.33 us
  transfers between devices with their start and end apart: 4, of which 1 were waited for; matrix products, arithmetic and copies ran while one was open for 5% of the time, Pallas kernels for 13%

profile of v3, /device:TPU:0, one launch (start us, length us, event | category | flops | bytes accessed | tf_op | source)
XLA Modules:
  0.0 55.5 jit_solution(2138838338271637665)
XLA Ops:
  0.6 1.0 %copy-done = s32[1,1,3,40960]{3,1,2,0:T(1,128)S(1)} copy-done((s32[1,1,3,40960]{3,1,2,0:T(1,128)S(1)}, s32[1,1,3,40960]{3,1,2,0:T(1,128)}, u32[]{:S(2)}) %copy-start) | copy-done | bytes 491544
  1.7 1.0 %copy-done.1 = f32[1,1,3,40960]{3,1,2,0:T(1,128)S(1)} copy-done((f32[1,1,3,40960]{3,1,2,0:T(1,128)S(1)}, f32[1,1,3,40960]{3,1,2,0:T(1,128)}, u32[]{:S(2)}) %copy-start.1) | copy-done | bytes 491544
  2.7 2.2 %positions.1 = f32[8,120,128]{2,1,0:T(8,128)} custom-call(s32[3,320,128]{2,1,0:T(8,128)S(1)} %bitcast.10, f32[3,320,128]{2,1,0:T(8,128)S(1)} %bitcast.11), custom_call_target="tpu_custom_call" | custom-call | flops 122880 | bytes 1474560 | tf_op jit(solution)/shard_map/positions/pallas_call | solution.py:60
  4.9 6.3 %all-to-all-start = ((f32[8,120,128]{2,1,0:T(8,128)}), f32[8,120,128]{2,1,0:T(8,128)S(1)}, u32[]{:S(2)}, u32[]{:S(2)}) async-start(f32[8,120,128]{2,1,0:T(8,128)} %positions.1), calls=%async_computation | async-start | bytes 983040 | tf_op jit(solution)/shard_map/all_to_all | solution.py:494
  11.2 1.3 %collective-permute-start.1 = (bf16[1,4,8,256]{3,1,2,0:T(4,128)(2,1)S(1)}, bf16[1,4,8,256]{3,1,2,0:T(4,128)(2,1)S(1)}, u32[]{:S(2)}, u32[]{:S(2)}) collective-permute-start(bf16[1,4,8,256]{3,1,2,0:T(4,128)(2,1)S(1)} %copy.28), channel_id=1, source_target_pairs={{1,0},{2,1},{3,2},{4,3},{5,4},{6,5},{7,6},{9,8},{10,9},{11,10},{12... | collective-permute-start | bytes 49160 | tf_op jit(solution)/shard_map/ppermute | solution.py:492
  12.5 3.0 %collective-permute-start = (bf16[1,4,8,256]{3,1,2,0:T(4,128)(2,1)S(1)}, bf16[1,4,8,256]{3,1,2,0:T(4,128)(2,1)S(1)}, u32[]{:S(2)}, u32[]{:S(2)}) collective-permute-start(bf16[1,4,8,256]{3,1,2,0:T(4,128)(2,1)S(1)} %copy.28), channel_id=1, source_target_pairs={{0,1},{1,2},{2,3},{3,4},{4,5},{5,6},{6,7},{8,9},{9,10},{10,11},{11... | collective-permute-start | bytes 49160 | tf_op jit(solution)/shard_map/ppermute | solution.py:491
  15.6 2.3 %reshape.13.cube_ref = bf16[16,34,1156]{2,1,0:T(8,128)(2,1)S(1)} reshape(bf16[16,39304]{1,0:T(8,128)(2,1)S(1)} %copy-done.8) | data formatting | bytes 2515456 | tf_op jit(solution)/shard_map/reshape | solution.py:112
  17.9 0.1 pad_add_fusion.where_ref
  18.0 0.0 copy-start.3
  18.0 0.0 copy-start.4
  18.0 0.0 copy-start.5
  18.0 1.5 %brick_windows.1.brick_ref = bf16[16,208,256]{2,1,0:T(8,128)(2,1)S(1)} custom-call(bf16[16,34,1156]{2,1,0:T(8,128)(2,1)S(1)} %reshape.13.cube_ref), custom_call_target="tpu_custom_call" | custom-call | flops 905969664 | bytes 4194304 | tf_op jit(solution)/shard_map/brick_windows/pallas_call | solution.py:113
  19.6 1.2 %copy-done.6 = bf16[16,208,256]{2,1,0:T(8,128)(2,1)} copy-done((bf16[16,208,256]{2,1,0:T(8,128)(2,1)}, bf16[16,208,256]{2,1,0:T(8,128)(2,1)S(1)}, u32[]{:S(2)}) %copy-start.6) | copy-done | bytes 1703960
  20.8 0.1 copy.25.picks_ref
  20.9 0.1 copy.23
  21.0 0.2 copy.24.w_down
  21.4 5.7 %unet.1 = (bf16[1,3,8,256]{3,2,1,0:T(8,128)(2,1)}, f32[8,128]{1,0:T(8,128)S(1)}) custom-call(s32[2]{0:T(128)S(1)} %pad_add_fusion.where_ref, bf16[24,16,256]{2,1,0:T(8,128)(2,1)S(1)} %pad.12.x_ref, bf16[9,32,16]{2,1,0:T(8,128)(2,1)S(1)} %pad.13.w_in, bf16[9,32,32]{2,1,0:T(8,128)(2,1)S(1)} %copy-done.5, bf16[9,112,32]{2,1,0:T(8,128)(2,1)S(1)} %copy.24.w_down, ...), custom_call_target="tpu_custom_call" | custom-call | flops 3000000000 | bytes 2097152 | tf_op jit(solution)/shard_map/unet/pallas_call | solution.py:438
  27.2 1.5 %copy-done.7 = bf16[16,208,256]{2,1,0:T(8,128)(2,1)S(1)} copy-done((bf16[16,208,256]{2,1,0:T(8,128)(2,1)S(1)}, bf16[16,208,256]{2,1,0:T(8,128)(2,1)}, u32[]{:S(2)}) %copy-start.7) | copy-done | bytes 1703960
  28.6 9.0 %sample_values.1 = bf16[8,40,128]{2,1,0:T(8,128)(2,1)S(1)} custom-call(s32[1,1,8,2]{3,2,1,0:T(8,128)S(1)} %copy.25.picks_ref, bf16[16,208,256]{2,1,0:T(8,128)(2,1)S(1)} %copy-done.7, f32[8,120,128]{2,1,0:T(8,128)S(1)} %all-to-all-done.place_ref, f32[8,128]{1,0:T(8,128)S(1)} %get-tuple-element.4.after_ref), custom_call_target="tpu_custom_call" | custom-call | flops 4362076160 | bytes 3145728 | tf_op jit(solution)/shard_map/sample_values/pallas_call | solution.py:217
  37.6 12.4 %all_to_all.10.value_ref = bf16[8,40,128]{2,1,0:T(8,128)(2,1)S(1)} all-to-all(bf16[8,40,128]{2,1,0:T(8,128)(2,1)S(1)} %sample_values.1), channel_id=1, replica_groups=mesh['section'=4,'tile'=8] {'tile'}, dimensions={0} | all-to-all | bytes 163840 | tf_op jit(solution)/shard_map/all_to_all | solution.py:514
  50.0 0.2 gbuffer.1
  50.2 1.6 %collective-permute-start.2 = (bf16[1,4,8,256]{3,2,1,0:T(8,128)(2,1)S(1)}, bf16[1,4,8,256]{3,2,1,0:T(8,128)(2,1)S(1)}, u32[]{:S(2)}, u32[]{:S(2)}) collective-permute-start(bf16[1,4,8,256]{3,2,1,0:T(8,128)(2,1)S(1)} %gbuffer.1), channel_id=1, source_target_pairs={{0,8},{8,16},{16,24},{24,0},{1,9},{9,17},{17,25},{25,1},{2,10},{10... | collective-permute-start | bytes 49160 | tf_op jit(solution)/shard_map/ppermute | solution.py:517
  51.7 3.1 %collective-permute-done.2 = bf16[1,4,8,256]{3,2,1,0:T(8,128)(2,1)S(1)} collective-permute-done((bf16[1,4,8,256]{3,2,1,0:T(8,128)(2,1)S(1)}, bf16[1,4,8,256]{3,2,1,0:T(8,128)(2,1)S(1)}, u32[]{:S(2)}, u32[]{:S(2)}) %collective-permute-start.2) | collective-permute-done | bytes 16416 | tf_op jit(solution)/shard_map/ppermute | solution.py:517
  54.9 0.6 %copy.30 = bf16[1,4,8,256]{3,2,1,0:T(8,128)(2,1)} copy(bf16[1,4,8,256]{3,2,1,0:T(8,128)(2,1)S(1)} %collective-permute-done.2) | data formatting | bytes 32768
  (29 shorter events, 0.2 us)
Async XLA Ops:
  0.6 1.0 %copy-start = (s32[1,1,3,40960]{3,1,2,0:T(1,128)S(1)}, s32[1,1,3,40960]{3,1,2,0:T(1,128)}, u32[]{:S(2)}) copy-start(s32[1,1,3,40960]{3,1,2,0:T(1,128)} %param.14) | copy-start | bytes 1474564
  1.7 1.0 %copy-start.1 = (f32[1,1,3,40960]{3,1,2,0:T(1,128)S(1)}, f32[1,1,3,40960]{3,1,2,0:T(1,128)}, u32[]{:S(2)}) copy-start(f32[1,1,3,40960]{3,1,2,0:T(1,128)} %param.15) | copy-start | bytes 1474564
  2.7 8.5 %copy-start.10 = (bf16[1,4,8,256]{3,2,1,0:T(8,128)(2,1)S(1)}, bf16[1,4,8,256]{3,2,1,0:T(8,128)(2,1)}, u32[]{:S(2)}) copy-start(bf16[1,4,8,256]{3,2,1,0:T(8,128)(2,1)} %param.17) | copy-start | bytes 49156
  2.7 12.9 %copy-start.8 = (bf16[16,39304]{1,0:T(8,128)(2,1)S(1)}, bf16[16,39304]{1,0:T(8,128)(2,1)}, u32[]{:S(2)}) copy-start(bf16[16,39304]{1,0:T(8,128)(2,1)} %param.12) | copy-start | bytes 3773188
  4.9 22.3 %all-to-all-start = ((f32[8,120,128]{2,1,0:T(8,128)}), f32[8,120,128]{2,1,0:T(8,128)S(1)}, u32[]{:S(2)}, u32[]{:S(2)}) async-start(f32[8,120,128]{2,1,0:T(8,128)} %positions.1), calls=%async_computation | async-start | bytes 983040 | tf_op jit(solution)/shard_map/all_to_all | solution.py:494
  11.2 10.1 %collective-permute-start.1 = (bf16[1,4,8,256]{3,1,2,0:T(4,128)(2,1)S(1)}, bf16[1,4,8,256]{3,1,2,0:T(4,128)(2,1)S(1)}, u32[]{:S(2)}, u32[]{:S(2)}) collective-permute-start(bf16[1,4,8,256]{3,1,2,0:T(4,128)(2,1)S(1)} %copy.28), channel_id=1, source_target_pairs={{1,0},{2,1},{3,2},{4,3},{5,4},{6,5},{7,6},{9,8},{10,9},{11,10},{12... | collective-permute-start | bytes 49160 | tf_op jit(solution)/shard_map/ppermute | solution.py:492
  12.5 8.8 %collective-permute-start = (bf16[1,4,8,256]{3,1,2,0:T(4,128)(2,1)S(1)}, bf16[1,4,8,256]{3,1,2,0:T(4,128)(2,1)S(1)}, u32[]{:S(2)}, u32[]{:S(2)}) collective-permute-start(bf16[1,4,8,256]{3,1,2,0:T(4,128)(2,1)S(1)} %copy.28), channel_id=1, source_target_pairs={{0,1},{1,2},{2,3},{3,4},{4,5},{5,6},{6,7},{8,9},{9,10},{10,11},{11... | collective-permute-start | bytes 49160 | tf_op jit(solution)/shard_map/ppermute | solution.py:491
  18.0 2.8 %copy-start.13 = (s32[1,1,8,2]{2,3,1,0:T(2,128)S(1)}, s32[1,1,8,2]{2,3,1,0:T(2,128)}, u32[]{:S(2)}) copy-start(s32[1,1,8,2]{2,3,1,0:T(2,128)} %param.13) | copy-start | bytes 196
  18.0 2.9 %copy-start.11 = (bf16[9,32,4]{1,2,0:T(4,128)(2,1)S(1)}, bf16[9,32,4]{1,2,0:T(4,128)(2,1)}, u32[]{:S(2)}) copy-start(bf16[9,32,4]{1,2,0:T(4,128)(2,1)} %param.18) | copy-start | bytes 6916
  18.0 3.0 %copy-start.9 = (bf16[9,112,32]{1,2,0:T(8,128)(2,1)S(1)}, bf16[9,112,32]{1,2,0:T(8,128)(2,1)}, u32[]{:S(2)}) copy-start(bf16[9,112,32]{1,2,0:T(8,128)(2,1)} %param.20) | copy-start | bytes 193540
  18.0 3.3 %copy-start.12 = (bf16[9,3,32]{2,1,0:T(4,128)(2,1)S(1)}, bf16[9,3,32]{2,1,0:T(4,128)(2,1)}, u32[]{:S(2)}) copy-start(bf16[9,3,32]{2,1,0:T(4,128)(2,1)} %param.23) | copy-start | bytes 5188
  18.0 3.4 %copy-start.3 = (bf16[9,112,112]{2,1,0:T(8,128)(2,1)S(1)}, bf16[9,112,112]{2,1,0:T(8,128)(2,1)}, u32[]{:S(2)}) copy-start(bf16[9,112,112]{2,1,0:T(8,128)(2,1)} %w_deep.1) | copy-start | bytes 677380
  18.0 3.4 %copy-start.4 = (bf16[9,32,144]{2,1,0:T(8,128)(2,1)S(1)}, bf16[9,32,144]{2,1,0:T(8,128)(2,1)}, u32[]{:S(2)}) copy-start(bf16[9,32,144]{2,1,0:T(8,128)(2,1)} %w_up.1) | copy-start | bytes 248836
  18.0 3.4 %copy-start.5 = (bf16[9,32,32]{2,1,0:T(8,128)(2,1)S(1)}, bf16[9,32,32]{2,1,0:T(8,128)(2,1)}, u32[]{:S(2)}) copy-start(bf16[9,32,32]{2,1,0:T(8,128)(2,1)} %w_mid.1) | copy-start | bytes 55300
  19.6 1.2 %copy-start.6 = (bf16[16,208,256]{2,1,0:T(8,128)(2,1)}, bf16[16,208,256]{2,1,0:T(8,128)(2,1)S(1)}, u32[]{:S(2)}) copy-start(bf16[16,208,256]{2,1,0:T(8,128)(2,1)S(1)} %brick_windows.1.brick_ref) | copy-start | bytes 5111812
  27.2 1.5 %copy-start.7 = (bf16[16,208,256]{2,1,0:T(8,128)(2,1)S(1)}, bf16[16,208,256]{2,1,0:T(8,128)(2,1)}, u32[]{:S(2)}) copy-start(bf16[16,208,256]{2,1,0:T(8,128)(2,1)} %copy-done.6) | copy-start | bytes 5111812
  28.6 21.4 %copy-start.2 = (s32[1,1,160,256]{3,2,1,0:T(8,128)S(1)}, s32[1,1,160,256]{3,2,1,0:T(8,128)}, u32[]{:S(2)}) copy-start(s32[1,1,160,256]{3,2,1,0:T(8,128)} %order_ref.1) | copy-start | bytes 491524
  50.2 4.7 %collective-permute-start.2 = (bf16[1,4,8,256]{3,2,1,0:T(8,128)(2,1)S(1)}, bf16[1,4,8,256]{3,2,1,0:T(8,128)(2,1)S(1)}, u32[]{:S(2)}, u32[]{:S(2)}) collective-permute-start(bf16[1,4,8,256]{3,2,1,0:T(8,128)(2,1)S(1)} %gbuffer.1), channel_id=1, source_target_pairs={{0,8},{8,16},{16,24},{24,0},{1,9},{9,17},{17,25},{25,1},{2,10},{10... | collective-permute-start | bytes 49160 | tf_op jit(solution)/shard_map/ppermute | solution.py:517

commit v4 on v3

--- a/solution.py
+++ b/solution.py
@@ -19,6 +19,7 @@
 TAIL = 16
 BRICK_ROWS = WINDOWS * MAIN + TAIL
 KDIM = 256
+RING = 8
 
 F32 = jnp.float32
 BF16 = jnp.bfloat16
@@ -67,7 +68,7 @@
             pltpu.VMEM(fracs.shape, F32),
             pltpu.SemaphoreType.DMA((6,)),
         ],
-        compiler_params=params(12),
+        compiler_params=params(60),
         cost_estimate=pl.CostEstimate(
             flops=3 * lines * LANES, bytes_accessed=36 * lines * LANES, transcendentals=0
         ),
@@ -75,7 +76,7 @@
     )(cells, fracs)
 
 
-def windows_kernel(cube_ref, out_ref, wide, tail):
+def windows_kernel(cube_ref, out_ref, wide, found_all, tail, departures):
     count = cube_ref.shape[0]
     plane = EDGE * EDGE
     wide[...] = jnp.zeros_like(wide)
@@ -87,6 +88,16 @@
     source = jnp.where(column < 7 * MAIN, main, last)
     unused = (column >= 7 * MAIN) & ((rest % 8 == 7) | (rest >= TAIL))
     source = jnp.where(unused, -(1 << 20), source)
+    copies = []
+
+    def send(start, size):
+        rows = pl.ds(start, size)
+        copy = pltpu.make_async_copy(
+            found_all.at[:, rows], out_ref.at[:, rows], departures.at[len(copies)]
+        )
+        copy.start()
+        copies.append(copy)
+
     for window in range(WINDOWS):
         first = window * STRIDE * EDGE
         low = first // LANES * LANES
@@ -99,29 +110,36 @@
             preferred_element_type=F32,
         )
         found = found.reshape(count, 48, KDIM)
-        out_ref[:, window * MAIN : (window + 1) * MAIN, :] = found[:, :MAIN, :].astype(BF16)
+        found_all[:, window * MAIN : (window + 1) * MAIN, :] = found[:, :MAIN, :].astype(BF16)
         tail[:, window : window + 1, :] = found[:, MAIN : MAIN + 1, :]
         tail[:, 8 + window : 9 + window, :] = found[:, MAIN + 1 : MAIN + 2, :]
+        send(window * MAIN, MAIN)
     for row in (6, 7, 14, 15):
         tail[:, row : row + 1, :] = jnp.zeros((count, 1, KDIM), F32)
-    out_ref[:, WINDOWS * MAIN :, :] = tail[...].astype(BF16)
+    found_all[:, WINDOWS * MAIN :, :] = tail[...].astype(BF16)
+    send(WINDOWS * MAIN, TAIL)
+    for copy in copies:
+        copy.wait()
 
 
 def windows_of(bricks):
     count = bricks.shape[0]
     cube = bricks.reshape(count, EDGE, EDGE * EDGE)
+    shape = (count, BRICK_ROWS, KDIM)
     return pl.pallas_call(
         windows_kernel,
-        out_shape=jax.ShapeDtypeStruct((count, BRICK_ROWS, KDIM), BF16),
+        out_shape=jax.ShapeDtypeStruct(shape, BF16),
         in_specs=[vmem()],
-        out_specs=vmem(),
+        out_specs=pl.BlockSpec(memory_space=pltpu.HBM),
         scratch_shapes=[
             pltpu.VMEM((count, 48, 10 * LANES), BF16),
+            pltpu.VMEM(shape, BF16),
             pltpu.VMEM((count, TAIL, KDIM), F32),
+            pltpu.SemaphoreType.DMA((WINDOWS + 1,)),
         ],
-        compiler_params=params(16),
+        compiler_params=params(60),
         cost_estimate=pl.CostEstimate(
-            flops=2 * count * 48 * 384 * KDIM * WINDOWS, bytes_accessed=4 * 1024 * 1024,
+            flops=2 * count * 48 * 384 * KDIM * WINDOWS, bytes_accessed=4 * MIB,
             transcendentals=0,
         ),
         name="brick_windows",
@@ -179,16 +197,30 @@
     return jnp.sum(total, axis=0, keepdims=True)
 
 
-def samples_kernel(picks_ref, brick_ref, place_ref, after_ref, out_ref, values):
+def samples_kernel(
+    picks_ref, brick_ref, place_ref, after_ref, out_ref, values, ring, arrivals
+):
     owners, rows, _ = place_ref.shape
-    cap = picks_ref.shape[3]
+    cap = picks_ref.shape[0]
+    slots = owners * cap
     lines = rows // 3
     per_slot = lines // 2 // cap
+
+    def fetch(slot):
+        held = slot % RING
+        return pltpu.make_async_copy(
+            brick_ref.at[picks_ref[slot % cap, slot // cap]], ring.at[held], arrivals.at[held]
+        )
+
+    for slot in range(RING):
+        fetch(slot).start()
 
     def one_slot(slot, carry):
         renderer = slot // cap
         piece = slot % cap
-        brick = brick_ref[picks_ref[0, 0, renderer, piece]]
+        held = slot % RING
+        fetch(slot).wait()
+        brick = ring[held]
         for step in range(per_slot):
             row = 2 * (piece * per_slot + step)
 
@@ -204,9 +236,14 @@
                 values[renderer, pl.ds(row + half, 1), :] = value[
                     :, half * LANES : (half + 1) * LANES
                 ]
+
+        @pl.when(slot + RING < slots)
+        def _():
+            fetch(slot + RING).start()
+
         return carry
 
-    lax.fori_loop(0, owners * cap, one_slot, 0)
+    lax.fori_loop(0, slots, one_slot, 0)
     out_ref[...] = values[...].astype(BF16)
 
 
@@ -217,12 +254,16 @@
     return pl.pallas_call(
         samples_kernel,
         out_shape=jax.ShapeDtypeStruct(shape, BF16),
-        in_specs=[smem(), vmem(), vmem(), vmem()],
+        in_specs=[smem(), pl.BlockSpec(memory_space=pltpu.HBM), vmem(), vmem()],
         out_specs=vmem(),
-        scratch_shapes=[pltpu.VMEM(shape, F32)],
-        compiler_params=params(16),
+        scratch_shapes=[
+            pltpu.VMEM(shape, F32),
+            pltpu.VMEM((RING, BRICK_ROWS, KDIM), BF16),
+            pltpu.SemaphoreType.DMA((RING,)),
+        ],
+        compiler_params=params(60),
         cost_estimate=pl.CostEstimate(
-            flops=2 * samples * KDIM * BRICK_ROWS, bytes_accessed=3 * 1024 * 1024,
+            flops=2 * samples * KDIM * BRICK_ROWS, bytes_accessed=3 * MIB,
             transcendentals=0,
         ),
         name="sample_values",
@@ -328,8 +369,8 @@
 
 
 def unet_kernel(
-    where_ref, x_ref, w_in, w_mid, w_down, w_deep, w_up, w_out, out_ref, token_ref,
-    first, second, pooled, third, fourth, joined, fifth, final,
+    where_ref, band_ref, w_in, w_mid, w_down, w_deep, w_up, w_out, out_ref, token_ref,
+    x_ref, first, second, pooled, third, fourth, joined, fifth, final,
 ):
     height = out_ref.shape[2]
     half_height = height // 2
@@ -353,6 +394,16 @@
             return carry
 
         lax.fori_loop(0, target.shape[0], step, 0, unroll=unroll)
+
+    tile = where_ref[0]
+    last = where_ref[1] - 1
+    inputs = band_ref.shape[1]
+    x_ref[...] = jnp.zeros_like(x_ref)
+    for part in range(3):
+        neighbour = jnp.clip(tile + part - 1, 0, last)
+        share = (above, 1.0, below)[part]
+        lines = band_ref[pl.ds(neighbour * height, height)].astype(F32) * share
+        x_ref[part * height : (part + 1) * height, :inputs, :] = lines.astype(BF16)
 
     full_layer(beside(w_in), x_ref, first, height - 1, 2 * height - 1, first.shape[0] // 2)
     full_layer(beside(w_mid), first, second, height - 2, 2 * height - 2, second.shape[0] // 2)
@@ -430,10 +481,9 @@
     out_ref[0] = final[...].astype(BF16)
 
 
-def unet(where, field, w_in, w_mid, w_down, w_deep, w_up, w_out, colours):
-    height = field.shape[0] // 3
+def unet(where, band, height, w_in, w_mid, w_down, w_deep, w_up, w_out, colours):
     half = height // 2
-    width = field.shape[2]
+    width = band.shape[2]
     one, two = w_mid.shape[1], w_deep.shape[1]
     return pl.pallas_call(
         unet_kernel,
@@ -444,6 +494,7 @@
         in_specs=[smem()] + [vmem()] * 7,
         out_specs=(vmem(), vmem()),
         scratch_shapes=[
+            pltpu.VMEM((3 * height, w_in.shape[2], width), BF16),
             pltpu.VMEM((3 * height - 2, one, width), BF16),
             pltpu.VMEM((3 * height - 4, one, width), BF16),
             pltpu.VMEM((3 * half - 2, one, width // 2), BF16),
@@ -458,7 +509,7 @@
             flops=3_000_000_000, bytes_accessed=2 * 1024 * 1024, transcendentals=500_000
         ),
         name="unet",
-    )(where, field, w_in, w_mid, w_down, w_deep, w_up, w_out)
+    )(where, band, w_in, w_mid, w_down, w_deep, w_up, w_out)
 
 
 def on_device(
@@ -486,21 +537,18 @@
             return found
         return found.reshape(slots, padded)[:, :per_slot].reshape(1, samples // LANES, LANES)
 
-    down = [(i, i + 1) for i in range(n_tile - 1)]
-    up = [(i + 1, i) for i in range(n_tile - 1)]
-    over = lax.ppermute(pending, "tile", down)
-    under = lax.ppermute(pending, "tile", up)
     places = positions(fill(cells), fill(fracs), n_tile)
     arrived = lax.all_to_all(places, "tile", split_axis=0, concat_axis=0, tiled=True)
 
+    own_rows = pending[0].transpose(1, 0, 2)
+    band = lax.all_gather(own_rows, "tile", axis=0, tiled=True)
     windows = windows_of(bricks)
-    field = jnp.concatenate([over[0], pending[0], under[0]], axis=1).transpose(1, 0, 2)
-    field = jnp.pad(field, ((0, 0), (0, 16 - field.shape[1]), (0, 0)))
     colours = w_out.shape[1]
     where = jnp.stack([tile, jnp.int32(n_tile)]).astype(jnp.int32)
     denoised, token = unet(
         where,
-        field,
+        band,
+        height,
         jnp.pad(w_in, ((0, 0), (0, 0), (0, 16 - w_in.shape[2]))),
         w_mid,
         w_down,
@@ -510,7 +558,7 @@
         colours,
     )
 
-    found = sample_values(sends, windows, arrived, token)
+    found = sample_values(sends[0, 0].T, windows, arrived, token)
     values = lax.all_to_all(found, "tile", split_axis=0, concat_axis=0, tiled=True)
     rendered = gbuffer(trim(values), sample_order, height, width)
     ring = [(i, (i + 1) % n_section) for i in range(n_section)]

time: 55.9 us -> 68.4 us (1.22)
  blocking collectives: 12.4 us -> 27.2 us
  Pallas kernels: 18.6 us -> 23.2 us
  starting transfers between devices: 12.2 us -> 7.85 us
  local copies, waits for them, and re-layouts: 8.19 us -> 5.67 us
    all_gather x0 -> x1, blocking collectives: none -> 17.4 us  [on_device(): band = lax.all_gather(own_rows, 'tile', axis=0, tiled=True)]
    ppermute x2 -> x0, starting transfers between devices: 4.32 us -> none  [the longest x1 3.03 us: on_device(): over = lax.ppermute(pending, 'tile', down)]
    unnamed x33 -> x26, local copies, waits for them, and re-layouts: 5.8 us -> 2.41 us
    all_to_all x1, blocking collectives: 12.4 us -> 9.81 us  [on_device(): lax.all_to_all(found, 'tile', split_axis=0, concat_axis=0, tiled=True)]
    pallas_call x1, Pallas kernels: 1.53 us -> 3.95 us  [windows_of(): pl.pallas_call(windows_kernel, out_shape=jax.ShapeDtypeStruct(shape, BF16...]
    pallas_call x1, Pallas kernels: 9 us -> 11.1 us  [sample_values(): pl.pallas_call(samples_kernel, out_shape=jax.ShapeDtypeStruct(shape, BF16...]
    reshape x1, local copies, waits for them, and re-layouts: 2.33 us -> 3.23 us  [windows_of(): cube = bricks.reshape(count, EDGE, EDGE * EDGE)]
  transfers between devices with their start and end apart: 4 -> 2, of which waited for: 1 -> 1; matrix products, arithmetic and copies ran while one was open for 5% -> 5% of each run, Pallas kernels for 13% -> 14%
where the time goes in v4:
time: 68.4 us; the launch traced here: 68 us
  blocking collectives  27.2 us (40%)
  Pallas kernels  23.2 us (34%)
  starting transfers between devices  7.85 us (11%)
  local copies, waits for them, and re-layouts  5.67 us (8%)
  waiting for transfers between devices  3.18 us (5%)
  between operations  0.76 us (1%)
    all_gather x1, blocking collectives, on_device(): band = lax.all_gather(own_rows, 'tile', axis=0, tiled=True)  17.4 us
    pallas_call x1, Pallas kernels, sample_values(): pl.pallas_call(samples_kernel, out_shape=jax.ShapeDtypeStruct(shape, BF16...  11.1 us
    all_to_all x1, blocking collectives, on_device(): lax.all_to_all(found, 'tile', split_axis=0, concat_axis=0, tiled=True)  9.81 us
    all_to_all x1, starting transfers between devices, on_device(): lax.all_to_all(places, 'tile', split_axis=0, concat_axis=0, tiled=True)  6.34 us
    pallas_call x1, Pallas kernels, unet(): pl.pallas_call(unet_kernel, out_shape=(jax.ShapeDtypeStruct((1, colours,...  5.76 us
    pallas_call x1, Pallas kernels, windows_of(): pl.pallas_call(windows_kernel, out_shape=jax.ShapeDtypeStruct(shape, BF16...  3.95 us
    reshape x1, local copies, waits for them, and re-layouts, windows_of(): cube = bricks.reshape(count, EDGE, EDGE * EDGE)  3.23 us
    ppermute x1, waiting for transfers between devices, on_device(): handoff = lax.ppermute(rendered, 'section', ring)  3.17 us
  transfers between devices with their start and end apart: 2, of which 1 were waited for; matrix products, arithmetic and copies ran while one was open for 5% of the time, Pallas kernels for 14%

profile of v4, /device:TPU:0, one launch (start us, length us, event | category | flops | bytes accessed | tf_op | source)
XLA Modules:
  0.0 68.0 jit_solution(6330830355782213703)
XLA Ops:
  0.6 0.0 copy-start.5
  0.6 2.2 %positions.1 = f32[8,120,128]{2,1,0:T(8,128)} custom-call(s32[3,320,128]{2,1,0:T(8,128)} %bitcast.11, f32[3,320,128]{2,1,0:T(8,128)} %bitcast.12), custom_call_target="tpu_custom_call" | custom-call | flops 122880 | bytes 1474560 | tf_op jit(solution)/shard_map/positions/pallas_call | solution.py:61
  2.9 6.3 %all-to-all-start = ((f32[8,120,128]{2,1,0:T(8,128)}), f32[8,120,128]{2,1,0:T(8,128)S(1)}, u32[]{:S(2)}, u32[]{:S(2)}) async-start(f32[8,120,128]{2,1,0:T(8,128)} %positions.1), calls=%async_computation | async-start | bytes 983040 | tf_op jit(solution)/shard_map/all_to_all | solution.py:541
  9.2 0.0 copy-start.9
  9.2 0.0 copy-start.7
  9.2 0.0 copy-done.5
  9.3 0.0 copy-start.10
  9.3 3.2 %reshape.13.cube_ref = bf16[16,34,1156]{2,1,0:T(8,128)(2,1)} reshape(bf16[16,39304]{1,0:T(8,128)(2,1)S(1)} %copy-done.5) | data formatting | bytes 2515456 | tf_op jit(solution)/shard_map/reshape | solution.py:127
  12.5 0.1 copy.21
  12.7 0.2 copy.22.w_down
  12.9 17.4 %all_gather.3.band_ref = bf16[64,4,256]{2,1,0:T(4,128)(2,1)S(1)} all-gather(bf16[8,4,256]{2,1,0:T(4,128)(2,1)S(1)} %bitcast.13), channel_id=1, replica_groups=mesh['section'=4,'tile'=8] {'tile'}, dimensions={0}, use_global_device_ids=true | all-gather | bytes 147456 | tf_op jit(solution)/shard_map/all_gather | solution.py:544
  30.4 4.0 %brick_windows.1.brick_ref = bf16[16,208,256]{2,1,0:T(8,128)(2,1)} custom-call(bf16[16,34,1156]{2,1,0:T(8,128)(2,1)} %reshape.13.cube_ref), custom_call_target="tpu_custom_call" | custom-call | flops 905969664 | bytes 4194304 | tf_op jit(solution)/shard_map/brick_windows/pallas_call | solution.py:129
  34.3 0.1 pad_add_fusion.where_ref
  34.4 0.0 copy-done.1
  34.4 5.8 %unet.1 = (bf16[1,3,8,256]{3,2,1,0:T(8,128)(2,1)}, f32[8,128]{1,0:T(8,128)S(1)}) custom-call(s32[2]{0:T(128)S(1)} %pad_add_fusion.where_ref, bf16[64,4,256]{2,1,0:T(4,128)(2,1)S(1)} %all_gather.3.band_ref, bf16[9,32,16]{2,1,0:T(8,128)(2,1)S(1)} %pad.8.w_in, bf16[9,32,32]{2,1,0:T(8,128)(2,1)S(1)} %copy-done.3, bf16[9,112,32]{2,1,0:T(8,128)(2,1)S(1)} %copy.22.w_down, ...), custom_call_target="tpu_custom_call" | custom-call | flops 3000000000 | bytes 2097152 | tf_op jit(solution)/shard_map/unet/pallas_call | solution.py:488
  40.2 0.6 copy-done.4
  40.8 0.0 all-to-all-done.place_ref
  40.8 0.8 %copy-done.6 = f32[8,120,128]{2,1,0:T(8,128)} copy-done((f32[8,120,128]{2,1,0:T(8,128)}, f32[8,120,128]{2,1,0:T(8,128)S(1)}, u32[]{:S(2)}) %copy-start.6) | copy-done | bytes 491544
  41.6 11.1 %sample_values.1 = bf16[8,40,128]{2,1,0:T(8,128)(2,1)} custom-call(s32[2,8]{1,0:T(2,128)} %bitcast.14, bf16[16,208,256]{2,1,0:T(8,128)(2,1)} %brick_windows.1.brick_ref, f32[8,120,128]{2,1,0:T(8,128)} %copy-done.6, f32[8,128]{1,0:T(8,128)} %copy-done.4), custom_call_target="tpu_custom_call" | custom-call | flops 4362076160 | bytes 3145728 | tf_op jit(solution)/shard_map/sample_values/pallas_call | solution.py:254
  52.7 9.8 %all_to_all.10.value_ref = bf16[8,40,128]{2,1,0:T(8,128)(2,1)S(1)} all-to-all(bf16[8,40,128]{2,1,0:T(8,128)(2,1)} %sample_values.1), channel_id=1, replica_groups=mesh['section'=4,'tile'=8] {'tile'}, dimensions={0} | all-to-all | bytes 163840 | tf_op jit(solution)/shard_map/all_to_all | solution.py:562
  62.5 0.2 gbuffer.1
  62.7 1.5 %collective-permute-start = (bf16[1,4,8,256]{3,2,1,0:T(8,128)(2,1)S(1)}, bf16[1,4,8,256]{3,2,1,0:T(8,128)(2,1)S(1)}, u32[]{:S(2)}, u32[]{:S(2)}) collective-permute-start(bf16[1,4,8,256]{3,2,1,0:T(8,128)(2,1)S(1)} %gbuffer.1), channel_id=1, source_target_pairs={{0,8},{8,16},{16,24},{24,0},{1,9},{9,17},{17,25},{25,1},{2,10},{10... | collective-permute-start | bytes 49160 | tf_op jit(solution)/shard_map/ppermute | solution.py:565
  64.2 3.2 %collective-permute-done = bf16[1,4,8,256]{3,2,1,0:T(8,128)(2,1)S(1)} collective-permute-done((bf16[1,4,8,256]{3,2,1,0:T(8,128)(2,1)S(1)}, bf16[1,4,8,256]{3,2,1,0:T(8,128)(2,1)S(1)}, u32[]{:S(2)}, u32[]{:S(2)}) %collective-permute-start) | collective-permute-done | bytes 16416 | tf_op jit(solution)/shard_map/ppermute | solution.py:565
  67.4 0.6 copy.26
  (17 shorter events, 0.1 us)
Async XLA Ops:
  0.6 8.6 %copy-start.5 = (bf16[16,39304]{1,0:T(8,128)(2,1)S(1)}, bf16[16,39304]{1,0:T(8,128)(2,1)}, u32[]{:S(2)}) copy-start(bf16[16,39304]{1,0:T(8,128)(2,1)} %param.12) | copy-start | bytes 3773188
  2.9 37.9 %all-to-all-start = ((f32[8,120,128]{2,1,0:T(8,128)}), f32[8,120,128]{2,1,0:T(8,128)S(1)}, u32[]{:S(2)}, u32[]{:S(2)}) async-start(f32[8,120,128]{2,1,0:T(8,128)} %positions.1), calls=%async_computation | async-start | bytes 983040 | tf_op jit(solution)/shard_map/all_to_all | solution.py:541
  9.2 3.3 %copy-start.8 = (bf16[1,4,8,256]{3,2,1,0:T(8,128)(2,1)S(1)}, bf16[1,4,8,256]{3,2,1,0:T(8,128)(2,1)}, u32[]{:S(2)}) copy-start(bf16[1,4,8,256]{3,2,1,0:T(8,128)(2,1)} %param.17) | copy-start | bytes 49156
  9.2 3.3 %copy-start.9 = (bf16[9,32,4]{1,2,0:T(4,128)(2,1)S(1)}, bf16[9,32,4]{1,2,0:T(4,128)(2,1)}, u32[]{:S(2)}) copy-start(bf16[9,32,4]{1,2,0:T(4,128)(2,1)} %param.18) | copy-start | bytes 6916
  9.2 3.4 %copy-start.7 = (bf16[9,112,32]{1,2,0:T(8,128)(2,1)S(1)}, bf16[9,112,32]{1,2,0:T(8,128)(2,1)}, u32[]{:S(2)}) copy-start(bf16[9,112,32]{1,2,0:T(8,128)(2,1)} %param.20) | copy-start | bytes 193540
  9.3 3.6 %copy-start.10 = (bf16[9,3,32]{2,1,0:T(4,128)(2,1)S(1)}, bf16[9,3,32]{2,1,0:T(4,128)(2,1)}, u32[]{:S(2)}) copy-start(bf16[9,3,32]{2,1,0:T(4,128)(2,1)} %param.23) | copy-start | bytes 5188
  30.3 4.1 %copy-start.1 = (bf16[9,112,112]{2,1,0:T(8,128)(2,1)S(1)}, bf16[9,112,112]{2,1,0:T(8,128)(2,1)}, u32[]{:S(2)}) copy-start(bf16[9,112,112]{2,1,0:T(8,128)(2,1)} %w_deep.1) | copy-start | bytes 677380
  30.3 4.1 %copy-start.2 = (bf16[9,32,144]{2,1,0:T(8,128)(2,1)S(1)}, bf16[9,32,144]{2,1,0:T(8,128)(2,1)}, u32[]{:S(2)}) copy-start(bf16[9,32,144]{2,1,0:T(8,128)(2,1)} %w_up.1) | copy-start | bytes 248836
  30.3 4.1 %copy-start.3 = (bf16[9,32,32]{2,1,0:T(8,128)(2,1)S(1)}, bf16[9,32,32]{2,1,0:T(8,128)(2,1)}, u32[]{:S(2)}) copy-start(bf16[9,32,32]{2,1,0:T(8,128)(2,1)} %w_mid.1) | copy-start | bytes 55300
  40.2 0.6 copy-start.4
  40.8 0.8 %copy-start.6 = (f32[8,120,128]{2,1,0:T(8,128)}, f32[8,120,128]{2,1,0:T(8,128)S(1)}, u32[]{:S(2)}) copy-start(f32[8,120,128]{2,1,0:T(8,128)S(1)} %all-to-all-done.place_ref) | copy-start | bytes 1474564
  41.6 20.9 %copy-start = (s32[1,1,160,256]{3,2,1,0:T(8,128)S(1)}, s32[1,1,160,256]{3,2,1,0:T(8,128)}, u32[]{:S(2)}) copy-start(s32[1,1,160,256]{3,2,1,0:T(8,128)} %order_ref.1) | copy-start | bytes 491524
  62.7 4.7 %collective-permute-start = (bf16[1,4,8,256]{3,2,1,0:T(8,128)(2,1)S(1)}, bf16[1,4,8,256]{3,2,1,0:T(8,128)(2,1)S(1)}, u32[]{:S(2)}, u32[]{:S(2)}) collective-permute-start(bf16[1,4,8,256]{3,2,1,0:T(8,128)(2,1)S(1)} %gbuffer.1), channel_id=1, source_target_pairs={{0,8},{8,16},{16,24},{24,0},{1,9},{9,17},{17,25},{25,1},{2,10},{10... | collective-permute-start | bytes 49160 | tf_op jit(solution)/shard_map/ppermute | solution.py:565

commit v5 on v3

--- a/solution.py
+++ b/solution.py
@@ -67,9 +67,9 @@
             pltpu.VMEM(fracs.shape, F32),
             pltpu.SemaphoreType.DMA((6,)),
         ],
-        compiler_params=params(12),
+        compiler_params=params(60),
         cost_estimate=pl.CostEstimate(
-            flops=3 * lines * LANES, bytes_accessed=36 * lines * LANES, transcendentals=0
+            flops=3 * lines * LANES, bytes_accessed=800 * lines * LANES, transcendentals=0
         ),
         name="positions",
     )(cells, fracs)
@@ -181,14 +181,14 @@
 
 def samples_kernel(picks_ref, brick_ref, place_ref, after_ref, out_ref, values):
     owners, rows, _ = place_ref.shape
-    cap = picks_ref.shape[3]
+    cap = picks_ref.shape[0]
     lines = rows // 3
     per_slot = lines // 2 // cap
 
     def one_slot(slot, carry):
         renderer = slot // cap
         piece = slot % cap
-        brick = brick_ref[picks_ref[0, 0, renderer, piece]]
+        brick = brick_ref[picks_ref[piece, renderer]]
         for step in range(per_slot):
             row = 2 * (piece * per_slot + step)
 
@@ -491,6 +491,7 @@
     over = lax.ppermute(pending, "tile", down)
     under = lax.ppermute(pending, "tile", up)
     places = positions(fill(cells), fill(fracs), n_tile)
+    places, over, under, bricks = lax.optimization_barrier((places, over, under, bricks))
     arrived = lax.all_to_all(places, "tile", split_axis=0, concat_axis=0, tiled=True)
 
     windows = windows_of(bricks)
@@ -510,7 +511,7 @@
         colours,
     )
 
-    found = sample_values(sends, windows, arrived, token)
+    found = sample_values(sends[0, 0].T, windows, arrived, token)
     values = lax.all_to_all(found, "tile", split_axis=0, concat_axis=0, tiled=True)
     rendered = gbuffer(trim(values), sample_order, height, width)
     ring = [(i, (i + 1) % n_section) for i in range(n_section)]

time: 55.9 us -> 55.4 us (level)
  waiting for transfers between devices: 3.14 us -> 7.21 us
  blocking collectives: 12.4 us -> 8.78 us
  starting transfers between devices: 12.2 us -> 11.6 us
    all_to_all x1, blocking collectives: 12.4 us -> 8.78 us  [on_device(): lax.all_to_all(found, 'tile', split_axis=0, concat_axis=0, tiled=True)]
    all_to_all x1, waiting for transfers between devices: 0.01 us -> 2.21 us  [on_device(): lax.all_to_all(places, 'tile', split_axis=0, concat_axis=0, tiled=True)]
    ppermute x1, waiting for transfers between devices: 0.01 us -> 1.79 us  [on_device(): under = lax.ppermute(pending, 'tile', up)]
    unnamed x33 -> x24, local copies, waits for them, and re-layouts: 5.8 us -> 4.4 us
    reshape x1, local copies, waits for them, and re-layouts: 2.33 us -> 3.29 us  [windows_of(): cube = bricks.reshape(count, EDGE, EDGE * EDGE)]
    ppermute x1, starting transfers between devices: 3.03 us -> 2.35 us  [on_device(): over = lax.ppermute(pending, 'tile', down)]
  transfers between devices with their start and end apart: 4 -> 4, of which waited for: 1 -> 3; matrix products, arithmetic and copies ran while one was open for 5% -> 7% of each run, Pallas kernels for 13% -> 17%
where the time goes in v5:
time: 55.4 us; the launch traced here: 55 us
  Pallas kernels  18.7 us (34%)
  starting transfers between devices  11.6 us (21%)
  blocking collectives  8.78 us (16%)
  local copies, waits for them, and re-layouts  7.75 us (14%)
  waiting for transfers between devices  7.21 us (13%)
  between operations  0.81 us (1%)
    pallas_call x1, Pallas kernels, sample_values(): pl.pallas_call(samples_kernel, out_shape=jax.ShapeDtypeStruct(shape, BF16...  9.06 us
    all_to_all x1, blocking collectives, on_device(): lax.all_to_all(found, 'tile', split_axis=0, concat_axis=0, tiled=True)  8.78 us
    all_to_all x1, starting transfers between devices, on_device(): lax.all_to_all(places, 'tile', split_axis=0, concat_axis=0, tiled=True)  6.47 us
    pallas_call x1, Pallas kernels, unet(): pl.pallas_call(unet_kernel, out_shape=(jax.ShapeDtypeStruct((1, colours,...  5.75 us
    unnamed x24, local copies, waits for them, and re-layouts  4.4 us
    reshape x1, local copies, waits for them, and re-layouts, windows_of(): cube = bricks.reshape(count, EDGE, EDGE * EDGE)  3.29 us
    ppermute x1, waiting for transfers between devices, on_device(): handoff = lax.ppermute(rendered, 'section', ring)  3.21 us
    ppermute x1, starting transfers between devices, on_device(): over = lax.ppermute(pending, 'tile', down)  2.35 us
  transfers between devices with their start and end apart: 4, of which 3 were waited for; matrix products, arithmetic and copies ran while one was open for 7% of the time, Pallas kernels for 17%

profile of v5, /device:TPU:0, one launch (start us, length us, event | category | flops | bytes accessed | tf_op | source)
XLA Modules:
  0.0 55.0 jit_solution(12604426436094729729)
XLA Ops:
  0.7 0.8 %copy.26 = bf16[1,4,8,256]{3,1,2,0:T(4,128)(2,1)S(1)} copy(bf16[1,4,8,256]{3,2,1,0:T(8,128)(2,1)} %param.17) | data formatting | bytes 32768 | tf_op args[5]
  1.4 2.3 %collective-permute-start = (bf16[1,4,8,256]{3,1,2,0:T(4,128)(2,1)S(1)}, bf16[1,4,8,256]{3,1,2,0:T(4,128)(2,1)S(1)}, u32[]{:S(2)}, u32[]{:S(2)}) collective-permute-start(bf16[1,4,8,256]{3,1,2,0:T(4,128)(2,1)S(1)} %copy.26), channel_id=1, source_target_pairs={{0,1},{1,2},{2,3},{3,4},{4,5},{5,6},{6,7},{8,9},{9,10},{10,11},{11... | collective-permute-start | bytes 49160 | tf_op jit(solution)/shard_map/ppermute | solution.py:491
  3.8 1.3 %collective-permute-start.1 = (bf16[1,4,8,256]{3,1,2,0:T(4,128)(2,1)S(1)}, bf16[1,4,8,256]{3,1,2,0:T(4,128)(2,1)S(1)}, u32[]{:S(2)}, u32[]{:S(2)}) collective-permute-start(bf16[1,4,8,256]{3,1,2,0:T(4,128)(2,1)S(1)} %copy.26), channel_id=1, source_target_pairs={{1,0},{2,1},{3,2},{4,3},{5,4},{6,5},{7,6},{9,8},{10,9},{11,10},{12... | collective-permute-start | bytes 49160 | tf_op jit(solution)/shard_map/ppermute | solution.py:492
  5.1 2.2 %positions.1 = f32[8,120,128]{2,1,0:T(8,128)} custom-call(s32[3,320,128]{2,1,0:T(8,128)} %bitcast.14, f32[3,320,128]{2,1,0:T(8,128)} %bitcast.15), custom_call_target="tpu_custom_call" | custom-call | flops 122880 | bytes 32768000 | tf_op jit(solution)/shard_map/positions/pallas_call | solution.py:60
  7.3 1.8 %collective-permute-done.1 = bf16[1,4,8,256]{3,1,2,0:T(4,128)(2,1)S(1)} collective-permute-done((bf16[1,4,8,256]{3,1,2,0:T(4,128)(2,1)S(1)}, bf16[1,4,8,256]{3,1,2,0:T(4,128)(2,1)S(1)}, u32[]{:S(2)}, u32[]{:S(2)}) %collective-permute-start.1) | collective-permute-done | bytes 16416 | tf_op jit(solution)/shard_map/ppermute | solution.py:492
  9.0 6.5 %all-to-all-start = ((f32[8,120,128]{2,1,0:T(8,128)}), f32[8,120,128]{2,1,0:T(8,128)S(1)}, u32[]{:S(2)}, u32[]{:S(2)}) async-start(f32[8,120,128]{2,1,0:T(8,128)} %positions.1), calls=%async_computation | async-start | bytes 983040 | tf_op jit(solution)/shard_map/all_to_all | solution.py:495
  15.5 0.1 copy.22
  15.7 0.2 copy.23.w_down
  15.9 0.1 pad_add_fusion.where_ref
  16.1 3.3 %reshape.15.cube_ref = bf16[16,34,1156]{2,1,0:T(8,128)(2,1)S(1)} reshape(bf16[16,39304]{1,0:T(8,128)(2,1)} %param.12) | data formatting | bytes 2515456 | tf_op jit(solution)/shard_map/reshape | solution.py:112
  19.4 0.0 copy-start.1
  19.4 0.0 copy-start.2
  19.4 0.0 copy-start.3
  19.4 1.6 %brick_windows.1.brick_ref = bf16[16,208,256]{2,1,0:T(8,128)(2,1)S(1)} custom-call(bf16[16,34,1156]{2,1,0:T(8,128)(2,1)S(1)} %reshape.15.cube_ref), custom_call_target="tpu_custom_call" | custom-call | flops 905969664 | bytes 4194304 | tf_op jit(solution)/shard_map/brick_windows/pallas_call | solution.py:113
  21.0 1.2 %copy-done.5 = bf16[16,208,256]{2,1,0:T(8,128)(2,1)} copy-done((bf16[16,208,256]{2,1,0:T(8,128)(2,1)}, bf16[16,208,256]{2,1,0:T(8,128)(2,1)S(1)}, u32[]{:S(2)}) %copy-start.5) | copy-done | bytes 1703960
  22.2 5.8 %unet.1 = (bf16[1,3,8,256]{3,2,1,0:T(8,128)(2,1)}, f32[8,128]{1,0:T(8,128)S(1)}) custom-call(s32[2]{0:T(128)S(1)} %pad_add_fusion.where_ref, bf16[24,16,256]{2,1,0:T(8,128)(2,1)S(1)} %pad.12.x_ref, bf16[9,32,16]{2,1,0:T(8,128)(2,1)S(1)} %pad.13.w_in, bf16[9,32,32]{2,1,0:T(8,128)(2,1)S(1)} %copy-done.3, bf16[9,112,32]{2,1,0:T(8,128)(2,1)S(1)} %copy.23.w_down, ...), custom_call_target="tpu_custom_call" | custom-call | flops 3000000000 | bytes 2097152 | tf_op jit(solution)/shard_map/unet/pallas_call | solution.py:438
  28.0 2.2 %all-to-all-done.place_ref = f32[8,120,128]{2,1,0:T(8,128)S(1)} async-done(((f32[8,120,128]{2,1,0:T(8,128)}), f32[8,120,128]{2,1,0:T(8,128)S(1)}, u32[]{:S(2)}, u32[]{:S(2)}) %all-to-all-start) | async-done | bytes 491552 | tf_op jit(solution)/shard_map/all_to_all | solution.py:495
  30.2 1.5 %copy-done.6 = bf16[16,208,256]{2,1,0:T(8,128)(2,1)S(1)} copy-done((bf16[16,208,256]{2,1,0:T(8,128)(2,1)S(1)}, bf16[16,208,256]{2,1,0:T(8,128)(2,1)}, u32[]{:S(2)}) %copy-start.6) | copy-done | bytes 1703960
  31.6 9.1 %sample_values.1 = bf16[8,40,128]{2,1,0:T(8,128)(2,1)S(1)} custom-call(s32[2,8]{1,0:T(2,128)S(1)} %bitcast.13, bf16[16,208,256]{2,1,0:T(8,128)(2,1)S(1)} %copy-done.6, f32[8,120,128]{2,1,0:T(8,128)S(1)} %all-to-all-done.place_ref, f32[8,128]{1,0:T(8,128)S(1)} %get-tuple-element.12.after_ref), custom_call_target="tpu_custom_call" | custom-call | flops 4362076160 | bytes 3145728 | tf_op jit(solution)/shard_map/sample_values/pallas_call | solution.py:217
  40.7 8.8 %all_to_all.10.value_ref = bf16[8,40,128]{2,1,0:T(8,128)(2,1)S(1)} all-to-all(bf16[8,40,128]{2,1,0:T(8,128)(2,1)S(1)} %sample_values.1), channel_id=1, replica_groups=mesh['section'=4,'tile'=8] {'tile'}, dimensions={0} | all-to-all | bytes 163840 | tf_op jit(solution)/shard_map/all_to_all | solution.py:515
  49.5 0.2 gbuffer.1
  49.7 1.5 %collective-permute-start.2 = (bf16[1,4,8,256]{3,2,1,0:T(8,128)(2,1)S(1)}, bf16[1,4,8,256]{3,2,1,0:T(8,128)(2,1)S(1)}, u32[]{:S(2)}, u32[]{:S(2)}) collective-permute-start(bf16[1,4,8,256]{3,2,1,0:T(8,128)(2,1)S(1)} %gbuffer.1), channel_id=1, source_target_pairs={{0,8},{8,16},{16,24},{24,0},{1,9},{9,17},{17,25},{25,1},{2,10},{10... | collective-permute-start | bytes 49160 | tf_op jit(solution)/shard_map/ppermute | solution.py:518
  51.2 3.2 %collective-permute-done.2 = bf16[1,4,8,256]{3,2,1,0:T(8,128)(2,1)S(1)} collective-permute-done((bf16[1,4,8,256]{3,2,1,0:T(8,128)(2,1)S(1)}, bf16[1,4,8,256]{3,2,1,0:T(8,128)(2,1)S(1)}, u32[]{:S(2)}, u32[]{:S(2)}) %collective-permute-start.2) | collective-permute-done | bytes 16416 | tf_op jit(solution)/shard_map/ppermute | solution.py:518
  54.4 0.6 %copy.28 = bf16[1,4,8,256]{3,2,1,0:T(8,128)(2,1)} copy(bf16[1,4,8,256]{3,2,1,0:T(8,128)(2,1)S(1)} %collective-permute-done.2) | data formatting | bytes 32768
  (20 shorter events, 0.1 us)
Async XLA Ops:
  0.6 14.9 %copy-start.8 = (bf16[9,32,4]{1,2,0:T(4,128)(2,1)S(1)}, bf16[9,32,4]{1,2,0:T(4,128)(2,1)}, u32[]{:S(2)}) copy-start(bf16[9,32,4]{1,2,0:T(4,128)(2,1)} %param.18) | copy-start | bytes 6916
  0.6 15.0 %copy-start.9 = (bf16[9,3,32]{2,1,0:T(4,128)(2,1)S(1)}, bf16[9,3,32]{2,1,0:T(4,128)(2,1)}, u32[]{:S(2)}) copy-start(bf16[9,3,32]{2,1,0:T(4,128)(2,1)} %param.23) | copy-start | bytes 5188
  0.7 15.1 %copy-start.7 = (bf16[9,112,32]{1,2,0:T(8,128)(2,1)S(1)}, bf16[9,112,32]{1,2,0:T(8,128)(2,1)}, u32[]{:S(2)}) copy-start(bf16[9,112,32]{1,2,0:T(8,128)(2,1)} %param.20) | copy-start | bytes 193540
  1.4 5.8 %collective-permute-start = (bf16[1,4,8,256]{3,1,2,0:T(4,128)(2,1)S(1)}, bf16[1,4,8,256]{3,1,2,0:T(4,128)(2,1)S(1)}, u32[]{:S(2)}, u32[]{:S(2)}) collective-permute-start(bf16[1,4,8,256]{3,1,2,0:T(4,128)(2,1)S(1)} %copy.26), channel_id=1, source_target_pairs={{0,1},{1,2},{2,3},{3,4},{4,5},{5,6},{6,7},{8,9},{9,10},{10,11},{11... | collective-permute-start | bytes 49160 | tf_op jit(solution)/shard_map/ppermute | solution.py:491
  3.8 5.3 %collective-permute-start.1 = (bf16[1,4,8,256]{3,1,2,0:T(4,128)(2,1)S(1)}, bf16[1,4,8,256]{3,1,2,0:T(4,128)(2,1)S(1)}, u32[]{:S(2)}, u32[]{:S(2)}) collective-permute-start(bf16[1,4,8,256]{3,1,2,0:T(4,128)(2,1)S(1)} %copy.26), channel_id=1, source_target_pairs={{1,0},{2,1},{3,2},{4,3},{5,4},{6,5},{7,6},{9,8},{10,9},{11,10},{12... | collective-permute-start | bytes 49160 | tf_op jit(solution)/shard_map/ppermute | solution.py:492
  9.0 21.1 %all-to-all-start = ((f32[8,120,128]{2,1,0:T(8,128)}), f32[8,120,128]{2,1,0:T(8,128)S(1)}, u32[]{:S(2)}, u32[]{:S(2)}) async-start(f32[8,120,128]{2,1,0:T(8,128)} %positions.1), calls=%async_computation | async-start | bytes 983040 | tf_op jit(solution)/shard_map/all_to_all | solution.py:495
  19.4 2.8 %copy-start.1 = (bf16[9,112,112]{2,1,0:T(8,128)(2,1)S(1)}, bf16[9,112,112]{2,1,0:T(8,128)(2,1)}, u32[]{:S(2)}) copy-start(bf16[9,112,112]{2,1,0:T(8,128)(2,1)} %w_deep.1) | copy-start | bytes 677380
  19.4 2.8 %copy-start.2 = (bf16[9,32,144]{2,1,0:T(8,128)(2,1)S(1)}, bf16[9,32,144]{2,1,0:T(8,128)(2,1)}, u32[]{:S(2)}) copy-start(bf16[9,32,144]{2,1,0:T(8,128)(2,1)} %w_up.1) | copy-start | bytes 248836
  19.4 2.8 %copy-start.3 = (bf16[9,32,32]{2,1,0:T(8,128)(2,1)S(1)}, bf16[9,32,32]{2,1,0:T(8,128)(2,1)}, u32[]{:S(2)}) copy-start(bf16[9,32,32]{2,1,0:T(8,128)(2,1)} %w_mid.1) | copy-start | bytes 55300
  21.0 1.2 %copy-start.5 = (bf16[16,208,256]{2,1,0:T(8,128)(2,1)}, bf16[16,208,256]{2,1,0:T(8,128)(2,1)S(1)}, u32[]{:S(2)}) copy-start(bf16[16,208,256]{2,1,0:T(8,128)(2,1)S(1)} %brick_windows.1.brick_ref) | copy-start | bytes 5111812
  22.2 8.0 %copy-start.4 = (s32[1,1,8,2]{2,3,1,0:T(2,128)S(1)}, s32[1,1,8,2]{2,3,1,0:T(2,128)}, u32[]{:S(2)}) copy-start(s32[1,1,8,2]{2,3,1,0:T(2,128)} %param.13) | copy-start | bytes 196
  30.2 1.5 %copy-start.6 = (bf16[16,208,256]{2,1,0:T(8,128)(2,1)S(1)}, bf16[16,208,256]{2,1,0:T(8,128)(2,1)}, u32[]{:S(2)}) copy-start(bf16[16,208,256]{2,1,0:T(8,128)(2,1)} %copy-done.5) | copy-start | bytes 5111812
  31.6 17.9 %copy-start = (s32[1,1,160,256]{3,2,1,0:T(8,128)S(1)}, s32[1,1,160,256]{3,2,1,0:T(8,128)}, u32[]{:S(2)}) copy-start(s32[1,1,160,256]{3,2,1,0:T(8,128)} %order_ref.1) | copy-start | bytes 491524
  49.7 4.7 %collective-permute-start.2 = (bf16[1,4,8,256]{3,2,1,0:T(8,128)(2,1)S(1)}, bf16[1,4,8,256]{3,2,1,0:T(8,128)(2,1)S(1)}, u32[]{:S(2)}, u32[]{:S(2)}) collective-permute-start(bf16[1,4,8,256]{3,2,1,0:T(8,128)(2,1)S(1)} %gbuffer.1), channel_id=1, source_target_pairs={{0,8},{8,16},{16,24},{24,0},{1,9},{9,17},{17,25},{25,1},{2,10},{10... | collective-permute-start | bytes 49160 | tf_op jit(solution)/shard_map/ppermute | solution.py:518

commit v6 on v5

--- a/solution.py
+++ b/solution.py
@@ -134,102 +134,153 @@
 
 def blend(brick, px, py, pz):
     width = px.shape[1]
-    places = lax.broadcasted_iota(jnp.int32, (MAIN, width), 0).astype(F32)
     eight = lax.broadcasted_iota(jnp.int32, (8, width), 0).astype(F32)
-    places_low = places.astype(BF16)
-
-    def tile(line):
-        return jnp.broadcast_to(line, (TAIL, width)).astype(BF16)
+    places = lax.broadcasted_iota(jnp.int32, (MAIN, width), 0).astype(F32).astype(BF16)
+
+    def tile(rows):
+        return jnp.concatenate([rows, rows], axis=0).astype(BF16)
 
     cell_y = jnp.floor(py)
     frac_y = py - cell_y
-    both = MAIN // TAIL
-    lower = jnp.concatenate([tile(cell_y)] * both, axis=0)
-    low_share = jnp.concatenate([tile(1.0 - frac_y)] * both, axis=0)
-    high_share = jnp.concatenate([tile(frac_y)] * both, axis=0)
-    nothing = jnp.zeros((MAIN, width), BF16)
-    offset = places_low - lower
-    weight_y = jnp.where(
-        offset == 0, low_share, jnp.where(offset == 1, high_share, nothing)
-    )
-    weight_z = hat(places - pz)
-    window = jnp.clip(jnp.floor(px * (1.0 / STRIDE)), 0.0, WINDOWS - 1.0)
+    lower, low_share, high_share = tile(cell_y), tile(1.0 - frac_y), tile(frac_y)
+    nothing = jnp.zeros((TAIL, width), BF16)
+    weight_y = []
+    for start in range(0, MAIN, TAIL):
+        offset = places[start : start + TAIL] - lower
+        weight_y.append(
+            jnp.where(offset == 0, low_share, jnp.where(offset == 1, high_share, nothing))
+        )
+    window = jnp.floor(px * (1.0 / STRIDE))
     weight_x = hat(eight - (px - STRIDE * window))
     parts = []
     for i in range(STRIDE + 1):
-        share = tile(weight_x[i : i + 1])
-        parts.append(weight_y * jnp.concatenate([share] * both, axis=0))
-    parts.append(
-        jnp.concatenate(
-            [weight_x * hat(MAIN - py), weight_x * hat(MAIN + 1 - py)], axis=0
-        ).astype(BF16)
-    )
-    parts.append(jnp.zeros((TAIL, width), BF16))
+        share = tile(jnp.broadcast_to(weight_x[i : i + 1], (8, width)))
+        parts += [share * part for part in weight_y]
+    tail = [weight_x * hat(MAIN - py), weight_x * jnp.maximum(py - MAIN, 0.0)]
+    parts.append(jnp.concatenate(tail, axis=0).astype(BF16))
+    parts.append(nothing)
     plane = jnp.concatenate(parts, axis=0)
     found = jnp.dot(brick, plane, preferred_element_type=F32)
-    chosen = found[:MAIN]
+    groups = range(0, MAIN, 8)
+    chosen = [found[row : row + 8] for row in groups]
     for other in range(1, WINDOWS):
-        chosen = jnp.where(
-            window == float(other), found[other * MAIN : (other + 1) * MAIN], chosen
-        )
-    total = (chosen * weight_z).reshape(MAIN // 8, 8, width).sum(axis=0)
+        here = window == float(other)
+        base = other * MAIN
+        chosen = [
+            jnp.where(here, found[base + row : base + row + 8], old)
+            for row, old in zip(groups, chosen)
+        ]
     base = WINDOWS * MAIN
-    edges = found[base : base + 8] * hat(MAIN - pz) + found[base + 8 :] * hat(MAIN + 1 - pz)
-    total = total + jnp.where(eight == window, edges, 0.0)
-    return jnp.sum(total, axis=0, keepdims=True)
-
-
-def samples_kernel(picks_ref, brick_ref, place_ref, after_ref, out_ref, values):
+    edges = found[base : base + 8] * hat(MAIN - pz)
+    edges = edges + found[base + 8 :] * jnp.maximum(pz - MAIN, 0.0)
+    total = jnp.where(eight == window, edges, 0.0)
+    for row, part in zip(groups, chosen):
+        total = total + part * hat((eight + float(row)) - pz)
+    return total
+
+
+def samples_kernel(
+    picks_ref, brick_ref, place_ref, out_ref, token_ref, bricks, places, sums, arrivals
+):
     owners, rows, _ = place_ref.shape
     cap = picks_ref.shape[0]
     lines = rows // 3
     per_slot = lines // 2 // cap
-
-    def one_slot(slot, carry):
-        renderer = slot // cap
-        piece = slot % cap
-        brick = brick_ref[picks_ref[piece, renderer]]
-        for step in range(per_slot):
-            row = 2 * (piece * per_slot + step)
-
-            def line(axis):
-                both = [
-                    place_ref[renderer, pl.ds(axis * lines + row + half, 1), :]
-                    for half in range(2)
-                ]
-                return jnp.concatenate(both, axis=1)
-
-            value = blend(brick, line(0), line(1), line(2))
-            for half in range(2):
-                values[renderer, pl.ds(row + half, 1), :] = value[
-                    :, half * LANES : (half + 1) * LANES
-                ]
+    token_ref[...] = jnp.zeros_like(token_ref)
+
+    def fetches(renderer):
+        held = renderer % 2
+        copies = [
+            pltpu.make_async_copy(
+                place_ref.at[renderer], places.at[held], arrivals.at[held, cap]
+            )
+        ]
+        for piece in range(cap):
+            copies.append(
+                pltpu.make_async_copy(
+                    brick_ref.at[picks_ref[piece, renderer]],
+                    bricks.at[held, piece],
+                    arrivals.at[held, piece],
+                )
+            )
+        return copies
+
+    for renderer in range(2):
+        for copy in fetches(renderer):
+            copy.start()
+
+    def one_renderer(renderer, carry):
+        held = renderer % 2
+        copies = fetches(renderer)
+        copies[0].wait()
+        for piece in range(cap):
+            copies[1 + piece].wait()
+            brick = bricks[held, piece]
+            for step in range(per_slot):
+                row = 2 * (piece * per_slot + step)
+
+                def line(axis):
+                    both = [
+                        jnp.broadcast_to(
+                            places[held, pl.ds(axis * lines + row + half, 1), :], (8, LANES)
+                        )
+                        for half in range(2)
+                    ]
+                    return jnp.concatenate(both, axis=1)
+
+                total = blend(brick, line(0), line(1), line(2))
+                for half in range(2):
+                    sums[8 * (row + half) : 8 * (row + half + 1), :] = total[
+                        :, half * LANES : (half + 1) * LANES
+                    ]
+
+        @pl.when(renderer + 2 < owners)
+        def _():
+            for copy in fetches(renderer + 2):
+                copy.start()
+
+        values = []
+        for row in range(0, lines, 8):
+            value = sums[pl.ds(8 * row, 8, stride=8), :]
+            for other in range(1, 8):
+                value = value + sums[pl.ds(8 * row + other, 8, stride=8), :]
+            values.append(value)
+        out_ref[renderer] = jnp.concatenate(values, axis=0).astype(BF16)
         return carry
 
-    lax.fori_loop(0, owners * cap, one_slot, 0)
-    out_ref[...] = values[...].astype(BF16)
-
-
-def sample_values(picks, windows, places, after):
+    lax.fori_loop(0, owners, one_renderer, 0)
+
+
+def sample_values(picks, windows, places):
     owners, rows, _ = places.shape
+    cap = picks.shape[0]
     samples = owners * rows * LANES // 3
-    shape = (owners, rows // 3, LANES)
+    hbm = pl.BlockSpec(memory_space=pltpu.HBM)
     return pl.pallas_call(
         samples_kernel,
-        out_shape=jax.ShapeDtypeStruct(shape, BF16),
-        in_specs=[smem(), vmem(), vmem(), vmem()],
-        out_specs=vmem(),
-        scratch_shapes=[pltpu.VMEM(shape, F32)],
-        compiler_params=params(16),
+        out_shape=(
+            jax.ShapeDtypeStruct((owners, rows // 3, LANES), BF16),
+            jax.ShapeDtypeStruct((8, LANES), F32),
+        ),
+        in_specs=[smem(), hbm, hbm],
+        out_specs=(vmem(), vmem()),
+        scratch_shapes=[
+            pltpu.VMEM((2, cap, BRICK_ROWS, KDIM), BF16),
+            pltpu.VMEM((2, rows, LANES), F32),
+            pltpu.VMEM((8 * rows // 3, LANES), F32),
+            pltpu.SemaphoreType.DMA((2, cap + 1)),
+        ],
+        compiler_params=params(60),
         cost_estimate=pl.CostEstimate(
-            flops=2 * samples * KDIM * BRICK_ROWS, bytes_accessed=3 * 1024 * 1024,
+            flops=2 * samples * KDIM * BRICK_ROWS, bytes_accessed=3 * MIB,
             transcendentals=0,
         ),
         name="sample_values",
-    )(picks, windows, places, after)
-
-
-def gbuffer_kernel(value_ref, order_ref, out_ref, values):
+    )(picks, windows, places)
+
+
+def gbuffer_kernel(value_ref, order_ref, after_ref, out_ref, token_ref, values):
+    token_ref[...] = jnp.zeros_like(token_ref)
     values[...] = value_ref[...].astype(F32).reshape(values.shape)
     height = out_ref.shape[2]
 
@@ -274,20 +325,23 @@
     out_ref[0, 3] = (occlusion * (1.0 / NRAY)).astype(BF16)
 
 
-def gbuffer(values, order, height, width):
+def gbuffer(values, order, after, height, width):
     total = order.shape[2]
     return pl.pallas_call(
         gbuffer_kernel,
-        out_shape=jax.ShapeDtypeStruct((1, 4, height, width), BF16),
-        in_specs=[vmem(), vmem()],
-        out_specs=vmem(),
+        out_shape=(
+            jax.ShapeDtypeStruct((1, 4, height, width), BF16),
+            jax.ShapeDtypeStruct((8, LANES), F32),
+        ),
+        in_specs=[vmem()] * 3,
+        out_specs=(vmem(), vmem()),
         scratch_shapes=[pltpu.VMEM((2 * total, LANES), F32)],
         compiler_params=params(16),
         cost_estimate=pl.CostEstimate(
             flops=20 * total * BLOCK, bytes_accessed=8 * total * BLOCK, transcendentals=0
         ),
         name="gbuffer",
-    )(values, order)
+    )(values, order, after)
 
 
 def silu(field):
@@ -327,20 +381,26 @@
     return jnp.concatenate([taps(weight_ref, tap) for tap in range(3)], axis=1)
 
 
-def unet_kernel(
-    where_ref, x_ref, w_in, w_mid, w_down, w_deep, w_up, w_out, out_ref, token_ref,
-    first, second, pooled, third, fourth, joined, fifth, final,
-):
-    height = out_ref.shape[2]
-    half_height = height // 2
-    width = out_ref.shape[3]
-    half_width = width // 2
-    token_ref[...] = jnp.zeros_like(token_ref)
+def sides(where_ref):
     above = jnp.where(where_ref[0] > 0, 1.0, 0.0)
     below = jnp.where(where_ref[0] < where_ref[1] - 1, 1.0, 0.0)
 
     def inside(row, low, high):
         return jnp.where(row < low, above, jnp.where(row >= high, below, 1.0))
+
+    return inside
+
+
+def encoder_kernel(
+    where_ref, x_ref, w_in, w_mid, w_down, w_deep, after_ref, skip_ref, fourth, token_ref,
+    first, second, pooled, third,
+):
+    height = x_ref.shape[0] // 3
+    half_height = height // 2
+    width = x_ref.shape[2]
+    half_width = width // 2
+    inside = sides(where_ref)
+    token_ref[...] = jnp.zeros_like(token_ref)
 
     def full_layer(weight, source, target, low, high, unroll):
         chans = target.shape[1]
@@ -397,6 +457,17 @@
     half_layer(down_product, third, half_height - 2, 2 * half_height - 2)
     half_layer(deep_product, fourth, half_height - 3, 2 * half_height - 3)
 
+    skip_ref[...] = second[4 : 4 + skip_ref.shape[0]]
+
+
+def decoder_kernel(
+    where_ref, skip_ref, fourth, w_up, w_out, after_ref, out_ref, joined, fifth, final
+):
+    height = out_ref.shape[2]
+    width = out_ref.shape[3]
+    half_width = width // 2
+    chans = skip_ref.shape[1]
+    inside = sides(where_ref)
     place = lax.broadcasted_iota(jnp.int32, (half_width, width), 0)
     target = lax.broadcasted_iota(jnp.int32, (half_width, width), 1) // 2
     spread = jnp.where(place == target, 1.0, 0.0).astype(BF16)
@@ -406,7 +477,7 @@
     ).astype(BF16).reshape(fourth.shape[0], deep, width)
     for row in range(2 * fourth.shape[0]):
         joined[row, chans:, :] = wide[row // 2]
-        joined[row, :chans, :] = second[row + 4]
+        joined[row, :chans, :] = skip_ref[row]
 
     def up_step(row, carry):
         total = None
@@ -430,35 +501,54 @@
     out_ref[0] = final[...].astype(BF16)
 
 
-def unet(where, field, w_in, w_mid, w_down, w_deep, w_up, w_out, colours):
+def encoder(where, field, w_in, w_mid, w_down, w_deep, after):
     height = field.shape[0] // 3
     half = height // 2
     width = field.shape[2]
     one, two = w_mid.shape[1], w_deep.shape[1]
     return pl.pallas_call(
-        unet_kernel,
+        encoder_kernel,
         out_shape=(
-            jax.ShapeDtypeStruct((1, colours, height, width), BF16),
+            jax.ShapeDtypeStruct((height + 4, one, width), BF16),
+            jax.ShapeDtypeStruct((3 * half - 6, two, width // 2), BF16),
             jax.ShapeDtypeStruct((8, LANES), F32),
         ),
-        in_specs=[smem()] + [vmem()] * 7,
-        out_specs=(vmem(), vmem()),
+        in_specs=[smem()] + [vmem()] * 6,
+        out_specs=(vmem(),) * 3,
         scratch_shapes=[
             pltpu.VMEM((3 * height - 2, one, width), BF16),
             pltpu.VMEM((3 * height - 4, one, width), BF16),
             pltpu.VMEM((3 * half - 2, one, width // 2), BF16),
             pltpu.VMEM((3 * half - 4, two, width // 2), BF16),
-            pltpu.VMEM((3 * half - 6, two, width // 2), BF16),
+        ],
+        compiler_params=params(16),
+        cost_estimate=pl.CostEstimate(
+            flops=2_000_000_000, bytes_accessed=2 * MIB, transcendentals=400_000
+        ),
+        name="encoder",
+    )(where, field, w_in, w_mid, w_down, w_deep, after)
+
+
+def decoder(where, skip, deep, w_up, w_out, after, height, colours):
+    one = skip.shape[1]
+    two = deep.shape[1]
+    width = skip.shape[2]
+    return pl.pallas_call(
+        decoder_kernel,
+        out_shape=jax.ShapeDtypeStruct((1, colours, height, width), BF16),
+        in_specs=[smem()] + [vmem()] * 5,
+        out_specs=vmem(),
+        scratch_shapes=[
             pltpu.VMEM((height + 4, one + two, width), BF16),
             pltpu.VMEM((height + 2, one, width), BF16),
             pltpu.VMEM((colours, height, width), F32),
         ],
-        compiler_params=params(20),
+        compiler_params=params(16),
         cost_estimate=pl.CostEstimate(
-            flops=3_000_000_000, bytes_accessed=2 * 1024 * 1024, transcendentals=500_000
-        ),
-        name="unet",
-    )(where, field, w_in, w_mid, w_down, w_deep, w_up, w_out)
+            flops=1_000_000_000, bytes_accessed=MIB, transcendentals=100_000
+        ),
+        name="decoder",
+    )(where, skip, deep, w_up, w_out, after)
 
 
 def on_device(
@@ -486,36 +576,29 @@
             return found
         return found.reshape(slots, padded)[:, :per_slot].reshape(1, samples // LANES, LANES)
 
+    places = positions(fill(cells), fill(fracs), n_tile)
+    places, bricks, pending = lax.optimization_barrier((places, bricks, pending))
+    arrived = lax.all_to_all(places, "tile", split_axis=0, concat_axis=0, tiled=True)
+
     down = [(i, i + 1) for i in range(n_tile - 1)]
     up = [(i + 1, i) for i in range(n_tile - 1)]
     over = lax.ppermute(pending, "tile", down)
     under = lax.ppermute(pending, "tile", up)
-    places = positions(fill(cells), fill(fracs), n_tile)
-    places, over, under, bricks = lax.optimization_barrier((places, over, under, bricks))
-    arrived = lax.all_to_all(places, "tile", split_axis=0, concat_axis=0, tiled=True)
-
     windows = windows_of(bricks)
     field = jnp.concatenate([over[0], pending[0], under[0]], axis=1).transpose(1, 0, 2)
     field = jnp.pad(field, ((0, 0), (0, 16 - field.shape[1]), (0, 0)))
     colours = w_out.shape[1]
     where = jnp.stack([tile, jnp.int32(n_tile)]).astype(jnp.int32)
-    denoised, token = unet(
-        where,
-        field,
-        jnp.pad(w_in, ((0, 0), (0, 0), (0, 16 - w_in.shape[2]))),
-        w_mid,
-        w_down,
-        w_deep,
-        w_up,
-        jnp.pad(w_out, ((0, 0), (0, 16 - colours), (0, 0))),
-        colours,
-    )
-
-    found = sample_values(sends[0, 0].T, windows, arrived, token)
+    w_in = jnp.pad(w_in, ((0, 0), (0, 0), (0, 16 - w_in.shape[2])))
+    w_out = jnp.pad(w_out, ((0, 0), (0, 16 - colours), (0, 0)))
+
+    found, sampled = sample_values(sends[0, 0].T, windows, arrived)
     values = lax.all_to_all(found, "tile", split_axis=0, concat_axis=0, tiled=True)
-    rendered = gbuffer(trim(values), sample_order, height, width)
+    skip, deep, encoded = encoder(where, field, w_in, w_mid, w_down, w_deep, sampled)
+    rendered, drawn = gbuffer(trim(values), sample_order, encoded, height, width)
     ring = [(i, (i + 1) % n_section) for i in range(n_section)]
     handoff = lax.ppermute(rendered, "section", ring)
+    denoised = decoder(where, skip, deep, w_up, w_out, drawn, height, colours)
     return (handoff, denoised)
 
 

time: 55.4 us -> 50.2 us (0.906)
  blocking collectives: 8.78 us -> 0 us
  starting transfers between devices: 11.6 us -> 15.6 us
  Pallas kernels: 18.7 us -> 20.5 us
  local copies, waits for them, and re-layouts: 7.75 us -> 6.06 us
    all_to_all x1 -> x0, blocking collectives: 8.78 us -> none  [on_device(): lax.all_to_all(found, 'tile', split_axis=0, concat_axis=0, tiled=True)]
    all_to_all x0 -> x1, starting transfers between devices: none -> 3.37 us  [on_device(): lax.all_to_all(found, 'tile', split_axis=0, concat_axis=0, tiled=True)]
    ppermute x1, waiting for transfers between devices: 3.21 us -> 0.58 us  [on_device(): handoff = lax.ppermute(rendered, 'section', ring)]
    all_to_all x1, waiting for transfers between devices: 2.21 us -> 4.55 us  [on_device(): lax.all_to_all(places, 'tile', split_axis=0, concat_axis=0, tiled=True)]
    ppermute x1, waiting for transfers between devices: 1.79 us -> 0.01 us  [on_device(): under = lax.ppermute(pending, 'tile', up)]
    pallas_call x3 -> x4, Pallas kernels: 15 us -> 16.7 us  [the longest x1 10.2 us: sample_values(): pl.pallas_call(samples_kernel, out_shape=(jax.ShapeDtypeStruct((owners, r...]
    all_to_all x0 -> x1, waiting for transfers between devices: none -> 1.62 us  [on_device(): lax.all_to_all(found, 'tile', split_axis=0, concat_axis=0, tiled=True)]
    reshape x1, local copies, waits for them, and re-layouts: 3.29 us -> 2.33 us  [windows_of(): cube = bricks.reshape(count, EDGE, EDGE * EDGE)]
  transfers between devices with their start and end apart: 4 -> 5, of which waited for: 3 -> 3; matrix products, arithmetic and copies ran while one was open for 7% -> 6% of each run, Pallas kernels for 17% -> 16%
where the time goes in v6:
time: 50.2 us; the launch traced here: 49.8 us
  Pallas kernels  20.5 us (41%)
  starting transfers between devices  15.6 us (31%)
  waiting for transfers between devices  6.76 us (13%)
  local copies, waits for them, and re-layouts  6.06 us (12%)
  between operations  0.84 us (2%)
    pallas_call x1, Pallas kernels, sample_values(): pl.pallas_call(samples_kernel, out_shape=(jax.ShapeDtypeStruct((owners, r...  10.2 us
    all_to_all x1, starting transfers between devices, on_device(): lax.all_to_all(places, 'tile', split_axis=0, concat_axis=0, tiled=True)  6.34 us
    all_to_all x1, waiting for transfers between devices, on_device(): lax.all_to_all(places, 'tile', split_axis=0, concat_axis=0, tiled=True)  4.55 us
    pallas_call x1, Pallas kernels, encoder(): pl.pallas_call(encoder_kernel, out_shape=(jax.ShapeDtypeStruct((height +...  3.71 us
    unnamed x27, local copies, waits for them, and re-layouts  3.66 us
    all_to_all x1, starting transfers between devices, on_device(): lax.all_to_all(found, 'tile', split_axis=0, concat_axis=0, tiled=True)  3.37 us
    ppermute x1, starting transfers between devices, on_device(): over = lax.ppermute(pending, 'tile', down)  3.03 us
    pallas_call x1, Pallas kernels, decoder(): pl.pallas_call(decoder_kernel, out_shape=jax.ShapeDtypeStruct((1, colours...  2.57 us
  transfers between devices with their start and end apart: 5, of which 3 were waited for; matrix products, arithmetic and copies ran while one was open for 6% of the time, Pallas kernels for 16%

profile of v6, /device:TPU:0, one launch (start us, length us, event | category | flops | bytes accessed | tf_op | source)
XLA Modules:
  0.0 49.8 jit_solution(5663287121971293393)
XLA Ops:
  0.7 2.2 %positions.1 = f32[8,120,128]{2,1,0:T(8,128)} custom-call(s32[3,320,128]{2,1,0:T(8,128)} %bitcast.13, f32[3,320,128]{2,1,0:T(8,128)} %bitcast.14), custom_call_target="tpu_custom_call" | custom-call | flops 122880 | bytes 32768000 | tf_op jit(solution)/shard_map/positions/pallas_call | solution.py:60
  2.9 6.3 %all-to-all-start = ((f32[8,120,128]{2,1,0:T(8,128)}), f32[8,120,128]{2,1,0:T(8,128)S(1)}, u32[]{:S(2)}, u32[]{:S(2)}) async-start(f32[8,120,128]{2,1,0:T(8,128)} %positions.1), calls=%async_computation | async-start | bytes 983040 | tf_op jit(solution)/shard_map/all_to_all | solution.py:581
  9.2 1.3 %collective-permute-start.1 = (bf16[1,4,8,256]{3,1,2,0:T(4,128)(2,1)S(1)}, bf16[1,4,8,256]{3,1,2,0:T(4,128)(2,1)S(1)}, u32[]{:S(2)}, u32[]{:S(2)}) collective-permute-start(bf16[1,4,8,256]{3,1,2,0:T(4,128)(2,1)S(1)} %copy.26), channel_id=1, source_target_pairs={{1,0},{2,1},{3,2},{4,3},{5,4},{6,5},{7,6},{9,8},{10,9},{11,10},{12... | collective-permute-start | bytes 49160 | tf_op jit(solution)/shard_map/ppermute | solution.py:586
  10.5 3.0 %collective-permute-start = (bf16[1,4,8,256]{3,1,2,0:T(4,128)(2,1)S(1)}, bf16[1,4,8,256]{3,1,2,0:T(4,128)(2,1)S(1)}, u32[]{:S(2)}, u32[]{:S(2)}) collective-permute-start(bf16[1,4,8,256]{3,1,2,0:T(4,128)(2,1)S(1)} %copy.26), channel_id=1, source_target_pairs={{0,1},{1,2},{2,3},{3,4},{4,5},{5,6},{6,7},{8,9},{9,10},{10,11},{11... | collective-permute-start | bytes 49160 | tf_op jit(solution)/shard_map/ppermute | solution.py:585
  13.6 2.3 %reshape.15.cube_ref = bf16[16,34,1156]{2,1,0:T(8,128)(2,1)S(1)} reshape(bf16[16,39304]{1,0:T(8,128)(2,1)S(1)} %copy-done.6) | data formatting | bytes 2515456 | tf_op jit(solution)/shard_map/reshape | solution.py:112
  15.9 0.1 pad_add_fusion.where_ref
  16.0 1.6 %brick_windows.1.brick_ref = bf16[16,208,256]{2,1,0:T(8,128)(2,1)S(1)} custom-call(bf16[16,34,1156]{2,1,0:T(8,128)(2,1)S(1)} %reshape.15.cube_ref), custom_call_target="tpu_custom_call" | custom-call | flops 905969664 | bytes 4194304 | tf_op jit(solution)/shard_map/brick_windows/pallas_call | solution.py:113
  17.6 1.2 %copy-done.4 = bf16[16,208,256]{2,1,0:T(8,128)(2,1)} copy-done((bf16[16,208,256]{2,1,0:T(8,128)(2,1)}, bf16[16,208,256]{2,1,0:T(8,128)(2,1)S(1)}, u32[]{:S(2)}) %copy-start.4) | copy-done | bytes 1703960
  18.8 0.1 copy.22
  19.0 0.2 copy.23.w_down
  19.2 0.0 collective-permute-done
  19.3 4.5 %all-to-all-done.place_ref = f32[8,120,128]{2,1,0:T(8,128)S(1)} async-done(((f32[8,120,128]{2,1,0:T(8,128)}), f32[8,120,128]{2,1,0:T(8,128)S(1)}, u32[]{:S(2)}, u32[]{:S(2)}) %all-to-all-start) | async-done | bytes 491552 | tf_op jit(solution)/shard_map/all_to_all | solution.py:581
  23.9 0.8 %copy-done.7 = f32[8,120,128]{2,1,0:T(8,128)} copy-done((f32[8,120,128]{2,1,0:T(8,128)}, f32[8,120,128]{2,1,0:T(8,128)S(1)}, u32[]{:S(2)}) %copy-start.7) | copy-done | bytes 491544
  24.7 10.2 %sample_values.1 = (bf16[8,40,128]{2,1,0:T(8,128)(2,1)}, f32[8,128]{1,0:T(8,128)}) custom-call(s32[2,8]{1,0:T(2,128)} %bitcast.18, bf16[16,208,256]{2,1,0:T(8,128)(2,1)} %copy-done.4, f32[8,120,128]{2,1,0:T(8,128)} %copy-done.7), custom_call_target="tpu_custom_call" | custom-call | flops 4362076160 | bytes 3145728 | tf_op jit(solution)/shard_map/sample_values/pallas_call | solution.py:259
  34.9 3.4 %all-to-all-start.1 = ((bf16[8,40,128]{2,1,0:T(8,128)(2,1)}), bf16[8,40,128]{2,1,0:T(8,128)(2,1)S(1)}, u32[]{:S(2)}, u32[]{:S(2)}) async-start(bf16[8,40,128]{2,1,0:T(8,128)(2,1)} %get-tuple-element.14), calls=%async_computation.1 | async-start | bytes 163840 | tf_op jit(solution)/shard_map/all_to_all | solution.py:596
  38.3 0.0 copy-start.5
  38.3 0.7 %copy-done.5 = f32[8,128]{1,0:T(8,128)S(1)} copy-done((f32[8,128]{1,0:T(8,128)S(1)}, f32[8,128]{1,0:T(8,128)}, u32[]{:S(2)}) %copy-start.5) | copy-done | bytes 4120
  39.0 3.7 %encoder.1 = (bf16[12,32,256]{2,1,0:T(8,128)(2,1)S(1)}, bf16[6,112,128]{2,1,0:T(8,128)(2,1)S(1)}, f32[8,128]{1,0:T(8,128)S(1)}) custom-call(s32[2]{0:T(128)S(1)} %pad_add_fusion.where_ref, bf16[24,16,256]{2,1,0:T(8,128)(2,1)S(1)} %pad.12.x_ref, bf16[9,32,16]{2,1,0:T(8,128)(2,1)S(1)} %pad.13.w_in, bf16[9,32,32]{2,1,0:T(8,128)(2,1)S(1)} %copy-done.3, ...), custom_call_target="tpu_custom_call" | custom-call | flops 2000000000 | bytes 2097152 | tf_op jit(solution)/shard_map/encoder/pallas_call | solution.py:509
  42.7 1.6 %all-to-all-done.1.value_ref = bf16[8,40,128]{2,1,0:T(8,128)(2,1)S(1)} async-done(((bf16[8,40,128]{2,1,0:T(8,128)(2,1)}), bf16[8,40,128]{2,1,0:T(8,128)(2,1)S(1)}, u32[]{:S(2)}, u32[]{:S(2)}) %all-to-all-start.1) | async-done | bytes 81952 | tf_op jit(solution)/shard_map/all_to_all | solution.py:596
  44.3 0.2 gbuffer.1
  44.5 1.5 %collective-permute-start.2 = (bf16[1,4,8,256]{3,2,1,0:T(8,128)(2,1)S(1)}, bf16[1,4,8,256]{3,2,1,0:T(8,128)(2,1)S(1)}, u32[]{:S(2)}, u32[]{:S(2)}) collective-permute-start(bf16[1,4,8,256]{3,2,1,0:T(8,128)(2,1)S(1)} %get-tuple-element.18), channel_id=1, source_target_pairs={{0,8},{8,16},{16,24},{24,0},{1,9},{9,17},{17,25},{25,1},{2,10},{10... | collective-permute-start | bytes 49160 | tf_op jit(solution)/shard_map/ppermute | solution.py:600
  46.1 2.6 %decoder.1 = bf16[1,3,8,256]{3,2,1,0:T(8,128)(2,1)} custom-call(s32[2]{0:T(128)S(1)} %pad_add_fusion.where_ref, bf16[12,32,256]{2,1,0:T(8,128)(2,1)S(1)} %get-tuple-element.19.skip_ref, bf16[6,112,128]{2,1,0:T(8,128)(2,1)S(1)} %get-tuple-element.20.fourth, bf16[9,32,144]{2,1,0:T(8,128)(2,1)S(1)} %copy-done.2, bf16[9,16,32]{2,1,0:T(8,128)(2,1)S(1)} %pad.14.w_out, ...), custom_call_target="tpu_custom_call" | custom-call | flops 1000000000 | bytes 1048576 | tf_op jit(solution)/shard_map/decoder/pallas_call | solution.py:536
  48.6 0.6 %collective-permute-done.2 = bf16[1,4,8,256]{3,2,1,0:T(8,128)(2,1)S(1)} collective-permute-done((bf16[1,4,8,256]{3,2,1,0:T(8,128)(2,1)S(1)}, bf16[1,4,8,256]{3,2,1,0:T(8,128)(2,1)S(1)}, u32[]{:S(2)}, u32[]{:S(2)}) %collective-permute-start.2) | collective-permute-done | bytes 16416 | tf_op jit(solution)/shard_map/ppermute | solution.py:600
  49.2 0.6 %copy.28 = bf16[1,4,8,256]{3,2,1,0:T(8,128)(2,1)} copy(bf16[1,4,8,256]{3,2,1,0:T(8,128)(2,1)S(1)} %collective-permute-done.2) | data formatting | bytes 32768
  (26 shorter events, 0.1 us)
Async XLA Ops:
  0.6 13.0 %copy-start.6 = (bf16[16,39304]{1,0:T(8,128)(2,1)S(1)}, bf16[16,39304]{1,0:T(8,128)(2,1)}, u32[]{:S(2)}) copy-start(bf16[16,39304]{1,0:T(8,128)(2,1)} %param.12) | copy-start | bytes 3773188
  0.6 8.6 %copy-start.9 = (bf16[1,4,8,256]{3,2,1,0:T(8,128)(2,1)S(1)}, bf16[1,4,8,256]{3,2,1,0:T(8,128)(2,1)}, u32[]{:S(2)}) copy-start(bf16[1,4,8,256]{3,2,1,0:T(8,128)(2,1)} %param.17) | copy-start | bytes 49156
  2.9 21.0 %all-to-all-start = ((f32[8,120,128]{2,1,0:T(8,128)}), f32[8,120,128]{2,1,0:T(8,128)S(1)}, u32[]{:S(2)}, u32[]{:S(2)}) async-start(f32[8,120,128]{2,1,0:T(8,128)} %positions.1), calls=%async_computation | async-start | bytes 983040 | tf_op jit(solution)/shard_map/all_to_all | solution.py:581
  9.2 10.0 %collective-permute-start.1 = (bf16[1,4,8,256]{3,1,2,0:T(4,128)(2,1)S(1)}, bf16[1,4,8,256]{3,1,2,0:T(4,128)(2,1)S(1)}, u32[]{:S(2)}, u32[]{:S(2)}) collective-permute-start(bf16[1,4,8,256]{3,1,2,0:T(4,128)(2,1)S(1)} %copy.26), channel_id=1, source_target_pairs={{1,0},{2,1},{3,2},{4,3},{5,4},{6,5},{7,6},{9,8},{10,9},{11,10},{12... | collective-permute-start | bytes 49160 | tf_op jit(solution)/shard_map/ppermute | solution.py:586
  10.5 8.7 %collective-permute-start = (bf16[1,4,8,256]{3,1,2,0:T(4,128)(2,1)S(1)}, bf16[1,4,8,256]{3,1,2,0:T(4,128)(2,1)S(1)}, u32[]{:S(2)}, u32[]{:S(2)}) collective-permute-start(bf16[1,4,8,256]{3,1,2,0:T(4,128)(2,1)S(1)} %copy.26), channel_id=1, source_target_pairs={{0,1},{1,2},{2,3},{3,4},{4,5},{5,6},{6,7},{8,9},{9,10},{10,11},{11... | collective-permute-start | bytes 49160 | tf_op jit(solution)/shard_map/ppermute | solution.py:585
  16.0 2.8 %copy-start.10 = (bf16[9,32,4]{1,2,0:T(4,128)(2,1)S(1)}, bf16[9,32,4]{1,2,0:T(4,128)(2,1)}, u32[]{:S(2)}) copy-start(bf16[9,32,4]{1,2,0:T(4,128)(2,1)} %param.18) | copy-start | bytes 6916
  16.0 3.0 %copy-start.8 = (bf16[9,112,32]{1,2,0:T(8,128)(2,1)S(1)}, bf16[9,112,32]{1,2,0:T(8,128)(2,1)}, u32[]{:S(2)}) copy-start(bf16[9,112,32]{1,2,0:T(8,128)(2,1)} %param.20) | copy-start | bytes 193540
  16.0 3.2 %copy-start.11 = (bf16[9,3,32]{2,1,0:T(4,128)(2,1)S(1)}, bf16[9,3,32]{2,1,0:T(4,128)(2,1)}, u32[]{:S(2)}) copy-start(bf16[9,3,32]{2,1,0:T(4,128)(2,1)} %param.23) | copy-start | bytes 5188
  17.6 1.2 %copy-start.4 = (bf16[16,208,256]{2,1,0:T(8,128)(2,1)}, bf16[16,208,256]{2,1,0:T(8,128)(2,1)S(1)}, u32[]{:S(2)}) copy-start(bf16[16,208,256]{2,1,0:T(8,128)(2,1)S(1)} %brick_windows.1.brick_ref) | copy-start | bytes 5111812
  23.9 0.8 %copy-start.7 = (f32[8,120,128]{2,1,0:T(8,128)}, f32[8,120,128]{2,1,0:T(8,128)S(1)}, u32[]{:S(2)}) copy-start(f32[8,120,128]{2,1,0:T(8,128)S(1)} %all-to-all-done.place_ref) | copy-start | bytes 1474564
  24.7 13.6 %copy-start.1 = (bf16[9,112,112]{2,1,0:T(8,128)(2,1)S(1)}, bf16[9,112,112]{2,1,0:T(8,128)(2,1)}, u32[]{:S(2)}) copy-start(bf16[9,112,112]{2,1,0:T(8,128)(2,1)} %w_deep.1) | copy-start | bytes 677380
  24.7 13.6 %copy-start.3 = (bf16[9,32,32]{2,1,0:T(8,128)(2,1)S(1)}, bf16[9,32,32]{2,1,0:T(8,128)(2,1)}, u32[]{:S(2)}) copy-start(bf16[9,32,32]{2,1,0:T(8,128)(2,1)} %w_mid.1) | copy-start | bytes 55300
  34.9 9.4 %all-to-all-start.1 = ((bf16[8,40,128]{2,1,0:T(8,128)(2,1)}), bf16[8,40,128]{2,1,0:T(8,128)(2,1)S(1)}, u32[]{:S(2)}, u32[]{:S(2)}) async-start(bf16[8,40,128]{2,1,0:T(8,128)(2,1)} %get-tuple-element.14), calls=%async_computation.1 | async-start | bytes 163840 | tf_op jit(solution)/shard_map/all_to_all | solution.py:596
  38.3 0.7 %copy-start.5 = (f32[8,128]{1,0:T(8,128)S(1)}, f32[8,128]{1,0:T(8,128)}, u32[]{:S(2)}) copy-start(f32[8,128]{1,0:T(8,128)} %get-tuple-element.16.after_ref) | copy-start | bytes 12292
  39.0 5.3 %copy-start = (s32[1,1,160,256]{3,2,1,0:T(8,128)S(1)}, s32[1,1,160,256]{3,2,1,0:T(8,128)}, u32[]{:S(2)}) copy-start(s32[1,1,160,256]{3,2,1,0:T(8,128)} %order_ref.1) | copy-start | bytes 491524
  39.0 7.1 %copy-start.2 = (bf16[9,32,144]{2,1,0:T(8,128)(2,1)S(1)}, bf16[9,32,144]{2,1,0:T(8,128)(2,1)}, u32[]{:S(2)}) copy-start(bf16[9,32,144]{2,1,0:T(8,128)(2,1)} %w_up.1) | copy-start | bytes 248836
  44.5 4.7 %collective-permute-start.2 = (bf16[1,4,8,256]{3,2,1,0:T(8,128)(2,1)S(1)}, bf16[1,4,8,256]{3,2,1,0:T(8,128)(2,1)S(1)}, u32[]{:S(2)}, u32[]{:S(2)}) collective-permute-start(bf16[1,4,8,256]{3,2,1,0:T(8,128)(2,1)S(1)} %get-tuple-element.18), channel_id=1, source_target_pairs={{0,8},{8,16},{16,24},{24,0},{1,9},{9,17},{17,25},{25,1},{2,10},{10... | collective-permute-start | bytes 49160 | tf_op jit(solution)/shard_map/ppermute | solution.py:600

commit v7 on v6

--- a/solution.py
+++ b/solution.py
@@ -37,39 +37,63 @@
     return pl.BlockSpec(memory_space=pltpu.SMEM)
 
 
-def positions_kernel(cells_ref, fracs_ref, out_ref, cells, fracs, arrivals):
+def positions_kernel(cells_ref, fracs_ref, out_ref, cells, fracs, found, arrivals, departures):
     owners, rows, _ = out_ref.shape
     lines = rows // 3
-    copies = []
-    for axis in range(3):
-        for number, (source, target) in enumerate(((cells_ref, cells), (fracs_ref, fracs))):
-            copy = pltpu.make_async_copy(
-                source.at[axis], target.at[axis], arrivals.at[2 * axis + number]
+    parts = arrivals.shape[1]
+    share = owners // parts
+    pieces = [(axis, part) for axis in range(3) for part in range(parts)]
+
+    def reads(axis, part):
+        span = pl.ds(part * share * lines, share * lines)
+        return [
+            pltpu.make_async_copy(
+                source.at[axis, span], target.at[axis, span], arrivals.at[axis, part, number]
             )
+            for number, (source, target) in enumerate(((cells_ref, cells), (fracs_ref, fracs)))
+        ]
+
+    def write(axis, part):
+        place = (pl.ds(part * share, share), pl.ds(axis * lines, lines))
+        return pltpu.make_async_copy(
+            found.at[place], out_ref.at[place], departures.at[axis, part]
+        )
+
+    for piece in pieces:
+        for copy in reads(*piece):
             copy.start()
-            copies.append(copy)
-    for axis in range(3):
-        copies[2 * axis].wait()
-        copies[2 * axis + 1].wait()
-        place = cells[axis].astype(F32) + fracs[axis]
-        out_ref[:, axis * lines : (axis + 1) * lines, :] = place.reshape(owners, lines, LANES)
+    for axis, part in pieces:
+        for copy in reads(axis, part):
+            copy.wait()
+        span = slice(part * share * lines, (part + 1) * share * lines)
+        place = cells[axis, span].astype(F32) + fracs[axis, span]
+        found[part * share : (part + 1) * share, axis * lines : (axis + 1) * lines, :] = (
+            place.reshape(share, lines, LANES)
+        )
+        write(axis, part).start()
+    for piece in pieces:
+        write(*piece).wait()
 
 
 def positions(cells, fracs, owners):
     lines = cells.shape[1]
+    shape = (owners, 3 * lines // owners, LANES)
+    hbm = pl.BlockSpec(memory_space=pltpu.HBM)
     return pl.pallas_call(
         positions_kernel,
-        out_shape=jax.ShapeDtypeStruct((owners, 3 * lines // owners, LANES), F32),
-        in_specs=[pl.BlockSpec(memory_space=pltpu.HBM)] * 2,
-        out_specs=vmem(),
+        out_shape=jax.ShapeDtypeStruct(shape, F32),
+        in_specs=[hbm, hbm],
+        out_specs=hbm,
         scratch_shapes=[
             pltpu.VMEM(cells.shape, jnp.int32),
             pltpu.VMEM(fracs.shape, F32),
-            pltpu.SemaphoreType.DMA((6,)),
+            pltpu.VMEM(shape, F32),
+            pltpu.SemaphoreType.DMA((3, 2, 2)),
+            pltpu.SemaphoreType.DMA((3, 2)),
         ],
         compiler_params=params(60),
         cost_estimate=pl.CostEstimate(
-            flops=3 * lines * LANES, bytes_accessed=800 * lines * LANES, transcendentals=0
+            flops=3 * lines * LANES, bytes_accessed=36 * lines * LANES, transcendentals=0
         ),
         name="positions",
     )(cells, fracs)
@@ -180,16 +204,27 @@
 
 
 def samples_kernel(
-    picks_ref, brick_ref, place_ref, out_ref, token_ref, bricks, places, sums, arrivals
+    own, where_ref, picks_ref, brick_ref, place_ref, *rest
 ):
+    if own:
+        out_ref, bricks, places, sums, arrivals = rest
+    else:
+        own_ref, out_ref, bricks, places, sums, arrivals = rest
     owners, rows, _ = place_ref.shape
     cap = picks_ref.shape[0]
     lines = rows // 3
     per_slot = lines // 2 // cap
-    token_ref[...] = jnp.zeros_like(token_ref)
-
-    def fetches(renderer):
-        held = renderer % 2
+    count = 1 if own else owners - 1
+    tile = where_ref[0]
+    if not own:
+        out_ref[tile] = own_ref[0]
+
+    def renderer_of(turn):
+        return tile if own else lax.rem(tile + 1 + turn, owners)
+
+    def fetches(turn):
+        held = turn % 2
+        renderer = renderer_of(turn)
         copies = [
             pltpu.make_async_copy(
                 place_ref.at[renderer], places.at[held], arrivals.at[held, cap]
@@ -205,13 +240,13 @@
             )
         return copies
 
-    for renderer in range(2):
-        for copy in fetches(renderer):
+    for turn in range(min(2, count)):
+        for copy in fetches(turn):
             copy.start()
 
-    def one_renderer(renderer, carry):
-        held = renderer % 2
-        copies = fetches(renderer)
+    def one_turn(turn, carry):
+        held = turn % 2
+        copies = fetches(turn)
         copies[0].wait()
         for piece in range(cap):
             copies[1 + piece].wait()
@@ -234,9 +269,9 @@
                         :, half * LANES : (half + 1) * LANES
                     ]
 
-        @pl.when(renderer + 2 < owners)
+        @pl.when(turn + 2 < count)
         def _():
-            for copy in fetches(renderer + 2):
+            for copy in fetches(turn + 2):
                 copy.start()
 
         values = []
@@ -245,42 +280,41 @@
             for other in range(1, 8):
                 value = value + sums[pl.ds(8 * row + other, 8, stride=8), :]
             values.append(value)
-        out_ref[renderer] = jnp.concatenate(values, axis=0).astype(BF16)
+        out_ref[0 if own else renderer_of(turn)] = jnp.concatenate(values, axis=0).astype(BF16)
         return carry
 
-    lax.fori_loop(0, owners, one_renderer, 0)
-
-
-def sample_values(picks, windows, places):
+    lax.fori_loop(0, count, one_turn, 0)
+
+
+def sample_values(where, picks, windows, places, own_values=None):
     owners, rows, _ = places.shape
     cap = picks.shape[0]
-    samples = owners * rows * LANES // 3
-    hbm = pl.BlockSpec(memory_space=pltpu.HBM)
+    own = own_values is None
+    count = 1 if own else owners - 1
+    samples = count * rows * LANES // 3
+    some = pl.BlockSpec(memory_space=pl.ANY)
+    extra = () if own else (own_values,)
     return pl.pallas_call(
-        samples_kernel,
-        out_shape=(
-            jax.ShapeDtypeStruct((owners, rows // 3, LANES), BF16),
-            jax.ShapeDtypeStruct((8, LANES), F32),
-        ),
-        in_specs=[smem(), hbm, hbm],
-        out_specs=(vmem(), vmem()),
+        functools.partial(samples_kernel, own),
+        out_shape=jax.ShapeDtypeStruct((1 if own else owners, rows // 3, LANES), BF16),
+        in_specs=[smem(), smem(), some, some] + [vmem()] * len(extra),
+        out_specs=vmem(),
         scratch_shapes=[
             pltpu.VMEM((2, cap, BRICK_ROWS, KDIM), BF16),
             pltpu.VMEM((2, rows, LANES), F32),
             pltpu.VMEM((8 * rows // 3, LANES), F32),
             pltpu.SemaphoreType.DMA((2, cap + 1)),
         ],
-        compiler_params=params(60),
+        compiler_params=params(59),
         cost_estimate=pl.CostEstimate(
-            flops=2 * samples * KDIM * BRICK_ROWS, bytes_accessed=3 * MIB,
+            flops=2 * samples * KDIM * BRICK_ROWS, bytes_accessed=count * MIB // 4,
             transcendentals=0,
         ),
-        name="sample_values",
-    )(picks, windows, places)
-
-
-def gbuffer_kernel(value_ref, order_ref, after_ref, out_ref, token_ref, values):
-    token_ref[...] = jnp.zeros_like(token_ref)
+        name="own_values" if own else "sample_values",
+    )(where, picks, windows, places, *extra)
+
+
+def gbuffer_kernel(value_ref, order_ref, out_ref, values):
     values[...] = value_ref[...].astype(F32).reshape(values.shape)
     height = out_ref.shape[2]
 
@@ -325,23 +359,20 @@
     out_ref[0, 3] = (occlusion * (1.0 / NRAY)).astype(BF16)
 
 
-def gbuffer(values, order, after, height, width):
+def gbuffer(values, order, height, width):
     total = order.shape[2]
     return pl.pallas_call(
         gbuffer_kernel,
-        out_shape=(
-            jax.ShapeDtypeStruct((1, 4, height, width), BF16),
-            jax.ShapeDtypeStruct((8, LANES), F32),
-        ),
-        in_specs=[vmem()] * 3,
-        out_specs=(vmem(), vmem()),
+        out_shape=jax.ShapeDtypeStruct((1, 4, height, width), BF16),
+        in_specs=[vmem(), vmem()],
+        out_specs=vmem(),
         scratch_shapes=[pltpu.VMEM((2 * total, LANES), F32)],
         compiler_params=params(16),
         cost_estimate=pl.CostEstimate(
             flops=20 * total * BLOCK, bytes_accessed=8 * total * BLOCK, transcendentals=0
         ),
         name="gbuffer",
-    )(values, order, after)
+    )(values, order)
 
 
 def silu(field):
@@ -392,7 +423,7 @@
 
 
 def encoder_kernel(
-    where_ref, x_ref, w_in, w_mid, w_down, w_deep, after_ref, skip_ref, fourth, token_ref,
+    where_ref, x_ref, w_in, w_mid, w_down, w_deep, skip_ref, fourth,
     first, second, pooled, third,
 ):
     height = x_ref.shape[0] // 3
@@ -400,7 +431,6 @@
     width = x_ref.shape[2]
     half_width = width // 2
     inside = sides(where_ref)
-    token_ref[...] = jnp.zeros_like(token_ref)
 
     def full_layer(weight, source, target, low, high, unroll):
         chans = target.shape[1]
@@ -461,7 +491,7 @@
 
 
 def decoder_kernel(
-    where_ref, skip_ref, fourth, w_up, w_out, after_ref, out_ref, joined, fifth, final
+    where_ref, skip_ref, fourth, w_up, w_out, out_ref, joined, fifth, final
 ):
     height = out_ref.shape[2]
     width = out_ref.shape[3]
@@ -501,7 +531,7 @@
     out_ref[0] = final[...].astype(BF16)
 
 
-def encoder(where, field, w_in, w_mid, w_down, w_deep, after):
+def encoder(where, field, w_in, w_mid, w_down, w_deep):
     height = field.shape[0] // 3
     half = height // 2
     width = field.shape[2]
@@ -511,10 +541,9 @@
         out_shape=(
             jax.ShapeDtypeStruct((height + 4, one, width), BF16),
             jax.ShapeDtypeStruct((3 * half - 6, two, width // 2), BF16),
-            jax.ShapeDtypeStruct((8, LANES), F32),
         ),
-        in_specs=[smem()] + [vmem()] * 6,
-        out_specs=(vmem(),) * 3,
+        in_specs=[smem()] + [vmem()] * 5,
+        out_specs=(vmem(), vmem()),
         scratch_shapes=[
             pltpu.VMEM((3 * height - 2, one, width), BF16),
             pltpu.VMEM((3 * height - 4, one, width), BF16),
@@ -526,17 +555,17 @@
             flops=2_000_000_000, bytes_accessed=2 * MIB, transcendentals=400_000
         ),
         name="encoder",
-    )(where, field, w_in, w_mid, w_down, w_deep, after)
-
-
-def decoder(where, skip, deep, w_up, w_out, after, height, colours):
+    )(where, field, w_in, w_mid, w_down, w_deep)
+
+
+def decoder(where, skip, deep, w_up, w_out, height, colours):
     one = skip.shape[1]
     two = deep.shape[1]
     width = skip.shape[2]
     return pl.pallas_call(
         decoder_kernel,
         out_shape=jax.ShapeDtypeStruct((1, colours, height, width), BF16),
-        in_specs=[smem()] + [vmem()] * 5,
+        in_specs=[smem()] + [vmem()] * 4,
         out_specs=vmem(),
         scratch_shapes=[
             pltpu.VMEM((height + 4, one + two, width), BF16),
@@ -548,7 +577,7 @@
             flops=1_000_000_000, bytes_accessed=MIB, transcendentals=100_000
         ),
         name="decoder",
-    )(where, skip, deep, w_up, w_out, after)
+    )(where, skip, deep, w_up, w_out)
 
 
 def on_device(
@@ -585,20 +614,25 @@
     over = lax.ppermute(pending, "tile", down)
     under = lax.ppermute(pending, "tile", up)
     windows = windows_of(bricks)
+    where = jnp.stack([tile, jnp.int32(n_tile)]).astype(jnp.int32)
+    picks = sends[0, 0].T
+    own_values = sample_values(where, picks, windows, places)
+    found = sample_values(where, picks, windows, arrived, own_values)
+
+    over, under, pending, found = lax.optimization_barrier((over, under, pending, found))
+    values = lax.all_to_all(found, "tile", split_axis=0, concat_axis=0, tiled=True)
     field = jnp.concatenate([over[0], pending[0], under[0]], axis=1).transpose(1, 0, 2)
     field = jnp.pad(field, ((0, 0), (0, 16 - field.shape[1]), (0, 0)))
     colours = w_out.shape[1]
-    where = jnp.stack([tile, jnp.int32(n_tile)]).astype(jnp.int32)
     w_in = jnp.pad(w_in, ((0, 0), (0, 0), (0, 16 - w_in.shape[2])))
     w_out = jnp.pad(w_out, ((0, 0), (0, 16 - colours), (0, 0)))
-
-    found, sampled = sample_values(sends[0, 0].T, windows, arrived)
-    values = lax.all_to_all(found, "tile", split_axis=0, concat_axis=0, tiled=True)
-    skip, deep, encoded = encoder(where, field, w_in, w_mid, w_down, w_deep, sampled)
-    rendered, drawn = gbuffer(trim(values), sample_order, encoded, height, width)
+    skip, deep = encoder(where, field, w_in, w_mid, w_down, w_deep)
+    values, skip, deep = lax.optimization_barrier((values, skip, deep))
+    rendered = gbuffer(trim(values), sample_order, height, width)
+    rendered, skip, deep = lax.optimization_barrier((rendered, skip, deep))
     ring = [(i, (i + 1) % n_section) for i in range(n_section)]
     handoff = lax.ppermute(rendered, "section", ring)
-    denoised = decoder(where, skip, deep, w_up, w_out, drawn, height, colours)
+    denoised = decoder(where, skip, deep, w_up, w_out, height, colours)
     return (handoff, denoised)
 
 

time: 50.2 us -> 50.9 us (1.014)
  waiting for transfers between devices: 6.76 us -> 4.38 us
  Pallas kernels: 20.5 us -> 22.6 us
  starting transfers between devices: 15.6 us -> 17.3 us
  local copies, waits for them, and re-layouts: 6.06 us -> 4.63 us
    all_to_all x1, waiting for transfers between devices: 4.55 us -> 1.45 us  [on_device(): lax.all_to_all(places, 'tile', split_axis=0, concat_axis=0, tiled=True)]
    all_to_all x1, starting transfers between devices: 3.37 us -> 5.63 us  [on_device(): lax.all_to_all(found, 'tile', split_axis=0, concat_axis=0, tiled=True)]
    pallas_call x3 -> x4, Pallas kernels: 12.6 us -> 14.8 us  [the longest x2 12.4 us: sample_values(): pl.pallas_call(functools.partial(samples_kernel, own), out_shape=jax.Shap...]
    unnamed x27 -> x25, local copies, waits for them, and re-layouts: 3.66 us -> 2.23 us
    all_to_all x1, waiting for transfers between devices: 1.62 us -> 2.34 us  [on_device(): lax.all_to_all(found, 'tile', split_axis=0, concat_axis=0, tiled=True)]
  transfers between devices with their start and end apart: 5 -> 5, of which waited for: 3 -> 3; matrix products, arithmetic and copies ran while one was open for 6% -> 7% of each run, Pallas kernels for 16% -> 40%
where the time goes in v7:
time: 50.9 us; the launch traced here: 50.4 us
  Pallas kernels  22.6 us (44%)
  starting transfers between devices  17.3 us (34%)
  local copies, waits for them, and re-layouts  4.63 us (9%)
  waiting for transfers between devices  4.38 us (9%)
  between operations  0.9 us (2%)
  other arithmetic  0.62 us (1%)
    pallas_call x2, Pallas kernels, sample_values(): pl.pallas_call(functools.partial(samples_kernel, own), out_shape=jax.Shap...  12.4 us
    all_to_all x1, starting transfers between devices, on_device(): lax.all_to_all(places, 'tile', split_axis=0, concat_axis=0, tiled=True)  6.34 us
    all_to_all x1, starting transfers between devices, on_device(): lax.all_to_all(found, 'tile', split_axis=0, concat_axis=0, tiled=True)  5.63 us
    pallas_call x1, Pallas kernels, encoder(): pl.pallas_call(encoder_kernel, out_shape=(jax.ShapeDtypeStruct((height +...  3.73 us
    pallas_call x1, Pallas kernels, decoder(): pl.pallas_call(decoder_kernel, out_shape=jax.ShapeDtypeStruct((1, colours...  2.57 us
    ppermute x1, starting transfers between devices, on_device(): over = lax.ppermute(pending, 'tile', down)  2.52 us
    all_to_all x1, waiting for transfers between devices, on_device(): lax.all_to_all(found, 'tile', split_axis=0, concat_axis=0, tiled=True)  2.34 us
    reshape x1, local copies, waits for them, and re-layouts, windows_of(): cube = bricks.reshape(count, EDGE, EDGE * EDGE)  2.33 us
  transfers between devices with their start and end apart: 5, of which 3 were waited for; matrix products, arithmetic and copies ran while one was open for 7% of the time, Pallas kernels for 40%

profile of v7, /device:TPU:0, one launch (start us, length us, event | category | flops | bytes accessed | tf_op | source)
XLA Modules:
  0.0 50.4 jit_solution(13067552915107687406)
XLA Ops:
  0.7 2.2 %positions.1.place_ref = f32[8,120,128]{2,1,0:T(8,128)} custom-call(s32[3,320,128]{2,1,0:T(8,128)} %bitcast.13, f32[3,320,128]{2,1,0:T(8,128)} %bitcast.14), custom_call_target="tpu_custom_call" | custom-call | flops 122880 | bytes 1474560 | tf_op jit(solution)/shard_map/positions/pallas_call | solution.py:82
  2.8 6.3 %all-to-all-start = ((f32[8,120,128]{2,1,0:T(8,128)}), f32[8,120,128]{2,1,0:T(8,128)}, u32[]{:S(2)}, u32[]{:S(2)}) async-start(f32[8,120,128]{2,1,0:T(8,128)} %positions.1.place_ref), calls=%async_computation | async-start | bytes 983040 | tf_op jit(solution)/shard_map/all_to_all | solution.py:610
  9.2 0.0 copy-start.7
  9.2 2.5 %collective-permute-start = (bf16[1,4,8,256]{3,1,2,0:T(4,128)(2,1)S(1)}, bf16[1,4,8,256]{3,1,2,0:T(4,128)(2,1)S(1)}, u32[]{:S(2)}, u32[]{:S(2)}) collective-permute-start(bf16[1,4,8,256]{3,1,2,0:T(4,128)(2,1)S(1)} %copy.19), channel_id=1, source_target_pairs={{0,1},{1,2},{2,3},{3,4},{4,5},{5,6},{6,7},{8,9},{9,10},{10,11},{11... | collective-permute-start | bytes 49160 | tf_op jit(solution)/shard_map/ppermute | solution.py:614
  11.7 1.3 %collective-permute-start.1 = (bf16[1,4,8,256]{3,1,2,0:T(4,128)(2,1)S(1)}, bf16[1,4,8,256]{3,1,2,0:T(4,128)(2,1)S(1)}, u32[]{:S(2)}, u32[]{:S(2)}) collective-permute-start(bf16[1,4,8,256]{3,1,2,0:T(4,128)(2,1)S(1)} %copy.19), channel_id=1, source_target_pairs={{1,0},{2,1},{3,2},{4,3},{5,4},{6,5},{7,6},{9,8},{10,9},{11,10},{12... | collective-permute-start | bytes 49160 | tf_op jit(solution)/shard_map/ppermute | solution.py:615
  13.1 2.3 %reshape.15.cube_ref = bf16[16,34,1156]{2,1,0:T(8,128)(2,1)S(1)} reshape(bf16[16,39304]{1,0:T(8,128)(2,1)S(1)} %copy-done.6) | data formatting | bytes 2515456 | tf_op jit(solution)/shard_map/reshape | solution.py:136
  15.4 0.2 copy.23.w_down
  15.6 0.1 copy.22
  15.8 1.5 %brick_windows.1.brick_ref = bf16[16,208,256]{2,1,0:T(8,128)(2,1)S(1)} custom-call(bf16[16,34,1156]{2,1,0:T(8,128)(2,1)S(1)} %reshape.15.cube_ref), custom_call_target="tpu_custom_call" | custom-call | flops 905969664 | bytes 4194304 | tf_op jit(solution)/shard_map/brick_windows/pallas_call | solution.py:137
  17.4 1.2 %copy-done = bf16[16,208,256]{2,1,0:T(8,128)(2,1)} copy-done((bf16[16,208,256]{2,1,0:T(8,128)(2,1)}, bf16[16,208,256]{2,1,0:T(8,128)(2,1)S(1)}, u32[]{:S(2)}) %copy-start) | copy-done | bytes 1703960
  18.6 0.6 %pad_add_fusion.where_ref = s32[2]{0:T(128)} fusion(s32[1]{0:T(128)} %constant.2.clone.1, s32[1]{0:T(128)} %bitcast.2), kind=kLoop, calls=%fused_computation.2 | loop fusion | flops 2 | bytes 16 | tf_op jit(solution)/shard_map/stack | solution.py:617
  19.2 3.3 %own_values.1.rest_0_ = bf16[1,40,128]{2,1,0:T(8,128)(2,1)} custom-call(s32[2]{0:T(128)} %pad_add_fusion.where_ref, s32[2,8]{1,0:T(2,128)} %bitcast.18, bf16[16,208,256]{2,1,0:T(8,128)(2,1)} %copy-done, f32[8,120,128]{2,1,0:T(8,128)} %positions.1.place_ref), custom_call_target="tpu_custom_call" | custom-call | flops 545259520 | bytes 262144 | tf_op jit(solution)/shard_map/own_values/pallas_call | solution.py:297
  22.4 0.0 copy-start.2
  22.5 1.5 %all-to-all-done.place_ref = f32[8,120,128]{2,1,0:T(8,128)} async-done(((f32[8,120,128]{2,1,0:T(8,128)}), f32[8,120,128]{2,1,0:T(8,128)}, u32[]{:S(2)}, u32[]{:S(2)}) %all-to-all-start) | async-done | bytes 491552 | tf_op jit(solution)/shard_map/all_to_all | solution.py:610
  23.9 9.1 %sample_values.1 = bf16[8,40,128]{2,1,0:T(8,128)(2,1)} custom-call(s32[2]{0:T(128)} %pad_add_fusion.where_ref, s32[2,8]{1,0:T(2,128)} %bitcast.19, bf16[16,208,256]{2,1,0:T(8,128)(2,1)} %copy-done, f32[8,120,128]{2,1,0:T(8,128)} %all-to-all-done.place_ref, bf16[1,40,128]{2,1,0:T(8,128)(2,1)} %own_values.1.rest_0_), custom_call_target="tpu_custom_call" | custom-call | flops 3816816640 | bytes 1835008 | tf_op jit(solution)/shard_map/sample_values/pallas_call | solution.py:297
  33.2 5.6 %all-to-all-start.1 = ((bf16[8,40,128]{2,1,0:T(8,128)(2,1)}), bf16[8,40,128]{2,1,0:T(8,128)(2,1)S(1)}, u32[]{:S(2)}, u32[]{:S(2)}) async-start(bf16[8,40,128]{2,1,0:T(8,128)(2,1)} %sample_values.1), calls=%async_computation.1 | async-start | bytes 163840 | tf_op jit(solution)/shard_map/all_to_all | solution.py:623
  38.8 0.0 copy-start.1
  38.9 3.7 %encoder.1 = (bf16[12,32,256]{2,1,0:T(8,128)(2,1)S(1)}, bf16[6,112,128]{2,1,0:T(8,128)(2,1)S(1)}) custom-call(s32[2]{0:T(128)S(1)} %copy-done.2, bf16[24,16,256]{2,1,0:T(8,128)(2,1)S(1)} %pad.12.x_ref, bf16[9,32,16]{2,1,0:T(8,128)(2,1)S(1)} %pad.13.w_in, bf16[9,32,32]{2,1,0:T(8,128)(2,1)S(1)} %copy-done.5, bf16[9,112,32]{2,1,0:T(8,128)(2,1)S(1)} %copy.23.w_down, ...), custom_call_target="tpu_custom_call" | custom-call | flops 2000000000 | bytes 2097152 | tf_op jit(solution)/shard_map/encoder/pallas_call | solution.py:539
  42.6 2.3 %all-to-all-done.1.value_ref = bf16[8,40,128]{2,1,0:T(8,128)(2,1)S(1)} async-done(((bf16[8,40,128]{2,1,0:T(8,128)(2,1)}), bf16[8,40,128]{2,1,0:T(8,128)(2,1)S(1)}, u32[]{:S(2)}, u32[]{:S(2)}) %all-to-all-start.1) | async-done | bytes 81952 | tf_op jit(solution)/shard_map/all_to_all | solution.py:623
  44.9 0.2 gbuffer.1
  45.2 1.5 %collective-permute-start.2 = (bf16[1,4,8,256]{3,2,1,0:T(8,128)(2,1)S(1)}, bf16[1,4,8,256]{3,2,1,0:T(8,128)(2,1)S(1)}, u32[]{:S(2)}, u32[]{:S(2)}) collective-permute-start(bf16[1,4,8,256]{3,2,1,0:T(8,128)(2,1)S(1)} %gbuffer.1), channel_id=1, source_target_pairs={{0,8},{8,16},{16,24},{24,0},{1,9},{9,17},{17,25},{25,1},{2,10},{10... | collective-permute-start | bytes 49160 | tf_op jit(solution)/shard_map/ppermute | solution.py:634
  46.7 2.6 %decoder.1 = bf16[1,3,8,256]{3,2,1,0:T(8,128)(2,1)} custom-call(s32[2]{0:T(128)S(1)} %copy-done.2, bf16[12,32,256]{2,1,0:T(8,128)(2,1)S(1)} %get-tuple-element.30.skip_ref, bf16[6,112,128]{2,1,0:T(8,128)(2,1)S(1)} %get-tuple-element.31.fourth, bf16[9,32,144]{2,1,0:T(8,128)(2,1)S(1)} %copy-done.4, bf16[9,16,32]{2,1,0:T(8,128)(2,1)S(1)} %pad.14.w_out), custom_call_target="tpu_custom_call" | custom-call | flops 1000000000 | bytes 1048576 | tf_op jit(solution)/shard_map/decoder/pallas_call | solution.py:565
  49.3 0.6 %collective-permute-done.2 = bf16[1,4,8,256]{3,2,1,0:T(8,128)(2,1)S(1)} collective-permute-done((bf16[1,4,8,256]{3,2,1,0:T(8,128)(2,1)S(1)}, bf16[1,4,8,256]{3,2,1,0:T(8,128)(2,1)S(1)}, u32[]{:S(2)}, u32[]{:S(2)}) %collective-permute-start.2) | collective-permute-done | bytes 16416 | tf_op jit(solution)/shard_map/ppermute | solution.py:634
  49.8 0.6 %copy.27 = bf16[1,4,8,256]{3,2,1,0:T(8,128)(2,1)} copy(bf16[1,4,8,256]{3,2,1,0:T(8,128)(2,1)S(1)} %collective-permute-done.2) | data formatting | bytes 32768
  (26 shorter events, 0.2 us)
Async XLA Ops:
  0.6 12.4 %copy-start.6 = (bf16[16,39304]{1,0:T(8,128)(2,1)S(1)}, bf16[16,39304]{1,0:T(8,128)(2,1)}, u32[]{:S(2)}) copy-start(bf16[16,39304]{1,0:T(8,128)(2,1)} %param.12) | copy-start | bytes 3773188
  0.6 8.5 %copy-start.8 = (bf16[1,4,8,256]{3,2,1,0:T(8,128)(2,1)S(1)}, bf16[1,4,8,256]{3,2,1,0:T(8,128)(2,1)}, u32[]{:S(2)}) copy-start(bf16[1,4,8,256]{3,2,1,0:T(8,128)(2,1)} %param.17) | copy-start | bytes 49156
  2.8 21.1 %all-to-all-start = ((f32[8,120,128]{2,1,0:T(8,128)}), f32[8,120,128]{2,1,0:T(8,128)}, u32[]{:S(2)}, u32[]{:S(2)}) async-start(f32[8,120,128]{2,1,0:T(8,128)} %positions.1.place_ref), calls=%async_computation | async-start | bytes 983040 | tf_op jit(solution)/shard_map/all_to_all | solution.py:610
  9.2 6.2 %copy-start.7 = (bf16[9,112,32]{1,2,0:T(8,128)(2,1)S(1)}, bf16[9,112,32]{1,2,0:T(8,128)(2,1)}, u32[]{:S(2)}) copy-start(bf16[9,112,32]{1,2,0:T(8,128)(2,1)} %param.20) | copy-start | bytes 193540
  9.2 6.4 %copy-start.9 = (bf16[9,32,4]{1,2,0:T(4,128)(2,1)S(1)}, bf16[9,32,4]{1,2,0:T(4,128)(2,1)}, u32[]{:S(2)}) copy-start(bf16[9,32,4]{1,2,0:T(4,128)(2,1)} %param.18) | copy-start | bytes 6916
  9.2 23.9 %collective-permute-start = (bf16[1,4,8,256]{3,1,2,0:T(4,128)(2,1)S(1)}, bf16[1,4,8,256]{3,1,2,0:T(4,128)(2,1)S(1)}, u32[]{:S(2)}, u32[]{:S(2)}) collective-permute-start(bf16[1,4,8,256]{3,1,2,0:T(4,128)(2,1)S(1)} %copy.19), channel_id=1, source_target_pairs={{0,1},{1,2},{2,3},{3,4},{4,5},{5,6},{6,7},{8,9},{9,10},{10,11},{11... | collective-permute-start | bytes 49160 | tf_op jit(solution)/shard_map/ppermute | solution.py:614
  11.7 21.4 %collective-permute-start.1 = (bf16[1,4,8,256]{3,1,2,0:T(4,128)(2,1)S(1)}, bf16[1,4,8,256]{3,1,2,0:T(4,128)(2,1)S(1)}, u32[]{:S(2)}, u32[]{:S(2)}) collective-permute-start(bf16[1,4,8,256]{3,1,2,0:T(4,128)(2,1)S(1)} %copy.19), channel_id=1, source_target_pairs={{1,0},{2,1},{3,2},{4,3},{5,4},{6,5},{7,6},{9,8},{10,9},{11,10},{12... | collective-permute-start | bytes 49160 | tf_op jit(solution)/shard_map/ppermute | solution.py:615
  13.1 2.7 %copy-start.10 = (bf16[9,3,32]{2,1,0:T(4,128)(2,1)S(1)}, bf16[9,3,32]{2,1,0:T(4,128)(2,1)}, u32[]{:S(2)}) copy-start(bf16[9,3,32]{2,1,0:T(4,128)(2,1)} %param.23) | copy-start | bytes 5188
  17.4 1.2 %copy-start = (bf16[16,208,256]{2,1,0:T(8,128)(2,1)}, bf16[16,208,256]{2,1,0:T(8,128)(2,1)S(1)}, u32[]{:S(2)}) copy-start(bf16[16,208,256]{2,1,0:T(8,128)(2,1)S(1)} %brick_windows.1.brick_ref) | copy-start | bytes 5111812
  22.4 16.4 %copy-start.2 = (s32[2]{0:T(128)S(1)}, s32[2]{0:T(128)}, u32[]{:S(2)}) copy-start(s32[2]{0:T(128)} %pad_add_fusion.where_ref) | copy-start | bytes 28
  22.4 16.4 %copy-start.3 = (bf16[9,112,112]{2,1,0:T(8,128)(2,1)S(1)}, bf16[9,112,112]{2,1,0:T(8,128)(2,1)}, u32[]{:S(2)}) copy-start(bf16[9,112,112]{2,1,0:T(8,128)(2,1)} %w_deep.1) | copy-start | bytes 677380
  22.5 16.4 %copy-start.5 = (bf16[9,32,32]{2,1,0:T(8,128)(2,1)S(1)}, bf16[9,32,32]{2,1,0:T(8,128)(2,1)}, u32[]{:S(2)}) copy-start(bf16[9,32,32]{2,1,0:T(8,128)(2,1)} %w_mid.1) | copy-start | bytes 55300
  33.2 11.7 %all-to-all-start.1 = ((bf16[8,40,128]{2,1,0:T(8,128)(2,1)}), bf16[8,40,128]{2,1,0:T(8,128)(2,1)S(1)}, u32[]{:S(2)}, u32[]{:S(2)}) async-start(bf16[8,40,128]{2,1,0:T(8,128)(2,1)} %sample_values.1), calls=%async_computation.1 | async-start | bytes 163840 | tf_op jit(solution)/shard_map/all_to_all | solution.py:623
  38.8 6.1 %copy-start.1 = (s32[1,1,160,256]{3,2,1,0:T(8,128)S(1)}, s32[1,1,160,256]{3,2,1,0:T(8,128)}, u32[]{:S(2)}) copy-start(s32[1,1,160,256]{3,2,1,0:T(8,128)} %order_ref.1) | copy-start | bytes 491524
  38.9 7.8 %copy-start.4 = (bf16[9,32,144]{2,1,0:T(8,128)(2,1)S(1)}, bf16[9,32,144]{2,1,0:T(8,128)(2,1)}, u32[]{:S(2)}) copy-start(bf16[9,32,144]{2,1,0:T(8,128)(2,1)} %w_up.1) | copy-start | bytes 248836
  45.2 4.7 %collective-permute-start.2 = (bf16[1,4,8,256]{3,2,1,0:T(8,128)(2,1)S(1)}, bf16[1,4,8,256]{3,2,1,0:T(8,128)(2,1)S(1)}, u32[]{:S(2)}, u32[]{:S(2)}) collective-permute-start(bf16[1,4,8,256]{3,2,1,0:T(8,128)(2,1)S(1)} %gbuffer.1), channel_id=1, source_target_pairs={{0,8},{8,16},{16,24},{24,0},{1,9},{9,17},{17,25},{25,1},{2,10},{10... | collective-permute-start | bytes 49160 | tf_op jit(solution)/shard_map/ppermute | solution.py:634

commit v8 on v7

--- a/solution.py
+++ b/solution.py
@@ -203,115 +203,107 @@
     return total
 
 
-def samples_kernel(
-    own, where_ref, picks_ref, brick_ref, place_ref, *rest
-):
-    if own:
-        out_ref, bricks, places, sums, arrivals = rest
-    else:
-        own_ref, out_ref, bricks, places, sums, arrivals = rest
+def samples_kernel(picks_ref, brick_ref, place_ref, out_ref, bricks, places, sums, arrivals):
     owners, rows, _ = place_ref.shape
     cap = picks_ref.shape[0]
     lines = rows // 3
     per_slot = lines // 2 // cap
-    count = 1 if own else owners - 1
-    tile = where_ref[0]
-    if not own:
-        out_ref[tile] = own_ref[0]
-
-    def renderer_of(turn):
-        return tile if own else lax.rem(tile + 1 + turn, owners)
+    group = places.shape[1]
+    turns = owners // group
 
     def fetches(turn):
         held = turn % 2
-        renderer = renderer_of(turn)
-        copies = [
-            pltpu.make_async_copy(
-                place_ref.at[renderer], places.at[held], arrivals.at[held, cap]
-            )
-        ]
-        for piece in range(cap):
+        copies = []
+        for member in range(group):
+            renderer = turn * group + member
             copies.append(
                 pltpu.make_async_copy(
-                    brick_ref.at[picks_ref[piece, renderer]],
-                    bricks.at[held, piece],
-                    arrivals.at[held, piece],
+                    place_ref.at[renderer],
+                    places.at[held, member],
+                    arrivals.at[held, member, cap],
                 )
             )
+            for piece in range(cap):
+                copies.append(
+                    pltpu.make_async_copy(
+                        brick_ref.at[picks_ref[piece, renderer]],
+                        bricks.at[held, member, piece],
+                        arrivals.at[held, member, piece],
+                    )
+                )
         return copies
 
-    for turn in range(min(2, count)):
+    for turn in range(min(2, turns)):
         for copy in fetches(turn):
             copy.start()
 
     def one_turn(turn, carry):
         held = turn % 2
-        copies = fetches(turn)
-        copies[0].wait()
-        for piece in range(cap):
-            copies[1 + piece].wait()
-            brick = bricks[held, piece]
-            for step in range(per_slot):
-                row = 2 * (piece * per_slot + step)
-
-                def line(axis):
-                    both = [
-                        jnp.broadcast_to(
-                            places[held, pl.ds(axis * lines + row + half, 1), :], (8, LANES)
-                        )
-                        for half in range(2)
-                    ]
-                    return jnp.concatenate(both, axis=1)
-
-                total = blend(brick, line(0), line(1), line(2))
-                for half in range(2):
-                    sums[8 * (row + half) : 8 * (row + half + 1), :] = total[
-                        :, half * LANES : (half + 1) * LANES
-                    ]
-
-        @pl.when(turn + 2 < count)
+        for copy in fetches(turn):
+            copy.wait()
+        for member in range(group):
+            for piece in range(cap):
+                brick = bricks[held, member, piece]
+                for step in range(per_slot):
+                    row = 2 * (piece * per_slot + step)
+
+                    def line(axis):
+                        both = [
+                            jnp.broadcast_to(
+                                places[held, member, pl.ds(axis * lines + row + half, 1), :],
+                                (8, LANES),
+                            )
+                            for half in range(2)
+                        ]
+                        return jnp.concatenate(both, axis=1)
+
+                    total = blend(brick, line(0), line(1), line(2))
+                    for half in range(2):
+                        sums[member, 8 * (row + half) : 8 * (row + half + 1), :] = total[
+                            :, half * LANES : (half + 1) * LANES
+                        ]
+            values = []
+            for row in range(0, lines, 8):
+                value = sums[member, pl.ds(8 * row, 8, stride=8), :]
+                for other in range(1, 8):
+                    value = value + sums[member, pl.ds(8 * row + other, 8, stride=8), :]
+                values.append(value)
+            out_ref[turn * group + member] = jnp.concatenate(values, axis=0).astype(BF16)
+
+        @pl.when(turn + 2 < turns)
         def _():
             for copy in fetches(turn + 2):
                 copy.start()
 
-        values = []
-        for row in range(0, lines, 8):
-            value = sums[pl.ds(8 * row, 8, stride=8), :]
-            for other in range(1, 8):
-                value = value + sums[pl.ds(8 * row + other, 8, stride=8), :]
-            values.append(value)
-        out_ref[0 if own else renderer_of(turn)] = jnp.concatenate(values, axis=0).astype(BF16)
         return carry
 
-    lax.fori_loop(0, count, one_turn, 0)
-
-
-def sample_values(where, picks, windows, places, own_values=None):
+    lax.fori_loop(0, turns, one_turn, 0)
+
+
+def sample_values(picks, windows, places):
     owners, rows, _ = places.shape
     cap = picks.shape[0]
-    own = own_values is None
-    count = 1 if own else owners - 1
-    samples = count * rows * LANES // 3
+    group = 2 if owners % 2 == 0 else 1
+    samples = owners * rows * LANES // 3
     some = pl.BlockSpec(memory_space=pl.ANY)
-    extra = () if own else (own_values,)
     return pl.pallas_call(
-        functools.partial(samples_kernel, own),
-        out_shape=jax.ShapeDtypeStruct((1 if own else owners, rows // 3, LANES), BF16),
-        in_specs=[smem(), smem(), some, some] + [vmem()] * len(extra),
+        samples_kernel,
+        out_shape=jax.ShapeDtypeStruct((owners, rows // 3, LANES), BF16),
+        in_specs=[smem(), some, some],
         out_specs=vmem(),
         scratch_shapes=[
-            pltpu.VMEM((2, cap, BRICK_ROWS, KDIM), BF16),
-            pltpu.VMEM((2, rows, LANES), F32),
-            pltpu.VMEM((8 * rows // 3, LANES), F32),
-            pltpu.SemaphoreType.DMA((2, cap + 1)),
+            pltpu.VMEM((2, group, cap, BRICK_ROWS, KDIM), BF16),
+            pltpu.VMEM((2, group, rows, LANES), F32),
+            pltpu.VMEM((group, 8 * rows // 3, LANES), F32),
+            pltpu.SemaphoreType.DMA((2, group, cap + 1)),
         ],
         compiler_params=params(59),
         cost_estimate=pl.CostEstimate(
-            flops=2 * samples * KDIM * BRICK_ROWS, bytes_accessed=count * MIB // 4,
+            flops=2 * samples * KDIM * BRICK_ROWS, bytes_accessed=3 * MIB,
             transcendentals=0,
         ),
-        name="own_values" if own else "sample_values",
-    )(where, picks, windows, places, *extra)
+        name="sample_values",
+    )(picks, windows, places)
 
 
 def gbuffer_kernel(value_ref, order_ref, out_ref, values):
@@ -422,14 +414,9 @@
     return inside
 
 
-def encoder_kernel(
-    where_ref, x_ref, w_in, w_mid, w_down, w_deep, skip_ref, fourth,
-    first, second, pooled, third,
-):
+def stem_kernel(where_ref, x_ref, w_in, w_mid, second, first):
     height = x_ref.shape[0] // 3
-    half_height = height // 2
     width = x_ref.shape[2]
-    half_width = width // 2
     inside = sides(where_ref)
 
     def full_layer(weight, source, target, low, high, unroll):
@@ -447,10 +434,15 @@
     full_layer(beside(w_in), x_ref, first, height - 1, 2 * height - 1, first.shape[0] // 2)
     full_layer(beside(w_mid), first, second, height - 2, 2 * height - 2, second.shape[0] // 2)
 
+
+def middle_kernel(where_ref, second, w_down, w_deep, fourth, pooled, third):
+    count, chans, width = second.shape
+    half_height = (count + 4) // 6
+    half_width = width // 2
+    inside = sides(where_ref)
     place = lax.broadcasted_iota(jnp.int32, (width, half_width), 0) // 2
     target = lax.broadcasted_iota(jnp.int32, (width, half_width), 1)
     shrink = jnp.where(place == target, 0.25, 0.0).astype(BF16)
-    count, chans = second.shape[0], second.shape[1]
     pairs = jnp.dot(
         second[...].reshape(count * chans, width), shrink, preferred_element_type=F32
     ).reshape(count // 2, 2, chans, half_width)
@@ -487,16 +479,14 @@
     half_layer(down_product, third, half_height - 2, 2 * half_height - 2)
     half_layer(deep_product, fourth, half_height - 3, 2 * half_height - 3)
 
-    skip_ref[...] = second[4 : 4 + skip_ref.shape[0]]
-
 
 def decoder_kernel(
-    where_ref, skip_ref, fourth, w_up, w_out, out_ref, joined, fifth, final
+    where_ref, second, fourth, w_up, w_out, out_ref, joined, fifth, final
 ):
     height = out_ref.shape[2]
     width = out_ref.shape[3]
     half_width = width // 2
-    chans = skip_ref.shape[1]
+    chans = second.shape[1]
     inside = sides(where_ref)
     place = lax.broadcasted_iota(jnp.int32, (half_width, width), 0)
     target = lax.broadcasted_iota(jnp.int32, (half_width, width), 1) // 2
@@ -507,7 +497,7 @@
     ).astype(BF16).reshape(fourth.shape[0], deep, width)
     for row in range(2 * fourth.shape[0]):
         joined[row, chans:, :] = wide[row // 2]
-        joined[row, :chans, :] = skip_ref[row]
+        joined[row, :chans, :] = second[row + 4]
 
     def up_step(row, carry):
         total = None
@@ -531,37 +521,49 @@
     out_ref[0] = final[...].astype(BF16)
 
 
-def encoder(where, field, w_in, w_mid, w_down, w_deep):
+def stem(where, field, w_in, w_mid):
     height = field.shape[0] // 3
-    half = height // 2
     width = field.shape[2]
-    one, two = w_mid.shape[1], w_deep.shape[1]
+    one = w_mid.shape[1]
     return pl.pallas_call(
-        encoder_kernel,
-        out_shape=(
-            jax.ShapeDtypeStruct((height + 4, one, width), BF16),
-            jax.ShapeDtypeStruct((3 * half - 6, two, width // 2), BF16),
+        stem_kernel,
+        out_shape=jax.ShapeDtypeStruct((3 * height - 4, one, width), BF16),
+        in_specs=[smem()] + [vmem()] * 3,
+        out_specs=vmem(),
+        scratch_shapes=[pltpu.VMEM((3 * height - 2, one, width), BF16)],
+        compiler_params=params(16),
+        cost_estimate=pl.CostEstimate(
+            flops=1_000_000_000, bytes_accessed=MIB, transcendentals=300_000
         ),
-        in_specs=[smem()] + [vmem()] * 5,
-        out_specs=(vmem(), vmem()),
+        name="stem",
+    )(where, field, w_in, w_mid)
+
+
+def middle(where, second, w_down, w_deep):
+    rows, one, width = second.shape
+    half = (rows + 4) // 6
+    two = w_deep.shape[1]
+    return pl.pallas_call(
+        middle_kernel,
+        out_shape=jax.ShapeDtypeStruct((3 * half - 6, two, width // 2), BF16),
+        in_specs=[smem()] + [vmem()] * 3,
+        out_specs=vmem(),
         scratch_shapes=[
-            pltpu.VMEM((3 * height - 2, one, width), BF16),
-            pltpu.VMEM((3 * height - 4, one, width), BF16),
             pltpu.VMEM((3 * half - 2, one, width // 2), BF16),
             pltpu.VMEM((3 * half - 4, two, width // 2), BF16),
         ],
         compiler_params=params(16),
         cost_estimate=pl.CostEstimate(
-            flops=2_000_000_000, bytes_accessed=2 * MIB, transcendentals=400_000
+            flops=1_000_000_000, bytes_accessed=MIB, transcendentals=200_000
         ),
-        name="encoder",
-    )(where, field, w_in, w_mid, w_down, w_deep)
-
-
-def decoder(where, skip, deep, w_up, w_out, height, colours):
-    one = skip.shape[1]
+        name="middle",
+    )(where, second, w_down, w_deep)
+
+
+def decoder(where, second, deep, w_up, w_out, height, colours):
+    one = second.shape[1]
     two = deep.shape[1]
-    width = skip.shape[2]
+    width = second.shape[2]
     return pl.pallas_call(
         decoder_kernel,
         out_shape=jax.ShapeDtypeStruct((1, colours, height, width), BF16),
@@ -577,7 +579,7 @@
             flops=1_000_000_000, bytes_accessed=MIB, transcendentals=100_000
         ),
         name="decoder",
-    )(where, skip, deep, w_up, w_out)
+    )(where, second, deep, w_up, w_out)
 
 
 def on_device(
@@ -616,23 +618,24 @@
     windows = windows_of(bricks)
     where = jnp.stack([tile, jnp.int32(n_tile)]).astype(jnp.int32)
     picks = sends[0, 0].T
-    own_values = sample_values(where, picks, windows, places)
-    found = sample_values(where, picks, windows, arrived, own_values)
-
-    over, under, pending, found = lax.optimization_barrier((over, under, pending, found))
-    values = lax.all_to_all(found, "tile", split_axis=0, concat_axis=0, tiled=True)
     field = jnp.concatenate([over[0], pending[0], under[0]], axis=1).transpose(1, 0, 2)
     field = jnp.pad(field, ((0, 0), (0, 16 - field.shape[1]), (0, 0)))
     colours = w_out.shape[1]
     w_in = jnp.pad(w_in, ((0, 0), (0, 0), (0, 16 - w_in.shape[2])))
     w_out = jnp.pad(w_out, ((0, 0), (0, 16 - colours), (0, 0)))
-    skip, deep = encoder(where, field, w_in, w_mid, w_down, w_deep)
-    values, skip, deep = lax.optimization_barrier((values, skip, deep))
+
+    second = stem(where, field, w_in, w_mid)
+    arrived, second, w_down, w_out = lax.optimization_barrier((arrived, second, w_down, w_out))
+    found = sample_values(picks, windows, arrived)
+    found, second = lax.optimization_barrier((found, second))
+    values = lax.all_to_all(found, "tile", split_axis=0, concat_axis=0, tiled=True)
+    deep = middle(where, second, w_down, w_deep)
+    values, deep = lax.optimization_barrier((values, deep))
     rendered = gbuffer(trim(values), sample_order, height, width)
-    rendered, skip, deep = lax.optimization_barrier((rendered, skip, deep))
+    rendered, deep = lax.optimization_barrier((rendered, deep))
     ring = [(i, (i + 1) % n_section) for i in range(n_section)]
     handoff = lax.ppermute(rendered, "section", ring)
-    denoised = decoder(where, skip, deep, w_up, w_out, height, colours)
+    denoised = decoder(where, second, deep, w_up, w_out, height, colours)
     return (handoff, denoised)
 
 

time: 50.9 us -> 49.4 us (0.971)
  waiting for transfers between devices: 4.38 us -> 7.21 us
  Pallas kernels: 22.6 us -> 19.9 us
  starting transfers between devices: 17.3 us -> 16.4 us
    pallas_call x3, Pallas kernels: 16.1 us -> 13.4 us  [the longest x1 9.19 us: sample_values(): pl.pallas_call(samples_kernel, out_shape=jax.ShapeDtypeStruct((owners, ro...]
    all_to_all x1, waiting for transfers between devices: 2.34 us -> 3.99 us  [on_device(): lax.all_to_all(found, 'tile', split_axis=0, concat_axis=0, tiled=True)]
    all_to_all x1, starting transfers between devices: 5.63 us -> 4.27 us  [on_device(): lax.all_to_all(found, 'tile', split_axis=0, concat_axis=0, tiled=True)]
    all_to_all x1, waiting for transfers between devices: 1.45 us -> 2.56 us  [on_device(): lax.all_to_all(places, 'tile', split_axis=0, concat_axis=0, tiled=True)]
    unnamed x25 -> x22, local copies, waits for them, and re-layouts: 2.23 us -> 1.98 us
  transfers between devices with their start and end apart: 5 -> 5, of which waited for: 3 -> 3; matrix products, arithmetic and copies ran while one was open for 7% -> 6% of each run, Pallas kernels for 40% -> 17%
where the time goes in v8:
time: 49.4 us; the launch traced here: 49 us
  Pallas kernels  19.9 us (40%)
  starting transfers between devices  16.4 us (33%)
  waiting for transfers between devices  7.21 us (15%)
  local copies, waits for them, and re-layouts  4.57 us (9%)
  between operations  0.84 us (2%)
    pallas_call x1, Pallas kernels, sample_values(): pl.pallas_call(samples_kernel, out_shape=jax.ShapeDtypeStruct((owners, ro...  9.19 us
    all_to_all x1, starting transfers between devices, on_device(): lax.all_to_all(places, 'tile', split_axis=0, concat_axis=0, tiled=True)  6.34 us
    all_to_all x1, starting transfers between devices, on_device(): lax.all_to_all(found, 'tile', split_axis=0, concat_axis=0, tiled=True)  4.27 us
    all_to_all x1, waiting for transfers between devices, on_device(): lax.all_to_all(found, 'tile', split_axis=0, concat_axis=0, tiled=True)  3.99 us
    ppermute x1, starting transfers between devices, on_device(): over = lax.ppermute(pending, 'tile', down)  3.03 us
    pallas_call x1, Pallas kernels, decoder(): pl.pallas_call(decoder_kernel, out_shape=jax.ShapeDtypeStruct((1, colours...  2.56 us
    all_to_all x1, waiting for transfers between devices, on_device(): lax.all_to_all(places, 'tile', split_axis=0, concat_axis=0, tiled=True)  2.56 us
    pallas_call x1, Pallas kernels, stem(): pl.pallas_call(stem_kernel, out_shape=jax.ShapeDtypeStruct((3 * height -...  2.35 us
  transfers between devices with their start and end apart: 5, of which 3 were waited for; matrix products, arithmetic and copies ran while one was open for 6% of the time, Pallas kernels for 17%

profile of v8, /device:TPU:0, one launch (start us, length us, event | category | flops | bytes accessed | tf_op | source)
XLA Modules:
  0.0 49.0 jit_solution(1633586100488090648)
XLA Ops:
  0.7 2.2 %positions.1 = f32[8,120,128]{2,1,0:T(8,128)} custom-call(s32[3,320,128]{2,1,0:T(8,128)} %bitcast.13, f32[3,320,128]{2,1,0:T(8,128)} %bitcast.14), custom_call_target="tpu_custom_call" | custom-call | flops 122880 | bytes 1474560 | tf_op jit(solution)/shard_map/positions/pallas_call | solution.py:82
  2.8 6.3 %all-to-all-start = ((f32[8,120,128]{2,1,0:T(8,128)}), f32[8,120,128]{2,1,0:T(8,128)}, u32[]{:S(2)}, u32[]{:S(2)}) async-start(f32[8,120,128]{2,1,0:T(8,128)} %positions.1), calls=%async_computation | async-start | bytes 983040 | tf_op jit(solution)/shard_map/all_to_all | solution.py:612
  9.2 1.3 %collective-permute-start.1 = (bf16[1,4,8,256]{3,1,2,0:T(4,128)(2,1)S(1)}, bf16[1,4,8,256]{3,1,2,0:T(4,128)(2,1)S(1)}, u32[]{:S(2)}, u32[]{:S(2)}) collective-permute-start(bf16[1,4,8,256]{3,1,2,0:T(4,128)(2,1)S(1)} %copy.26), channel_id=1, source_target_pairs={{1,0},{2,1},{3,2},{4,3},{5,4},{6,5},{7,6},{9,8},{10,9},{11,10},{12... | collective-permute-start | bytes 49160 | tf_op jit(solution)/shard_map/ppermute | solution.py:617
  10.5 3.0 %collective-permute-start = (bf16[1,4,8,256]{3,1,2,0:T(4,128)(2,1)S(1)}, bf16[1,4,8,256]{3,1,2,0:T(4,128)(2,1)S(1)}, u32[]{:S(2)}, u32[]{:S(2)}) collective-permute-start(bf16[1,4,8,256]{3,1,2,0:T(4,128)(2,1)S(1)} %copy.26), channel_id=1, source_target_pairs={{0,1},{1,2},{2,3},{3,4},{4,5},{5,6},{6,7},{8,9},{9,10},{10,11},{11... | collective-permute-start | bytes 49160 | tf_op jit(solution)/shard_map/ppermute | solution.py:616
  13.5 2.3 %reshape.15.cube_ref = bf16[16,34,1156]{2,1,0:T(8,128)(2,1)S(1)} reshape(bf16[16,39304]{1,0:T(8,128)(2,1)S(1)} %copy-done.5) | data formatting | bytes 2515456 | tf_op jit(solution)/shard_map/reshape | solution.py:136
  15.9 0.1 pad_add_fusion.where_ref
  16.0 1.5 %brick_windows.1.brick_ref = bf16[16,208,256]{2,1,0:T(8,128)(2,1)S(1)} custom-call(bf16[16,34,1156]{2,1,0:T(8,128)(2,1)S(1)} %reshape.15.cube_ref), custom_call_target="tpu_custom_call" | custom-call | flops 905969664 | bytes 4194304 | tf_op jit(solution)/shard_map/brick_windows/pallas_call | solution.py:137
  17.5 1.2 %copy-done.4 = bf16[16,208,256]{2,1,0:T(8,128)(2,1)} copy-done((bf16[16,208,256]{2,1,0:T(8,128)(2,1)}, bf16[16,208,256]{2,1,0:T(8,128)(2,1)S(1)}, u32[]{:S(2)}) %copy-start.4) | copy-done | bytes 1703960
  18.7 0.1 copy.22
  18.9 0.0 collective-permute-done
  19.0 2.3 %stem.1.second = bf16[20,32,256]{2,1,0:T(8,128)(2,1)S(1)} custom-call(s32[2]{0:T(128)S(1)} %pad_add_fusion.where_ref, bf16[24,16,256]{2,1,0:T(8,128)(2,1)S(1)} %pad.12.x_ref, bf16[9,32,16]{2,1,0:T(8,128)(2,1)S(1)} %pad.13.w_in, bf16[9,32,32]{2,1,0:T(8,128)(2,1)S(1)} %copy-done.3), custom_call_target="tpu_custom_call" | custom-call | flops 1000000000 | bytes 1048576 | tf_op jit(solution)/shard_map/stem/pallas_call | solution.py:528
  21.4 2.6 %all-to-all-done.place_ref = f32[8,120,128]{2,1,0:T(8,128)} async-done(((f32[8,120,128]{2,1,0:T(8,128)}), f32[8,120,128]{2,1,0:T(8,128)}, u32[]{:S(2)}, u32[]{:S(2)}) %all-to-all-start) | async-done | bytes 491552 | tf_op jit(solution)/shard_map/all_to_all | solution.py:612
  23.9 9.2 %sample_values.1 = bf16[8,40,128]{2,1,0:T(8,128)(2,1)} custom-call(s32[2,8]{1,0:T(2,128)} %bitcast.18, bf16[16,208,256]{2,1,0:T(8,128)(2,1)} %copy-done.4, f32[8,120,128]{2,1,0:T(8,128)} %all-to-all-done.place_ref), custom_call_target="tpu_custom_call" | custom-call | flops 4362076160 | bytes 3145728 | tf_op jit(solution)/shard_map/sample_values/pallas_call | solution.py:289
  33.1 4.3 %all-to-all-start.1 = ((bf16[8,40,128]{2,1,0:T(8,128)(2,1)}), bf16[8,40,128]{2,1,0:T(8,128)(2,1)S(1)}, u32[]{:S(2)}, u32[]{:S(2)}) async-start(bf16[8,40,128]{2,1,0:T(8,128)(2,1)} %sample_values.1), calls=%async_computation.1 | async-start | bytes 163840 | tf_op jit(solution)/shard_map/all_to_all | solution.py:631
  37.4 0.2 copy.23.w_down
  37.6 0.0 copy-start
  37.6 0.0 copy-start.2
  37.6 1.9 %middle.1.fourth = bf16[6,112,128]{2,1,0:T(8,128)(2,1)S(1)} custom-call(s32[2]{0:T(128)S(1)} %pad_add_fusion.where_ref, bf16[20,32,256]{2,1,0:T(8,128)(2,1)S(1)} %stem.1.second, bf16[9,112,32]{2,1,0:T(8,128)(2,1)S(1)} %copy.23.w_down, bf16[9,112,112]{2,1,0:T(8,128)(2,1)S(1)} %copy-done.1), custom_call_target="tpu_custom_call" | custom-call | flops 1000000000 | bytes 1048576 | tf_op jit(solution)/shard_map/middle/pallas_call | solution.py:546
  39.5 4.0 %all-to-all-done.1.value_ref = bf16[8,40,128]{2,1,0:T(8,128)(2,1)S(1)} async-done(((bf16[8,40,128]{2,1,0:T(8,128)(2,1)}), bf16[8,40,128]{2,1,0:T(8,128)(2,1)S(1)}, u32[]{:S(2)}, u32[]{:S(2)}) %all-to-all-start.1) | async-done | bytes 81952 | tf_op jit(solution)/shard_map/all_to_all | solution.py:631
  43.5 0.2 gbuffer.1
  43.7 1.5 %collective-permute-start.2 = (bf16[1,4,8,256]{3,2,1,0:T(8,128)(2,1)S(1)}, bf16[1,4,8,256]{3,2,1,0:T(8,128)(2,1)S(1)}, u32[]{:S(2)}, u32[]{:S(2)}) collective-permute-start(bf16[1,4,8,256]{3,2,1,0:T(8,128)(2,1)S(1)} %gbuffer.1), channel_id=1, source_target_pairs={{0,8},{8,16},{16,24},{24,0},{1,9},{9,17},{17,25},{25,1},{2,10},{10... | collective-permute-start | bytes 49160 | tf_op jit(solution)/shard_map/ppermute | solution.py:637
  45.2 2.6 %decoder.1 = bf16[1,3,8,256]{3,2,1,0:T(8,128)(2,1)} custom-call(s32[2]{0:T(128)S(1)} %pad_add_fusion.where_ref, bf16[20,32,256]{2,1,0:T(8,128)(2,1)S(1)} %stem.1.second, bf16[6,112,128]{2,1,0:T(8,128)(2,1)S(1)} %middle.1.fourth, bf16[9,32,144]{2,1,0:T(8,128)(2,1)S(1)} %copy-done.2, bf16[9,16,32]{2,1,0:T(8,128)(2,1)S(1)} %pad.14.w_out), custom_call_target="tpu_custom_call" | custom-call | flops 1000000000 | bytes 1048576 | tf_op jit(solution)/shard_map/decoder/pallas_call | solution.py:567
  47.8 0.7 %collective-permute-done.2 = bf16[1,4,8,256]{3,2,1,0:T(8,128)(2,1)S(1)} collective-permute-done((bf16[1,4,8,256]{3,2,1,0:T(8,128)(2,1)S(1)}, bf16[1,4,8,256]{3,2,1,0:T(8,128)(2,1)S(1)}, u32[]{:S(2)}, u32[]{:S(2)}) %collective-permute-start.2) | collective-permute-done | bytes 16416 | tf_op jit(solution)/shard_map/ppermute | solution.py:637
  48.4 0.6 %copy.28 = bf16[1,4,8,256]{3,2,1,0:T(8,128)(2,1)} copy(bf16[1,4,8,256]{3,2,1,0:T(8,128)(2,1)S(1)} %collective-permute-done.2) | data formatting | bytes 32768
  (23 shorter events, 0.1 us)
Async XLA Ops:
  0.6 12.9 %copy-start.5 = (bf16[16,39304]{1,0:T(8,128)(2,1)S(1)}, bf16[16,39304]{1,0:T(8,128)(2,1)}, u32[]{:S(2)}) copy-start(bf16[16,39304]{1,0:T(8,128)(2,1)} %param.12) | copy-start | bytes 3773188
  0.6 8.5 %copy-start.7 = (bf16[1,4,8,256]{3,2,1,0:T(8,128)(2,1)S(1)}, bf16[1,4,8,256]{3,2,1,0:T(8,128)(2,1)}, u32[]{:S(2)}) copy-start(bf16[1,4,8,256]{3,2,1,0:T(8,128)(2,1)} %param.17) | copy-start | bytes 49156
  2.8 21.1 %all-to-all-start = ((f32[8,120,128]{2,1,0:T(8,128)}), f32[8,120,128]{2,1,0:T(8,128)}, u32[]{:S(2)}, u32[]{:S(2)}) async-start(f32[8,120,128]{2,1,0:T(8,128)} %positions.1), calls=%async_computation | async-start | bytes 983040 | tf_op jit(solution)/shard_map/all_to_all | solution.py:612
  9.2 9.7 %collective-permute-start.1 = (bf16[1,4,8,256]{3,1,2,0:T(4,128)(2,1)S(1)}, bf16[1,4,8,256]{3,1,2,0:T(4,128)(2,1)S(1)}, u32[]{:S(2)}, u32[]{:S(2)}) collective-permute-start(bf16[1,4,8,256]{3,1,2,0:T(4,128)(2,1)S(1)} %copy.26), channel_id=1, source_target_pairs={{1,0},{2,1},{3,2},{4,3},{5,4},{6,5},{7,6},{9,8},{10,9},{11,10},{12... | collective-permute-start | bytes 49160 | tf_op jit(solution)/shard_map/ppermute | solution.py:617
  10.5 8.4 %collective-permute-start = (bf16[1,4,8,256]{3,1,2,0:T(4,128)(2,1)S(1)}, bf16[1,4,8,256]{3,1,2,0:T(4,128)(2,1)S(1)}, u32[]{:S(2)}, u32[]{:S(2)}) collective-permute-start(bf16[1,4,8,256]{3,1,2,0:T(4,128)(2,1)S(1)} %copy.26), channel_id=1, source_target_pairs={{0,1},{1,2},{2,3},{3,4},{4,5},{5,6},{6,7},{8,9},{9,10},{10,11},{11... | collective-permute-start | bytes 49160 | tf_op jit(solution)/shard_map/ppermute | solution.py:616
  16.0 2.7 %copy-start.8 = (bf16[9,32,4]{1,2,0:T(4,128)(2,1)S(1)}, bf16[9,32,4]{1,2,0:T(4,128)(2,1)}, u32[]{:S(2)}) copy-start(bf16[9,32,4]{1,2,0:T(4,128)(2,1)} %param.18) | copy-start | bytes 6916
  16.0 2.9 %copy-start.9 = (bf16[9,3,32]{2,1,0:T(4,128)(2,1)S(1)}, bf16[9,3,32]{2,1,0:T(4,128)(2,1)}, u32[]{:S(2)}) copy-start(bf16[9,3,32]{2,1,0:T(4,128)(2,1)} %param.23) | copy-start | bytes 5188
  16.0 3.1 %copy-start.3 = (bf16[9,32,32]{2,1,0:T(8,128)(2,1)S(1)}, bf16[9,32,32]{2,1,0:T(8,128)(2,1)}, u32[]{:S(2)}) copy-start(bf16[9,32,32]{2,1,0:T(8,128)(2,1)} %w_mid.1) | copy-start | bytes 55300
  17.5 1.2 %copy-start.4 = (bf16[16,208,256]{2,1,0:T(8,128)(2,1)}, bf16[16,208,256]{2,1,0:T(8,128)(2,1)S(1)}, u32[]{:S(2)}) copy-start(bf16[16,208,256]{2,1,0:T(8,128)(2,1)S(1)} %brick_windows.1.brick_ref) | copy-start | bytes 5111812
  23.9 13.5 %copy-start.6 = (bf16[9,112,32]{1,2,0:T(8,128)(2,1)S(1)}, bf16[9,112,32]{1,2,0:T(8,128)(2,1)}, u32[]{:S(2)}) copy-start(bf16[9,112,32]{1,2,0:T(8,128)(2,1)} %param.20) | copy-start | bytes 193540
  23.9 13.7 %copy-start.1 = (bf16[9,112,112]{2,1,0:T(8,128)(2,1)S(1)}, bf16[9,112,112]{2,1,0:T(8,128)(2,1)}, u32[]{:S(2)}) copy-start(bf16[9,112,112]{2,1,0:T(8,128)(2,1)} %w_deep.1) | copy-start | bytes 677380
  33.1 10.4 %all-to-all-start.1 = ((bf16[8,40,128]{2,1,0:T(8,128)(2,1)}), bf16[8,40,128]{2,1,0:T(8,128)(2,1)S(1)}, u32[]{:S(2)}, u32[]{:S(2)}) async-start(bf16[8,40,128]{2,1,0:T(8,128)(2,1)} %sample_values.1), calls=%async_computation.1 | async-start | bytes 163840 | tf_op jit(solution)/shard_map/all_to_all | solution.py:631
  37.6 5.9 %copy-start = (s32[1,1,160,256]{3,2,1,0:T(8,128)S(1)}, s32[1,1,160,256]{3,2,1,0:T(8,128)}, u32[]{:S(2)}) copy-start(s32[1,1,160,256]{3,2,1,0:T(8,128)} %order_ref.1) | copy-start | bytes 491524
  37.6 7.6 %copy-start.2 = (bf16[9,32,144]{2,1,0:T(8,128)(2,1)S(1)}, bf16[9,32,144]{2,1,0:T(8,128)(2,1)}, u32[]{:S(2)}) copy-start(bf16[9,32,144]{2,1,0:T(8,128)(2,1)} %w_up.1) | copy-start | bytes 248836
  43.7 4.7 %collective-permute-start.2 = (bf16[1,4,8,256]{3,2,1,0:T(8,128)(2,1)S(1)}, bf16[1,4,8,256]{3,2,1,0:T(8,128)(2,1)S(1)}, u32[]{:S(2)}, u32[]{:S(2)}) collective-permute-start(bf16[1,4,8,256]{3,2,1,0:T(8,128)(2,1)S(1)} %gbuffer.1), channel_id=1, source_target_pairs={{0,8},{8,16},{16,24},{24,0},{1,9},{9,17},{17,25},{25,1},{2,10},{10... | collective-permute-start | bytes 49160 | tf_op jit(solution)/shard_map/ppermute | solution.py:637

commit v9 on v8

--- a/solution.py
+++ b/solution.py
@@ -618,17 +618,18 @@
     windows = windows_of(bricks)
     where = jnp.stack([tile, jnp.int32(n_tile)]).astype(jnp.int32)
     picks = sends[0, 0].T
+    found = sample_values(picks, windows, arrived)
+
+    found, over, under, pending, w_in, w_down, w_out = lax.optimization_barrier(
+        (found, over, under, pending, w_in, w_down, w_out)
+    )
+    values = lax.all_to_all(found, "tile", split_axis=0, concat_axis=0, tiled=True)
     field = jnp.concatenate([over[0], pending[0], under[0]], axis=1).transpose(1, 0, 2)
     field = jnp.pad(field, ((0, 0), (0, 16 - field.shape[1]), (0, 0)))
     colours = w_out.shape[1]
     w_in = jnp.pad(w_in, ((0, 0), (0, 0), (0, 16 - w_in.shape[2])))
     w_out = jnp.pad(w_out, ((0, 0), (0, 16 - colours), (0, 0)))
-
     second = stem(where, field, w_in, w_mid)
-    arrived, second, w_down, w_out = lax.optimization_barrier((arrived, second, w_down, w_out))
-    found = sample_values(picks, windows, arrived)
-    found, second = lax.optimization_barrier((found, second))
-    values = lax.all_to_all(found, "tile", split_axis=0, concat_axis=0, tiled=True)
     deep = middle(where, second, w_down, w_deep)
     values, deep = lax.optimization_barrier((values, deep))
     rendered = gbuffer(trim(values), sample_order, height, width)

time: 49.4 us -> 49.7 us (level)
  starting transfers between devices: 16.4 us -> 14.9 us
  local copies, waits for them, and re-layouts: 4.57 us -> 5.4 us
  waiting for transfers between devices: 7.21 us -> 8.03 us
    all_to_all x1, waiting for transfers between devices: 2.56 us -> 5.75 us  [on_device(): lax.all_to_all(places, 'tile', split_axis=0, concat_axis=0, tiled=True)]
    all_to_all x1, waiting for transfers between devices: 3.99 us -> 1.7 us  [on_device(): lax.all_to_all(found, 'tile', split_axis=0, concat_axis=0, tiled=True)]
    all_to_all x1, starting transfers between devices: 4.27 us -> 3.37 us  [on_device(): lax.all_to_all(found, 'tile', split_axis=0, concat_axis=0, tiled=True)]
    unnamed x22 -> x23, local copies, waits for them, and re-layouts: 1.98 us -> 2.65 us
    ppermute x1, starting transfers between devices: 3.03 us -> 2.4 us  [on_device(): over = lax.ppermute(pending, 'tile', down)]
  transfers between devices with their start and end apart: 5 -> 5, of which waited for: 3 -> 3; matrix products, arithmetic and copies ran while one was open for 6% -> 5% of each run, Pallas kernels for 17% -> 36%
where the time goes in v9:
time: 49.7 us; the launch traced here: 49.3 us
  Pallas kernels  19.9 us (40%)
  starting transfers between devices  14.9 us (30%)
  waiting for transfers between devices  8.03 us (16%)
  local copies, waits for them, and re-layouts  5.4 us (11%)
  between operations  0.88 us (2%)
    pallas_call x1, Pallas kernels, sample_values(): pl.pallas_call(samples_kernel, out_shape=jax.ShapeDtypeStruct((owners, ro...  9.2 us
    all_to_all x1, starting transfers between devices, on_device(): lax.all_to_all(places, 'tile', split_axis=0, concat_axis=0, tiled=True)  6.34 us
    all_to_all x1, waiting for transfers between devices, on_device(): lax.all_to_all(places, 'tile', split_axis=0, concat_axis=0, tiled=True)  5.75 us
    all_to_all x1, starting transfers between devices, on_device(): lax.all_to_all(found, 'tile', split_axis=0, concat_axis=0, tiled=True)  3.37 us
    unnamed x23, local copies, waits for them, and re-layouts  2.65 us
    pallas_call x1, Pallas kernels, decoder(): pl.pallas_call(decoder_kernel, out_shape=jax.ShapeDtypeStruct((1, colours...  2.57 us
    ppermute x1, starting transfers between devices, on_device(): over = lax.ppermute(pending, 'tile', down)  2.4 us
    pallas_call x1, Pallas kernels, stem(): pl.pallas_call(stem_kernel, out_shape=jax.ShapeDtypeStruct((3 * height -...  2.36 us
  transfers between devices with their start and end apart: 5, of which 3 were waited for; matrix products, arithmetic and copies ran while one was open for 5% of the time, Pallas kernels for 36%

profile of v9, /device:TPU:0, one launch (start us, length us, event | category | flops | bytes accessed | tf_op | source)
XLA Modules:
  0.0 49.3 jit_solution(12388218579872998785)
XLA Ops:
  0.7 2.2 %positions.1 = f32[8,120,128]{2,1,0:T(8,128)} custom-call(s32[3,320,128]{2,1,0:T(8,128)} %bitcast.13, f32[3,320,128]{2,1,0:T(8,128)} %bitcast.14), custom_call_target="tpu_custom_call" | custom-call | flops 122880 | bytes 1474560 | tf_op jit(solution)/shard_map/positions/pallas_call | solution.py:82
  2.8 6.3 %all-to-all-start = ((f32[8,120,128]{2,1,0:T(8,128)}), f32[8,120,128]{2,1,0:T(8,128)S(1)}, u32[]{:S(2)}, u32[]{:S(2)}) async-start(f32[8,120,128]{2,1,0:T(8,128)} %positions.1), calls=%async_computation | async-start | bytes 983040 | tf_op jit(solution)/shard_map/all_to_all | solution.py:612
  9.2 2.4 %collective-permute-start = (bf16[1,4,8,256]{3,1,2,0:T(4,128)(2,1)S(1)}, bf16[1,4,8,256]{3,1,2,0:T(4,128)(2,1)S(1)}, u32[]{:S(2)}, u32[]{:S(2)}) collective-permute-start(bf16[1,4,8,256]{3,1,2,0:T(4,128)(2,1)S(1)} %copy.19), channel_id=1, source_target_pairs={{0,1},{1,2},{2,3},{3,4},{4,5},{5,6},{6,7},{8,9},{9,10},{10,11},{11... | collective-permute-start | bytes 49160 | tf_op jit(solution)/shard_map/ppermute | solution.py:616
  11.6 1.3 %collective-permute-start.1 = (bf16[1,4,8,256]{3,1,2,0:T(4,128)(2,1)S(1)}, bf16[1,4,8,256]{3,1,2,0:T(4,128)(2,1)S(1)}, u32[]{:S(2)}, u32[]{:S(2)}) collective-permute-start(bf16[1,4,8,256]{3,1,2,0:T(4,128)(2,1)S(1)} %copy.19), channel_id=1, source_target_pairs={{1,0},{2,1},{3,2},{4,3},{5,4},{6,5},{7,6},{9,8},{10,9},{11,10},{12... | collective-permute-start | bytes 49160 | tf_op jit(solution)/shard_map/ppermute | solution.py:617
  12.9 2.3 %reshape.15.cube_ref = bf16[16,34,1156]{2,1,0:T(8,128)(2,1)S(1)} reshape(bf16[16,39304]{1,0:T(8,128)(2,1)S(1)} %copy-done.5) | data formatting | bytes 2515456 | tf_op jit(solution)/shard_map/reshape | solution.py:136
  15.2 1.5 %brick_windows.1.brick_ref = bf16[16,208,256]{2,1,0:T(8,128)(2,1)S(1)} custom-call(bf16[16,34,1156]{2,1,0:T(8,128)(2,1)S(1)} %reshape.15.cube_ref), custom_call_target="tpu_custom_call" | custom-call | flops 905969664 | bytes 4194304 | tf_op jit(solution)/shard_map/brick_windows/pallas_call | solution.py:137
  16.8 1.2 %copy-done.4 = bf16[16,208,256]{2,1,0:T(8,128)(2,1)} copy-done((bf16[16,208,256]{2,1,0:T(8,128)(2,1)}, bf16[16,208,256]{2,1,0:T(8,128)(2,1)S(1)}, u32[]{:S(2)}) %copy-start.4) | copy-done | bytes 1703960
  18.0 0.1 pad_add_fusion.where_ref
  18.1 5.8 %all-to-all-done.place_ref = f32[8,120,128]{2,1,0:T(8,128)S(1)} async-done(((f32[8,120,128]{2,1,0:T(8,128)}), f32[8,120,128]{2,1,0:T(8,128)S(1)}, u32[]{:S(2)}, u32[]{:S(2)}) %all-to-all-start) | async-done | bytes 491552 | tf_op jit(solution)/shard_map/all_to_all | solution.py:612
  23.8 0.8 %copy-done.6 = f32[8,120,128]{2,1,0:T(8,128)} copy-done((f32[8,120,128]{2,1,0:T(8,128)}, f32[8,120,128]{2,1,0:T(8,128)S(1)}, u32[]{:S(2)}) %copy-start.6) | copy-done | bytes 491544
  24.6 9.2 %sample_values.1 = bf16[8,40,128]{2,1,0:T(8,128)(2,1)} custom-call(s32[2,8]{1,0:T(2,128)} %bitcast.18, bf16[16,208,256]{2,1,0:T(8,128)(2,1)} %copy-done.4, f32[8,120,128]{2,1,0:T(8,128)} %copy-done.6), custom_call_target="tpu_custom_call" | custom-call | flops 4362076160 | bytes 3145728 | tf_op jit(solution)/shard_map/sample_values/pallas_call | solution.py:289
  33.9 0.1 copy.22
  34.2 0.2 copy.23.w_down
  34.4 3.4 %all-to-all-start.1 = ((bf16[8,40,128]{2,1,0:T(8,128)(2,1)}), bf16[8,40,128]{2,1,0:T(8,128)(2,1)S(1)}, u32[]{:S(2)}, u32[]{:S(2)}) async-start(bf16[8,40,128]{2,1,0:T(8,128)(2,1)} %sample_values.1), calls=%async_computation.1 | async-start | bytes 163840 | tf_op jit(solution)/shard_map/all_to_all | solution.py:626
  37.8 0.0 copy-start.1
  37.8 2.4 %stem.1.second = bf16[20,32,256]{2,1,0:T(8,128)(2,1)S(1)} custom-call(s32[2]{0:T(128)S(1)} %pad_add_fusion.where_ref, bf16[24,16,256]{2,1,0:T(8,128)(2,1)S(1)} %pad.12.x_ref, bf16[9,32,16]{2,1,0:T(8,128)(2,1)S(1)} %pad.13.w_in, bf16[9,32,32]{2,1,0:T(8,128)(2,1)S(1)} %copy-done.3), custom_call_target="tpu_custom_call" | custom-call | flops 1000000000 | bytes 1048576 | tf_op jit(solution)/shard_map/stem/pallas_call | solution.py:528
  40.2 0.0 copy-start.2
  40.2 1.9 %middle.1.fourth = bf16[6,112,128]{2,1,0:T(8,128)(2,1)S(1)} custom-call(s32[2]{0:T(128)S(1)} %pad_add_fusion.where_ref, bf16[20,32,256]{2,1,0:T(8,128)(2,1)S(1)} %stem.1.second, bf16[9,112,32]{2,1,0:T(8,128)(2,1)S(1)} %copy.23.w_down, bf16[9,112,112]{2,1,0:T(8,128)(2,1)S(1)} %copy-done.1), custom_call_target="tpu_custom_call" | custom-call | flops 1000000000 | bytes 1048576 | tf_op jit(solution)/shard_map/middle/pallas_call | solution.py:546
  42.1 1.7 %all-to-all-done.1.value_ref = bf16[8,40,128]{2,1,0:T(8,128)(2,1)S(1)} async-done(((bf16[8,40,128]{2,1,0:T(8,128)(2,1)}), bf16[8,40,128]{2,1,0:T(8,128)(2,1)S(1)}, u32[]{:S(2)}, u32[]{:S(2)}) %all-to-all-start.1) | async-done | bytes 81952 | tf_op jit(solution)/shard_map/all_to_all | solution.py:626
  43.8 0.2 gbuffer.1
  44.0 1.5 %collective-permute-start.2 = (bf16[1,4,8,256]{3,2,1,0:T(8,128)(2,1)S(1)}, bf16[1,4,8,256]{3,2,1,0:T(8,128)(2,1)S(1)}, u32[]{:S(2)}, u32[]{:S(2)}) collective-permute-start(bf16[1,4,8,256]{3,2,1,0:T(8,128)(2,1)S(1)} %gbuffer.1), channel_id=1, source_target_pairs={{0,8},{8,16},{16,24},{24,0},{1,9},{9,17},{17,25},{25,1},{2,10},{10... | collective-permute-start | bytes 49160 | tf_op jit(solution)/shard_map/ppermute | solution.py:638
  45.5 2.6 %decoder.1 = bf16[1,3,8,256]{3,2,1,0:T(8,128)(2,1)} custom-call(s32[2]{0:T(128)S(1)} %pad_add_fusion.where_ref, bf16[20,32,256]{2,1,0:T(8,128)(2,1)S(1)} %stem.1.second, bf16[6,112,128]{2,1,0:T(8,128)(2,1)S(1)} %middle.1.fourth, bf16[9,32,144]{2,1,0:T(8,128)(2,1)S(1)} %copy-done.2, bf16[9,16,32]{2,1,0:T(8,128)(2,1)S(1)} %pad.14.w_out), custom_call_target="tpu_custom_call" | custom-call | flops 1000000000 | bytes 1048576 | tf_op jit(solution)/shard_map/decoder/pallas_call | solution.py:567
  48.1 0.6 %collective-permute-done.2 = bf16[1,4,8,256]{3,2,1,0:T(8,128)(2,1)S(1)} collective-permute-done((bf16[1,4,8,256]{3,2,1,0:T(8,128)(2,1)S(1)}, bf16[1,4,8,256]{3,2,1,0:T(8,128)(2,1)S(1)}, u32[]{:S(2)}, u32[]{:S(2)}) %collective-permute-start.2) | collective-permute-done | bytes 16416 | tf_op jit(solution)/shard_map/ppermute | solution.py:638
  48.7 0.6 %copy.27 = bf16[1,4,8,256]{3,2,1,0:T(8,128)(2,1)} copy(bf16[1,4,8,256]{3,2,1,0:T(8,128)(2,1)S(1)} %collective-permute-done.2) | data formatting | bytes 32768
  (26 shorter events, 0.2 us)
Async XLA Ops:
  0.6 12.3 %copy-start.5 = (bf16[16,39304]{1,0:T(8,128)(2,1)S(1)}, bf16[16,39304]{1,0:T(8,128)(2,1)}, u32[]{:S(2)}) copy-start(bf16[16,39304]{1,0:T(8,128)(2,1)} %param.12) | copy-start | bytes 3773188
  0.6 8.5 %copy-start.8 = (bf16[1,4,8,256]{3,2,1,0:T(8,128)(2,1)S(1)}, bf16[1,4,8,256]{3,2,1,0:T(8,128)(2,1)}, u32[]{:S(2)}) copy-start(bf16[1,4,8,256]{3,2,1,0:T(8,128)(2,1)} %param.17) | copy-start | bytes 49156
  2.8 21.0 %all-to-all-start = ((f32[8,120,128]{2,1,0:T(8,128)}), f32[8,120,128]{2,1,0:T(8,128)S(1)}, u32[]{:S(2)}, u32[]{:S(2)}) async-start(f32[8,120,128]{2,1,0:T(8,128)} %positions.1), calls=%async_computation | async-start | bytes 983040 | tf_op jit(solution)/shard_map/all_to_all | solution.py:612
  9.2 24.7 %collective-permute-start = (bf16[1,4,8,256]{3,1,2,0:T(4,128)(2,1)S(1)}, bf16[1,4,8,256]{3,1,2,0:T(4,128)(2,1)S(1)}, u32[]{:S(2)}, u32[]{:S(2)}) collective-permute-start(bf16[1,4,8,256]{3,1,2,0:T(4,128)(2,1)S(1)} %copy.19), channel_id=1, source_target_pairs={{0,1},{1,2},{2,3},{3,4},{4,5},{5,6},{6,7},{8,9},{9,10},{10,11},{11... | collective-permute-start | bytes 49160 | tf_op jit(solution)/shard_map/ppermute | solution.py:616
  11.6 22.3 %collective-permute-start.1 = (bf16[1,4,8,256]{3,1,2,0:T(4,128)(2,1)S(1)}, bf16[1,4,8,256]{3,1,2,0:T(4,128)(2,1)S(1)}, u32[]{:S(2)}, u32[]{:S(2)}) collective-permute-start(bf16[1,4,8,256]{3,1,2,0:T(4,128)(2,1)S(1)} %copy.19), channel_id=1, source_target_pairs={{1,0},{2,1},{3,2},{4,3},{5,4},{6,5},{7,6},{9,8},{10,9},{11,10},{12... | collective-permute-start | bytes 49160 | tf_op jit(solution)/shard_map/ppermute | solution.py:617
  16.8 1.2 %copy-start.4 = (bf16[16,208,256]{2,1,0:T(8,128)(2,1)}, bf16[16,208,256]{2,1,0:T(8,128)(2,1)S(1)}, u32[]{:S(2)}) copy-start(bf16[16,208,256]{2,1,0:T(8,128)(2,1)S(1)} %brick_windows.1.brick_ref) | copy-start | bytes 5111812
  23.8 0.8 %copy-start.6 = (f32[8,120,128]{2,1,0:T(8,128)}, f32[8,120,128]{2,1,0:T(8,128)S(1)}, u32[]{:S(2)}) copy-start(f32[8,120,128]{2,1,0:T(8,128)S(1)} %all-to-all-done.place_ref) | copy-start | bytes 1474564
  24.6 9.3 %copy-start.9 = (bf16[9,32,4]{1,2,0:T(4,128)(2,1)S(1)}, bf16[9,32,4]{1,2,0:T(4,128)(2,1)}, u32[]{:S(2)}) copy-start(bf16[9,32,4]{1,2,0:T(4,128)(2,1)} %param.18) | copy-start | bytes 6916
  24.6 9.5 %copy-start.7 = (bf16[9,112,32]{1,2,0:T(8,128)(2,1)S(1)}, bf16[9,112,32]{1,2,0:T(8,128)(2,1)}, u32[]{:S(2)}) copy-start(bf16[9,112,32]{1,2,0:T(8,128)(2,1)} %param.20) | copy-start | bytes 193540
  24.6 13.1 %copy-start.10 = (bf16[9,3,32]{2,1,0:T(4,128)(2,1)S(1)}, bf16[9,3,32]{2,1,0:T(4,128)(2,1)}, u32[]{:S(2)}) copy-start(bf16[9,3,32]{2,1,0:T(4,128)(2,1)} %param.23) | copy-start | bytes 5188
  24.6 13.1 %copy-start.3 = (bf16[9,32,32]{2,1,0:T(8,128)(2,1)S(1)}, bf16[9,32,32]{2,1,0:T(8,128)(2,1)}, u32[]{:S(2)}) copy-start(bf16[9,32,32]{2,1,0:T(8,128)(2,1)} %w_mid.1) | copy-start | bytes 55300
  34.4 9.4 %all-to-all-start.1 = ((bf16[8,40,128]{2,1,0:T(8,128)(2,1)}), bf16[8,40,128]{2,1,0:T(8,128)(2,1)S(1)}, u32[]{:S(2)}, u32[]{:S(2)}) async-start(bf16[8,40,128]{2,1,0:T(8,128)(2,1)} %sample_values.1), calls=%async_computation.1 | async-start | bytes 163840 | tf_op jit(solution)/shard_map/all_to_all | solution.py:626
  37.8 2.4 %copy-start.1 = (bf16[9,112,112]{2,1,0:T(8,128)(2,1)S(1)}, bf16[9,112,112]{2,1,0:T(8,128)(2,1)}, u32[]{:S(2)}) copy-start(bf16[9,112,112]{2,1,0:T(8,128)(2,1)} %w_deep.1) | copy-start | bytes 677380
  40.2 3.6 %copy-start = (s32[1,1,160,256]{3,2,1,0:T(8,128)S(1)}, s32[1,1,160,256]{3,2,1,0:T(8,128)}, u32[]{:S(2)}) copy-start(s32[1,1,160,256]{3,2,1,0:T(8,128)} %order_ref.1) | copy-start | bytes 491524
  40.2 5.4 %copy-start.2 = (bf16[9,32,144]{2,1,0:T(8,128)(2,1)S(1)}, bf16[9,32,144]{2,1,0:T(8,128)(2,1)}, u32[]{:S(2)}) copy-start(bf16[9,32,144]{2,1,0:T(8,128)(2,1)} %w_up.1) | copy-start | bytes 248836
  44.0 4.7 %collective-permute-start.2 = (bf16[1,4,8,256]{3,2,1,0:T(8,128)(2,1)S(1)}, bf16[1,4,8,256]{3,2,1,0:T(8,128)(2,1)S(1)}, u32[]{:S(2)}, u32[]{:S(2)}) collective-permute-start(bf16[1,4,8,256]{3,2,1,0:T(8,128)(2,1)S(1)} %gbuffer.1), channel_id=1, source_target_pairs={{0,8},{8,16},{16,24},{24,0},{1,9},{9,17},{17,25},{25,1},{2,10},{10... | collective-permute-start | bytes 49160 | tf_op jit(solution)/shard_map/ppermute | solution.py:638

commit v10 on v9

--- a/solution.py
+++ b/solution.py
@@ -99,7 +99,13 @@
     )(cells, fracs)
 
 
-def windows_kernel(cube_ref, out_ref, wide, tail):
+def windows_kernel(
+    where_ref, picks_ref, cube_ref, place_ref, out_ref, own_ref,
+    wide, tail, places, sums, arrival,
+):
+    tile = where_ref[0]
+    own_places = pltpu.make_async_copy(place_ref.at[tile], places, arrival)
+    own_places.start()
     count = cube_ref.shape[0]
     plane = EDGE * EDGE
     wide[...] = jnp.zeros_like(wide)
@@ -130,26 +136,46 @@
         tail[:, row : row + 1, :] = jnp.zeros((count, 1, KDIM), F32)
     out_ref[:, WINDOWS * MAIN :, :] = tail[...].astype(BF16)
 
-
-def windows_of(bricks):
+    own_places.wait()
+    cap = picks_ref.shape[0]
+    lines = places.shape[0] // 3
+    part = lines // cap
+
+    def one_slot(piece, carry):
+        brick = out_ref[picks_ref[piece, tile]]
+        slot_sums(brick, places, sums, piece * part, part // 2)
+        return carry
+
+    lax.fori_loop(0, cap, one_slot, 0)
+    own_ref[0] = line_values(sums, lines)
+
+
+def windows_of(where, picks, bricks, places):
     count = bricks.shape[0]
     cube = bricks.reshape(count, EDGE, EDGE * EDGE)
+    rows = places.shape[1]
     return pl.pallas_call(
         windows_kernel,
-        out_shape=jax.ShapeDtypeStruct((count, BRICK_ROWS, KDIM), BF16),
-        in_specs=[vmem()],
-        out_specs=vmem(),
+        out_shape=(
+            jax.ShapeDtypeStruct((count, BRICK_ROWS, KDIM), BF16),
+            jax.ShapeDtypeStruct((1, rows // 3, LANES), BF16),
+        ),
+        in_specs=[smem(), smem(), vmem(), pl.BlockSpec(memory_space=pl.ANY)],
+        out_specs=(vmem(), vmem()),
         scratch_shapes=[
             pltpu.VMEM((count, 48, 10 * LANES), BF16),
             pltpu.VMEM((count, TAIL, KDIM), F32),
+            pltpu.VMEM((rows, LANES), F32),
+            pltpu.VMEM((8 * rows // 3, LANES), F32),
+            pltpu.SemaphoreType.DMA,
         ],
         compiler_params=params(16),
         cost_estimate=pl.CostEstimate(
-            flops=2 * count * 48 * 384 * KDIM * WINDOWS, bytes_accessed=4 * 1024 * 1024,
+            flops=2 * count * 48 * 384 * KDIM * WINDOWS, bytes_accessed=4 * MIB,
             transcendentals=0,
         ),
         name="brick_windows",
-    )(cube)
+    )(where, picks, cube, places)
 
 
 def hat(distance):
@@ -203,34 +229,65 @@
     return total
 
 
-def samples_kernel(picks_ref, brick_ref, place_ref, out_ref, bricks, places, sums, arrivals):
+def slot_sums(brick, places, sums, first, blocks):
+    lines = places.shape[0] // 3
+    for step in range(blocks):
+        row = first + 2 * step
+
+        def line(axis):
+            both = [
+                jnp.broadcast_to(places[pl.ds(axis * lines + row + half, 1), :], (8, LANES))
+                for half in range(2)
+            ]
+            return jnp.concatenate(both, axis=1)
+
+        total = blend(brick, line(0), line(1), line(2))
+        for half in range(2):
+            sums[pl.ds(pl.multiple_of(8 * (row + half), 8), 8), :] = total[
+                :, half * LANES : (half + 1) * LANES
+            ]
+
+
+def line_values(sums, lines):
+    values = []
+    for row in range(0, lines, 8):
+        value = sums[pl.ds(8 * row, 8, stride=8), :]
+        for other in range(1, 8):
+            value = value + sums[pl.ds(8 * row + other, 8, stride=8), :]
+        values.append(value)
+    return jnp.concatenate(values, axis=0).astype(BF16)
+
+
+def samples_kernel(
+    where_ref, picks_ref, brick_ref, place_ref, own_ref, out_ref, bricks, places, sums, arrivals
+):
     owners, rows, _ = place_ref.shape
     cap = picks_ref.shape[0]
     lines = rows // 3
-    per_slot = lines // 2 // cap
-    group = places.shape[1]
-    turns = owners // group
+    part = lines // cap
+    turns = owners - 1
+    tile = where_ref[0]
+    out_ref[tile] = own_ref[0]
+
+    def renderer_of(turn):
+        return lax.rem(tile + 1 + turn, owners)
 
     def fetches(turn):
         held = turn % 2
-        copies = []
-        for member in range(group):
-            renderer = turn * group + member
+        renderer = renderer_of(turn)
+        copies = [
+            pltpu.make_async_copy(
+                place_ref.at[renderer], places.at[held], arrivals.at[held, cap]
+            )
+        ]
+        for piece in range(cap):
             copies.append(
                 pltpu.make_async_copy(
-                    place_ref.at[renderer],
-                    places.at[held, member],
-                    arrivals.at[held, member, cap],
+                    brick_ref.at[picks_ref[piece, renderer]],
+                    bricks.at[held, piece],
+                    arrivals.at[held, piece],
                 )
             )
-            for piece in range(cap):
-                copies.append(
-                    pltpu.make_async_copy(
-                        brick_ref.at[picks_ref[piece, renderer]],
-                        bricks.at[held, member, piece],
-                        arrivals.at[held, member, piece],
-                    )
-                )
         return copies
 
     for turn in range(min(2, turns)):
@@ -241,34 +298,9 @@
         held = turn % 2
         for copy in fetches(turn):
             copy.wait()
-        for member in range(group):
-            for piece in range(cap):
-                brick = bricks[held, member, piece]
-                for step in range(per_slot):
-                    row = 2 * (piece * per_slot + step)
-
-                    def line(axis):
-                        both = [
-                            jnp.broadcast_to(
-                                places[held, member, pl.ds(axis * lines + row + half, 1), :],
-                                (8, LANES),
-                            )
-                            for half in range(2)
-                        ]
-                        return jnp.concatenate(both, axis=1)
-
-                    total = blend(brick, line(0), line(1), line(2))
-                    for half in range(2):
-                        sums[member, 8 * (row + half) : 8 * (row + half + 1), :] = total[
-                            :, half * LANES : (half + 1) * LANES
-                        ]
-            values = []
-            for row in range(0, lines, 8):
-                value = sums[member, pl.ds(8 * row, 8, stride=8), :]
-                for other in range(1, 8):
-                    value = value + sums[member, pl.ds(8 * row + other, 8, stride=8), :]
-                values.append(value)
-            out_ref[turn * group + member] = jnp.concatenate(values, axis=0).astype(BF16)
+        for piece in range(cap):
+            slot_sums(bricks[held, piece], places.at[held], sums, piece * part, part // 2)
+        out_ref[renderer_of(turn)] = line_values(sums, lines)
 
         @pl.when(turn + 2 < turns)
         def _():
@@ -280,30 +312,29 @@
     lax.fori_loop(0, turns, one_turn, 0)
 
 
-def sample_values(picks, windows, places):
+def sample_values(where, picks, windows, places, own):
     owners, rows, _ = places.shape
     cap = picks.shape[0]
-    group = 2 if owners % 2 == 0 else 1
     samples = owners * rows * LANES // 3
     some = pl.BlockSpec(memory_space=pl.ANY)
     return pl.pallas_call(
         samples_kernel,
         out_shape=jax.ShapeDtypeStruct((owners, rows // 3, LANES), BF16),
-        in_specs=[smem(), some, some],
+        in_specs=[smem(), smem(), some, some, vmem()],
         out_specs=vmem(),
         scratch_shapes=[
-            pltpu.VMEM((2, group, cap, BRICK_ROWS, KDIM), BF16),
-            pltpu.VMEM((2, group, rows, LANES), F32),
-            pltpu.VMEM((group, 8 * rows // 3, LANES), F32),
-            pltpu.SemaphoreType.DMA((2, group, cap + 1)),
+            pltpu.VMEM((2, cap, BRICK_ROWS, KDIM), BF16),
+            pltpu.VMEM((2, rows, LANES), F32),
+            pltpu.VMEM((8 * rows // 3, LANES), F32),
+            pltpu.SemaphoreType.DMA((2, cap + 1)),
         ],
-        compiler_params=params(59),
+        compiler_params=pltpu.CompilerParams(vmem_limit_bytes=61_600_000),
         cost_estimate=pl.CostEstimate(
             flops=2 * samples * KDIM * BRICK_ROWS, bytes_accessed=3 * MIB,
             transcendentals=0,
         ),
         name="sample_values",
-    )(picks, windows, places)
+    )(where, picks, windows, places, own)
 
 
 def gbuffer_kernel(value_ref, order_ref, out_ref, values):
@@ -414,6 +445,22 @@
     return inside
 
 
+def turned(weight_ref):
+    _, chans, out_chans = weight_ref.shape
+    here = lax.broadcasted_iota(jnp.int32, (out_chans, out_chans), 0)
+    there = lax.broadcasted_iota(jnp.int32, (out_chans, out_chans), 1)
+    unit = jnp.where(here == there, 1.0, 0.0).astype(BF16)
+    rows = []
+    for column in range(3):
+        stack = jnp.concatenate([weight_ref[3 * tap + column] for tap in range(3)], axis=0)
+        rows.append(
+            lax.dot_general(
+                unit, stack, (((1,), (1,)), ((), ())), preferred_element_type=F32
+            )
+        )
+    return jnp.concatenate(rows, axis=0).astype(BF16)
+
+
 def stem_kernel(where_ref, x_ref, w_in, w_mid, second, first):
     height = x_ref.shape[0] // 3
     width = x_ref.shape[2]
@@ -431,8 +478,8 @@
 
         lax.fori_loop(0, target.shape[0], step, 0, unroll=unroll)
 
-    full_layer(beside(w_in), x_ref, first, height - 1, 2 * height - 1, first.shape[0] // 2)
-    full_layer(beside(w_mid), first, second, height - 2, 2 * height - 2, second.shape[0] // 2)
+    full_layer(turned(w_in), x_ref, first, height - 1, 2 * height - 1, first.shape[0] // 2)
+    full_layer(beside(w_mid), first, second, height - 2, 2 * height - 2, second.shape[0] // 4)
 
 
 def middle_kernel(where_ref, second, w_down, w_deep, fourth, pooled, third):
@@ -461,7 +508,7 @@
                     line = line * inside(row + now, low, high)
                 target[row + now] = line.astype(BF16)
 
-    weight_down = beside(w_down)
+    weight_down = turned(w_down)
 
     def down_product(row):
         lines = jnp.concatenate([half_pair(pooled, row, tap) for tap in range(3)], axis=0)
@@ -615,22 +662,22 @@
     up = [(i + 1, i) for i in range(n_tile - 1)]
     over = lax.ppermute(pending, "tile", down)
     under = lax.ppermute(pending, "tile", up)
-    windows = windows_of(bricks)
     where = jnp.stack([tile, jnp.int32(n_tile)]).astype(jnp.int32)
     picks = sends[0, 0].T
-    found = sample_values(picks, windows, arrived)
-
-    found, over, under, pending, w_in, w_down, w_out = lax.optimization_barrier(
-        (found, over, under, pending, w_in, w_down, w_out)
-    )
+    colours = w_out.shape[1]
+    w_in = w_in.transpose(0, 2, 1)
+    w_in = jnp.pad(w_in, ((0, 0), (0, 16 - w_in.shape[1]), (0, 0)))
+    w_out = jnp.pad(w_out, ((0, 0), (0, 16 - colours), (0, 0)))
+    windows, own = windows_of(where, picks, bricks, places)
+    arrived, w_in, w_out = lax.optimization_barrier((arrived, w_in, w_out))
+    found = sample_values(where, picks, windows, arrived, own)
+
+    found, over, under, pending = lax.optimization_barrier((found, over, under, pending))
     values = lax.all_to_all(found, "tile", split_axis=0, concat_axis=0, tiled=True)
     field = jnp.concatenate([over[0], pending[0], under[0]], axis=1).transpose(1, 0, 2)
     field = jnp.pad(field, ((0, 0), (0, 16 - field.shape[1]), (0, 0)))
-    colours = w_out.shape[1]
-    w_in = jnp.pad(w_in, ((0, 0), (0, 0), (0, 16 - w_in.shape[2])))
-    w_out = jnp.pad(w_out, ((0, 0), (0, 16 - colours), (0, 0)))
     second = stem(where, field, w_in, w_mid)
-    deep = middle(where, second, w_down, w_deep)
+    deep = middle(where, second, w_down.transpose(0, 2, 1), w_deep)
     values, deep = lax.optimization_barrier((values, deep))
     rendered = gbuffer(trim(values), sample_order, height, width)
     rendered, deep = lax.optimization_barrier((rendered, deep))

time: 49.7 us -> 48.5 us (0.976)
  waiting for transfers between devices: 8.03 us -> 5.09 us
  Pallas kernels: 19.9 us -> 21.5 us
  local copies, waits for them, and re-layouts: 5.4 us -> 4.9 us
    all_to_all x1, waiting for transfers between devices: 5.75 us -> 3.33 us  [on_device(): lax.all_to_all(places, 'tile', split_axis=0, concat_axis=0, tiled=True)]
    pallas_call x1, Pallas kernels: 1.54 us -> 3.19 us  [windows_of(): pl.pallas_call(windows_kernel, out_shape=(jax.ShapeDtypeStruct((count, BR...]
    pallas_call x1, Pallas kernels: 9.2 us -> 8.57 us  [sample_values(): pl.pallas_call(samples_kernel, out_shape=jax.ShapeDtypeStruct((owners, ro...]
    pallas_call x1, Pallas kernels: 2.36 us -> 2.88 us  [stem(): pl.pallas_call(stem_kernel, out_shape=jax.ShapeDtypeStruct((3 * height -...]
    all_to_all x1, waiting for transfers between devices: 1.7 us -> 1.18 us  [on_device(): lax.all_to_all(found, 'tile', split_axis=0, concat_axis=0, tiled=True)]
    unnamed x23 -> x31, local copies, waits for them, and re-layouts: 2.65 us -> 2.5 us
  transfers between devices with their start and end apart: 5 -> 5, of which waited for: 3 -> 3; matrix products, arithmetic and copies ran while one was open for 5% -> 5% of each run, Pallas kernels for 36% -> 40%
where the time goes in v10:
time: 48.5 us; the launch traced here: 47.9 us
  Pallas kernels  21.5 us (44%)
  starting transfers between devices  15.3 us (32%)
  waiting for transfers between devices  5.09 us (10%)
  local copies, waits for them, and re-layouts  4.9 us (10%)
  between operations  0.92 us (2%)
    pallas_call x1, Pallas kernels, sample_values(): pl.pallas_call(samples_kernel, out_shape=jax.ShapeDtypeStruct((owners, ro...  8.57 us
    all_to_all x1, starting transfers between devices, on_device(): lax.all_to_all(places, 'tile', split_axis=0, concat_axis=0, tiled=True)  6.34 us
    all_to_all x1, starting transfers between devices, on_device(): lax.all_to_all(found, 'tile', split_axis=0, concat_axis=0, tiled=True)  3.65 us
    all_to_all x1, waiting for transfers between devices, on_device(): lax.all_to_all(places, 'tile', split_axis=0, concat_axis=0, tiled=True)  3.33 us
    pallas_call x1, Pallas kernels, windows_of(): pl.pallas_call(windows_kernel, out_shape=(jax.ShapeDtypeStruct((count, BR...  3.19 us
    pallas_call x1, Pallas kernels, stem(): pl.pallas_call(stem_kernel, out_shape=jax.ShapeDtypeStruct((3 * height -...  2.88 us
    pallas_call x1, Pallas kernels, decoder(): pl.pallas_call(decoder_kernel, out_shape=jax.ShapeDtypeStruct((1, colours...  2.56 us
    ppermute x1, starting transfers between devices, on_device(): over = lax.ppermute(pending, 'tile', down)  2.52 us
  transfers between devices with their start and end apart: 5, of which 3 were waited for; matrix products, arithmetic and copies ran while one was open for 5% of the time, Pallas kernels for 40%

profile of v10, /device:TPU:0, one launch (start us, length us, event | category | flops | bytes accessed | tf_op | source)
XLA Modules:
  0.0 47.9 jit_solution(2512505582155196358)
XLA Ops:
  0.7 2.2 %positions.1.place_ref = f32[8,120,128]{2,1,0:T(8,128)} custom-call(s32[3,320,128]{2,1,0:T(8,128)} %bitcast.18, f32[3,320,128]{2,1,0:T(8,128)} %bitcast.19), custom_call_target="tpu_custom_call" | custom-call | flops 122880 | bytes 1474560 | tf_op jit(solution)/shard_map/positions/pallas_call | solution.py:82
  2.8 6.3 %all-to-all-start = ((f32[8,120,128]{2,1,0:T(8,128)}), f32[8,120,128]{2,1,0:T(8,128)}, u32[]{:S(2)}, u32[]{:S(2)}) async-start(f32[8,120,128]{2,1,0:T(8,128)} %positions.1.place_ref), calls=%async_computation | async-start | bytes 983040 | tf_op jit(solution)/shard_map/all_to_all | solution.py:659
  9.2 0.0 copy-start.13
  9.2 0.0 copy-start.14
  9.2 0.0 copy-start.6
  9.2 2.5 %collective-permute-start = (bf16[1,4,8,256]{3,1,2,0:T(4,128)(2,1)S(1)}, bf16[1,4,8,256]{3,1,2,0:T(4,128)(2,1)S(1)}, u32[]{:S(2)}, u32[]{:S(2)}) collective-permute-start(bf16[1,4,8,256]{3,1,2,0:T(4,128)(2,1)S(1)} %copy.17), channel_id=1, source_target_pairs={{0,1},{1,2},{2,3},{3,4},{4,5},{5,6},{6,7},{8,9},{9,10},{10,11},{11... | collective-permute-start | bytes 49160 | tf_op jit(solution)/shard_map/ppermute | solution.py:663
  11.8 1.3 %collective-permute-start.1 = (bf16[1,4,8,256]{3,1,2,0:T(4,128)(2,1)S(1)}, bf16[1,4,8,256]{3,1,2,0:T(4,128)(2,1)S(1)}, u32[]{:S(2)}, u32[]{:S(2)}) collective-permute-start(bf16[1,4,8,256]{3,1,2,0:T(4,128)(2,1)S(1)} %copy.17), channel_id=1, source_target_pairs={{1,0},{2,1},{3,2},{4,3},{5,4},{6,5},{7,6},{9,8},{10,9},{11,10},{12... | collective-permute-start | bytes 49160 | tf_op jit(solution)/shard_map/ppermute | solution.py:664
  13.1 2.3 %reshape.15.cube_ref = bf16[16,34,1156]{2,1,0:T(8,128)(2,1)S(1)} reshape(bf16[16,39304]{1,0:T(8,128)(2,1)S(1)} %copy-done.11) | data formatting | bytes 2515456 | tf_op jit(solution)/shard_map/reshape | solution.py:155
  15.5 0.1 pad_add_fusion.where_ref
  15.6 3.2 %brick_windows.1 = (bf16[16,208,256]{2,1,0:T(8,128)(2,1)S(1)}, bf16[1,40,128]{2,1,0:T(8,128)(2,1)S(1)}) custom-call(s32[2]{0:T(128)S(1)} %pad_add_fusion.where_ref, s32[2,8]{1,0:T(2,128)S(1)} %bitcast.17, bf16[16,34,1156]{2,1,0:T(8,128)(2,1)S(1)} %reshape.15.cube_ref, f32[8,120,128]{2,1,0:T(8,128)S(1)} %copy-done), custom_call_target="tpu_custom_call" | custom-call | flops 905969664 | bytes 4194304 | tf_op jit(solution)/shard_map/brick_windows/pallas_call | solution.py:157
  18.8 1.2 %copy-done.9 = bf16[16,208,256]{2,1,0:T(8,128)(2,1)} copy-done((bf16[16,208,256]{2,1,0:T(8,128)(2,1)}, bf16[16,208,256]{2,1,0:T(8,128)(2,1)S(1)}, u32[]{:S(2)}) %copy-start.9) | copy-done | bytes 1703960
  20.0 0.6 %copy-done.10 = bf16[1,40,128]{2,1,0:T(8,128)(2,1)} copy-done((bf16[1,40,128]{2,1,0:T(8,128)(2,1)}, bf16[1,40,128]{2,1,0:T(8,128)(2,1)S(1)}, u32[]{:S(2)}) %copy-start.10) | copy-done | bytes 10264
  20.6 3.3 %all-to-all-done.place_ref = f32[8,120,128]{2,1,0:T(8,128)} async-done(((f32[8,120,128]{2,1,0:T(8,128)}), f32[8,120,128]{2,1,0:T(8,128)}, u32[]{:S(2)}, u32[]{:S(2)}) %all-to-all-start) | async-done | bytes 491552 | tf_op jit(solution)/shard_map/all_to_all | solution.py:659
  23.9 8.6 %sample_values.1 = bf16[8,40,128]{2,1,0:T(8,128)(2,1)} custom-call(s32[2]{0:T(128)} %copy-done.7, s32[2,8]{1,0:T(2,128)} %bitcast.16, bf16[16,208,256]{2,1,0:T(8,128)(2,1)} %copy-done.9, f32[8,120,128]{2,1,0:T(8,128)} %all-to-all-done.place_ref, bf16[1,40,128]{2,1,0:T(8,128)(2,1)} %copy-done.10), custom_call_target="tpu_custom_call" | custom-call | flops 4362076160 | bytes 3145728 | tf_op jit(solution)/shard_map/sample_values/pallas_call | solution.py:320
  32.6 3.6 %all-to-all-start.1 = ((bf16[8,40,128]{2,1,0:T(8,128)(2,1)}), bf16[8,40,128]{2,1,0:T(8,128)(2,1)S(1)}, u32[]{:S(2)}, u32[]{:S(2)}) async-start(bf16[8,40,128]{2,1,0:T(8,128)(2,1)} %sample_values.1), calls=%async_computation.1 | async-start | bytes 163840 | tf_op jit(solution)/shard_map/all_to_all | solution.py:676
  36.3 0.0 copy-start.2
  36.3 2.9 %stem.1.second = bf16[20,32,256]{2,1,0:T(8,128)(2,1)S(1)} custom-call(s32[2]{0:T(128)S(1)} %copy-done.8, bf16[24,16,256]{2,1,0:T(8,128)(2,1)S(1)} %pad.14.x_ref, bf16[9,16,32]{2,1,0:T(8,128)(2,1)S(1)} %pad.12.w_in, bf16[9,32,32]{2,1,0:T(8,128)(2,1)S(1)} %copy-done.4), custom_call_target="tpu_custom_call" | custom-call | flops 1000000000 | bytes 1048576 | tf_op jit(solution)/shard_map/stem/pallas_call | solution.py:575
  39.3 2.0 %middle.1.fourth = bf16[6,112,128]{2,1,0:T(8,128)(2,1)S(1)} custom-call(s32[2]{0:T(128)S(1)} %copy-done.8, bf16[20,32,256]{2,1,0:T(8,128)(2,1)S(1)} %stem.1.second, bf16[9,32,112]{2,1,0:T(8,128)(2,1)S(1)} %bitcast.15, bf16[9,112,112]{2,1,0:T(8,128)(2,1)S(1)} %copy-done.2), custom_call_target="tpu_custom_call" | custom-call | flops 1000000000 | bytes 1048576 | tf_op jit(solution)/shard_map/middle/pallas_call | solution.py:593
  41.2 1.2 %all-to-all-done.1.value_ref = bf16[8,40,128]{2,1,0:T(8,128)(2,1)S(1)} async-done(((bf16[8,40,128]{2,1,0:T(8,128)(2,1)}), bf16[8,40,128]{2,1,0:T(8,128)(2,1)S(1)}, u32[]{:S(2)}, u32[]{:S(2)}) %all-to-all-start.1) | async-done | bytes 81952 | tf_op jit(solution)/shard_map/all_to_all | solution.py:676
  42.4 0.2 gbuffer.1
  42.6 1.6 %collective-permute-start.2 = (bf16[1,4,8,256]{3,2,1,0:T(8,128)(2,1)S(1)}, bf16[1,4,8,256]{3,2,1,0:T(8,128)(2,1)S(1)}, u32[]{:S(2)}, u32[]{:S(2)}) collective-permute-start(bf16[1,4,8,256]{3,2,1,0:T(8,128)(2,1)S(1)} %gbuffer.1), channel_id=1, source_target_pairs={{0,8},{8,16},{16,24},{24,0},{1,9},{9,17},{17,25},{25,1},{2,10},{10... | collective-permute-start | bytes 49160 | tf_op jit(solution)/shard_map/ppermute | solution.py:685
  44.2 2.6 %decoder.1 = bf16[1,3,8,256]{3,2,1,0:T(8,128)(2,1)} custom-call(s32[2]{0:T(128)S(1)} %copy-done.8, bf16[20,32,256]{2,1,0:T(8,128)(2,1)S(1)} %stem.1.second, bf16[6,112,128]{2,1,0:T(8,128)(2,1)S(1)} %middle.1.fourth, bf16[9,32,144]{2,1,0:T(8,128)(2,1)S(1)} %copy-done.3, bf16[9,16,32]{2,1,0:T(8,128)(2,1)S(1)} %pad.13.w_out), custom_call_target="tpu_custom_call" | custom-call | flops 1000000000 | bytes 1048576 | tf_op jit(solution)/shard_map/decoder/pallas_call | solution.py:614
  46.7 0.6 %collective-permute-done.2 = bf16[1,4,8,256]{3,2,1,0:T(8,128)(2,1)S(1)} collective-permute-done((bf16[1,4,8,256]{3,2,1,0:T(8,128)(2,1)S(1)}, bf16[1,4,8,256]{3,2,1,0:T(8,128)(2,1)S(1)}, u32[]{:S(2)}, u32[]{:S(2)}) %collective-permute-start.2) | collective-permute-done | bytes 16416 | tf_op jit(solution)/shard_map/ppermute | solution.py:685
  47.3 0.6 %copy.23 = bf16[1,4,8,256]{3,2,1,0:T(8,128)(2,1)} copy(bf16[1,4,8,256]{3,2,1,0:T(8,128)(2,1)S(1)} %collective-permute-done.2) | data formatting | bytes 32768
  (32 shorter events, 0.2 us)
Async XLA Ops:
  0.6 12.4 %copy-start.11 = (bf16[16,39304]{1,0:T(8,128)(2,1)S(1)}, bf16[16,39304]{1,0:T(8,128)(2,1)}, u32[]{:S(2)}) copy-start(bf16[16,39304]{1,0:T(8,128)(2,1)} %param.12) | copy-start | bytes 3773188
  0.6 8.5 %copy-start.12 = (bf16[1,4,8,256]{3,2,1,0:T(8,128)(2,1)S(1)}, bf16[1,4,8,256]{3,2,1,0:T(8,128)(2,1)}, u32[]{:S(2)}) copy-start(bf16[1,4,8,256]{3,2,1,0:T(8,128)(2,1)} %param.17) | copy-start | bytes 49156
  2.8 21.1 %all-to-all-start = ((f32[8,120,128]{2,1,0:T(8,128)}), f32[8,120,128]{2,1,0:T(8,128)}, u32[]{:S(2)}, u32[]{:S(2)}) async-start(f32[8,120,128]{2,1,0:T(8,128)} %positions.1.place_ref), calls=%async_computation | async-start | bytes 983040 | tf_op jit(solution)/shard_map/all_to_all | solution.py:659
  9.2 6.2 %copy-start.13 = (bf16[9,32,4]{1,2,0:T(4,128)(2,1)S(1)}, bf16[9,32,4]{1,2,0:T(4,128)(2,1)}, u32[]{:S(2)}) copy-start(bf16[9,32,4]{1,2,0:T(4,128)(2,1)} %param.18) | copy-start | bytes 6916
  9.2 6.3 %copy-start.14 = (bf16[9,3,32]{2,1,0:T(4,128)(2,1)S(1)}, bf16[9,3,32]{2,1,0:T(4,128)(2,1)}, u32[]{:S(2)}) copy-start(bf16[9,3,32]{2,1,0:T(4,128)(2,1)} %param.23) | copy-start | bytes 5188
  9.2 6.4 %copy-start = (f32[8,120,128]{2,1,0:T(8,128)S(1)}, f32[8,120,128]{2,1,0:T(8,128)}, u32[]{:S(2)}) copy-start(f32[8,120,128]{2,1,0:T(8,128)} %positions.1.place_ref) | copy-start | bytes 1474564
  9.2 6.4 %copy-start.6 = (s32[1,1,8,2]{2,3,1,0:T(2,128)S(1)}, s32[1,1,8,2]{2,3,1,0:T(2,128)}, u32[]{:S(2)}) copy-start(s32[1,1,8,2]{2,3,1,0:T(2,128)} %param.13) | copy-start | bytes 196
  9.2 23.3 %collective-permute-start = (bf16[1,4,8,256]{3,1,2,0:T(4,128)(2,1)S(1)}, bf16[1,4,8,256]{3,1,2,0:T(4,128)(2,1)S(1)}, u32[]{:S(2)}, u32[]{:S(2)}) collective-permute-start(bf16[1,4,8,256]{3,1,2,0:T(4,128)(2,1)S(1)} %copy.17), channel_id=1, source_target_pairs={{0,1},{1,2},{2,3},{3,4},{4,5},{5,6},{6,7},{8,9},{9,10},{10,11},{11... | collective-permute-start | bytes 49160 | tf_op jit(solution)/shard_map/ppermute | solution.py:663
  11.8 20.8 %collective-permute-start.1 = (bf16[1,4,8,256]{3,1,2,0:T(4,128)(2,1)S(1)}, bf16[1,4,8,256]{3,1,2,0:T(4,128)(2,1)S(1)}, u32[]{:S(2)}, u32[]{:S(2)}) collective-permute-start(bf16[1,4,8,256]{3,1,2,0:T(4,128)(2,1)S(1)} %copy.17), channel_id=1, source_target_pairs={{1,0},{2,1},{3,2},{4,3},{5,4},{6,5},{7,6},{9,8},{10,9},{11,10},{12... | collective-permute-start | bytes 49160 | tf_op jit(solution)/shard_map/ppermute | solution.py:664
  15.6 3.2 %copy-start.7 = (s32[2]{0:T(128)}, s32[2]{0:T(128)S(1)}, u32[]{:S(2)}) copy-start(s32[2]{0:T(128)S(1)} %pad_add_fusion.where_ref) | copy-start | bytes 28
  18.8 1.2 %copy-start.9 = (bf16[16,208,256]{2,1,0:T(8,128)(2,1)}, bf16[16,208,256]{2,1,0:T(8,128)(2,1)S(1)}, u32[]{:S(2)}) copy-start(bf16[16,208,256]{2,1,0:T(8,128)(2,1)S(1)} %get-tuple-element.20.brick_ref) | copy-start | bytes 5111812
  20.0 0.6 %copy-start.10 = (bf16[1,40,128]{2,1,0:T(8,128)(2,1)}, bf16[1,40,128]{2,1,0:T(8,128)(2,1)S(1)}, u32[]{:S(2)}) copy-start(bf16[1,40,128]{2,1,0:T(8,128)(2,1)S(1)} %get-tuple-element.22.own_ref) | copy-start | bytes 30724
  23.9 12.4 %copy-start.4 = (bf16[9,32,32]{2,1,0:T(8,128)(2,1)S(1)}, bf16[9,32,32]{2,1,0:T(8,128)(2,1)}, u32[]{:S(2)}) copy-start(bf16[9,32,32]{2,1,0:T(8,128)(2,1)} %w_mid.1) | copy-start | bytes 55300
  23.9 12.4 %copy-start.8 = (s32[2]{0:T(128)S(1)}, s32[2]{0:T(128)}, u32[]{:S(2)}) copy-start(s32[2]{0:T(128)} %copy-done.7) | copy-start | bytes 28
  32.6 9.8 %all-to-all-start.1 = ((bf16[8,40,128]{2,1,0:T(8,128)(2,1)}), bf16[8,40,128]{2,1,0:T(8,128)(2,1)S(1)}, u32[]{:S(2)}, u32[]{:S(2)}) async-start(bf16[8,40,128]{2,1,0:T(8,128)(2,1)} %sample_values.1), calls=%async_computation.1 | async-start | bytes 163840 | tf_op jit(solution)/shard_map/all_to_all | solution.py:676
  36.3 2.9 %copy-start.2 = (bf16[9,112,112]{2,1,0:T(8,128)(2,1)S(1)}, bf16[9,112,112]{2,1,0:T(8,128)(2,1)}, u32[]{:S(2)}) copy-start(bf16[9,112,112]{2,1,0:T(8,128)(2,1)} %w_deep.1) | copy-start | bytes 677380
  36.3 2.9 %copy-start.5 = (bf16[9,112,32]{1,2,0:T(8,128)(2,1)S(1)}, bf16[9,112,32]{1,2,0:T(8,128)(2,1)}, u32[]{:S(2)}) copy-start(bf16[9,112,32]{1,2,0:T(8,128)(2,1)} %param.20) | copy-start | bytes 193540
  39.2 3.2 %copy-start.1 = (s32[1,1,160,256]{3,2,1,0:T(8,128)S(1)}, s32[1,1,160,256]{3,2,1,0:T(8,128)}, u32[]{:S(2)}) copy-start(s32[1,1,160,256]{3,2,1,0:T(8,128)} %order_ref.1) | copy-start | bytes 491524
  39.3 4.9 %copy-start.3 = (bf16[9,32,144]{2,1,0:T(8,128)(2,1)S(1)}, bf16[9,32,144]{2,1,0:T(8,128)(2,1)}, u32[]{:S(2)}) copy-start(bf16[9,32,144]{2,1,0:T(8,128)(2,1)} %w_up.1) | copy-start | bytes 248836
  42.6 4.7 %collective-permute-start.2 = (bf16[1,4,8,256]{3,2,1,0:T(8,128)(2,1)S(1)}, bf16[1,4,8,256]{3,2,1,0:T(8,128)(2,1)S(1)}, u32[]{:S(2)}, u32[]{:S(2)}) collective-permute-start(bf16[1,4,8,256]{3,2,1,0:T(8,128)(2,1)S(1)} %gbuffer.1), channel_id=1, source_target_pairs={{0,8},{8,16},{16,24},{24,0},{1,9},{9,17},{17,25},{25,1},{2,10},{10... | collective-permute-start | bytes 49160 | tf_op jit(solution)/shard_map/ppermute | solution.py:685

commit v11 on v10

--- a/solution.py
+++ b/solution.py
@@ -37,71 +37,8 @@
     return pl.BlockSpec(memory_space=pltpu.SMEM)
 
 
-def positions_kernel(cells_ref, fracs_ref, out_ref, cells, fracs, found, arrivals, departures):
-    owners, rows, _ = out_ref.shape
-    lines = rows // 3
-    parts = arrivals.shape[1]
-    share = owners // parts
-    pieces = [(axis, part) for axis in range(3) for part in range(parts)]
-
-    def reads(axis, part):
-        span = pl.ds(part * share * lines, share * lines)
-        return [
-            pltpu.make_async_copy(
-                source.at[axis, span], target.at[axis, span], arrivals.at[axis, part, number]
-            )
-            for number, (source, target) in enumerate(((cells_ref, cells), (fracs_ref, fracs)))
-        ]
-
-    def write(axis, part):
-        place = (pl.ds(part * share, share), pl.ds(axis * lines, lines))
-        return pltpu.make_async_copy(
-            found.at[place], out_ref.at[place], departures.at[axis, part]
-        )
-
-    for piece in pieces:
-        for copy in reads(*piece):
-            copy.start()
-    for axis, part in pieces:
-        for copy in reads(axis, part):
-            copy.wait()
-        span = slice(part * share * lines, (part + 1) * share * lines)
-        place = cells[axis, span].astype(F32) + fracs[axis, span]
-        found[part * share : (part + 1) * share, axis * lines : (axis + 1) * lines, :] = (
-            place.reshape(share, lines, LANES)
-        )
-        write(axis, part).start()
-    for piece in pieces:
-        write(*piece).wait()
-
-
-def positions(cells, fracs, owners):
-    lines = cells.shape[1]
-    shape = (owners, 3 * lines // owners, LANES)
-    hbm = pl.BlockSpec(memory_space=pltpu.HBM)
-    return pl.pallas_call(
-        positions_kernel,
-        out_shape=jax.ShapeDtypeStruct(shape, F32),
-        in_specs=[hbm, hbm],
-        out_specs=hbm,
-        scratch_shapes=[
-            pltpu.VMEM(cells.shape, jnp.int32),
-            pltpu.VMEM(fracs.shape, F32),
-            pltpu.VMEM(shape, F32),
-            pltpu.SemaphoreType.DMA((3, 2, 2)),
-            pltpu.SemaphoreType.DMA((3, 2)),
-        ],
-        compiler_params=params(60),
-        cost_estimate=pl.CostEstimate(
-            flops=3 * lines * LANES, bytes_accessed=36 * lines * LANES, transcendentals=0
-        ),
-        name="positions",
-    )(cells, fracs)
-
-
 def windows_kernel(
-    where_ref, picks_ref, cube_ref, place_ref, out_ref, own_ref,
-    wide, tail, places, sums, arrival,
+    where_ref, picks_ref, cube_ref, place_ref, out_ref, wide, tail, places, sums, arrival
 ):
     tile = where_ref[0]
     own_places = pltpu.make_async_copy(place_ref.at[tile], places, arrival)
@@ -129,12 +66,12 @@
             preferred_element_type=F32,
         )
         found = found.reshape(count, 48, KDIM)
-        out_ref[:, window * MAIN : (window + 1) * MAIN, :] = found[:, :MAIN, :].astype(BF16)
+        out_ref[:count, window * MAIN : (window + 1) * MAIN, :] = found[:, :MAIN, :].astype(BF16)
         tail[:, window : window + 1, :] = found[:, MAIN : MAIN + 1, :]
         tail[:, 8 + window : 9 + window, :] = found[:, MAIN + 1 : MAIN + 2, :]
     for row in (6, 7, 14, 15):
         tail[:, row : row + 1, :] = jnp.zeros((count, 1, KDIM), F32)
-    out_ref[:, WINDOWS * MAIN :, :] = tail[...].astype(BF16)
+    out_ref[:count, WINDOWS * MAIN :, :] = tail[...].astype(BF16)
 
     own_places.wait()
     cap = picks_ref.shape[0]
@@ -147,7 +84,7 @@
         return carry
 
     lax.fori_loop(0, cap, one_slot, 0)
-    own_ref[0] = line_values(sums, lines)
+    out_ref[count, : whole_tiles(lines), :LANES] = line_values(sums, lines, whole_tiles(lines))
 
 
 def windows_of(where, picks, bricks, places):
@@ -156,12 +93,9 @@
     rows = places.shape[1]
     return pl.pallas_call(
         windows_kernel,
-        out_shape=(
-            jax.ShapeDtypeStruct((count, BRICK_ROWS, KDIM), BF16),
-            jax.ShapeDtypeStruct((1, rows // 3, LANES), BF16),
-        ),
+        out_shape=jax.ShapeDtypeStruct((count + 1, BRICK_ROWS, KDIM), BF16),
         in_specs=[smem(), smem(), vmem(), pl.BlockSpec(memory_space=pl.ANY)],
-        out_specs=(vmem(), vmem()),
+        out_specs=vmem(),
         scratch_shapes=[
             pltpu.VMEM((count, 48, 10 * LANES), BF16),
             pltpu.VMEM((count, TAIL, KDIM), F32),
@@ -248,18 +182,25 @@
             ]
 
 
-def line_values(sums, lines):
+def whole_tiles(lines):
+    return -(-lines // TAIL) * TAIL
+
+
+def line_values(sums, lines, height):
     values = []
     for row in range(0, lines, 8):
         value = sums[pl.ds(8 * row, 8, stride=8), :]
         for other in range(1, 8):
             value = value + sums[pl.ds(8 * row + other, 8, stride=8), :]
         values.append(value)
+    if height > lines:
+        values.append(jnp.zeros((height - lines, LANES), F32))
     return jnp.concatenate(values, axis=0).astype(BF16)
 
 
 def samples_kernel(
-    where_ref, picks_ref, brick_ref, place_ref, own_ref, out_ref, bricks, places, sums, arrivals
+    where_ref, picks_ref, brick_ref, place_ref, out_ref, bricks, places, sums, own, arrivals,
+    own_arrival,
 ):
     owners, rows, _ = place_ref.shape
     cap = picks_ref.shape[0]
@@ -267,7 +208,11 @@
     part = lines // cap
     turns = owners - 1
     tile = where_ref[0]
-    out_ref[tile] = own_ref[0]
+    own_values = pltpu.make_async_copy(
+        brick_ref.at[brick_ref.shape[0] - 1, pl.ds(0, own.shape[0]), pl.ds(0, LANES)],
+        own,
+        own_arrival,
+    )
 
     def renderer_of(turn):
         return lax.rem(tile + 1 + turn, owners)
@@ -300,7 +245,7 @@
             copy.wait()
         for piece in range(cap):
             slot_sums(bricks[held, piece], places.at[held], sums, piece * part, part // 2)
-        out_ref[renderer_of(turn)] = line_values(sums, lines)
+        out_ref[renderer_of(turn)] = line_values(sums, lines, lines)
 
         @pl.when(turn + 2 < turns)
         def _():
@@ -309,10 +254,13 @@
 
         return carry
 
+    own_values.start()
     lax.fori_loop(0, turns, one_turn, 0)
-
-
-def sample_values(where, picks, windows, places, own):
+    own_values.wait()
+    out_ref[tile] = own[...].astype(F32)[:lines].astype(BF16)
+
+
+def sample_values(where, picks, windows, places):
     owners, rows, _ = places.shape
     cap = picks.shape[0]
     samples = owners * rows * LANES // 3
@@ -320,13 +268,15 @@
     return pl.pallas_call(
         samples_kernel,
         out_shape=jax.ShapeDtypeStruct((owners, rows // 3, LANES), BF16),
-        in_specs=[smem(), smem(), some, some, vmem()],
+        in_specs=[smem(), smem(), some, some],
         out_specs=vmem(),
         scratch_shapes=[
             pltpu.VMEM((2, cap, BRICK_ROWS, KDIM), BF16),
             pltpu.VMEM((2, rows, LANES), F32),
             pltpu.VMEM((8 * rows // 3, LANES), F32),
+            pltpu.VMEM((whole_tiles(rows // 3), LANES), BF16),
             pltpu.SemaphoreType.DMA((2, cap + 1)),
+            pltpu.SemaphoreType.DMA,
         ],
         compiler_params=pltpu.CompilerParams(vmem_limit_bytes=61_600_000),
         cost_estimate=pl.CostEstimate(
@@ -334,7 +284,7 @@
             transcendentals=0,
         ),
         name="sample_values",
-    )(where, picks, windows, places, own)
+    )(where, picks, windows, places)
 
 
 def gbuffer_kernel(value_ref, order_ref, out_ref, values):
@@ -478,8 +428,8 @@
 
         lax.fori_loop(0, target.shape[0], step, 0, unroll=unroll)
 
-    full_layer(turned(w_in), x_ref, first, height - 1, 2 * height - 1, first.shape[0] // 2)
-    full_layer(beside(w_mid), first, second, height - 2, 2 * height - 2, second.shape[0] // 4)
+    full_layer(turned(w_in), x_ref, first, height - 1, 2 * height - 1, first.shape[0])
+    full_layer(beside(w_mid), first, second, height - 2, 2 * height - 2, second.shape[0])
 
 
 def middle_kernel(where_ref, second, w_down, w_deep, fourth, pooled, third):
@@ -555,7 +505,7 @@
         fifth[row] = (line * inside(row, 1, height + 1)).astype(BF16)
         return carry
 
-    lax.fori_loop(0, fifth.shape[0], up_step, 0, unroll=fifth.shape[0] // 2)
+    lax.fori_loop(0, fifth.shape[0], up_step, 0, unroll=fifth.shape[0])
 
     colours = out_ref.shape[1]
     weight_out = beside(w_out)
@@ -654,7 +604,8 @@
             return found
         return found.reshape(slots, padded)[:, :per_slot].reshape(1, samples // LANES, LANES)
 
-    places = positions(fill(cells), fill(fracs), n_tile)
+    places = fill(cells).astype(F32) + fill(fracs)
+    places = places.reshape(3, n_tile, -1, LANES).transpose(1, 0, 2, 3).reshape(n_tile, -1, LANES)
     places, bricks, pending = lax.optimization_barrier((places, bricks, pending))
     arrived = lax.all_to_all(places, "tile", split_axis=0, concat_axis=0, tiled=True)
 
@@ -668,9 +619,9 @@
     w_in = w_in.transpose(0, 2, 1)
     w_in = jnp.pad(w_in, ((0, 0), (0, 16 - w_in.shape[1]), (0, 0)))
     w_out = jnp.pad(w_out, ((0, 0), (0, 16 - colours), (0, 0)))
-    windows, own = windows_of(where, picks, bricks, places)
+    windows = windows_of(where, picks, bricks, places)
     arrived, w_in, w_out = lax.optimization_barrier((arrived, w_in, w_out))
-    found = sample_values(where, picks, windows, arrived, own)
+    found = sample_values(where, picks, windows, arrived)
 
     found, over, under, pending = lax.optimization_barrier((found, over, under, pending))
     values = lax.all_to_all(found, "tile", split_axis=0, concat_axis=0, tiled=True)

time: 48.5 us -> 49.3 us (1.016)
  Pallas kernels: 21.5 us -> 17.7 us
  waiting for transfers between devices: 5.09 us -> 7.35 us
  other arithmetic: 0.12 us -> 1.91 us
  local copies, waits for them, and re-layouts: 4.9 us -> 5.9 us
    pallas_call x2 -> x1, Pallas kernels: 5.36 us -> 3.11 us  [windows_of(): pl.pallas_call(windows_kernel, out_shape=jax.ShapeDtypeStruct((count + 1,...]
    add x0 -> x1, other arithmetic: none -> 1.79 us  [on_device(): places = fill(cells).astype(F32) + fill(fracs)]
    pallas_call x1, Pallas kernels: 2.88 us -> 1.66 us  [stem(): pl.pallas_call(stem_kernel, out_shape=jax.ShapeDtypeStruct((3 * height -...]
    all_to_all x1, waiting for transfers between devices: 1.18 us -> 2.34 us  [on_device(): lax.all_to_all(found, 'tile', split_axis=0, concat_axis=0, tiled=True)]
    add x0 -> x1, local copies, waits for them, and re-layouts: none -> 0.81 us  [on_device(): places = fill(cells).astype(F32) + fill(fracs)]
    all_to_all x1, waiting for transfers between devices: 3.33 us -> 4.03 us  [on_device(): lax.all_to_all(places, 'tile', split_axis=0, concat_axis=0, tiled=True)]
    unnamed x31 -> x29, local copies, waits for them, and re-layouts: 2.5 us -> 2.69 us
  transfers between devices with their start and end apart: 5 -> 5, of which waited for: 3 -> 3; matrix products, arithmetic and copies ran while one was open for 5% -> 5% of each run, Pallas kernels for 40% -> 36%
where the time goes in v11:
time: 49.3 us; the launch traced here: 48.7 us
  Pallas kernels  17.7 us (36%)
  starting transfers between devices  14.9 us (30%)
  waiting for transfers between devices  7.35 us (15%)
  local copies, waits for them, and re-layouts  5.9 us (12%)
  other arithmetic  1.91 us (4%)
  between operations  0.92 us (2%)
    pallas_call x1, Pallas kernels, sample_values(): pl.pallas_call(samples_kernel, out_shape=jax.ShapeDtypeStruct((owners, ro...  8.6 us
    all_to_all x1, starting transfers between devices, on_device(): lax.all_to_all(places, 'tile', split_axis=0, concat_axis=0, tiled=True)  6.33 us
    all_to_all x1, waiting for transfers between devices, on_device(): lax.all_to_all(places, 'tile', split_axis=0, concat_axis=0, tiled=True)  4.03 us
    all_to_all x1, starting transfers between devices, on_device(): lax.all_to_all(found, 'tile', split_axis=0, concat_axis=0, tiled=True)  3.37 us
    pallas_call x1, Pallas kernels, windows_of(): pl.pallas_call(windows_kernel, out_shape=jax.ShapeDtypeStruct((count + 1,...  3.11 us
    unnamed x29, local copies, waits for them, and re-layouts  2.69 us
    ppermute x1, starting transfers between devices, on_device(): over = lax.ppermute(pending, 'tile', down)  2.39 us
    all_to_all x1, waiting for transfers between devices, on_device(): lax.all_to_all(found, 'tile', split_axis=0, concat_axis=0, tiled=True)  2.34 us
  transfers between devices with their start and end apart: 5, of which 3 were waited for; matrix products, arithmetic and copies ran while one was open for 5% of the time, Pallas kernels for 36%

profile of v11, /device:TPU:0, one launch (start us, length us, event | category | flops | bytes accessed | tf_op | source)
XLA Modules:
  0.0 48.7 jit_solution(11310342821601060778)
XLA Ops:
  0.7 1.8 %convert_add_fusion = f32[1,1,3,40960]{3,1,2,0:T(1,128)S(1)} fusion(f32[1,1,3,40960]{3,1,2,0:T(1,128)} %param.15, s32[1,1,3,40960]{3,1,2,0:T(1,128)} %param.14), kind=kLoop, calls=%fused_computation | loop fusion | flops 245760 | bytes 1474560 | tf_op jit(solution)/shard_map/add | solution.py:607
  2.4 0.8 %copy.18 = f32[3,8,40,128]{3,2,0,1:T(8,128)} copy(f32[3,8,40,128]{3,2,1,0:T(8,128)S(1)} %bitcast.20) | data formatting | bytes 983040 | tf_op jit(solution)/shard_map/add | solution.py:607
  3.3 6.3 %all-to-all-start = ((f32[8,120,128]{2,1,0:T(8,128)}), f32[8,120,128]{2,1,0:T(8,128)S(1)}, u32[]{:S(2)}, u32[]{:S(2)}) async-start(f32[8,120,128]{2,1,0:T(8,128)} %bitcast.6.place_ref), calls=%async_computation | async-start | bytes 983040 | tf_op jit(solution)/shard_map/all_to_all | solution.py:610
  9.6 0.0 copy-start.12
  9.6 2.4 %collective-permute-start = (bf16[1,4,8,256]{3,1,2,0:T(4,128)(2,1)S(1)}, bf16[1,4,8,256]{3,1,2,0:T(4,128)(2,1)S(1)}, u32[]{:S(2)}, u32[]{:S(2)}) collective-permute-start(bf16[1,4,8,256]{3,1,2,0:T(4,128)(2,1)S(1)} %copy.19), channel_id=1, source_target_pairs={{0,1},{1,2},{2,3},{3,4},{4,5},{5,6},{6,7},{8,9},{9,10},{10,11},{11... | collective-permute-start | bytes 49160 | tf_op jit(solution)/shard_map/ppermute | solution.py:614
  12.0 1.3 %collective-permute-start.1 = (bf16[1,4,8,256]{3,1,2,0:T(4,128)(2,1)S(1)}, bf16[1,4,8,256]{3,1,2,0:T(4,128)(2,1)S(1)}, u32[]{:S(2)}, u32[]{:S(2)}) collective-permute-start(bf16[1,4,8,256]{3,1,2,0:T(4,128)(2,1)S(1)} %copy.19), channel_id=1, source_target_pairs={{1,0},{2,1},{3,2},{4,3},{5,4},{6,5},{7,6},{9,8},{10,9},{11,10},{12... | collective-permute-start | bytes 49160 | tf_op jit(solution)/shard_map/ppermute | solution.py:615
  13.4 2.3 %reshape.18.cube_ref = bf16[16,34,1156]{2,1,0:T(8,128)(2,1)S(1)} reshape(bf16[16,39304]{1,0:T(8,128)(2,1)S(1)} %copy-done.9) | data formatting | bytes 2515456 | tf_op jit(solution)/shard_map/reshape | solution.py:92
  15.7 0.1 pad_add_fusion.where_ref
  15.8 3.1 %brick_windows.1.brick_ref = bf16[17,208,256]{2,1,0:T(8,128)(2,1)S(1)} custom-call(s32[2]{0:T(128)S(1)} %pad_add_fusion.where_ref, s32[2,8]{1,0:T(2,128)S(1)} %bitcast.18, bf16[16,34,1156]{2,1,0:T(8,128)(2,1)S(1)} %reshape.18.cube_ref, f32[8,120,128]{2,1,0:T(8,128)} %bitcast.6.place_ref), custom_call_target="tpu_custom_call" | custom-call | flops 905969664 | bytes 4194304 | tf_op jit(solution)/shard_map/brick_windows/pallas_call | solution.py:94
  19.0 1.2 %copy-done = bf16[17,208,256]{2,1,0:T(8,128)(2,1)} copy-done((bf16[17,208,256]{2,1,0:T(8,128)(2,1)}, bf16[17,208,256]{2,1,0:T(8,128)(2,1)S(1)}, u32[]{:S(2)}) %copy-start) | copy-done | bytes 1810456
  20.2 4.0 %all-to-all-done.place_ref = f32[8,120,128]{2,1,0:T(8,128)S(1)} async-done(((f32[8,120,128]{2,1,0:T(8,128)}), f32[8,120,128]{2,1,0:T(8,128)S(1)}, u32[]{:S(2)}, u32[]{:S(2)}) %all-to-all-start) | async-done | bytes 491552 | tf_op jit(solution)/shard_map/all_to_all | solution.py:610
  24.2 0.8 %copy-done.10 = f32[8,120,128]{2,1,0:T(8,128)} copy-done((f32[8,120,128]{2,1,0:T(8,128)}, f32[8,120,128]{2,1,0:T(8,128)S(1)}, u32[]{:S(2)}) %copy-start.10) | copy-done | bytes 491544
  25.0 8.6 %sample_values.1 = bf16[8,40,128]{2,1,0:T(8,128)(2,1)} custom-call(s32[2]{0:T(128)} %copy-done.3, s32[2,8]{1,0:T(2,128)} %bitcast.17, bf16[17,208,256]{2,1,0:T(8,128)(2,1)} %copy-done, f32[8,120,128]{2,1,0:T(8,128)} %copy-done.10), custom_call_target="tpu_custom_call" | custom-call | flops 4362076160 | bytes 3145728 | tf_op jit(solution)/shard_map/sample_values/pallas_call | solution.py:268
  33.8 3.4 %all-to-all-start.1 = ((bf16[8,40,128]{2,1,0:T(8,128)(2,1)}), bf16[8,40,128]{2,1,0:T(8,128)(2,1)S(1)}, u32[]{:S(2)}, u32[]{:S(2)}) async-start(bf16[8,40,128]{2,1,0:T(8,128)(2,1)} %sample_values.1), calls=%async_computation.1 | async-start | bytes 163840 | tf_op jit(solution)/shard_map/all_to_all | solution.py:627
  37.2 0.0 copy-start.5
  37.2 0.0 copy-start.8
  37.2 1.7 %stem.1.second = bf16[20,32,256]{2,1,0:T(8,128)(2,1)S(1)} custom-call(s32[2]{0:T(128)S(1)} %copy-done.4, bf16[24,16,256]{2,1,0:T(8,128)(2,1)S(1)} %pad.14.x_ref, bf16[9,16,32]{2,1,0:T(8,128)(2,1)S(1)} %pad.12.w_in, bf16[9,32,32]{2,1,0:T(8,128)(2,1)S(1)} %copy-done.7), custom_call_target="tpu_custom_call" | custom-call | flops 1000000000 | bytes 1048576 | tf_op jit(solution)/shard_map/stem/pallas_call | solution.py:525
  38.9 2.0 %middle.1.fourth = bf16[6,112,128]{2,1,0:T(8,128)(2,1)S(1)} custom-call(s32[2]{0:T(128)S(1)} %copy-done.4, bf16[20,32,256]{2,1,0:T(8,128)(2,1)S(1)} %stem.1.second, bf16[9,32,112]{2,1,0:T(8,128)(2,1)S(1)} %bitcast.19, bf16[9,112,112]{2,1,0:T(8,128)(2,1)S(1)} %copy-done.5), custom_call_target="tpu_custom_call" | custom-call | flops 1000000000 | bytes 1048576 | tf_op jit(solution)/shard_map/middle/pallas_call | solution.py:543
  40.8 2.3 %all-to-all-done.1.value_ref = bf16[8,40,128]{2,1,0:T(8,128)(2,1)S(1)} async-done(((bf16[8,40,128]{2,1,0:T(8,128)(2,1)}), bf16[8,40,128]{2,1,0:T(8,128)(2,1)S(1)}, u32[]{:S(2)}, u32[]{:S(2)}) %all-to-all-start.1) | async-done | bytes 81952 | tf_op jit(solution)/shard_map/all_to_all | solution.py:627
  43.2 0.2 gbuffer.1
  43.4 1.5 %collective-permute-start.2 = (bf16[1,4,8,256]{3,2,1,0:T(8,128)(2,1)S(1)}, bf16[1,4,8,256]{3,2,1,0:T(8,128)(2,1)S(1)}, u32[]{:S(2)}, u32[]{:S(2)}) collective-permute-start(bf16[1,4,8,256]{3,2,1,0:T(8,128)(2,1)S(1)} %gbuffer.1), channel_id=1, source_target_pairs={{0,8},{8,16},{16,24},{24,0},{1,9},{9,17},{17,25},{25,1},{2,10},{10... | collective-permute-start | bytes 49160 | tf_op jit(solution)/shard_map/ppermute | solution.py:636
  44.9 2.2 %decoder.1 = bf16[1,3,8,256]{3,2,1,0:T(8,128)(2,1)} custom-call(s32[2]{0:T(128)S(1)} %copy-done.4, bf16[20,32,256]{2,1,0:T(8,128)(2,1)S(1)} %stem.1.second, bf16[6,112,128]{2,1,0:T(8,128)(2,1)S(1)} %middle.1.fourth, bf16[9,32,144]{2,1,0:T(8,128)(2,1)S(1)} %copy-done.6, bf16[9,16,32]{2,1,0:T(8,128)(2,1)S(1)} %pad.13.w_out), custom_call_target="tpu_custom_call" | custom-call | flops 1000000000 | bytes 1048576 | tf_op jit(solution)/shard_map/decoder/pallas_call | solution.py:564
  47.1 1.0 %collective-permute-done.2 = bf16[1,4,8,256]{3,2,1,0:T(8,128)(2,1)S(1)} collective-permute-done((bf16[1,4,8,256]{3,2,1,0:T(8,128)(2,1)S(1)}, bf16[1,4,8,256]{3,2,1,0:T(8,128)(2,1)S(1)}, u32[]{:S(2)}, u32[]{:S(2)}) %collective-permute-start.2) | collective-permute-done | bytes 16416 | tf_op jit(solution)/shard_map/ppermute | solution.py:636
  48.1 0.6 %copy.25 = bf16[1,4,8,256]{3,2,1,0:T(8,128)(2,1)} copy(bf16[1,4,8,256]{3,2,1,0:T(8,128)(2,1)S(1)} %collective-permute-done.2) | data formatting | bytes 32768
  (31 shorter events, 0.2 us)
Async XLA Ops:
  0.6 12.7 %copy-start.9 = (bf16[16,39304]{1,0:T(8,128)(2,1)S(1)}, bf16[16,39304]{1,0:T(8,128)(2,1)}, u32[]{:S(2)}) copy-start(bf16[16,39304]{1,0:T(8,128)(2,1)} %param.12) | copy-start | bytes 3773188
  0.6 8.9 %copy-start.11 = (bf16[1,4,8,256]{3,2,1,0:T(8,128)(2,1)S(1)}, bf16[1,4,8,256]{3,2,1,0:T(8,128)(2,1)}, u32[]{:S(2)}) copy-start(bf16[1,4,8,256]{3,2,1,0:T(8,128)(2,1)} %param.17) | copy-start | bytes 49156
  3.3 21.0 %all-to-all-start = ((f32[8,120,128]{2,1,0:T(8,128)}), f32[8,120,128]{2,1,0:T(8,128)S(1)}, u32[]{:S(2)}, u32[]{:S(2)}) async-start(f32[8,120,128]{2,1,0:T(8,128)} %bitcast.6.place_ref), calls=%async_computation | async-start | bytes 983040 | tf_op jit(solution)/shard_map/all_to_all | solution.py:610
  9.6 6.1 %copy-start.12 = (bf16[9,32,4]{1,2,0:T(4,128)(2,1)S(1)}, bf16[9,32,4]{1,2,0:T(4,128)(2,1)}, u32[]{:S(2)}) copy-start(bf16[9,32,4]{1,2,0:T(4,128)(2,1)} %param.18) | copy-start | bytes 6916
  9.6 6.1 %copy-start.13 = (bf16[9,3,32]{2,1,0:T(4,128)(2,1)S(1)}, bf16[9,3,32]{2,1,0:T(4,128)(2,1)}, u32[]{:S(2)}) copy-start(bf16[9,3,32]{2,1,0:T(4,128)(2,1)} %param.23) | copy-start | bytes 5188
  9.6 6.2 %copy-start.2 = (s32[1,1,8,2]{2,3,1,0:T(2,128)S(1)}, s32[1,1,8,2]{2,3,1,0:T(2,128)}, u32[]{:S(2)}) copy-start(s32[1,1,8,2]{2,3,1,0:T(2,128)} %param.13) | copy-start | bytes 196
  9.6 24.0 %collective-permute-start = (bf16[1,4,8,256]{3,1,2,0:T(4,128)(2,1)S(1)}, bf16[1,4,8,256]{3,1,2,0:T(4,128)(2,1)S(1)}, u32[]{:S(2)}, u32[]{:S(2)}) collective-permute-start(bf16[1,4,8,256]{3,1,2,0:T(4,128)(2,1)S(1)} %copy.19), channel_id=1, source_target_pairs={{0,1},{1,2},{2,3},{3,4},{4,5},{5,6},{6,7},{8,9},{9,10},{10,11},{11... | collective-permute-start | bytes 49160 | tf_op jit(solution)/shard_map/ppermute | solution.py:614
  12.0 21.6 %collective-permute-start.1 = (bf16[1,4,8,256]{3,1,2,0:T(4,128)(2,1)S(1)}, bf16[1,4,8,256]{3,1,2,0:T(4,128)(2,1)S(1)}, u32[]{:S(2)}, u32[]{:S(2)}) collective-permute-start(bf16[1,4,8,256]{3,1,2,0:T(4,128)(2,1)S(1)} %copy.19), channel_id=1, source_target_pairs={{1,0},{2,1},{3,2},{4,3},{5,4},{6,5},{7,6},{9,8},{10,9},{11,10},{12... | collective-permute-start | bytes 49160 | tf_op jit(solution)/shard_map/ppermute | solution.py:615
  15.8 3.1 %copy-start.3 = (s32[2]{0:T(128)}, s32[2]{0:T(128)S(1)}, u32[]{:S(2)}) copy-start(s32[2]{0:T(128)S(1)} %pad_add_fusion.where_ref) | copy-start | bytes 28
  19.0 1.2 %copy-start = (bf16[17,208,256]{2,1,0:T(8,128)(2,1)}, bf16[17,208,256]{2,1,0:T(8,128)(2,1)S(1)}, u32[]{:S(2)}) copy-start(bf16[17,208,256]{2,1,0:T(8,128)(2,1)S(1)} %brick_windows.1.brick_ref) | copy-start | bytes 5431300
  20.2 16.9 %copy-start.7 = (bf16[9,32,32]{2,1,0:T(8,128)(2,1)S(1)}, bf16[9,32,32]{2,1,0:T(8,128)(2,1)}, u32[]{:S(2)}) copy-start(bf16[9,32,32]{2,1,0:T(8,128)(2,1)} %w_mid.1) | copy-start | bytes 55300
  24.2 0.8 %copy-start.10 = (f32[8,120,128]{2,1,0:T(8,128)}, f32[8,120,128]{2,1,0:T(8,128)S(1)}, u32[]{:S(2)}) copy-start(f32[8,120,128]{2,1,0:T(8,128)S(1)} %all-to-all-done.place_ref) | copy-start | bytes 1474564
  25.0 12.1 %copy-start.4 = (s32[2]{0:T(128)S(1)}, s32[2]{0:T(128)}, u32[]{:S(2)}) copy-start(s32[2]{0:T(128)} %copy-done.3) | copy-start | bytes 28
  33.8 9.4 %all-to-all-start.1 = ((bf16[8,40,128]{2,1,0:T(8,128)(2,1)}), bf16[8,40,128]{2,1,0:T(8,128)(2,1)S(1)}, u32[]{:S(2)}, u32[]{:S(2)}) async-start(bf16[8,40,128]{2,1,0:T(8,128)(2,1)} %sample_values.1), calls=%async_computation.1 | async-start | bytes 163840 | tf_op jit(solution)/shard_map/all_to_all | solution.py:627
  37.2 1.7 %copy-start.5 = (bf16[9,112,112]{2,1,0:T(8,128)(2,1)S(1)}, bf16[9,112,112]{2,1,0:T(8,128)(2,1)}, u32[]{:S(2)}) copy-start(bf16[9,112,112]{2,1,0:T(8,128)(2,1)} %w_deep.1) | copy-start | bytes 677380
  37.2 1.7 %copy-start.8 = (bf16[9,112,32]{1,2,0:T(8,128)(2,1)S(1)}, bf16[9,112,32]{1,2,0:T(8,128)(2,1)}, u32[]{:S(2)}) copy-start(bf16[9,112,32]{1,2,0:T(8,128)(2,1)} %param.20) | copy-start | bytes 193540
  38.9 4.3 %copy-start.1 = (s32[1,1,160,256]{3,2,1,0:T(8,128)S(1)}, s32[1,1,160,256]{3,2,1,0:T(8,128)}, u32[]{:S(2)}) copy-start(s32[1,1,160,256]{3,2,1,0:T(8,128)} %order_ref.1) | copy-start | bytes 491524
  38.9 6.0 %copy-start.6 = (bf16[9,32,144]{2,1,0:T(8,128)(2,1)S(1)}, bf16[9,32,144]{2,1,0:T(8,128)(2,1)}, u32[]{:S(2)}) copy-start(bf16[9,32,144]{2,1,0:T(8,128)(2,1)} %w_up.1) | copy-start | bytes 248836
  43.4 4.7 %collective-permute-start.2 = (bf16[1,4,8,256]{3,2,1,0:T(8,128)(2,1)S(1)}, bf16[1,4,8,256]{3,2,1,0:T(8,128)(2,1)S(1)}, u32[]{:S(2)}, u32[]{:S(2)}) collective-permute-start(bf16[1,4,8,256]{3,2,1,0:T(8,128)(2,1)S(1)} %gbuffer.1), channel_id=1, source_target_pairs={{0,8},{8,16},{16,24},{24,0},{1,9},{9,17},{17,25},{25,1},{2,10},{10... | collective-permute-start | bytes 49160 | tf_op jit(solution)/shard_map/ppermute | solution.py:636

commit v12 on v10

--- a/solution.py
+++ b/solution.py
@@ -100,8 +100,7 @@
 
 
 def windows_kernel(
-    where_ref, picks_ref, cube_ref, place_ref, out_ref, own_ref,
-    wide, tail, places, sums, arrival,
+    where_ref, picks_ref, cube_ref, place_ref, out_ref, wide, tail, places, sums, arrival
 ):
     tile = where_ref[0]
     own_places = pltpu.make_async_copy(place_ref.at[tile], places, arrival)
@@ -129,12 +128,12 @@
             preferred_element_type=F32,
         )
         found = found.reshape(count, 48, KDIM)
-        out_ref[:, window * MAIN : (window + 1) * MAIN, :] = found[:, :MAIN, :].astype(BF16)
+        out_ref[:count, window * MAIN : (window + 1) * MAIN, :] = found[:, :MAIN, :].astype(BF16)
         tail[:, window : window + 1, :] = found[:, MAIN : MAIN + 1, :]
         tail[:, 8 + window : 9 + window, :] = found[:, MAIN + 1 : MAIN + 2, :]
     for row in (6, 7, 14, 15):
         tail[:, row : row + 1, :] = jnp.zeros((count, 1, KDIM), F32)
-    out_ref[:, WINDOWS * MAIN :, :] = tail[...].astype(BF16)
+    out_ref[:count, WINDOWS * MAIN :, :] = tail[...].astype(BF16)
 
     own_places.wait()
     cap = picks_ref.shape[0]
@@ -147,7 +146,7 @@
         return carry
 
     lax.fori_loop(0, cap, one_slot, 0)
-    own_ref[0] = line_values(sums, lines)
+    out_ref[count, : whole_tiles(lines), :LANES] = line_values(sums, lines, whole_tiles(lines))
 
 
 def windows_of(where, picks, bricks, places):
@@ -156,12 +155,9 @@
     rows = places.shape[1]
     return pl.pallas_call(
         windows_kernel,
-        out_shape=(
-            jax.ShapeDtypeStruct((count, BRICK_ROWS, KDIM), BF16),
-            jax.ShapeDtypeStruct((1, rows // 3, LANES), BF16),
-        ),
+        out_shape=jax.ShapeDtypeStruct((count + 1, BRICK_ROWS, KDIM), BF16),
         in_specs=[smem(), smem(), vmem(), pl.BlockSpec(memory_space=pl.ANY)],
-        out_specs=(vmem(), vmem()),
+        out_specs=vmem(),
         scratch_shapes=[
             pltpu.VMEM((count, 48, 10 * LANES), BF16),
             pltpu.VMEM((count, TAIL, KDIM), F32),
@@ -248,18 +244,25 @@
             ]
 
 
-def line_values(sums, lines):
+def whole_tiles(lines):
+    return -(-lines // TAIL) * TAIL
+
+
+def line_values(sums, lines, height):
     values = []
     for row in range(0, lines, 8):
         value = sums[pl.ds(8 * row, 8, stride=8), :]
         for other in range(1, 8):
             value = value + sums[pl.ds(8 * row + other, 8, stride=8), :]
         values.append(value)
+    if height > lines:
+        values.append(jnp.zeros((height - lines, LANES), F32))
     return jnp.concatenate(values, axis=0).astype(BF16)
 
 
 def samples_kernel(
-    where_ref, picks_ref, brick_ref, place_ref, own_ref, out_ref, bricks, places, sums, arrivals
+    where_ref, picks_ref, brick_ref, place_ref, out_ref, bricks, places, sums, own, arrivals,
+    own_arrival,
 ):
     owners, rows, _ = place_ref.shape
     cap = picks_ref.shape[0]
@@ -267,52 +270,88 @@
     part = lines // cap
     turns = owners - 1
     tile = where_ref[0]
-    out_ref[tile] = own_ref[0]
-
-    def renderer_of(turn):
-        return lax.rem(tile + 1 + turn, owners)
-
-    def fetches(turn):
+    pairs, rest = turns // 2, turns % 2
+    own_values = pltpu.make_async_copy(
+        brick_ref.at[brick_ref.shape[0] - 1, pl.ds(0, own.shape[0]), pl.ds(0, LANES)],
+        own,
+        own_arrival,
+    )
+
+    def renderer_of(number):
+        return lax.rem(tile + 1 + number, owners)
+
+    def fetches(turn, members):
         held = turn % 2
-        renderer = renderer_of(turn)
-        copies = [
-            pltpu.make_async_copy(
-                place_ref.at[renderer], places.at[held], arrivals.at[held, cap]
-            )
-        ]
-        for piece in range(cap):
+        copies = []
+        for member in range(members):
+            renderer = renderer_of(2 * turn + member)
             copies.append(
                 pltpu.make_async_copy(
-                    brick_ref.at[picks_ref[piece, renderer]],
-                    bricks.at[held, piece],
-                    arrivals.at[held, piece],
+                    place_ref.at[renderer],
+                    places.at[held, member],
+                    arrivals.at[held, member, cap],
                 )
             )
+            for piece in range(cap):
+                copies.append(
+                    pltpu.make_async_copy(
+                        brick_ref.at[picks_ref[piece, renderer]],
+                        bricks.at[held, member, piece],
+                        arrivals.at[held, member, piece],
+                    )
+                )
         return copies
 
-    for turn in range(min(2, turns)):
-        for copy in fetches(turn):
+    def start(turn, members):
+        for copy in fetches(turn, members):
             copy.start()
 
-    def one_turn(turn, carry):
+    def work(turn, members):
         held = turn % 2
-        for copy in fetches(turn):
+        for copy in fetches(turn, members):
             copy.wait()
-        for piece in range(cap):
-            slot_sums(bricks[held, piece], places.at[held], sums, piece * part, part // 2)
-        out_ref[renderer_of(turn)] = line_values(sums, lines)
-
-        @pl.when(turn + 2 < turns)
+        for member in range(members):
+            for piece in range(cap):
+                slot_sums(
+                    bricks[held, member, piece],
+                    places.at[held, member],
+                    sums.at[member],
+                    piece * part,
+                    part // 2,
+                )
+        for member in range(members):
+            out_ref[renderer_of(2 * turn + member)] = line_values(
+                sums.at[member], lines, lines
+            )
+
+    def one_pair(turn, carry):
+        work(turn, 2)
+
+        @pl.when(turn + 2 < pairs)
         def _():
-            for copy in fetches(turn + 2):
-                copy.start()
+            start(turn + 2, 2)
+
+        if rest:
+
+            @pl.when(turn + 2 == pairs)
+            def _():
+                start(pairs, 1)
 
         return carry
 
-    lax.fori_loop(0, turns, one_turn, 0)
-
-
-def sample_values(where, picks, windows, places, own):
+    for turn in range(min(2, pairs)):
+        start(turn, 2)
+    if rest and pairs < 2:
+        start(pairs, 1)
+    own_values.start()
+    lax.fori_loop(0, pairs, one_pair, 0)
+    if rest:
+        work(pairs, 1)
+    own_values.wait()
+    out_ref[tile] = own[...].astype(F32)[:lines].astype(BF16)
+
+
+def sample_values(where, picks, windows, places):
     owners, rows, _ = places.shape
     cap = picks.shape[0]
     samples = owners * rows * LANES // 3
@@ -320,13 +359,15 @@
     return pl.pallas_call(
         samples_kernel,
         out_shape=jax.ShapeDtypeStruct((owners, rows // 3, LANES), BF16),
-        in_specs=[smem(), smem(), some, some, vmem()],
+        in_specs=[smem(), smem(), some, some],
         out_specs=vmem(),
         scratch_shapes=[
-            pltpu.VMEM((2, cap, BRICK_ROWS, KDIM), BF16),
-            pltpu.VMEM((2, rows, LANES), F32),
-            pltpu.VMEM((8 * rows // 3, LANES), F32),
-            pltpu.SemaphoreType.DMA((2, cap + 1)),
+            pltpu.VMEM((2, 2, cap, BRICK_ROWS, KDIM), BF16),
+            pltpu.VMEM((2, 2, rows, LANES), F32),
+            pltpu.VMEM((2, 8 * rows // 3, LANES), F32),
+            pltpu.VMEM((whole_tiles(rows // 3), LANES), BF16),
+            pltpu.SemaphoreType.DMA((2, 2, cap + 1)),
+            pltpu.SemaphoreType.DMA,
         ],
         compiler_params=pltpu.CompilerParams(vmem_limit_bytes=61_600_000),
         cost_estimate=pl.CostEstimate(
@@ -334,7 +375,7 @@
             transcendentals=0,
         ),
         name="sample_values",
-    )(where, picks, windows, places, own)
+    )(where, picks, windows, places)
 
 
 def gbuffer_kernel(value_ref, order_ref, out_ref, values):
@@ -478,11 +519,26 @@
 
         lax.fori_loop(0, target.shape[0], step, 0, unroll=unroll)
 
-    full_layer(turned(w_in), x_ref, first, height - 1, 2 * height - 1, first.shape[0] // 2)
-    full_layer(beside(w_mid), first, second, height - 2, 2 * height - 2, second.shape[0] // 4)
-
-
-def middle_kernel(where_ref, second, w_down, w_deep, fourth, pooled, third):
+    full_layer(turned(w_in), x_ref, first, height - 1, 2 * height - 1, first.shape[0])
+    full_layer(beside(w_mid), first, second, height - 2, 2 * height - 2, second.shape[0])
+
+
+def half_pair(source, row, tap):
+    return jnp.concatenate([source[row + tap], source[row + tap + 1]], axis=1)
+
+
+def half_layer(product, target, inside, low, high):
+    chans, half_width = target.shape[1], target.shape[2]
+    for row in range(0, target.shape[0], 2):
+        both = silu(across(product(row), chans, half_width))
+        for now in range(2):
+            line = both[:, now * half_width : (now + 1) * half_width]
+            if row + now < low or row + now >= high:
+                line = line * inside(row + now, low, high)
+            target[row + now] = line.astype(BF16)
+
+
+def middle_kernel(where_ref, second, w_down, third, pooled):
     count, chans, width = second.shape
     half_height = (count + 4) // 6
     half_width = width // 2
@@ -494,25 +550,24 @@
         second[...].reshape(count * chans, width), shrink, preferred_element_type=F32
     ).reshape(count // 2, 2, chans, half_width)
     pooled[...] = (pairs[:, 0] + pairs[:, 1]).astype(BF16)
-
-    def half_pair(source, row, tap):
-        return jnp.concatenate([source[row + tap], source[row + tap + 1]], axis=1)
-
-    def half_layer(product, target, low, high):
-        chans = target.shape[1]
-        for row in range(0, target.shape[0], 2):
-            both = silu(across(product(row), chans, half_width))
-            for now in range(2):
-                line = both[:, now * half_width : (now + 1) * half_width]
-                if row + now < low or row + now >= high:
-                    line = line * inside(row + now, low, high)
-                target[row + now] = line.astype(BF16)
-
     weight_down = turned(w_down)
 
     def down_product(row):
         lines = jnp.concatenate([half_pair(pooled, row, tap) for tap in range(3)], axis=0)
         return jnp.dot(weight_down, lines, preferred_element_type=F32)
+
+    half_layer(down_product, third, inside, half_height - 2, 2 * half_height - 2)
+
+
+def decoder_kernel(
+    where_ref, second, third, w_deep, w_up, w_out, out_ref, fourth, joined, fifth, final
+):
+    height = out_ref.shape[2]
+    half_height = height // 2
+    width = out_ref.shape[3]
+    half_width = width // 2
+    chans = second.shape[1]
+    inside = sides(where_ref)
 
     def deep_product(row):
         total = None
@@ -523,18 +578,7 @@
             total = part if total is None else total + part
         return total
 
-    half_layer(down_product, third, half_height - 2, 2 * half_height - 2)
-    half_layer(deep_product, fourth, half_height - 3, 2 * half_height - 3)
-
-
-def decoder_kernel(
-    where_ref, second, fourth, w_up, w_out, out_ref, joined, fifth, final
-):
-    height = out_ref.shape[2]
-    width = out_ref.shape[3]
-    half_width = width // 2
-    chans = second.shape[1]
-    inside = sides(where_ref)
+    half_layer(deep_product, fourth, inside, half_height - 3, 2 * half_height - 3)
     place = lax.broadcasted_iota(jnp.int32, (half_width, width), 0)
     target = lax.broadcasted_iota(jnp.int32, (half_width, width), 1) // 2
     spread = jnp.where(place == target, 1.0, 0.0).astype(BF16)
@@ -555,7 +599,7 @@
         fifth[row] = (line * inside(row, 1, height + 1)).astype(BF16)
         return carry
 
-    lax.fori_loop(0, fifth.shape[0], up_step, 0, unroll=fifth.shape[0] // 2)
+    lax.fori_loop(0, fifth.shape[0], up_step, 0, unroll=fifth.shape[0])
 
     colours = out_ref.shape[1]
     weight_out = beside(w_out)
@@ -586,47 +630,45 @@
     )(where, field, w_in, w_mid)
 
 
-def middle(where, second, w_down, w_deep):
+def middle(where, second, w_down):
     rows, one, width = second.shape
     half = (rows + 4) // 6
-    two = w_deep.shape[1]
+    two = w_down.shape[2]
     return pl.pallas_call(
         middle_kernel,
-        out_shape=jax.ShapeDtypeStruct((3 * half - 6, two, width // 2), BF16),
-        in_specs=[smem()] + [vmem()] * 3,
+        out_shape=jax.ShapeDtypeStruct((3 * half - 4, two, width // 2), BF16),
+        in_specs=[smem()] + [vmem()] * 2,
         out_specs=vmem(),
-        scratch_shapes=[
-            pltpu.VMEM((3 * half - 2, one, width // 2), BF16),
-            pltpu.VMEM((3 * half - 4, two, width // 2), BF16),
-        ],
+        scratch_shapes=[pltpu.VMEM((3 * half - 2, one, width // 2), BF16)],
         compiler_params=params(16),
         cost_estimate=pl.CostEstimate(
-            flops=1_000_000_000, bytes_accessed=MIB, transcendentals=200_000
+            flops=500_000_000, bytes_accessed=MIB, transcendentals=100_000
         ),
         name="middle",
-    )(where, second, w_down, w_deep)
-
-
-def decoder(where, second, deep, w_up, w_out, height, colours):
+    )(where, second, w_down)
+
+
+def decoder(where, second, third, w_deep, w_up, w_out, height, colours):
     one = second.shape[1]
-    two = deep.shape[1]
+    two = third.shape[1]
     width = second.shape[2]
     return pl.pallas_call(
         decoder_kernel,
         out_shape=jax.ShapeDtypeStruct((1, colours, height, width), BF16),
-        in_specs=[smem()] + [vmem()] * 4,
+        in_specs=[smem()] + [vmem()] * 5,
         out_specs=vmem(),
         scratch_shapes=[
+            pltpu.VMEM((third.shape[0] - 2, two, width // 2), BF16),
             pltpu.VMEM((height + 4, one + two, width), BF16),
             pltpu.VMEM((height + 2, one, width), BF16),
             pltpu.VMEM((colours, height, width), F32),
         ],
         compiler_params=params(16),
         cost_estimate=pl.CostEstimate(
-            flops=1_000_000_000, bytes_accessed=MIB, transcendentals=100_000
+            flops=1_500_000_000, bytes_accessed=MIB, transcendentals=200_000
         ),
         name="decoder",
-    )(where, second, deep, w_up, w_out)
+    )(where, second, third, w_deep, w_up, w_out)
 
 
 def on_device(
@@ -668,22 +710,22 @@
     w_in = w_in.transpose(0, 2, 1)
     w_in = jnp.pad(w_in, ((0, 0), (0, 16 - w_in.shape[1]), (0, 0)))
     w_out = jnp.pad(w_out, ((0, 0), (0, 16 - colours), (0, 0)))
-    windows, own = windows_of(where, picks, bricks, places)
+    windows = windows_of(where, picks, bricks, places)
     arrived, w_in, w_out = lax.optimization_barrier((arrived, w_in, w_out))
-    found = sample_values(where, picks, windows, arrived, own)
+    found = sample_values(where, picks, windows, arrived)
 
     found, over, under, pending = lax.optimization_barrier((found, over, under, pending))
     values = lax.all_to_all(found, "tile", split_axis=0, concat_axis=0, tiled=True)
     field = jnp.concatenate([over[0], pending[0], under[0]], axis=1).transpose(1, 0, 2)
     field = jnp.pad(field, ((0, 0), (0, 16 - field.shape[1]), (0, 0)))
     second = stem(where, field, w_in, w_mid)
-    deep = middle(where, second, w_down.transpose(0, 2, 1), w_deep)
-    values, deep = lax.optimization_barrier((values, deep))
+    third = middle(where, second, w_down.transpose(0, 2, 1))
+    values, third = lax.optimization_barrier((values, third))
     rendered = gbuffer(trim(values), sample_order, height, width)
-    rendered, deep = lax.optimization_barrier((rendered, deep))
+    rendered, third = lax.optimization_barrier((rendered, third))
     ring = [(i, (i + 1) % n_section) for i in range(n_section)]
     handoff = lax.ppermute(rendered, "section", ring)
-    denoised = decoder(where, second, deep, w_up, w_out, height, colours)
+    denoised = decoder(where, second, third, w_deep, w_up, w_out, height, colours)
     return (handoff, denoised)
 
 

time: 48.5 us -> 47.8 us (0.986)
  waiting for transfers between devices: 5.09 us -> 7.15 us
  Pallas kernels: 21.5 us -> 19.8 us
  local copies, waits for them, and re-layouts: 4.9 us -> 4.31 us
    all_to_all x1, waiting for transfers between devices: 1.18 us -> 2.96 us  [on_device(): lax.all_to_all(found, 'tile', split_axis=0, concat_axis=0, tiled=True)]
    pallas_call x1, Pallas kernels: 2.88 us -> 1.66 us  [stem(): pl.pallas_call(stem_kernel, out_shape=jax.ShapeDtypeStruct((3 * height -...]
    pallas_call x1, Pallas kernels: 1.96 us -> 1.26 us  [middle(): pl.pallas_call(middle_kernel, out_shape=jax.ShapeDtypeStruct((3 * half -...]
    unnamed x31 -> x29, local copies, waits for them, and re-layouts: 2.5 us -> 1.91 us
    all_to_all x1, waiting for transfers between devices: 3.33 us -> 3.91 us  [on_device(): lax.all_to_all(places, 'tile', split_axis=0, concat_axis=0, tiled=True)]
  transfers between devices with their start and end apart: 5 -> 5, of which waited for: 3 -> 3; matrix products, arithmetic and copies ran while one was open for 5% -> 5% of each run, Pallas kernels for 40% -> 37%
where the time goes in v12:
time: 47.8 us; the launch traced here: 47.4 us
  Pallas kernels  19.8 us (41%)
  starting transfers between devices  15.1 us (32%)
  waiting for transfers between devices  7.15 us (15%)
  local copies, waits for them, and re-layouts  4.31 us (9%)
  between operations  0.92 us (2%)
    pallas_call x1, Pallas kernels, sample_values(): pl.pallas_call(samples_kernel, out_shape=jax.ShapeDtypeStruct((owners, ro...  8.47 us
    all_to_all x1, starting transfers between devices, on_device(): lax.all_to_all(places, 'tile', split_axis=0, concat_axis=0, tiled=True)  6.34 us
    all_to_all x1, waiting for transfers between devices, on_device(): lax.all_to_all(places, 'tile', split_axis=0, concat_axis=0, tiled=True)  3.91 us
    all_to_all x1, starting transfers between devices, on_device(): lax.all_to_all(found, 'tile', split_axis=0, concat_axis=0, tiled=True)  3.37 us
    pallas_call x1, Pallas kernels, windows_of(): pl.pallas_call(windows_kernel, out_shape=jax.ShapeDtypeStruct((count + 1,...  3.19 us
    all_to_all x1, waiting for transfers between devices, on_device(): lax.all_to_all(found, 'tile', split_axis=0, concat_axis=0, tiled=True)  2.96 us
    pallas_call x1, Pallas kernels, decoder(): pl.pallas_call(decoder_kernel, out_shape=jax.ShapeDtypeStruct((1, colours...  2.87 us
    ppermute x1, starting transfers between devices, on_device(): over = lax.ppermute(pending, 'tile', down)  2.52 us
  transfers between devices with their start and end apart: 5, of which 3 were waited for; matrix products, arithmetic and copies ran while one was open for 5% of the time, Pallas kernels for 37%

profile of v12, /device:TPU:0, one launch (start us, length us, event | category | flops | bytes accessed | tf_op | source)
XLA Modules:
  0.0 47.4 jit_solution(1521427747380850751)
XLA Ops:
  0.7 2.2 %positions.1.place_ref = f32[8,120,128]{2,1,0:T(8,128)} custom-call(s32[3,320,128]{2,1,0:T(8,128)} %bitcast.18, f32[3,320,128]{2,1,0:T(8,128)} %bitcast.19), custom_call_target="tpu_custom_call" | custom-call | flops 122880 | bytes 1474560 | tf_op jit(solution)/shard_map/positions/pallas_call | solution.py:82
  2.8 6.3 %all-to-all-start = ((f32[8,120,128]{2,1,0:T(8,128)}), f32[8,120,128]{2,1,0:T(8,128)}, u32[]{:S(2)}, u32[]{:S(2)}) async-start(f32[8,120,128]{2,1,0:T(8,128)} %positions.1.place_ref), calls=%async_computation | async-start | bytes 983040 | tf_op jit(solution)/shard_map/all_to_all | solution.py:701
  9.2 0.0 copy-start.12
  9.2 0.0 copy-start.3
  9.2 2.5 %collective-permute-start = (bf16[1,4,8,256]{3,1,2,0:T(4,128)(2,1)S(1)}, bf16[1,4,8,256]{3,1,2,0:T(4,128)(2,1)S(1)}, u32[]{:S(2)}, u32[]{:S(2)}) collective-permute-start(bf16[1,4,8,256]{3,1,2,0:T(4,128)(2,1)S(1)} %copy.17), channel_id=1, source_target_pairs={{0,1},{1,2},{2,3},{3,4},{4,5},{5,6},{6,7},{8,9},{9,10},{10,11},{11... | collective-permute-start | bytes 49160 | tf_op jit(solution)/shard_map/ppermute | solution.py:705
  11.8 1.3 %collective-permute-start.1 = (bf16[1,4,8,256]{3,1,2,0:T(4,128)(2,1)S(1)}, bf16[1,4,8,256]{3,1,2,0:T(4,128)(2,1)S(1)}, u32[]{:S(2)}, u32[]{:S(2)}) collective-permute-start(bf16[1,4,8,256]{3,1,2,0:T(4,128)(2,1)S(1)} %copy.17), channel_id=1, source_target_pairs={{1,0},{2,1},{3,2},{4,3},{5,4},{6,5},{7,6},{9,8},{10,9},{11,10},{12... | collective-permute-start | bytes 49160 | tf_op jit(solution)/shard_map/ppermute | solution.py:706
  13.1 2.3 %reshape.15.cube_ref = bf16[16,34,1156]{2,1,0:T(8,128)(2,1)S(1)} reshape(bf16[16,39304]{1,0:T(8,128)(2,1)S(1)} %copy-done.10) | data formatting | bytes 2515456 | tf_op jit(solution)/shard_map/reshape | solution.py:154
  15.5 0.1 pad_add_fusion.where_ref
  15.6 3.2 %brick_windows.1.brick_ref = bf16[17,208,256]{2,1,0:T(8,128)(2,1)S(1)} custom-call(s32[2]{0:T(128)S(1)} %pad_add_fusion.where_ref, s32[2,8]{1,0:T(2,128)S(1)} %bitcast.16, bf16[16,34,1156]{2,1,0:T(8,128)(2,1)S(1)} %reshape.15.cube_ref, f32[8,120,128]{2,1,0:T(8,128)S(1)} %copy-done), custom_call_target="tpu_custom_call" | custom-call | flops 905969664 | bytes 4194304 | tf_op jit(solution)/shard_map/brick_windows/pallas_call | solution.py:156
  18.8 1.2 %copy-done.1 = bf16[17,208,256]{2,1,0:T(8,128)(2,1)} copy-done((bf16[17,208,256]{2,1,0:T(8,128)(2,1)}, bf16[17,208,256]{2,1,0:T(8,128)(2,1)S(1)}, u32[]{:S(2)}) %copy-start.1) | copy-done | bytes 1810456
  20.0 3.9 %all-to-all-done.place_ref = f32[8,120,128]{2,1,0:T(8,128)} async-done(((f32[8,120,128]{2,1,0:T(8,128)}), f32[8,120,128]{2,1,0:T(8,128)}, u32[]{:S(2)}, u32[]{:S(2)}) %all-to-all-start) | async-done | bytes 491552 | tf_op jit(solution)/shard_map/all_to_all | solution.py:701
  23.9 8.5 %sample_values.1 = bf16[8,40,128]{2,1,0:T(8,128)(2,1)} custom-call(s32[2]{0:T(128)} %copy-done.4, s32[2,8]{1,0:T(2,128)} %bitcast.15, bf16[17,208,256]{2,1,0:T(8,128)(2,1)} %copy-done.1, f32[8,120,128]{2,1,0:T(8,128)} %all-to-all-done.place_ref), custom_call_target="tpu_custom_call" | custom-call | flops 4362076160 | bytes 3145728 | tf_op jit(solution)/shard_map/sample_values/pallas_call | solution.py:359
  32.5 3.4 %all-to-all-start.1 = ((bf16[8,40,128]{2,1,0:T(8,128)(2,1)}), bf16[8,40,128]{2,1,0:T(8,128)(2,1)S(1)}, u32[]{:S(2)}, u32[]{:S(2)}) async-start(bf16[8,40,128]{2,1,0:T(8,128)(2,1)} %sample_values.1), calls=%async_computation.1 | async-start | bytes 163840 | tf_op jit(solution)/shard_map/all_to_all | solution.py:718
  35.9 0.0 copy-start.9
  35.9 1.7 %stem.1.second = bf16[20,32,256]{2,1,0:T(8,128)(2,1)S(1)} custom-call(s32[2]{0:T(128)S(1)} %copy-done.5, bf16[24,16,256]{2,1,0:T(8,128)(2,1)S(1)} %pad.14.x_ref, bf16[9,16,32]{2,1,0:T(8,128)(2,1)S(1)} %pad.12.w_in, bf16[9,32,32]{2,1,0:T(8,128)(2,1)S(1)} %copy-done.8), custom_call_target="tpu_custom_call" | custom-call | flops 1000000000 | bytes 1048576 | tf_op jit(solution)/shard_map/stem/pallas_call | solution.py:619
  37.6 0.0 copy-start.2
  37.6 0.0 copy-start.6
  37.7 1.3 %middle.1.third = bf16[8,112,128]{2,1,0:T(8,128)(2,1)S(1)} custom-call(s32[2]{0:T(128)S(1)} %copy-done.5, bf16[20,32,256]{2,1,0:T(8,128)(2,1)S(1)} %stem.1.second, bf16[9,32,112]{2,1,0:T(8,128)(2,1)S(1)} %bitcast.17), custom_call_target="tpu_custom_call" | custom-call | flops 500000000 | bytes 1048576 | tf_op jit(solution)/shard_map/middle/pallas_call | solution.py:637
  38.9 3.0 %all-to-all-done.1.value_ref = bf16[8,40,128]{2,1,0:T(8,128)(2,1)S(1)} async-done(((bf16[8,40,128]{2,1,0:T(8,128)(2,1)}), bf16[8,40,128]{2,1,0:T(8,128)(2,1)S(1)}, u32[]{:S(2)}, u32[]{:S(2)}) %all-to-all-start.1) | async-done | bytes 81952 | tf_op jit(solution)/shard_map/all_to_all | solution.py:718
  41.9 0.2 gbuffer.1
  42.1 1.5 %collective-permute-start.2 = (bf16[1,4,8,256]{3,2,1,0:T(8,128)(2,1)S(1)}, bf16[1,4,8,256]{3,2,1,0:T(8,128)(2,1)S(1)}, u32[]{:S(2)}, u32[]{:S(2)}) collective-permute-start(bf16[1,4,8,256]{3,2,1,0:T(8,128)(2,1)S(1)} %gbuffer.1), channel_id=1, source_target_pairs={{0,8},{8,16},{16,24},{24,0},{1,9},{9,17},{17,25},{25,1},{2,10},{10... | collective-permute-start | bytes 49160 | tf_op jit(solution)/shard_map/ppermute | solution.py:727
  43.6 2.9 %decoder.1 = bf16[1,3,8,256]{3,2,1,0:T(8,128)(2,1)} custom-call(s32[2]{0:T(128)S(1)} %copy-done.5, bf16[20,32,256]{2,1,0:T(8,128)(2,1)S(1)} %stem.1.second, bf16[8,112,128]{2,1,0:T(8,128)(2,1)S(1)} %middle.1.third, bf16[9,112,112]{2,1,0:T(8,128)(2,1)S(1)} %copy-done.6, bf16[9,32,144]{2,1,0:T(8,128)(2,1)S(1)} %copy-done.7, bf16[9,16,32]{2,1,0:T(8,128)(2,1)S(1)} %pad.13.w_out), custom_call_target="tpu_custom_call" | custom-call | flops 1500000000 | bytes 1048576 | tf_op jit(solution)/shard_map/decoder/pallas_call | solution.py:655
  46.5 0.3 collective-permute-done.2
  46.8 0.6 %copy.23 = bf16[1,4,8,256]{3,2,1,0:T(8,128)(2,1)} copy(bf16[1,4,8,256]{3,2,1,0:T(8,128)(2,1)S(1)} %collective-permute-done.2) | data formatting | bytes 32768
  (30 shorter events, 0.2 us)
Async XLA Ops:
  0.6 12.5 %copy-start.10 = (bf16[16,39304]{1,0:T(8,128)(2,1)S(1)}, bf16[16,39304]{1,0:T(8,128)(2,1)}, u32[]{:S(2)}) copy-start(bf16[16,39304]{1,0:T(8,128)(2,1)} %param.12) | copy-start | bytes 3773188
  0.6 8.5 %copy-start.11 = (bf16[1,4,8,256]{3,2,1,0:T(8,128)(2,1)S(1)}, bf16[1,4,8,256]{3,2,1,0:T(8,128)(2,1)}, u32[]{:S(2)}) copy-start(bf16[1,4,8,256]{3,2,1,0:T(8,128)(2,1)} %param.17) | copy-start | bytes 49156
  2.8 21.1 %all-to-all-start = ((f32[8,120,128]{2,1,0:T(8,128)}), f32[8,120,128]{2,1,0:T(8,128)}, u32[]{:S(2)}, u32[]{:S(2)}) async-start(f32[8,120,128]{2,1,0:T(8,128)} %positions.1.place_ref), calls=%async_computation | async-start | bytes 983040 | tf_op jit(solution)/shard_map/all_to_all | solution.py:701
  9.2 6.2 %copy-start.12 = (bf16[9,32,4]{1,2,0:T(4,128)(2,1)S(1)}, bf16[9,32,4]{1,2,0:T(4,128)(2,1)}, u32[]{:S(2)}) copy-start(bf16[9,32,4]{1,2,0:T(4,128)(2,1)} %param.18) | copy-start | bytes 6916
  9.2 6.3 %copy-start.13 = (bf16[9,3,32]{2,1,0:T(4,128)(2,1)S(1)}, bf16[9,3,32]{2,1,0:T(4,128)(2,1)}, u32[]{:S(2)}) copy-start(bf16[9,3,32]{2,1,0:T(4,128)(2,1)} %param.23) | copy-start | bytes 5188
  9.2 6.4 %copy-start = (f32[8,120,128]{2,1,0:T(8,128)S(1)}, f32[8,120,128]{2,1,0:T(8,128)}, u32[]{:S(2)}) copy-start(f32[8,120,128]{2,1,0:T(8,128)} %positions.1.place_ref) | copy-start | bytes 1474564
  9.2 6.4 %copy-start.3 = (s32[1,1,8,2]{2,3,1,0:T(2,128)S(1)}, s32[1,1,8,2]{2,3,1,0:T(2,128)}, u32[]{:S(2)}) copy-start(s32[1,1,8,2]{2,3,1,0:T(2,128)} %param.13) | copy-start | bytes 196
  9.2 23.2 %collective-permute-start = (bf16[1,4,8,256]{3,1,2,0:T(4,128)(2,1)S(1)}, bf16[1,4,8,256]{3,1,2,0:T(4,128)(2,1)S(1)}, u32[]{:S(2)}, u32[]{:S(2)}) collective-permute-start(bf16[1,4,8,256]{3,1,2,0:T(4,128)(2,1)S(1)} %copy.17), channel_id=1, source_target_pairs={{0,1},{1,2},{2,3},{3,4},{4,5},{5,6},{6,7},{8,9},{9,10},{10,11},{11... | collective-permute-start | bytes 49160 | tf_op jit(solution)/shard_map/ppermute | solution.py:705
  11.8 20.7 %collective-permute-start.1 = (bf16[1,4,8,256]{3,1,2,0:T(4,128)(2,1)S(1)}, bf16[1,4,8,256]{3,1,2,0:T(4,128)(2,1)S(1)}, u32[]{:S(2)}, u32[]{:S(2)}) collective-permute-start(bf16[1,4,8,256]{3,1,2,0:T(4,128)(2,1)S(1)} %copy.17), channel_id=1, source_target_pairs={{1,0},{2,1},{3,2},{4,3},{5,4},{6,5},{7,6},{9,8},{10,9},{11,10},{12... | collective-permute-start | bytes 49160 | tf_op jit(solution)/shard_map/ppermute | solution.py:706
  15.6 3.2 %copy-start.4 = (s32[2]{0:T(128)}, s32[2]{0:T(128)S(1)}, u32[]{:S(2)}) copy-start(s32[2]{0:T(128)S(1)} %pad_add_fusion.where_ref) | copy-start | bytes 28
  18.8 1.2 %copy-start.1 = (bf16[17,208,256]{2,1,0:T(8,128)(2,1)}, bf16[17,208,256]{2,1,0:T(8,128)(2,1)S(1)}, u32[]{:S(2)}) copy-start(bf16[17,208,256]{2,1,0:T(8,128)(2,1)S(1)} %brick_windows.1.brick_ref) | copy-start | bytes 5431300
  20.0 15.9 %copy-start.8 = (bf16[9,32,32]{2,1,0:T(8,128)(2,1)S(1)}, bf16[9,32,32]{2,1,0:T(8,128)(2,1)}, u32[]{:S(2)}) copy-start(bf16[9,32,32]{2,1,0:T(8,128)(2,1)} %w_mid.1) | copy-start | bytes 55300
  23.9 12.0 %copy-start.5 = (s32[2]{0:T(128)S(1)}, s32[2]{0:T(128)}, u32[]{:S(2)}) copy-start(s32[2]{0:T(128)} %copy-done.4) | copy-start | bytes 28
  32.5 9.4 %all-to-all-start.1 = ((bf16[8,40,128]{2,1,0:T(8,128)(2,1)}), bf16[8,40,128]{2,1,0:T(8,128)(2,1)S(1)}, u32[]{:S(2)}, u32[]{:S(2)}) async-start(bf16[8,40,128]{2,1,0:T(8,128)(2,1)} %sample_values.1), calls=%async_computation.1 | async-start | bytes 163840 | tf_op jit(solution)/shard_map/all_to_all | solution.py:718
  35.9 1.7 %copy-start.9 = (bf16[9,112,32]{1,2,0:T(8,128)(2,1)S(1)}, bf16[9,112,32]{1,2,0:T(8,128)(2,1)}, u32[]{:S(2)}) copy-start(bf16[9,112,32]{1,2,0:T(8,128)(2,1)} %param.20) | copy-start | bytes 193540
  37.6 4.3 %copy-start.2 = (s32[1,1,160,256]{3,2,1,0:T(8,128)S(1)}, s32[1,1,160,256]{3,2,1,0:T(8,128)}, u32[]{:S(2)}) copy-start(s32[1,1,160,256]{3,2,1,0:T(8,128)} %order_ref.1) | copy-start | bytes 491524
  37.6 6.0 %copy-start.6 = (bf16[9,112,112]{2,1,0:T(8,128)(2,1)S(1)}, bf16[9,112,112]{2,1,0:T(8,128)(2,1)}, u32[]{:S(2)}) copy-start(bf16[9,112,112]{2,1,0:T(8,128)(2,1)} %w_deep.1) | copy-start | bytes 677380
  37.6 6.0 %copy-start.7 = (bf16[9,32,144]{2,1,0:T(8,128)(2,1)S(1)}, bf16[9,32,144]{2,1,0:T(8,128)(2,1)}, u32[]{:S(2)}) copy-start(bf16[9,32,144]{2,1,0:T(8,128)(2,1)} %w_up.1) | copy-start | bytes 248836
  42.1 4.7 %collective-permute-start.2 = (bf16[1,4,8,256]{3,2,1,0:T(8,128)(2,1)S(1)}, bf16[1,4,8,256]{3,2,1,0:T(8,128)(2,1)S(1)}, u32[]{:S(2)}, u32[]{:S(2)}) collective-permute-start(bf16[1,4,8,256]{3,2,1,0:T(8,128)(2,1)S(1)} %gbuffer.1), channel_id=1, source_target_pairs={{0,8},{8,16},{16,24},{24,0},{1,9},{9,17},{17,25},{25,1},{2,10},{10... | collective-permute-start | bytes 49160 | tf_op jit(solution)/shard_map/ppermute | solution.py:727

commit v13 on v12

--- a/solution.py
+++ b/solution.py
@@ -19,6 +19,7 @@
 TAIL = 16
 BRICK_ROWS = WINDOWS * MAIN + TAIL
 KDIM = 256
+HBM_ROWS = 640
 
 F32 = jnp.float32
 BF16 = jnp.bfloat16
@@ -100,13 +101,25 @@
 
 
 def windows_kernel(
-    where_ref, picks_ref, cube_ref, place_ref, out_ref, wide, tail, places, sums, arrival
+    where_ref, picks_ref, cube_ref, place_ref, out_ref,
+    wide, found_all, tail, places, sums, own, arrival, departures,
 ):
     tile = where_ref[0]
     own_places = pltpu.make_async_copy(place_ref.at[tile], places, arrival)
     own_places.start()
     count = cube_ref.shape[0]
     plane = EDGE * EDGE
+    copies = []
+
+    def send(source, target):
+        copy = pltpu.make_async_copy(source, target, departures.at[len(copies)])
+        copy.start()
+        copies.append(copy)
+
+    def send_rows(first, size):
+        rows = pl.ds(first, size)
+        send(found_all.at[:, rows], out_ref.at[pl.ds(0, count), rows])
+
     wide[...] = jnp.zeros_like(wide)
     wide[:, :EDGE, :plane] = cube_ref[...]
     column = lax.broadcasted_iota(jnp.int32, (1, KDIM), 1)
@@ -128,25 +141,27 @@
             preferred_element_type=F32,
         )
         found = found.reshape(count, 48, KDIM)
-        out_ref[:count, window * MAIN : (window + 1) * MAIN, :] = found[:, :MAIN, :].astype(BF16)
+        found_all[:, window * MAIN : (window + 1) * MAIN, :] = found[:, :MAIN, :].astype(BF16)
+        send_rows(window * MAIN, MAIN)
         tail[:, window : window + 1, :] = found[:, MAIN : MAIN + 1, :]
         tail[:, 8 + window : 9 + window, :] = found[:, MAIN + 1 : MAIN + 2, :]
     for row in (6, 7, 14, 15):
         tail[:, row : row + 1, :] = jnp.zeros((count, 1, KDIM), F32)
-    out_ref[:count, WINDOWS * MAIN :, :] = tail[...].astype(BF16)
+    found_all[:, WINDOWS * MAIN :, :] = tail[...].astype(BF16)
+    send_rows(WINDOWS * MAIN, TAIL)
 
     own_places.wait()
     cap = picks_ref.shape[0]
     lines = places.shape[0] // 3
     part = lines // cap
 
-    def one_slot(piece, carry):
-        brick = out_ref[picks_ref[piece, tile]]
+    for piece in range(cap):
+        brick = found_all[picks_ref[piece, tile]]
         slot_sums(brick, places, sums, piece * part, part // 2)
-        return carry
-
-    lax.fori_loop(0, cap, one_slot, 0)
-    out_ref[count, : whole_tiles(lines), :LANES] = line_values(sums, lines, whole_tiles(lines))
+    own[...] = line_values(sums, lines, own.shape[0])
+    send(own, out_ref.at[count, pl.ds(0, own.shape[0]), pl.ds(0, LANES)])
+    for copy in copies:
+        copy.wait()
 
 
 def windows_of(where, picks, bricks, places):
@@ -155,15 +170,18 @@
     rows = places.shape[1]
     return pl.pallas_call(
         windows_kernel,
-        out_shape=jax.ShapeDtypeStruct((count + 1, BRICK_ROWS, KDIM), BF16),
+        out_shape=jax.ShapeDtypeStruct((max(count + 1, HBM_ROWS), BRICK_ROWS, KDIM), BF16),
         in_specs=[smem(), smem(), vmem(), pl.BlockSpec(memory_space=pl.ANY)],
-        out_specs=vmem(),
+        out_specs=pl.BlockSpec(memory_space=pl.ANY),
         scratch_shapes=[
             pltpu.VMEM((count, 48, 10 * LANES), BF16),
+            pltpu.VMEM((count, BRICK_ROWS, KDIM), BF16),
             pltpu.VMEM((count, TAIL, KDIM), F32),
             pltpu.VMEM((rows, LANES), F32),
             pltpu.VMEM((8 * rows // 3, LANES), F32),
+            pltpu.VMEM((whole_tiles(rows // 3), LANES), BF16),
             pltpu.SemaphoreType.DMA,
+            pltpu.SemaphoreType.DMA((WINDOWS + 2,)),
         ],
         compiler_params=params(16),
         cost_estimate=pl.CostEstimate(
@@ -261,7 +279,7 @@
 
 
 def samples_kernel(
-    where_ref, picks_ref, brick_ref, place_ref, out_ref, bricks, places, sums, own, arrivals,
+    count, where_ref, picks_ref, brick_ref, place_ref, out_ref, bricks, places, sums, own, arrivals,
     own_arrival,
 ):
     owners, rows, _ = place_ref.shape
@@ -272,7 +290,7 @@
     tile = where_ref[0]
     pairs, rest = turns // 2, turns % 2
     own_values = pltpu.make_async_copy(
-        brick_ref.at[brick_ref.shape[0] - 1, pl.ds(0, own.shape[0]), pl.ds(0, LANES)],
+        brick_ref.at[count, pl.ds(0, own.shape[0]), pl.ds(0, LANES)],
         own,
         own_arrival,
     )
@@ -280,11 +298,10 @@
     def renderer_of(number):
         return lax.rem(tile + 1 + number, owners)
 
-    def fetches(turn, members):
-        held = turn % 2
+    def fetches(held, first, members):
         copies = []
         for member in range(members):
-            renderer = renderer_of(2 * turn + member)
+            renderer = renderer_of(first + member)
             copies.append(
                 pltpu.make_async_copy(
                     place_ref.at[renderer],
@@ -302,62 +319,66 @@
                 )
         return copies
 
-    def start(turn, members):
-        for copy in fetches(turn, members):
+    def pair_fetches(turn):
+        return fetches((turn + rest) % 2, rest + 2 * turn, 2)
+
+    def start(copies):
+        for copy in copies:
             copy.start()
 
-    def work(turn, members):
-        held = turn % 2
-        for copy in fetches(turn, members):
+    def blend_slot(held, member, piece):
+        slot_sums(
+            bricks[held, member, piece],
+            places.at[held, member],
+            sums.at[member],
+            piece * part,
+            part // 2,
+        )
+
+    def one_pair(turn, carry):
+        for copy in pair_fetches(turn):
             copy.wait()
-        for member in range(members):
+        for member in range(2):
             for piece in range(cap):
-                slot_sums(
-                    bricks[held, member, piece],
-                    places.at[held, member],
-                    sums.at[member],
-                    piece * part,
-                    part // 2,
-                )
-        for member in range(members):
-            out_ref[renderer_of(2 * turn + member)] = line_values(
+                blend_slot((turn + rest) % 2, member, piece)
+        for member in range(2):
+            out_ref[renderer_of(rest + 2 * turn + member)] = line_values(
                 sums.at[member], lines, lines
             )
 
-    def one_pair(turn, carry):
-        work(turn, 2)
-
         @pl.when(turn + 2 < pairs)
         def _():
-            start(turn + 2, 2)
-
-        if rest:
-
-            @pl.when(turn + 2 == pairs)
-            def _():
-                start(pairs, 1)
+            start(pair_fetches(turn + 2))
 
         return carry
 
-    for turn in range(min(2, pairs)):
-        start(turn, 2)
-    if rest and pairs < 2:
-        start(pairs, 1)
+    if rest:
+        copies = fetches(0, 0, 1)
+        start(copies)
+        copies[0].wait()
+        for piece in range(cap):
+            copies[1 + piece].wait()
+            if piece == 0 and pairs > 0:
+                start(pair_fetches(0))
+            blend_slot(0, 0, piece)
+        out_ref[renderer_of(0)] = line_values(sums.at[0], lines, lines)
+    elif pairs > 0:
+        start(pair_fetches(0))
+    if pairs > 1:
+        start(pair_fetches(1))
     own_values.start()
     lax.fori_loop(0, pairs, one_pair, 0)
-    if rest:
-        work(pairs, 1)
     own_values.wait()
     out_ref[tile] = own[...].astype(F32)[:lines].astype(BF16)
 
 
-def sample_values(where, picks, windows, places):
+def sample_values(where, picks, windows, places, count):
     owners, rows, _ = places.shape
     cap = picks.shape[0]
     samples = owners * rows * LANES // 3
     some = pl.BlockSpec(memory_space=pl.ANY)
     return pl.pallas_call(
-        samples_kernel,
+        functools.partial(samples_kernel, count),
         out_shape=jax.ShapeDtypeStruct((owners, rows // 3, LANES), BF16),
         in_specs=[smem(), smem(), some, some],
         out_specs=vmem(),
@@ -369,7 +390,7 @@
             pltpu.SemaphoreType.DMA((2, 2, cap + 1)),
             pltpu.SemaphoreType.DMA,
         ],
-        compiler_params=pltpu.CompilerParams(vmem_limit_bytes=61_600_000),
+        compiler_params=params(16),
         cost_estimate=pl.CostEstimate(
             flops=2 * samples * KDIM * BRICK_ROWS, bytes_accessed=3 * MIB,
             transcendentals=0,
@@ -712,7 +733,7 @@
     w_out = jnp.pad(w_out, ((0, 0), (0, 16 - colours), (0, 0)))
     windows = windows_of(where, picks, bricks, places)
     arrived, w_in, w_out = lax.optimization_barrier((arrived, w_in, w_out))
-    found = sample_values(where, picks, windows, arrived)
+    found = sample_values(where, picks, windows, arrived, bricks.shape[0])
 
     found, over, under, pending = lax.optimization_barrier((found, over, under, pending))
     values = lax.all_to_all(found, "tile", split_axis=0, concat_axis=0, tiled=True)

time: 47.8 us -> 48 us (level)
  Pallas kernels: 19.8 us -> 20.5 us
    unnamed x29 -> x21, local copies, waits for them, and re-layouts: 1.91 us -> 0.66 us
    reshape x1, local copies, waits for them, and re-layouts: 2.33 us -> 3.3 us  [windows_of(): cube = bricks.reshape(count, EDGE, EDGE * EDGE)]
    pallas_call x2, Pallas kernels: 11.7 us -> 12.4 us  [the longest x1 8.7 us: sample_values(): pl.pallas_call(functools.partial(samples_kernel, count), out_shape=jax.Sh...]
  transfers between devices with their start and end apart: 5 -> 5, of which waited for: 3 -> 3; matrix products, arithmetic and copies ran while one was open for 5% -> 7% of each run, Pallas kernels for 37% -> 38%
where the time goes in v13:
time: 48 us; the launch traced here: 47.6 us
  Pallas kernels  20.5 us (43%)
  starting transfers between devices  15.1 us (31%)
  waiting for transfers between devices  6.88 us (14%)
  local copies, waits for them, and re-layouts  4.03 us (8%)
  between operations  0.88 us (2%)
    pallas_call x1, Pallas kernels, sample_values(): pl.pallas_call(functools.partial(samples_kernel, count), out_shape=jax.Sh...  8.7 us
    all_to_all x1, starting transfers between devices, on_device(): lax.all_to_all(places, 'tile', split_axis=0, concat_axis=0, tiled=True)  6.34 us
    pallas_call x1, Pallas kernels, windows_of(): pl.pallas_call(windows_kernel, out_shape=jax.ShapeDtypeStruct((max(count...  3.74 us
    all_to_all x1, waiting for transfers between devices, on_device(): lax.all_to_all(places, 'tile', split_axis=0, concat_axis=0, tiled=True)  3.55 us
    all_to_all x1, starting transfers between devices, on_device(): lax.all_to_all(found, 'tile', split_axis=0, concat_axis=0, tiled=True)  3.44 us
    reshape x1, local copies, waits for them, and re-layouts, windows_of(): cube = bricks.reshape(count, EDGE, EDGE * EDGE)  3.3 us
    all_to_all x1, waiting for transfers between devices, on_device(): lax.all_to_all(found, 'tile', split_axis=0, concat_axis=0, tiled=True)  3.04 us
    pallas_call x1, Pallas kernels, decoder(): pl.pallas_call(decoder_kernel, out_shape=jax.ShapeDtypeStruct((1, colours...  2.88 us
  transfers between devices with their start and end apart: 5, of which 3 were waited for; matrix products, arithmetic and copies ran while one was open for 7% of the time, Pallas kernels for 38%

profile of v13, /device:TPU:0, one launch (start us, length us, event | category | flops | bytes accessed | tf_op | source)
XLA Modules:
  0.0 47.6 jit_solution(559607397342313296)
XLA Ops:
  0.6 2.1 %positions.1.place_ref = f32[8,120,128]{2,1,0:T(8,128)} custom-call(s32[3,320,128]{2,1,0:T(8,128)} %bitcast.18, f32[3,320,128]{2,1,0:T(8,128)} %bitcast.19), custom_call_target="tpu_custom_call" | custom-call | flops 122880 | bytes 1474560 | tf_op jit(solution)/shard_map/positions/pallas_call | solution.py:83
  2.7 6.3 %all-to-all-start = ((f32[8,120,128]{2,1,0:T(8,128)}), f32[8,120,128]{2,1,0:T(8,128)S(1)}, u32[]{:S(2)}, u32[]{:S(2)}) async-start(f32[8,120,128]{2,1,0:T(8,128)} %positions.1.place_ref), calls=%async_computation | async-start | bytes 983040 | tf_op jit(solution)/shard_map/all_to_all | solution.py:722
  9.1 0.0 copy-start.8
  9.1 0.0 copy-start.9
  9.1 0.0 copy-start.2
  9.1 2.5 %collective-permute-start = (bf16[1,4,8,256]{3,1,2,0:T(4,128)(2,1)S(1)}, bf16[1,4,8,256]{3,1,2,0:T(4,128)(2,1)S(1)}, u32[]{:S(2)}, u32[]{:S(2)}) collective-permute-start(bf16[1,4,8,256]{3,1,2,0:T(4,128)(2,1)S(1)} %copy.17), channel_id=1, source_target_pairs={{0,1},{1,2},{2,3},{3,4},{4,5},{5,6},{6,7},{8,9},{9,10},{10,11},{11... | collective-permute-start | bytes 49160 | tf_op jit(solution)/shard_map/ppermute | solution.py:726
  11.7 1.3 %collective-permute-start.1 = (bf16[1,4,8,256]{3,1,2,0:T(4,128)(2,1)S(1)}, bf16[1,4,8,256]{3,1,2,0:T(4,128)(2,1)S(1)}, u32[]{:S(2)}, u32[]{:S(2)}) collective-permute-start(bf16[1,4,8,256]{3,1,2,0:T(4,128)(2,1)S(1)} %copy.17), channel_id=1, source_target_pairs={{1,0},{2,1},{3,2},{4,3},{5,4},{6,5},{7,6},{9,8},{10,9},{11,10},{12... | collective-permute-start | bytes 49160 | tf_op jit(solution)/shard_map/ppermute | solution.py:727
  13.0 3.3 %reshape.15.cube_ref = bf16[16,34,1156]{2,1,0:T(8,128)(2,1)S(1)} reshape(bf16[16,39304]{1,0:T(8,128)(2,1)} %param.12) | data formatting | bytes 2515456 | tf_op jit(solution)/shard_map/reshape | solution.py:169
  16.3 0.1 pad_add_fusion.where_ref
  16.4 3.7 %brick_windows.1.brick_ref = bf16[640,208,256]{2,1,0:T(8,128)(2,1)} custom-call(s32[2]{0:T(128)S(1)} %pad_add_fusion.where_ref, s32[2,8]{1,0:T(2,128)S(1)} %bitcast.15, bf16[16,34,1156]{2,1,0:T(8,128)(2,1)S(1)} %reshape.15.cube_ref, f32[8,120,128]{2,1,0:T(8,128)S(1)} %copy-done), custom_call_target="tpu_custom_call" | custom-call | flops 905969664 | bytes 4194304 | tf_op jit(solution)/shard_map/brick_windows/pallas_call | solution.py:171
  20.2 3.6 %all-to-all-done.place_ref = f32[8,120,128]{2,1,0:T(8,128)S(1)} async-done(((f32[8,120,128]{2,1,0:T(8,128)}), f32[8,120,128]{2,1,0:T(8,128)S(1)}, u32[]{:S(2)}, u32[]{:S(2)}) %all-to-all-start) | async-done | bytes 491552 | tf_op jit(solution)/shard_map/all_to_all | solution.py:722
  23.7 8.7 %sample_values.1 = bf16[8,40,128]{2,1,0:T(8,128)(2,1)} custom-call(s32[2]{0:T(128)S(1)} %pad_add_fusion.where_ref, s32[2,8]{1,0:T(2,128)S(1)} %bitcast.16, bf16[640,208,256]{2,1,0:T(8,128)(2,1)} %brick_windows.1.brick_ref, f32[8,120,128]{2,1,0:T(8,128)S(1)} %all-to-all-done.place_ref), custom_call_target="tpu_custom_call" | custom-call | flops 4362076160 | bytes 3145728 | tf_op jit(solution)/shard_map/sample_values/pallas_call | solution.py:380
  32.5 3.4 %all-to-all-start.1 = ((bf16[8,40,128]{2,1,0:T(8,128)(2,1)}), bf16[8,40,128]{2,1,0:T(8,128)(2,1)S(1)}, u32[]{:S(2)}, u32[]{:S(2)}) async-start(bf16[8,40,128]{2,1,0:T(8,128)(2,1)} %sample_values.1), calls=%async_computation.1 | async-start | bytes 163840 | tf_op jit(solution)/shard_map/all_to_all | solution.py:739
  36.0 0.0 copy-start.6
  36.0 1.7 %stem.1.second = bf16[20,32,256]{2,1,0:T(8,128)(2,1)S(1)} custom-call(s32[2]{0:T(128)S(1)} %pad_add_fusion.where_ref, bf16[24,16,256]{2,1,0:T(8,128)(2,1)S(1)} %pad.14.x_ref, bf16[9,16,32]{2,1,0:T(8,128)(2,1)S(1)} %pad.12.w_in, bf16[9,32,32]{2,1,0:T(8,128)(2,1)S(1)} %copy-done.5), custom_call_target="tpu_custom_call" | custom-call | flops 1000000000 | bytes 1048576 | tf_op jit(solution)/shard_map/stem/pallas_call | solution.py:640
  37.7 0.0 copy-start.3
  37.7 0.0 copy-start.4
  37.7 1.3 %middle.1.third = bf16[8,112,128]{2,1,0:T(8,128)(2,1)S(1)} custom-call(s32[2]{0:T(128)S(1)} %pad_add_fusion.where_ref, bf16[20,32,256]{2,1,0:T(8,128)(2,1)S(1)} %stem.1.second, bf16[9,32,112]{2,1,0:T(8,128)(2,1)S(1)} %bitcast.17), custom_call_target="tpu_custom_call" | custom-call | flops 500000000 | bytes 1048576 | tf_op jit(solution)/shard_map/middle/pallas_call | solution.py:658
  39.0 3.0 %all-to-all-done.1.value_ref = bf16[8,40,128]{2,1,0:T(8,128)(2,1)S(1)} async-done(((bf16[8,40,128]{2,1,0:T(8,128)(2,1)}), bf16[8,40,128]{2,1,0:T(8,128)(2,1)S(1)}, u32[]{:S(2)}, u32[]{:S(2)}) %all-to-all-start.1) | async-done | bytes 81952 | tf_op jit(solution)/shard_map/all_to_all | solution.py:739
  42.1 0.2 gbuffer.1
  42.3 1.5 %collective-permute-start.2 = (bf16[1,4,8,256]{3,2,1,0:T(8,128)(2,1)S(1)}, bf16[1,4,8,256]{3,2,1,0:T(8,128)(2,1)S(1)}, u32[]{:S(2)}, u32[]{:S(2)}) collective-permute-start(bf16[1,4,8,256]{3,2,1,0:T(8,128)(2,1)S(1)} %gbuffer.1), channel_id=1, source_target_pairs={{0,8},{8,16},{16,24},{24,0},{1,9},{9,17},{17,25},{25,1},{2,10},{10... | collective-permute-start | bytes 49160 | tf_op jit(solution)/shard_map/ppermute | solution.py:748
  43.8 2.9 %decoder.1 = bf16[1,3,8,256]{3,2,1,0:T(8,128)(2,1)} custom-call(s32[2]{0:T(128)S(1)} %pad_add_fusion.where_ref, bf16[20,32,256]{2,1,0:T(8,128)(2,1)S(1)} %stem.1.second, bf16[8,112,128]{2,1,0:T(8,128)(2,1)S(1)} %middle.1.third, bf16[9,112,112]{2,1,0:T(8,128)(2,1)S(1)} %copy-done.3, bf16[9,32,144]{2,1,0:T(8,128)(2,1)S(1)} %copy-done.4, ...), custom_call_target="tpu_custom_call" | custom-call | flops 1500000000 | bytes 1048576 | tf_op jit(solution)/shard_map/decoder/pallas_call | solution.py:676
  46.7 0.3 collective-permute-done.2
  46.9 0.6 %copy.23 = bf16[1,4,8,256]{3,2,1,0:T(8,128)(2,1)} copy(bf16[1,4,8,256]{3,2,1,0:T(8,128)(2,1)S(1)} %collective-permute-done.2) | data formatting | bytes 32768
  (22 shorter events, 0.1 us)
Async XLA Ops:
  0.6 8.4 %copy-start.7 = (bf16[1,4,8,256]{3,2,1,0:T(8,128)(2,1)S(1)}, bf16[1,4,8,256]{3,2,1,0:T(8,128)(2,1)}, u32[]{:S(2)}) copy-start(bf16[1,4,8,256]{3,2,1,0:T(8,128)(2,1)} %param.17) | copy-start | bytes 49156
  2.7 21.0 %all-to-all-start = ((f32[8,120,128]{2,1,0:T(8,128)}), f32[8,120,128]{2,1,0:T(8,128)S(1)}, u32[]{:S(2)}, u32[]{:S(2)}) async-start(f32[8,120,128]{2,1,0:T(8,128)} %positions.1.place_ref), calls=%async_computation | async-start | bytes 983040 | tf_op jit(solution)/shard_map/all_to_all | solution.py:722
  9.1 7.2 %copy-start.8 = (bf16[9,32,4]{1,2,0:T(4,128)(2,1)S(1)}, bf16[9,32,4]{1,2,0:T(4,128)(2,1)}, u32[]{:S(2)}) copy-start(bf16[9,32,4]{1,2,0:T(4,128)(2,1)} %param.18) | copy-start | bytes 6916
  9.1 7.2 %copy-start.9 = (bf16[9,3,32]{2,1,0:T(4,128)(2,1)S(1)}, bf16[9,3,32]{2,1,0:T(4,128)(2,1)}, u32[]{:S(2)}) copy-start(bf16[9,3,32]{2,1,0:T(4,128)(2,1)} %param.23) | copy-start | bytes 5188
  9.1 7.3 %copy-start = (f32[8,120,128]{2,1,0:T(8,128)S(1)}, f32[8,120,128]{2,1,0:T(8,128)}, u32[]{:S(2)}) copy-start(f32[8,120,128]{2,1,0:T(8,128)} %positions.1.place_ref) | copy-start | bytes 1474564
  9.1 7.3 %copy-start.2 = (s32[1,1,8,2]{2,3,1,0:T(2,128)S(1)}, s32[1,1,8,2]{2,3,1,0:T(2,128)}, u32[]{:S(2)}) copy-start(s32[1,1,8,2]{2,3,1,0:T(2,128)} %param.13) | copy-start | bytes 196
  9.1 23.3 %collective-permute-start = (bf16[1,4,8,256]{3,1,2,0:T(4,128)(2,1)S(1)}, bf16[1,4,8,256]{3,1,2,0:T(4,128)(2,1)S(1)}, u32[]{:S(2)}, u32[]{:S(2)}) collective-permute-start(bf16[1,4,8,256]{3,1,2,0:T(4,128)(2,1)S(1)} %copy.17), channel_id=1, source_target_pairs={{0,1},{1,2},{2,3},{3,4},{4,5},{5,6},{6,7},{8,9},{9,10},{10,11},{11... | collective-permute-start | bytes 49160 | tf_op jit(solution)/shard_map/ppermute | solution.py:726
  11.7 20.8 %collective-permute-start.1 = (bf16[1,4,8,256]{3,1,2,0:T(4,128)(2,1)S(1)}, bf16[1,4,8,256]{3,1,2,0:T(4,128)(2,1)S(1)}, u32[]{:S(2)}, u32[]{:S(2)}) collective-permute-start(bf16[1,4,8,256]{3,1,2,0:T(4,128)(2,1)S(1)} %copy.17), channel_id=1, source_target_pairs={{1,0},{2,1},{3,2},{4,3},{5,4},{6,5},{7,6},{9,8},{10,9},{11,10},{12... | collective-permute-start | bytes 49160 | tf_op jit(solution)/shard_map/ppermute | solution.py:727
  20.2 15.8 %copy-start.5 = (bf16[9,32,32]{2,1,0:T(8,128)(2,1)S(1)}, bf16[9,32,32]{2,1,0:T(8,128)(2,1)}, u32[]{:S(2)}) copy-start(bf16[9,32,32]{2,1,0:T(8,128)(2,1)} %w_mid.1) | copy-start | bytes 55300
  32.5 9.6 %all-to-all-start.1 = ((bf16[8,40,128]{2,1,0:T(8,128)(2,1)}), bf16[8,40,128]{2,1,0:T(8,128)(2,1)S(1)}, u32[]{:S(2)}, u32[]{:S(2)}) async-start(bf16[8,40,128]{2,1,0:T(8,128)(2,1)} %sample_values.1), calls=%async_computation.1 | async-start | bytes 163840 | tf_op jit(solution)/shard_map/all_to_all | solution.py:739
  36.0 1.7 %copy-start.6 = (bf16[9,112,32]{1,2,0:T(8,128)(2,1)S(1)}, bf16[9,112,32]{1,2,0:T(8,128)(2,1)}, u32[]{:S(2)}) copy-start(bf16[9,112,32]{1,2,0:T(8,128)(2,1)} %param.20) | copy-start | bytes 193540
  37.7 4.4 %copy-start.1 = (s32[1,1,160,256]{3,2,1,0:T(8,128)S(1)}, s32[1,1,160,256]{3,2,1,0:T(8,128)}, u32[]{:S(2)}) copy-start(s32[1,1,160,256]{3,2,1,0:T(8,128)} %order_ref.1) | copy-start | bytes 491524
  37.7 6.1 %copy-start.3 = (bf16[9,112,112]{2,1,0:T(8,128)(2,1)S(1)}, bf16[9,112,112]{2,1,0:T(8,128)(2,1)}, u32[]{:S(2)}) copy-start(bf16[9,112,112]{2,1,0:T(8,128)(2,1)} %w_deep.1) | copy-start | bytes 677380
  37.7 6.1 %copy-start.4 = (bf16[9,32,144]{2,1,0:T(8,128)(2,1)S(1)}, bf16[9,32,144]{2,1,0:T(8,128)(2,1)}, u32[]{:S(2)}) copy-start(bf16[9,32,144]{2,1,0:T(8,128)(2,1)} %w_up.1) | copy-start | bytes 248836
  42.3 4.7 %collective-permute-start.2 = (bf16[1,4,8,256]{3,2,1,0:T(8,128)(2,1)S(1)}, bf16[1,4,8,256]{3,2,1,0:T(8,128)(2,1)S(1)}, u32[]{:S(2)}, u32[]{:S(2)}) collective-permute-start(bf16[1,4,8,256]{3,2,1,0:T(8,128)(2,1)S(1)} %gbuffer.1), channel_id=1, source_target_pairs={{0,8},{8,16},{16,24},{24,0},{1,9},{9,17},{17,25},{25,1},{2,10},{10... | collective-permute-start | bytes 49160 | tf_op jit(solution)/shard_map/ppermute | solution.py:748

commit v14 on v12

--- a/solution.py
+++ b/solution.py
@@ -88,8 +88,8 @@
             pltpu.VMEM(cells.shape, jnp.int32),
             pltpu.VMEM(fracs.shape, F32),
             pltpu.VMEM(shape, F32),
-            pltpu.SemaphoreType.DMA((3, 2, 2)),
-            pltpu.SemaphoreType.DMA((3, 2)),
+            pltpu.SemaphoreType.DMA((3, 4, 2)),
+            pltpu.SemaphoreType.DMA((3, 4)),
         ],
         compiler_params=params(60),
         cost_estimate=pl.CostEstimate(
@@ -140,12 +140,9 @@
     lines = places.shape[0] // 3
     part = lines // cap
 
-    def one_slot(piece, carry):
+    for piece in range(cap):
         brick = out_ref[picks_ref[piece, tile]]
         slot_sums(brick, places, sums, piece * part, part // 2)
-        return carry
-
-    lax.fori_loop(0, cap, one_slot, 0)
     out_ref[count, : whole_tiles(lines), :LANES] = line_values(sums, lines, whole_tiles(lines))
 
 
@@ -204,9 +201,8 @@
         parts += [share * part for part in weight_y]
     tail = [weight_x * hat(MAIN - py), weight_x * jnp.maximum(py - MAIN, 0.0)]
     parts.append(jnp.concatenate(tail, axis=0).astype(BF16))
-    parts.append(nothing)
     plane = jnp.concatenate(parts, axis=0)
-    found = jnp.dot(brick, plane, preferred_element_type=F32)
+    found = jnp.dot(brick[:, : plane.shape[0]], plane, preferred_element_type=F32)
     groups = range(0, MAIN, 8)
     chosen = [found[row : row + 8] for row in groups]
     for other in range(1, WINDOWS):
@@ -700,10 +696,12 @@
     places, bricks, pending = lax.optimization_barrier((places, bricks, pending))
     arrived = lax.all_to_all(places, "tile", split_axis=0, concat_axis=0, tiled=True)
 
-    down = [(i, i + 1) for i in range(n_tile - 1)]
-    up = [(i + 1, i) for i in range(n_tile - 1)]
-    over = lax.ppermute(pending, "tile", down)
-    under = lax.ppermute(pending, "tile", up)
+    mates = [(i, i ^ 1) for i in range(n_tile) if i ^ 1 < n_tile]
+    across_chips = [
+        pair for i in range(1, n_tile - 1, 2) for pair in ((i, i + 1), (i + 1, i))
+    ]
+    near = lax.ppermute(pending, "tile", mates)
+    far = lax.ppermute(pending, "tile", across_chips)
     where = jnp.stack([tile, jnp.int32(n_tile)]).astype(jnp.int32)
     picks = sends[0, 0].T
     colours = w_out.shape[1]
@@ -714,8 +712,11 @@
     arrived, w_in, w_out = lax.optimization_barrier((arrived, w_in, w_out))
     found = sample_values(where, picks, windows, arrived)
 
-    found, over, under, pending = lax.optimization_barrier((found, over, under, pending))
+    found, near, far, pending = lax.optimization_barrier((found, near, far, pending))
     values = lax.all_to_all(found, "tile", split_axis=0, concat_axis=0, tiled=True)
+    first_core = tile % 2 == 0
+    over = jnp.where(first_core, far, near)
+    under = jnp.where(first_core, near, far)
     field = jnp.concatenate([over[0], pending[0], under[0]], axis=1).transpose(1, 0, 2)
     field = jnp.pad(field, ((0, 0), (0, 16 - field.shape[1]), (0, 0)))
     second = stem(where, field, w_in, w_mid)

time: 47.8 us -> 47.8 us (level)
  waiting for transfers between devices: 7.15 us -> 9.84 us
  starting transfers between devices: 15.1 us -> 12.5 us
    all_to_all x1, waiting for transfers between devices: 3.91 us -> 6.64 us  [on_device(): lax.all_to_all(places, 'tile', split_axis=0, concat_axis=0, tiled=True)]
    ppermute x2, starting transfers between devices: 3.82 us -> 1.2 us  [the longest x1 0.65 us: on_device(): far = lax.ppermute(pending, 'tile', across_chips)]
where the time goes in v14:
time: 47.8 us; the launch traced here: 47.4 us
  Pallas kernels  19.8 us (41%)
  starting transfers between devices  12.5 us (26%)
  waiting for transfers between devices  9.84 us (21%)
  local copies, waits for them, and re-layouts  4.29 us (9%)
  between operations  0.92 us (2%)
    pallas_call x1, Pallas kernels, sample_values(): pl.pallas_call(samples_kernel, out_shape=jax.ShapeDtypeStruct((owners, ro...  8.48 us
    all_to_all x1, waiting for transfers between devices, on_device(): lax.all_to_all(places, 'tile', split_axis=0, concat_axis=0, tiled=True)  6.64 us
    all_to_all x1, starting transfers between devices, on_device(): lax.all_to_all(places, 'tile', split_axis=0, concat_axis=0, tiled=True)  6.34 us
    all_to_all x1, starting transfers between devices, on_device(): lax.all_to_all(found, 'tile', split_axis=0, concat_axis=0, tiled=True)  3.37 us
    pallas_call x1, Pallas kernels, windows_of(): pl.pallas_call(windows_kernel, out_shape=jax.ShapeDtypeStruct((count + 1,...  3.08 us
    all_to_all x1, waiting for transfers between devices, on_device(): lax.all_to_all(found, 'tile', split_axis=0, concat_axis=0, tiled=True)  2.93 us
    pallas_call x1, Pallas kernels, decoder(): pl.pallas_call(decoder_kernel, out_shape=jax.ShapeDtypeStruct((1, colours...  2.87 us
    reshape x1, local copies, waits for them, and re-layouts, windows_of(): cube = bricks.reshape(count, EDGE, EDGE * EDGE)  2.33 us
  transfers between devices with their start and end apart: 5, of which 3 were waited for; matrix products, arithmetic and copies ran while one was open for 5% of the time, Pallas kernels for 37%

profile of v14, /device:TPU:0, one launch (start us, length us, event | category | flops | bytes accessed | tf_op | source)
XLA Modules:
  0.0 47.4 jit_solution(17561687163671204996)
XLA Ops:
  0.7 2.2 %positions.1.place_ref = f32[8,120,128]{2,1,0:T(8,128)} custom-call(s32[3,320,128]{2,1,0:T(8,128)} %bitcast.19, f32[3,320,128]{2,1,0:T(8,128)} %bitcast.20), custom_call_target="tpu_custom_call" | custom-call | flops 122880 | bytes 1474560 | tf_op jit(solution)/shard_map/positions/pallas_call | solution.py:82
  2.9 6.3 %all-to-all-start = ((f32[8,120,128]{2,1,0:T(8,128)}), f32[8,120,128]{2,1,0:T(8,128)}, u32[]{:S(2)}, u32[]{:S(2)}) async-start(f32[8,120,128]{2,1,0:T(8,128)} %positions.1.place_ref), calls=%async_computation | async-start | bytes 983040 | tf_op jit(solution)/shard_map/all_to_all | solution.py:697
  9.2 0.0 copy-start.12
  9.2 0.0 copy-start.13
  9.2 0.0 copy-start.3
  9.3 0.6 %collective-permute-start = (bf16[1,4,8,256]{3,1,2,0:T(4,128)(2,1)S(1)}, bf16[1,4,8,256]{3,1,2,0:T(4,128)(2,1)S(1)}, u32[]{:S(2)}, u32[]{:S(2)}) collective-permute-start(bf16[1,4,8,256]{3,1,2,0:T(4,128)(2,1)S(1)} %copy.17), channel_id=1, source_target_pairs={{0,1},{1,0},{2,3},{3,2},{4,5},{5,4},{6,7},{7,6},{8,9},{9,8},{10,11... | collective-permute-start | bytes 49160 | tf_op jit(solution)/shard_map/ppermute | solution.py:703
  9.8 0.7 %collective-permute-start.1 = (bf16[1,4,8,256]{3,1,2,0:T(4,128)(2,1)S(1)}, bf16[1,4,8,256]{3,1,2,0:T(4,128)(2,1)S(1)}, u32[]{:S(2)}, u32[]{:S(2)}) collective-permute-start(bf16[1,4,8,256]{3,1,2,0:T(4,128)(2,1)S(1)} %copy.17), channel_id=1, source_target_pairs={{1,2},{2,1},{3,4},{4,3},{5,6},{6,5},{9,10},{10,9},{11,12},{12,11},... | collective-permute-start | bytes 49160 | tf_op jit(solution)/shard_map/ppermute | solution.py:704
  10.5 2.3 %reshape.15.cube_ref = bf16[16,34,1156]{2,1,0:T(8,128)(2,1)S(1)} reshape(bf16[16,39304]{1,0:T(8,128)(2,1)S(1)} %copy-done.10) | data formatting | bytes 2515456 | tf_op jit(solution)/shard_map/reshape | solution.py:151
  12.9 0.1 pad_add_fusion.where_ref
  13.0 3.1 %brick_windows.1.brick_ref = bf16[17,208,256]{2,1,0:T(8,128)(2,1)S(1)} custom-call(s32[2]{0:T(128)S(1)} %pad_add_fusion.where_ref, s32[2,8]{1,0:T(2,128)S(1)} %bitcast.17, bf16[16,34,1156]{2,1,0:T(8,128)(2,1)S(1)} %reshape.15.cube_ref, f32[8,120,128]{2,1,0:T(8,128)S(1)} %copy-done), custom_call_target="tpu_custom_call" | custom-call | flops 905969664 | bytes 4194304 | tf_op jit(solution)/shard_map/brick_windows/pallas_call | solution.py:153
  16.1 1.2 %copy-done.1 = bf16[17,208,256]{2,1,0:T(8,128)(2,1)} copy-done((bf16[17,208,256]{2,1,0:T(8,128)(2,1)}, bf16[17,208,256]{2,1,0:T(8,128)(2,1)S(1)}, u32[]{:S(2)}) %copy-start.1) | copy-done | bytes 1810456
  17.3 6.6 %all-to-all-done.place_ref = f32[8,120,128]{2,1,0:T(8,128)} async-done(((f32[8,120,128]{2,1,0:T(8,128)}), f32[8,120,128]{2,1,0:T(8,128)}, u32[]{:S(2)}, u32[]{:S(2)}) %all-to-all-start) | async-done | bytes 491552 | tf_op jit(solution)/shard_map/all_to_all | solution.py:697
  24.0 8.5 %sample_values.1 = bf16[8,40,128]{2,1,0:T(8,128)(2,1)} custom-call(s32[2]{0:T(128)} %copy-done.4, s32[2,8]{1,0:T(2,128)} %bitcast.16, bf16[17,208,256]{2,1,0:T(8,128)(2,1)} %copy-done.1, f32[8,120,128]{2,1,0:T(8,128)} %all-to-all-done.place_ref), custom_call_target="tpu_custom_call" | custom-call | flops 4362076160 | bytes 3145728 | tf_op jit(solution)/shard_map/sample_values/pallas_call | solution.py:355
  32.5 3.4 %all-to-all-start.1 = ((bf16[8,40,128]{2,1,0:T(8,128)(2,1)}), bf16[8,40,128]{2,1,0:T(8,128)(2,1)S(1)}, u32[]{:S(2)}, u32[]{:S(2)}) async-start(bf16[8,40,128]{2,1,0:T(8,128)(2,1)} %sample_values.1), calls=%async_computation.1 | async-start | bytes 163840 | tf_op jit(solution)/shard_map/all_to_all | solution.py:716
  36.0 1.7 %stem.1.second = bf16[20,32,256]{2,1,0:T(8,128)(2,1)S(1)} custom-call(s32[2]{0:T(128)S(1)} %copy-done.5, bf16[24,16,256]{2,1,0:T(8,128)(2,1)S(1)} %pad.14.x_ref, bf16[9,16,32]{2,1,0:T(8,128)(2,1)S(1)} %pad.12.w_in, bf16[9,32,32]{2,1,0:T(8,128)(2,1)S(1)} %copy-done.8), custom_call_target="tpu_custom_call" | custom-call | flops 1000000000 | bytes 1048576 | tf_op jit(solution)/shard_map/stem/pallas_call | solution.py:615
  37.7 0.0 copy-start.2
  37.7 0.0 copy-start.6
  37.7 1.3 %middle.1.third = bf16[8,112,128]{2,1,0:T(8,128)(2,1)S(1)} custom-call(s32[2]{0:T(128)S(1)} %copy-done.5, bf16[20,32,256]{2,1,0:T(8,128)(2,1)S(1)} %stem.1.second, bf16[9,32,112]{2,1,0:T(8,128)(2,1)S(1)} %bitcast.18), custom_call_target="tpu_custom_call" | custom-call | flops 500000000 | bytes 1048576 | tf_op jit(solution)/shard_map/middle/pallas_call | solution.py:633
  39.0 2.9 %all-to-all-done.1.value_ref = bf16[8,40,128]{2,1,0:T(8,128)(2,1)S(1)} async-done(((bf16[8,40,128]{2,1,0:T(8,128)(2,1)}), bf16[8,40,128]{2,1,0:T(8,128)(2,1)S(1)}, u32[]{:S(2)}, u32[]{:S(2)}) %all-to-all-start.1) | async-done | bytes 81952 | tf_op jit(solution)/shard_map/all_to_all | solution.py:716
  41.9 0.2 gbuffer.1
  42.1 1.5 %collective-permute-start.2 = (bf16[1,4,8,256]{3,2,1,0:T(8,128)(2,1)S(1)}, bf16[1,4,8,256]{3,2,1,0:T(8,128)(2,1)S(1)}, u32[]{:S(2)}, u32[]{:S(2)}) collective-permute-start(bf16[1,4,8,256]{3,2,1,0:T(8,128)(2,1)S(1)} %gbuffer.1), channel_id=1, source_target_pairs={{0,8},{8,16},{16,24},{24,0},{1,9},{9,17},{17,25},{25,1},{2,10},{10... | collective-permute-start | bytes 49160 | tf_op jit(solution)/shard_map/ppermute | solution.py:728
  43.7 2.9 %decoder.1 = bf16[1,3,8,256]{3,2,1,0:T(8,128)(2,1)} custom-call(s32[2]{0:T(128)S(1)} %copy-done.5, bf16[20,32,256]{2,1,0:T(8,128)(2,1)S(1)} %stem.1.second, bf16[8,112,128]{2,1,0:T(8,128)(2,1)S(1)} %middle.1.third, bf16[9,112,112]{2,1,0:T(8,128)(2,1)S(1)} %copy-done.6, bf16[9,32,144]{2,1,0:T(8,128)(2,1)S(1)} %copy-done.7, bf16[9,16,32]{2,1,0:T(8,128)(2,1)S(1)} %pad.13.w_out), custom_call_target="tpu_custom_call" | custom-call | flops 1500000000 | bytes 1048576 | tf_op jit(solution)/shard_map/decoder/pallas_call | solution.py:651
  46.5 0.3 collective-permute-done.2
  46.8 0.6 %copy.22 = bf16[1,4,8,256]{3,2,1,0:T(8,128)(2,1)} copy(bf16[1,4,8,256]{3,2,1,0:T(8,128)(2,1)S(1)} %collective-permute-done.2) | data formatting | bytes 32768
  (30 shorter events, 0.2 us)
Async XLA Ops:
  0.6 9.9 %copy-start.10 = (bf16[16,39304]{1,0:T(8,128)(2,1)S(1)}, bf16[16,39304]{1,0:T(8,128)(2,1)}, u32[]{:S(2)}) copy-start(bf16[16,39304]{1,0:T(8,128)(2,1)} %param.12) | copy-start | bytes 3773188
  0.6 8.6 %copy-start.11 = (bf16[1,4,8,256]{3,2,1,0:T(8,128)(2,1)S(1)}, bf16[1,4,8,256]{3,2,1,0:T(8,128)(2,1)}, u32[]{:S(2)}) copy-start(bf16[1,4,8,256]{3,2,1,0:T(8,128)(2,1)} %param.17) | copy-start | bytes 49156
  2.9 21.1 %all-to-all-start = ((f32[8,120,128]{2,1,0:T(8,128)}), f32[8,120,128]{2,1,0:T(8,128)}, u32[]{:S(2)}, u32[]{:S(2)}) async-start(f32[8,120,128]{2,1,0:T(8,128)} %positions.1.place_ref), calls=%async_computation | async-start | bytes 983040 | tf_op jit(solution)/shard_map/all_to_all | solution.py:697
  9.2 3.6 %copy-start.12 = (bf16[9,32,4]{1,2,0:T(4,128)(2,1)S(1)}, bf16[9,32,4]{1,2,0:T(4,128)(2,1)}, u32[]{:S(2)}) copy-start(bf16[9,32,4]{1,2,0:T(4,128)(2,1)} %param.18) | copy-start | bytes 6916
  9.2 3.7 %copy-start.13 = (bf16[9,3,32]{2,1,0:T(4,128)(2,1)S(1)}, bf16[9,3,32]{2,1,0:T(4,128)(2,1)}, u32[]{:S(2)}) copy-start(bf16[9,3,32]{2,1,0:T(4,128)(2,1)} %param.23) | copy-start | bytes 5188
  9.2 3.7 %copy-start = (f32[8,120,128]{2,1,0:T(8,128)S(1)}, f32[8,120,128]{2,1,0:T(8,128)}, u32[]{:S(2)}) copy-start(f32[8,120,128]{2,1,0:T(8,128)} %positions.1.place_ref) | copy-start | bytes 1474564
  9.2 3.7 %copy-start.3 = (s32[1,1,8,2]{2,3,1,0:T(2,128)S(1)}, s32[1,1,8,2]{2,3,1,0:T(2,128)}, u32[]{:S(2)}) copy-start(s32[1,1,8,2]{2,3,1,0:T(2,128)} %param.13) | copy-start | bytes 196
  9.3 23.2 %collective-permute-start = (bf16[1,4,8,256]{3,1,2,0:T(4,128)(2,1)S(1)}, bf16[1,4,8,256]{3,1,2,0:T(4,128)(2,1)S(1)}, u32[]{:S(2)}, u32[]{:S(2)}) collective-permute-start(bf16[1,4,8,256]{3,1,2,0:T(4,128)(2,1)S(1)} %copy.17), channel_id=1, source_target_pairs={{0,1},{1,0},{2,3},{3,2},{4,5},{5,4},{6,7},{7,6},{8,9},{9,8},{10,11... | collective-permute-start | bytes 49160 | tf_op jit(solution)/shard_map/ppermute | solution.py:703
  9.8 22.6 %collective-permute-start.1 = (bf16[1,4,8,256]{3,1,2,0:T(4,128)(2,1)S(1)}, bf16[1,4,8,256]{3,1,2,0:T(4,128)(2,1)S(1)}, u32[]{:S(2)}, u32[]{:S(2)}) collective-permute-start(bf16[1,4,8,256]{3,1,2,0:T(4,128)(2,1)S(1)} %copy.17), channel_id=1, source_target_pairs={{1,2},{2,1},{3,4},{4,3},{5,6},{6,5},{9,10},{10,9},{11,12},{12,11},... | collective-permute-start | bytes 49160 | tf_op jit(solution)/shard_map/ppermute | solution.py:704
  13.0 3.1 %copy-start.4 = (s32[2]{0:T(128)}, s32[2]{0:T(128)S(1)}, u32[]{:S(2)}) copy-start(s32[2]{0:T(128)S(1)} %pad_add_fusion.where_ref) | copy-start | bytes 28
  16.1 1.2 %copy-start.1 = (bf16[17,208,256]{2,1,0:T(8,128)(2,1)}, bf16[17,208,256]{2,1,0:T(8,128)(2,1)S(1)}, u32[]{:S(2)}) copy-start(bf16[17,208,256]{2,1,0:T(8,128)(2,1)S(1)} %brick_windows.1.brick_ref) | copy-start | bytes 5431300
  17.3 18.6 %copy-start.8 = (bf16[9,32,32]{2,1,0:T(8,128)(2,1)S(1)}, bf16[9,32,32]{2,1,0:T(8,128)(2,1)}, u32[]{:S(2)}) copy-start(bf16[9,32,32]{2,1,0:T(8,128)(2,1)} %w_mid.1) | copy-start | bytes 55300
  24.0 12.0 %copy-start.5 = (s32[2]{0:T(128)S(1)}, s32[2]{0:T(128)}, u32[]{:S(2)}) copy-start(s32[2]{0:T(128)} %copy-done.4) | copy-start | bytes 28
  32.5 9.4 %all-to-all-start.1 = ((bf16[8,40,128]{2,1,0:T(8,128)(2,1)}), bf16[8,40,128]{2,1,0:T(8,128)(2,1)S(1)}, u32[]{:S(2)}, u32[]{:S(2)}) async-start(bf16[8,40,128]{2,1,0:T(8,128)(2,1)} %sample_values.1), calls=%async_computation.1 | async-start | bytes 163840 | tf_op jit(solution)/shard_map/all_to_all | solution.py:716
  36.0 1.7 %copy-start.9 = (bf16[9,112,32]{1,2,0:T(8,128)(2,1)S(1)}, bf16[9,112,32]{1,2,0:T(8,128)(2,1)}, u32[]{:S(2)}) copy-start(bf16[9,112,32]{1,2,0:T(8,128)(2,1)} %param.20) | copy-start | bytes 193540
  37.7 4.2 %copy-start.2 = (s32[1,1,160,256]{3,2,1,0:T(8,128)S(1)}, s32[1,1,160,256]{3,2,1,0:T(8,128)}, u32[]{:S(2)}) copy-start(s32[1,1,160,256]{3,2,1,0:T(8,128)} %order_ref.1) | copy-start | bytes 491524
  37.7 6.0 %copy-start.6 = (bf16[9,112,112]{2,1,0:T(8,128)(2,1)S(1)}, bf16[9,112,112]{2,1,0:T(8,128)(2,1)}, u32[]{:S(2)}) copy-start(bf16[9,112,112]{2,1,0:T(8,128)(2,1)} %w_deep.1) | copy-start | bytes 677380
  37.7 6.0 %copy-start.7 = (bf16[9,32,144]{2,1,0:T(8,128)(2,1)S(1)}, bf16[9,32,144]{2,1,0:T(8,128)(2,1)}, u32[]{:S(2)}) copy-start(bf16[9,32,144]{2,1,0:T(8,128)(2,1)} %w_up.1) | copy-start | bytes 248836
  42.1 4.7 %collective-permute-start.2 = (bf16[1,4,8,256]{3,2,1,0:T(8,128)(2,1)S(1)}, bf16[1,4,8,256]{3,2,1,0:T(8,128)(2,1)S(1)}, u32[]{:S(2)}, u32[]{:S(2)}) collective-permute-start(bf16[1,4,8,256]{3,2,1,0:T(8,128)(2,1)S(1)} %gbuffer.1), channel_id=1, source_target_pairs={{0,8},{8,16},{16,24},{24,0},{1,9},{9,17},{17,25},{25,1},{2,10},{10... | collective-permute-start | bytes 49160 | tf_op jit(solution)/shard_map/ppermute | solution.py:728

commit v15 on v14

--- a/solution.py
+++ b/solution.py
@@ -37,7 +37,10 @@
     return pl.BlockSpec(memory_space=pltpu.SMEM)
 
 
-def positions_kernel(cells_ref, fracs_ref, out_ref, cells, fracs, found, arrivals, departures):
+def positions_kernel(
+    where_ref, cells_ref, fracs_ref, out_ref, mate_ref,
+    cells, fracs, found, arrivals, departures, mate_departure,
+):
     owners, rows, _ = out_ref.shape
     lines = rows // 3
     parts = arrivals.shape[1]
@@ -71,40 +74,59 @@
             place.reshape(share, lines, LANES)
         )
         write(axis, part).start()
+    for_mate = pltpu.make_async_copy(
+        found.at[mate_of(where_ref[0])], mate_ref.at[0], mate_departure
+    )
+    for_mate.start()
     for piece in pieces:
         write(*piece).wait()
-
-
-def positions(cells, fracs, owners):
+    for_mate.wait()
+
+
+def mate_of(tile):
+    return tile + 1 - 2 * lax.rem(tile, 2)
+
+
+def positions(where, cells, fracs, owners):
     lines = cells.shape[1]
     shape = (owners, 3 * lines // owners, LANES)
     hbm = pl.BlockSpec(memory_space=pltpu.HBM)
     return pl.pallas_call(
         positions_kernel,
-        out_shape=jax.ShapeDtypeStruct(shape, F32),
-        in_specs=[hbm, hbm],
-        out_specs=hbm,
+        out_shape=(
+            jax.ShapeDtypeStruct(shape, F32),
+            jax.ShapeDtypeStruct((1,) + shape[1:], F32),
+        ),
+        in_specs=[smem(), hbm, hbm],
+        out_specs=(hbm, hbm),
         scratch_shapes=[
             pltpu.VMEM(cells.shape, jnp.int32),
             pltpu.VMEM(fracs.shape, F32),
             pltpu.VMEM(shape, F32),
             pltpu.SemaphoreType.DMA((3, 4, 2)),
             pltpu.SemaphoreType.DMA((3, 4)),
+            pltpu.SemaphoreType.DMA,
         ],
         compiler_params=params(60),
         cost_estimate=pl.CostEstimate(
             flops=3 * lines * LANES, bytes_accessed=36 * lines * LANES, transcendentals=0
         ),
         name="positions",
-    )(cells, fracs)
+    )(where, cells, fracs)
 
 
 def windows_kernel(
-    where_ref, picks_ref, cube_ref, place_ref, out_ref, wide, tail, places, sums, arrival
+    where_ref, picks_ref, cube_ref, place_ref, mate_place_ref, out_ref,
+    wide, tail, places, sums, arrivals,
 ):
     tile = where_ref[0]
-    own_places = pltpu.make_async_copy(place_ref.at[tile], places, arrival)
-    own_places.start()
+    near = ((tile, place_ref.at[tile]), (mate_of(tile), mate_place_ref.at[0]))
+    copies = [
+        pltpu.make_async_copy(source, places.at[i], arrivals.at[i])
+        for i, (_, source) in enumerate(near)
+    ]
+    for copy in copies:
+        copy.start()
     count = cube_ref.shape[0]
     plane = EDGE * EDGE
     wide[...] = jnp.zeros_like(wide)
@@ -135,32 +157,37 @@
         tail[:, row : row + 1, :] = jnp.zeros((count, 1, KDIM), F32)
     out_ref[:count, WINDOWS * MAIN :, :] = tail[...].astype(BF16)
 
-    own_places.wait()
+    for copy in copies:
+        copy.wait()
     cap = picks_ref.shape[0]
-    lines = places.shape[0] // 3
+    lines = places.shape[1] // 3
     part = lines // cap
-
-    for piece in range(cap):
-        brick = out_ref[picks_ref[piece, tile]]
-        slot_sums(brick, places, sums, piece * part, part // 2)
-    out_ref[count, : whole_tiles(lines), :LANES] = line_values(sums, lines, whole_tiles(lines))
-
-
-def windows_of(where, picks, bricks, places):
+    height = whole_tiles(lines)
+    for i, (renderer, _) in enumerate(near):
+        for piece in range(cap):
+            brick = out_ref[picks_ref[piece, renderer]]
+            slot_sums(brick, places.at[i], sums.at[i], piece * part, part // 2)
+    for i in range(len(near)):
+        out_ref[count, i * height : (i + 1) * height, :LANES] = line_values(
+            sums.at[i], lines, height
+        )
+
+
+def windows_of(where, picks, bricks, places, mate_places):
     count = bricks.shape[0]
     cube = bricks.reshape(count, EDGE, EDGE * EDGE)
     rows = places.shape[1]
     return pl.pallas_call(
         windows_kernel,
         out_shape=jax.ShapeDtypeStruct((count + 1, BRICK_ROWS, KDIM), BF16),
-        in_specs=[smem(), smem(), vmem(), pl.BlockSpec(memory_space=pl.ANY)],
+        in_specs=[smem(), smem(), vmem()] + [pl.BlockSpec(memory_space=pl.ANY)] * 2,
         out_specs=vmem(),
         scratch_shapes=[
             pltpu.VMEM((count, 48, 10 * LANES), BF16),
             pltpu.VMEM((count, TAIL, KDIM), F32),
-            pltpu.VMEM((rows, LANES), F32),
-            pltpu.VMEM((8 * rows // 3, LANES), F32),
-            pltpu.SemaphoreType.DMA,
+            pltpu.VMEM((2, rows, LANES), F32),
+            pltpu.VMEM((2, 8 * rows // 3, LANES), F32),
+            pltpu.SemaphoreType.DMA((2,)),
         ],
         compiler_params=params(16),
         cost_estimate=pl.CostEstimate(
@@ -168,7 +195,7 @@
             transcendentals=0,
         ),
         name="brick_windows",
-    )(where, picks, cube, places)
+    )(where, picks, cube, places, mate_places)
 
 
 def hat(distance):
@@ -264,7 +291,7 @@
     cap = picks_ref.shape[0]
     lines = rows // 3
     part = lines // cap
-    turns = owners - 1
+    turns = owners - 2
     tile = where_ref[0]
     pairs, rest = turns // 2, turns % 2
     own_values = pltpu.make_async_copy(
@@ -274,7 +301,7 @@
     )
 
     def renderer_of(number):
-        return lax.rem(tile + 1 + number, owners)
+        return lax.rem(2 * (tile // 2) + 2 + number, owners)
 
     def fetches(turn, members):
         held = turn % 2
@@ -344,7 +371,10 @@
     if rest:
         work(pairs, 1)
     own_values.wait()
-    out_ref[tile] = own[...].astype(F32)[:lines].astype(BF16)
+    height = whole_tiles(lines)
+    for i, renderer in enumerate((tile, mate_of(tile))):
+        values = own[i * height : (i + 1) * height, :].astype(F32)
+        out_ref[renderer] = values[:lines].astype(BF16)
 
 
 def sample_values(where, picks, windows, places):
@@ -361,7 +391,7 @@
             pltpu.VMEM((2, 2, cap, BRICK_ROWS, KDIM), BF16),
             pltpu.VMEM((2, 2, rows, LANES), F32),
             pltpu.VMEM((2, 8 * rows // 3, LANES), F32),
-            pltpu.VMEM((whole_tiles(rows // 3), LANES), BF16),
+            pltpu.VMEM((2 * whole_tiles(rows // 3), LANES), BF16),
             pltpu.SemaphoreType.DMA((2, 2, cap + 1)),
             pltpu.SemaphoreType.DMA,
         ],
@@ -374,8 +404,20 @@
     )(where, picks, windows, places)
 
 
-def gbuffer_kernel(value_ref, order_ref, out_ref, values):
-    values[...] = value_ref[...].astype(F32).reshape(values.shape)
+def gbuffer_kernel(*refs):
+    *parts, order_ref, out_ref, values = refs
+    if len(parts) == 1:
+        values[...] = parts[0][...].astype(F32).reshape(values.shape)
+    else:
+        where_ref, chips_ref, others_ref = parts
+        chips, lines, _ = others_ref.shape
+        core = lax.rem(where_ref[0], 2)
+        for chip in range(chips):
+            for straight in range(2):
+                owner = 2 * chip + (core if straight else 1 - core)
+                first = pl.multiple_of(owner * lines, 8)
+                line = chips_ref[chip, core] if straight else others_ref[chip]
+                values[pl.ds(first, lines), :] = line.astype(F32)
     height = out_ref.shape[2]
 
     def ray_of(number):
@@ -419,12 +461,12 @@
     out_ref[0, 3] = (occlusion * (1.0 / NRAY)).astype(BF16)
 
 
-def gbuffer(values, order, height, width):
+def gbuffer(parts, order, height, width):
     total = order.shape[2]
     return pl.pallas_call(
         gbuffer_kernel,
         out_shape=jax.ShapeDtypeStruct((1, 4, height, width), BF16),
-        in_specs=[vmem(), vmem()],
+        in_specs=[smem()] * (len(parts) == 3) + [vmem()] * min(len(parts), 2) + [vmem()],
         out_specs=vmem(),
         scratch_shapes=[pltpu.VMEM((2 * total, LANES), F32)],
         compiler_params=params(16),
@@ -432,7 +474,7 @@
             flops=20 * total * BLOCK, bytes_accessed=8 * total * BLOCK, transcendentals=0
         ),
         name="gbuffer",
-    )(values, order)
+    )(*parts, order)
 
 
 def silu(field):
@@ -692,28 +734,35 @@
             return found
         return found.reshape(slots, padded)[:, :per_slot].reshape(1, samples // LANES, LANES)
 
-    places = positions(fill(cells), fill(fracs), n_tile)
-    places, bricks, pending = lax.optimization_barrier((places, bricks, pending))
+    where = jnp.stack([tile, jnp.int32(n_tile)]).astype(jnp.int32)
+    places, for_mate = positions(where, fill(cells), fill(fracs), n_tile)
+    places, for_mate, bricks, pending = lax.optimization_barrier(
+        (places, for_mate, bricks, pending)
+    )
     arrived = lax.all_to_all(places, "tile", split_axis=0, concat_axis=0, tiled=True)
 
     mates = [(i, i ^ 1) for i in range(n_tile) if i ^ 1 < n_tile]
     across_chips = [
         pair for i in range(1, n_tile - 1, 2) for pair in ((i, i + 1), (i + 1, i))
     ]
+    mate_places = lax.ppermute(for_mate, "tile", mates)
     near = lax.ppermute(pending, "tile", mates)
     far = lax.ppermute(pending, "tile", across_chips)
-    where = jnp.stack([tile, jnp.int32(n_tile)]).astype(jnp.int32)
     picks = sends[0, 0].T
     colours = w_out.shape[1]
     w_in = w_in.transpose(0, 2, 1)
     w_in = jnp.pad(w_in, ((0, 0), (0, 16 - w_in.shape[1]), (0, 0)))
     w_out = jnp.pad(w_out, ((0, 0), (0, 16 - colours), (0, 0)))
-    windows = windows_of(where, picks, bricks, places)
+    windows = windows_of(where, picks, bricks, places, mate_places)
     arrived, w_in, w_out = lax.optimization_barrier((arrived, w_in, w_out))
     found = sample_values(where, picks, windows, arrived)
 
     found, near, far, pending = lax.optimization_barrier((found, near, far, pending))
-    values = lax.all_to_all(found, "tile", split_axis=0, concat_axis=0, tiled=True)
+    same_core = [list(range(core, n_tile, 2)) for core in range(2)]
+    chips = found.reshape((n_tile // 2, 2) + found.shape[1:])
+    chips = lax.all_to_all(
+        chips, "tile", split_axis=0, concat_axis=0, axis_index_groups=same_core, tiled=True
+    )
     first_core = tile % 2 == 0
     over = jnp.where(first_core, far, near)
     under = jnp.where(first_core, near, far)
@@ -721,8 +770,19 @@
     field = jnp.pad(field, ((0, 0), (0, 16 - field.shape[1]), (0, 0)))
     second = stem(where, field, w_in, w_mid)
     third = middle(where, second, w_down.transpose(0, 2, 1))
-    values, third = lax.optimization_barrier((values, third))
-    rendered = gbuffer(trim(values), sample_order, height, width)
+    chips, third = lax.optimization_barrier((chips, third))
+    core = tile % 2
+    others = lax.dynamic_index_in_dim(chips, 1 - core, 1, keepdims=False)
+    others = lax.ppermute(others, "tile", mates)
+    if padded == per_slot:
+        parts = (where, chips, others)
+    else:
+        mine = lax.dynamic_index_in_dim(chips, core, 1, keepdims=False)
+        values = jnp.where(
+            first_core, jnp.stack([mine, others], axis=1), jnp.stack([others, mine], axis=1)
+        )
+        parts = (trim(values.reshape(found.shape)),)
+    rendered = gbuffer(parts, sample_order, height, width)
     rendered, third = lax.optimization_barrier((rendered, third))
     ring = [(i, (i + 1) % n_section) for i in range(n_section)]
     handoff = lax.ppermute(rendered, "section", ring)

time: 47.8 us -> 49.7 us (1.040)
  Pallas kernels: 19.8 us -> 20.9 us
  other arithmetic: 0.14 us -> 0.65 us
    ppermute x0 -> x2, waiting for transfers between devices: none -> 1.22 us  [the longest x1 1.21 us: on_device(): others = lax.ppermute(others, 'tile', mates)]
    all_to_all x1, waiting for transfers between devices: 6.64 us -> 5.66 us  [on_device(): lax.all_to_all(places, 'tile', split_axis=0, concat_axis=0, tiled=True)]
    pallas_call x1, Pallas kernels: 8.48 us -> 7.53 us  [sample_values(): pl.pallas_call(samples_kernel, out_shape=jax.ShapeDtypeStruct((owners, ro...]
    pallas_call x1, Pallas kernels: 3.08 us -> 3.99 us  [windows_of(): pl.pallas_call(windows_kernel, out_shape=jax.ShapeDtypeStruct((count + 1,...]
    pallas_call x1, Pallas kernels: 0.2 us -> 0.82 us  [gbuffer(): pl.pallas_call(gbuffer_kernel, out_shape=jax.ShapeDtypeStruct((1, 4, heig...]
    pallas_call x1, Pallas kernels: 2.21 us -> 2.81 us  [positions(): pl.pallas_call(positions_kernel, out_shape=(jax.ShapeDtypeStruct(shape, F...]
    ppermute x0 -> x2, starting transfers between devices: none -> 0.56 us  [the longest x1 0.55 us: on_device(): mate_places = lax.ppermute(for_mate, 'tile', mates)]
    another operation x1, other arithmetic: 0.08 us -> 0.59 us  [on_device(): where = jnp.stack([tile, jnp.int32(n_tile)]).astype(jnp.int32)]
  transfers between devices with their start and end apart: 5 -> 7, of which waited for: 3 -> 4; matrix products, arithmetic and copies ran while one was open for 5% -> 5% of each run, Pallas kernels for 37% -> 35%
where the time goes in v15:
time: 49.7 us; the launch traced here: 49.2 us
  Pallas kernels  20.9 us (42%)
  starting transfers between devices  12.5 us (25%)
  waiting for transfers between devices  9.9 us (20%)
  local copies, waits for them, and re-layouts  4.32 us (9%)
  between operations  0.96 us (2%)
  other arithmetic  0.65 us (1%)
    pallas_call x1, Pallas kernels, sample_values(): pl.pallas_call(samples_kernel, out_shape=jax.ShapeDtypeStruct((owners, ro...  7.53 us
    all_to_all x1, starting transfers between devices, on_device(): lax.all_to_all(places, 'tile', split_axis=0, concat_axis=0, tiled=True)  6.34 us
    all_to_all x1, waiting for transfers between devices, on_device(): lax.all_to_all(places, 'tile', split_axis=0, concat_axis=0, tiled=True)  5.66 us
    pallas_call x1, Pallas kernels, windows_of(): pl.pallas_call(windows_kernel, out_shape=jax.ShapeDtypeStruct((count + 1,...  3.99 us
    all_to_all x1, starting transfers between devices, on_device(): lax.all_to_all(chips, 'tile', split_axis=0, concat_axis=0, axis_index_gro...  3.31 us
    pallas_call x1, Pallas kernels, decoder(): pl.pallas_call(decoder_kernel, out_shape=jax.ShapeDtypeStruct((1, colours...  2.87 us
    pallas_call x1, Pallas kernels, positions(): pl.pallas_call(positions_kernel, out_shape=(jax.ShapeDtypeStruct(shape, F...  2.81 us
    all_to_all x1, waiting for transfers between devices, on_device(): lax.all_to_all(chips, 'tile', split_axis=0, concat_axis=0, axis_index_gro...  2.74 us
  transfers between devices with their start and end apart: 7, of which 4 were waited for; matrix products, arithmetic and copies ran while one was open for 5% of the time, Pallas kernels for 35%

profile of v15, /device:TPU:0, one launch (start us, length us, event | category | flops | bytes accessed | tf_op | source)
XLA Modules:
  0.0 49.2 jit_solution(11374871770212398948)
XLA Ops:
  0.7 0.6 %pad_add_fusion.where_ref.refs_0_ = s32[2]{0:T(128)} fusion(s32[1]{0:T(128)} %constant.25.clone.1, s32[1]{0:T(128)} %bitcast), kind=kLoop, calls=%fused_computation.5 | loop fusion | flops 2 | bytes 16 | tf_op jit(solution)/shard_map/stack | solution.py:737
  1.2 2.8 %positions.1 = (f32[8,120,128]{2,1,0:T(8,128)}, f32[1,120,128]{2,1,0:T(8,128)}) custom-call(s32[2]{0:T(128)} %pad_add_fusion.where_ref.refs_0_, s32[3,320,128]{2,1,0:T(8,128)} %bitcast.22, f32[3,320,128]{2,1,0:T(8,128)} %bitcast.23), custom_call_target="tpu_custom_call" | custom-call | flops 122880 | bytes 1474560 | tf_op jit(solution)/shard_map/positions/pallas_call | solution.py:94
  4.1 6.3 %all-to-all-start = ((f32[8,120,128]{2,1,0:T(8,128)}), f32[8,120,128]{2,1,0:T(8,128)}, u32[]{:S(2)}, u32[]{:S(2)}) async-start(f32[8,120,128]{2,1,0:T(8,128)} %get-tuple-element.22.place_ref), calls=%async_computation | async-start | bytes 983040 | tf_op jit(solution)/shard_map/all_to_all | solution.py:742
  10.4 0.0 copy-start.3
  10.4 0.0 copy-start.5
  10.4 0.6 %collective-permute-start = (f32[1,120,128]{2,1,0:T(8,128)}, f32[1,120,128]{2,1,0:T(8,128)S(1)}, u32[]{:S(2)}, u32[]{:S(2)}) collective-permute-start(f32[1,120,128]{2,1,0:T(8,128)} %get-tuple-element.23), channel_id=1, source_target_pairs={{0,1},{1,0},{2,3},{3,2},{4,5},{5,4},{6,7},{7,6},{8,9},{9,8},{10,11... | collective-permute-start | bytes 184328 | tf_op jit(solution)/shard_map/ppermute | solution.py:748
  11.0 0.1 collective-permute-start.1
  11.1 0.7 %collective-permute-start.2 = (bf16[1,4,8,256]{3,1,2,0:T(4,128)(2,1)S(1)}, bf16[1,4,8,256]{3,1,2,0:T(4,128)(2,1)S(1)}, u32[]{:S(2)}, u32[]{:S(2)}) collective-permute-start(bf16[1,4,8,256]{3,1,2,0:T(4,128)(2,1)S(1)} %copy.17), channel_id=1, source_target_pairs={{1,2},{2,1},{3,4},{4,3},{5,6},{6,5},{9,10},{10,9},{11,12},{12,11},... | collective-permute-start | bytes 49160 | tf_op jit(solution)/shard_map/ppermute | solution.py:750
  11.8 2.3 %reshape.18.cube_ref = bf16[16,34,1156]{2,1,0:T(8,128)(2,1)S(1)} reshape(bf16[16,39304]{1,0:T(8,128)(2,1)S(1)} %copy-done.10) | data formatting | bytes 2515456 | tf_op jit(solution)/shard_map/reshape | solution.py:178
  14.2 4.0 %brick_windows.1.brick_ref = bf16[17,208,256]{2,1,0:T(8,128)(2,1)S(1)} custom-call(s32[2]{0:T(128)S(1)} %copy-done.3, s32[2,8]{1,0:T(2,128)S(1)} %bitcast.20, bf16[16,34,1156]{2,1,0:T(8,128)(2,1)S(1)} %reshape.18.cube_ref, f32[8,120,128]{2,1,0:T(8,128)S(1)} %copy-done, f32[1,120,128]{2,1,0:T(8,128)S(1)} %collective-permute-done.mate_place_ref), custom_call_target="tpu_custom_call" | custom-call | flops 905969664 | bytes 4194304 | tf_op jit(solution)/shard_map/brick_windows/pallas_call | solution.py:180
  18.2 1.3 %copy-done.1 = bf16[17,208,256]{2,1,0:T(8,128)(2,1)} copy-done((bf16[17,208,256]{2,1,0:T(8,128)(2,1)}, bf16[17,208,256]{2,1,0:T(8,128)(2,1)S(1)}, u32[]{:S(2)}) %copy-start.1) | copy-done | bytes 1810456
  19.5 5.7 %all-to-all-done.place_ref = f32[8,120,128]{2,1,0:T(8,128)} async-done(((f32[8,120,128]{2,1,0:T(8,128)}), f32[8,120,128]{2,1,0:T(8,128)}, u32[]{:S(2)}, u32[]{:S(2)}) %all-to-all-start) | async-done | bytes 491552 | tf_op jit(solution)/shard_map/all_to_all | solution.py:742
  25.2 7.5 %sample_values.1 = bf16[8,40,128]{2,1,0:T(8,128)(2,1)} custom-call(s32[2]{0:T(128)} %pad_add_fusion.where_ref.refs_0_, s32[2,8]{1,0:T(2,128)} %bitcast.19, bf16[17,208,256]{2,1,0:T(8,128)(2,1)} %copy-done.1, f32[8,120,128]{2,1,0:T(8,128)} %all-to-all-done.place_ref), custom_call_target="tpu_custom_call" | custom-call | flops 4362076160 | bytes 3145728 | tf_op jit(solution)/shard_map/sample_values/pallas_call | solution.py:385
  32.8 3.3 %all-to-all-start.1 = ((bf16[4,2,40,128]{3,2,1,0:T(8,128)(2,1)}), bf16[4,2,40,128]{3,2,1,0:T(8,128)(2,1)S(1)}, u32[]{:S(2)}, u32[]{:S(2)}) async-start(bf16[4,2,40,128]{3,2,1,0:T(8,128)(2,1)} %bitcast.24), calls=%async_computation.1 | async-start | bytes 163840 | tf_op jit(solution)/shard_map/all_to_all | solution.py:763
  36.2 0.0 copy-start.9
  36.2 1.7 %stem.1.second = bf16[20,32,256]{2,1,0:T(8,128)(2,1)S(1)} custom-call(s32[2]{0:T(128)S(1)} %copy-done.4, bf16[24,16,256]{2,1,0:T(8,128)(2,1)S(1)} %pad.14.x_ref, bf16[9,16,32]{2,1,0:T(8,128)(2,1)S(1)} %pad.12.w_in, bf16[9,32,32]{2,1,0:T(8,128)(2,1)S(1)} %copy-done.8), custom_call_target="tpu_custom_call" | custom-call | flops 1000000000 | bytes 1048576 | tf_op jit(solution)/shard_map/stem/pallas_call | solution.py:657
  37.9 1.3 %middle.1.third = bf16[8,112,128]{2,1,0:T(8,128)(2,1)S(1)} custom-call(s32[2]{0:T(128)S(1)} %copy-done.4, bf16[20,32,256]{2,1,0:T(8,128)(2,1)S(1)} %stem.1.second, bf16[9,32,112]{2,1,0:T(8,128)(2,1)S(1)} %bitcast.21), custom_call_target="tpu_custom_call" | custom-call | flops 500000000 | bytes 1048576 | tf_op jit(solution)/shard_map/middle/pallas_call | solution.py:675
  39.2 2.7 %all-to-all-done.1.refs_1_ = bf16[4,2,40,128]{3,2,1,0:T(8,128)(2,1)S(1)} async-done(((bf16[4,2,40,128]{3,2,1,0:T(8,128)(2,1)}), bf16[4,2,40,128]{3,2,1,0:T(8,128)(2,1)S(1)}, u32[]{:S(2)}, u32[]{:S(2)}) %all-to-all-start.1) | async-done | bytes 81952 | tf_op jit(solution)/shard_map/all_to_all | solution.py:763
  41.9 1.2 %collective-permute-done.3.refs_2_ = bf16[4,40,128]{2,1,0:T(8,128)(2,1)S(1)} collective-permute-done((bf16[4,40,128]{2,1,0:T(8,128)(2,1)S(1)}, bf16[4,40,128]{2,1,0:T(8,128)(2,1)S(1)}, u32[]{:S(2)}, u32[]{:S(2)}) %collective-permute-start.3) | collective-permute-done | bytes 40992 | tf_op jit(solution)/shard_map/ppermute | solution.py:776
  43.1 0.8 %gbuffer.1 = bf16[1,4,8,256]{3,2,1,0:T(8,128)(2,1)S(1)} custom-call(s32[2]{0:T(128)S(1)} %copy-done.4, bf16[4,2,40,128]{3,2,1,0:T(8,128)(2,1)S(1)} %all-to-all-done.1.refs_1_, bf16[4,40,128]{2,1,0:T(8,128)(2,1)S(1)} %collective-permute-done.3.refs_2_, s32[1,1,160,256]{3,2,1,0:T(8,128)S(1)} %copy-done.2), custom_call_target="tpu_custom_call" | custom-call | flops 819200 | bytes 327680 | tf_op jit(solution)/shard_map/gbuffer/pallas_call | solution.py:466
  43.9 1.5 %collective-permute-start.4 = (bf16[1,4,8,256]{3,2,1,0:T(8,128)(2,1)S(1)}, bf16[1,4,8,256]{3,2,1,0:T(8,128)(2,1)S(1)}, u32[]{:S(2)}, u32[]{:S(2)}) collective-permute-start(bf16[1,4,8,256]{3,2,1,0:T(8,128)(2,1)S(1)} %gbuffer.1), channel_id=1, source_target_pairs={{0,8},{8,16},{16,24},{24,0},{1,9},{9,17},{17,25},{25,1},{2,10},{10... | collective-permute-start | bytes 49160 | tf_op jit(solution)/shard_map/ppermute | solution.py:788
  45.5 2.9 %decoder.1 = bf16[1,3,8,256]{3,2,1,0:T(8,128)(2,1)} custom-call(s32[2]{0:T(128)S(1)} %copy-done.4, bf16[20,32,256]{2,1,0:T(8,128)(2,1)S(1)} %stem.1.second, bf16[8,112,128]{2,1,0:T(8,128)(2,1)S(1)} %middle.1.third, bf16[9,112,112]{2,1,0:T(8,128)(2,1)S(1)} %copy-done.6, bf16[9,32,144]{2,1,0:T(8,128)(2,1)S(1)} %copy-done.7, bf16[9,16,32]{2,1,0:T(8,128)(2,1)S(1)} %pad.13.w_out), custom_call_target="tpu_custom_call" | custom-call | flops 1500000000 | bytes 1048576 | tf_op jit(solution)/shard_map/decoder/pallas_call | solution.py:693
  48.4 0.3 collective-permute-done.4
  48.6 0.6 %copy.22 = bf16[1,4,8,256]{3,2,1,0:T(8,128)(2,1)} copy(bf16[1,4,8,256]{3,2,1,0:T(8,128)(2,1)S(1)} %collective-permute-done.4) | data formatting | bytes 32768
  (35 shorter events, 0.2 us)
Async XLA Ops:
  0.6 11.1 %copy-start.10 = (bf16[16,39304]{1,0:T(8,128)(2,1)S(1)}, bf16[16,39304]{1,0:T(8,128)(2,1)}, u32[]{:S(2)}) copy-start(bf16[16,39304]{1,0:T(8,128)(2,1)} %param.12) | copy-start | bytes 3773188
  0.6 10.4 %copy-start.11 = (bf16[1,4,8,256]{3,2,1,0:T(8,128)(2,1)S(1)}, bf16[1,4,8,256]{3,2,1,0:T(8,128)(2,1)}, u32[]{:S(2)}) copy-start(bf16[1,4,8,256]{3,2,1,0:T(8,128)(2,1)} %param.17) | copy-start | bytes 49156
  4.1 21.1 %all-to-all-start = ((f32[8,120,128]{2,1,0:T(8,128)}), f32[8,120,128]{2,1,0:T(8,128)}, u32[]{:S(2)}, u32[]{:S(2)}) async-start(f32[8,120,128]{2,1,0:T(8,128)} %get-tuple-element.22.place_ref), calls=%async_computation | async-start | bytes 983040 | tf_op jit(solution)/shard_map/all_to_all | solution.py:742
  10.4 3.7 %copy-start.12 = (bf16[9,32,4]{1,2,0:T(4,128)(2,1)S(1)}, bf16[9,32,4]{1,2,0:T(4,128)(2,1)}, u32[]{:S(2)}) copy-start(bf16[9,32,4]{1,2,0:T(4,128)(2,1)} %param.18) | copy-start | bytes 6916
  10.4 3.8 %copy-start.13 = (bf16[9,3,32]{2,1,0:T(4,128)(2,1)S(1)}, bf16[9,3,32]{2,1,0:T(4,128)(2,1)}, u32[]{:S(2)}) copy-start(bf16[9,3,32]{2,1,0:T(4,128)(2,1)} %param.23) | copy-start | bytes 5188
  10.4 3.8 %copy-start = (f32[8,120,128]{2,1,0:T(8,128)S(1)}, f32[8,120,128]{2,1,0:T(8,128)}, u32[]{:S(2)}) copy-start(f32[8,120,128]{2,1,0:T(8,128)} %get-tuple-element.22.place_ref) | copy-start | bytes 1474564
  10.4 3.8 %copy-start.3 = (s32[2]{0:T(128)S(1)}, s32[2]{0:T(128)}, u32[]{:S(2)}) copy-start(s32[2]{0:T(128)} %pad_add_fusion.where_ref.refs_0_) | copy-start | bytes 28
  10.4 3.8 %copy-start.5 = (s32[1,1,8,2]{2,3,1,0:T(2,128)S(1)}, s32[1,1,8,2]{2,3,1,0:T(2,128)}, u32[]{:S(2)}) copy-start(s32[1,1,8,2]{2,3,1,0:T(2,128)} %param.13) | copy-start | bytes 196
  10.4 3.7 %collective-permute-start = (f32[1,120,128]{2,1,0:T(8,128)}, f32[1,120,128]{2,1,0:T(8,128)S(1)}, u32[]{:S(2)}, u32[]{:S(2)}) collective-permute-start(f32[1,120,128]{2,1,0:T(8,128)} %get-tuple-element.23), channel_id=1, source_target_pairs={{0,1},{1,0},{2,3},{3,2},{4,5},{5,4},{6,7},{7,6},{8,9},{9,8},{10,11... | collective-permute-start | bytes 184328 | tf_op jit(solution)/shard_map/ppermute | solution.py:748
  11.0 21.7 %collective-permute-start.1 = (bf16[1,4,8,256]{3,1,2,0:T(4,128)(2,1)S(1)}, bf16[1,4,8,256]{3,1,2,0:T(4,128)(2,1)S(1)}, u32[]{:S(2)}, u32[]{:S(2)}) collective-permute-start(bf16[1,4,8,256]{3,1,2,0:T(4,128)(2,1)S(1)} %copy.17), channel_id=1, source_target_pairs={{0,1},{1,0},{2,3},{3,2},{4,5},{5,4},{6,7},{7,6},{8,9},{9,8},{10,11... | collective-permute-start | bytes 49160 | tf_op jit(solution)/shard_map/ppermute | solution.py:749
  11.1 21.6 %collective-permute-start.2 = (bf16[1,4,8,256]{3,1,2,0:T(4,128)(2,1)S(1)}, bf16[1,4,8,256]{3,1,2,0:T(4,128)(2,1)S(1)}, u32[]{:S(2)}, u32[]{:S(2)}) collective-permute-start(bf16[1,4,8,256]{3,1,2,0:T(4,128)(2,1)S(1)} %copy.17), channel_id=1, source_target_pairs={{1,2},{2,1},{3,4},{4,3},{5,6},{6,5},{9,10},{10,9},{11,12},{12,11},... | collective-permute-start | bytes 49160 | tf_op jit(solution)/shard_map/ppermute | solution.py:750
  18.2 1.3 %copy-start.1 = (bf16[17,208,256]{2,1,0:T(8,128)(2,1)}, bf16[17,208,256]{2,1,0:T(8,128)(2,1)S(1)}, u32[]{:S(2)}) copy-start(bf16[17,208,256]{2,1,0:T(8,128)(2,1)S(1)} %brick_windows.1.brick_ref) | copy-start | bytes 5431300
  19.5 16.7 %copy-start.4 = (s32[2]{0:T(128)S(1)}, s32[2]{0:T(128)}, u32[]{:S(2)}) copy-start(s32[2]{0:T(128)} %pad_add_fusion.where_ref.refs_0_) | copy-start | bytes 28
  19.5 16.7 %copy-start.8 = (bf16[9,32,32]{2,1,0:T(8,128)(2,1)S(1)}, bf16[9,32,32]{2,1,0:T(8,128)(2,1)}, u32[]{:S(2)}) copy-start(bf16[9,32,32]{2,1,0:T(8,128)(2,1)} %w_mid.1) | copy-start | bytes 55300
  32.8 9.1 %all-to-all-start.1 = ((bf16[4,2,40,128]{3,2,1,0:T(8,128)(2,1)}), bf16[4,2,40,128]{3,2,1,0:T(8,128)(2,1)S(1)}, u32[]{:S(2)}, u32[]{:S(2)}) async-start(bf16[4,2,40,128]{3,2,1,0:T(8,128)(2,1)} %bitcast.24), calls=%async_computation.1 | async-start | bytes 163840 | tf_op jit(solution)/shard_map/all_to_all | solution.py:763
  36.2 1.7 %copy-start.9 = (bf16[9,112,32]{1,2,0:T(8,128)(2,1)S(1)}, bf16[9,112,32]{1,2,0:T(8,128)(2,1)}, u32[]{:S(2)}) copy-start(bf16[9,112,32]{1,2,0:T(8,128)(2,1)} %param.20) | copy-start | bytes 193540
  37.8 5.3 %copy-start.2 = (s32[1,1,160,256]{3,2,1,0:T(8,128)S(1)}, s32[1,1,160,256]{3,2,1,0:T(8,128)}, u32[]{:S(2)}) copy-start(s32[1,1,160,256]{3,2,1,0:T(8,128)} %refs_3_.1) | copy-start | bytes 491524
  37.9 7.6 %copy-start.6 = (bf16[9,112,112]{2,1,0:T(8,128)(2,1)S(1)}, bf16[9,112,112]{2,1,0:T(8,128)(2,1)}, u32[]{:S(2)}) copy-start(bf16[9,112,112]{2,1,0:T(8,128)(2,1)} %w_deep.1) | copy-start | bytes 677380
  37.9 7.6 %copy-start.7 = (bf16[9,32,144]{2,1,0:T(8,128)(2,1)S(1)}, bf16[9,32,144]{2,1,0:T(8,128)(2,1)}, u32[]{:S(2)}) copy-start(bf16[9,32,144]{2,1,0:T(8,128)(2,1)} %w_up.1) | copy-start | bytes 248836
  41.9 1.2 %collective-permute-start.3 = (bf16[4,40,128]{2,1,0:T(8,128)(2,1)S(1)}, bf16[4,40,128]{2,1,0:T(8,128)(2,1)S(1)}, u32[]{:S(2)}, u32[]{:S(2)}) collective-permute-start(bf16[4,40,128]{2,1,0:T(8,128)(2,1)S(1)} %dynamic-slice_bitcast_fusion), channel_id=1, source_target_pairs={{0,1},{1,0},{2,3},{3,2},{4,5},{5,4},{6,7},{7,6},{8,9},{9,8},{10,11... | collective-permute-start | bytes 122888 | tf_op jit(solution)/shard_map/ppermute | solution.py:776
  43.9 4.7 %collective-permute-start.4 = (bf16[1,4,8,256]{3,2,1,0:T(8,128)(2,1)S(1)}, bf16[1,4,8,256]{3,2,1,0:T(8,128)(2,1)S(1)}, u32[]{:S(2)}, u32[]{:S(2)}) collective-permute-start(bf16[1,4,8,256]{3,2,1,0:T(8,128)(2,1)S(1)} %gbuffer.1), channel_id=1, source_target_pairs={{0,8},{8,16},{16,24},{24,0},{1,9},{9,17},{17,25},{25,1},{2,10},{10... | collective-permute-start | bytes 49160 | tf_op jit(solution)/shard_map/ppermute | solution.py:788

commit v16 on v14

--- a/solution.py
+++ b/solution.py
@@ -99,12 +99,22 @@
     )(cells, fracs)
 
 
+def mate_of(tile):
+    return tile + 1 - 2 * lax.rem(tile, 2)
+
+
 def windows_kernel(
-    where_ref, picks_ref, cube_ref, place_ref, out_ref, wide, tail, places, sums, arrival
+    where_ref, picks_ref, cube_ref, place_ref, mate_place_ref, out_ref,
+    wide, tail, places, sums, arrivals,
 ):
     tile = where_ref[0]
-    own_places = pltpu.make_async_copy(place_ref.at[tile], places, arrival)
-    own_places.start()
+    near = ((tile, place_ref.at[tile]), (mate_of(tile), mate_place_ref.at[0]))
+    copies = [
+        pltpu.make_async_copy(source, places.at[i], arrivals.at[i])
+        for i, (_, source) in enumerate(near)
+    ]
+    for copy in copies:
+        copy.start()
     count = cube_ref.shape[0]
     plane = EDGE * EDGE
     wide[...] = jnp.zeros_like(wide)
@@ -135,32 +145,37 @@
         tail[:, row : row + 1, :] = jnp.zeros((count, 1, KDIM), F32)
     out_ref[:count, WINDOWS * MAIN :, :] = tail[...].astype(BF16)
 
-    own_places.wait()
+    for copy in copies:
+        copy.wait()
     cap = picks_ref.shape[0]
-    lines = places.shape[0] // 3
+    lines = places.shape[1] // 3
     part = lines // cap
-
-    for piece in range(cap):
-        brick = out_ref[picks_ref[piece, tile]]
-        slot_sums(brick, places, sums, piece * part, part // 2)
-    out_ref[count, : whole_tiles(lines), :LANES] = line_values(sums, lines, whole_tiles(lines))
-
-
-def windows_of(where, picks, bricks, places):
+    height = whole_tiles(lines)
+    for i, (renderer, _) in enumerate(near):
+        for piece in range(cap):
+            brick = out_ref[picks_ref[piece, renderer]]
+            slot_sums(brick, places.at[i], sums.at[i], piece * part, part // 2)
+    for i in range(len(near)):
+        out_ref[count, i * height : (i + 1) * height, :LANES] = line_values(
+            sums.at[i], lines, height
+        )
+
+
+def windows_of(where, picks, bricks, places, mate_places):
     count = bricks.shape[0]
     cube = bricks.reshape(count, EDGE, EDGE * EDGE)
     rows = places.shape[1]
     return pl.pallas_call(
         windows_kernel,
         out_shape=jax.ShapeDtypeStruct((count + 1, BRICK_ROWS, KDIM), BF16),
-        in_specs=[smem(), smem(), vmem(), pl.BlockSpec(memory_space=pl.ANY)],
+        in_specs=[smem(), smem(), vmem()] + [pl.BlockSpec(memory_space=pl.ANY)] * 2,
         out_specs=vmem(),
         scratch_shapes=[
             pltpu.VMEM((count, 48, 10 * LANES), BF16),
             pltpu.VMEM((count, TAIL, KDIM), F32),
-            pltpu.VMEM((rows, LANES), F32),
-            pltpu.VMEM((8 * rows // 3, LANES), F32),
-            pltpu.SemaphoreType.DMA,
+            pltpu.VMEM((2, rows, LANES), F32),
+            pltpu.VMEM((2, 8 * rows // 3, LANES), F32),
+            pltpu.SemaphoreType.DMA((2,)),
         ],
         compiler_params=params(16),
         cost_estimate=pl.CostEstimate(
@@ -168,7 +183,7 @@
             transcendentals=0,
         ),
         name="brick_windows",
-    )(where, picks, cube, places)
+    )(where, picks, cube, places, mate_places)
 
 
 def hat(distance):
@@ -264,7 +279,7 @@
     cap = picks_ref.shape[0]
     lines = rows // 3
     part = lines // cap
-    turns = owners - 1
+    turns = owners - 2
     tile = where_ref[0]
     pairs, rest = turns // 2, turns % 2
     own_values = pltpu.make_async_copy(
@@ -274,7 +289,7 @@
     )
 
     def renderer_of(number):
-        return lax.rem(tile + 1 + number, owners)
+        return lax.rem(2 * (tile // 2) + 2 + number, owners)
 
     def fetches(turn, members):
         held = turn % 2
@@ -344,7 +359,10 @@
     if rest:
         work(pairs, 1)
     own_values.wait()
-    out_ref[tile] = own[...].astype(F32)[:lines].astype(BF16)
+    height = whole_tiles(lines)
+    for i, renderer in enumerate((tile, mate_of(tile))):
+        values = own[i * height : (i + 1) * height, :].astype(F32)
+        out_ref[renderer] = values[:lines].astype(BF16)
 
 
 def sample_values(where, picks, windows, places):
@@ -361,7 +379,7 @@
             pltpu.VMEM((2, 2, cap, BRICK_ROWS, KDIM), BF16),
             pltpu.VMEM((2, 2, rows, LANES), F32),
             pltpu.VMEM((2, 8 * rows // 3, LANES), F32),
-            pltpu.VMEM((whole_tiles(rows // 3), LANES), BF16),
+            pltpu.VMEM((2 * whole_tiles(rows // 3), LANES), BF16),
             pltpu.SemaphoreType.DMA((2, 2, cap + 1)),
             pltpu.SemaphoreType.DMA,
         ],
@@ -693,22 +711,24 @@
         return found.reshape(slots, padded)[:, :per_slot].reshape(1, samples // LANES, LANES)
 
     places = positions(fill(cells), fill(fracs), n_tile)
-    places, bricks, pending = lax.optimization_barrier((places, bricks, pending))
+    places, bricks, pending, tile = lax.optimization_barrier((places, bricks, pending, tile))
     arrived = lax.all_to_all(places, "tile", split_axis=0, concat_axis=0, tiled=True)
+    where = jnp.stack([tile, jnp.int32(n_tile)]).astype(jnp.int32)
 
     mates = [(i, i ^ 1) for i in range(n_tile) if i ^ 1 < n_tile]
     across_chips = [
         pair for i in range(1, n_tile - 1, 2) for pair in ((i, i + 1), (i + 1, i))
     ]
+    for_mate = lax.dynamic_slice_in_dim(places, mate_of(tile), 1, 0)
+    mate_places = lax.ppermute(for_mate, "tile", mates)
     near = lax.ppermute(pending, "tile", mates)
     far = lax.ppermute(pending, "tile", across_chips)
-    where = jnp.stack([tile, jnp.int32(n_tile)]).astype(jnp.int32)
     picks = sends[0, 0].T
     colours = w_out.shape[1]
     w_in = w_in.transpose(0, 2, 1)
     w_in = jnp.pad(w_in, ((0, 0), (0, 16 - w_in.shape[1]), (0, 0)))
     w_out = jnp.pad(w_out, ((0, 0), (0, 16 - colours), (0, 0)))
-    windows = windows_of(where, picks, bricks, places)
+    windows = windows_of(where, picks, bricks, places, mate_places)
     arrived, w_in, w_out = lax.optimization_barrier((arrived, w_in, w_out))
     found = sample_values(where, picks, windows, arrived)
 

time: 47.8 us -> 47.2 us (0.987)
  waiting for transfers between devices: 9.84 us -> 3.04 us
  starting transfers between devices: 12.5 us -> 15.5 us
  local copies, waits for them, and re-layouts: 4.29 us -> 6.48 us
  other arithmetic: 0.14 us -> 0.87 us
    all_to_all x1, waiting for transfers between devices: 6.64 us -> 0.57 us  [on_device(): lax.all_to_all(places, 'tile', split_axis=0, concat_axis=0, tiled=True)]
    ppermute x0 -> x1, starting transfers between devices: none -> 2.46 us  [on_device(): mate_places = lax.ppermute(for_mate, 'tile', mates)]
    pallas_call x1, Pallas kernels: 3.08 us -> 3.98 us  [windows_of(): pl.pallas_call(windows_kernel, out_shape=jax.ShapeDtypeStruct((count + 1,...]
    dynamic_slice x0 -> x1, local copies, waits for them, and re-layouts: none -> 0.83 us  [on_device(): for_mate = lax.dynamic_slice_in_dim(places, mate_of(tile), 1, 0)]
    pallas_call x1, Pallas kernels: 8.48 us -> 7.66 us  [sample_values(): pl.pallas_call(samples_kernel, out_shape=jax.ShapeDtypeStruct((owners, ro...]
    squeeze x1, other arithmetic: 0.02 us -> 0.76 us  [on_device(): over[0]]
    all_to_all x1, waiting for transfers between devices: 2.93 us -> 2.19 us  [on_device(): lax.all_to_all(found, 'tile', split_axis=0, concat_axis=0, tiled=True)]
    pad x1, local copies, waits for them, and re-layouts: 0.01 us -> 0.71 us  [on_device(): w_in = jnp.pad(w_in, ((0, 0), (0, 16 - w_in.shape[1]), (0, 0)))]
  transfers between devices with their start and end apart: 5 -> 6, of which waited for: 3 -> 3; matrix products, arithmetic and copies ran while one was open for 5% -> 12% of each run, Pallas kernels for 37% -> 37%
where the time goes in v16:
time: 47.2 us; the launch traced here: 46.6 us
  Pallas kernels  19.8 us (42%)
  starting transfers between devices  15.5 us (33%)
  local copies, waits for them, and re-layouts  6.48 us (14%)
  waiting for transfers between devices  3.04 us (6%)
  other arithmetic  0.87 us (2%)
  between operations  0.85 us (2%)
    pallas_call x1, Pallas kernels, sample_values(): pl.pallas_call(samples_kernel, out_shape=jax.ShapeDtypeStruct((owners, ro...  7.66 us
    all_to_all x1, starting transfers between devices, on_device(): lax.all_to_all(places, 'tile', split_axis=0, concat_axis=0, tiled=True)  6.34 us
    pallas_call x1, Pallas kernels, windows_of(): pl.pallas_call(windows_kernel, out_shape=jax.ShapeDtypeStruct((count + 1,...  3.98 us
    all_to_all x1, starting transfers between devices, on_device(): lax.all_to_all(found, 'tile', split_axis=0, concat_axis=0, tiled=True)  3.37 us
    pallas_call x1, Pallas kernels, decoder(): pl.pallas_call(decoder_kernel, out_shape=jax.ShapeDtypeStruct((1, colours...  2.87 us
    ppermute x1, starting transfers between devices, on_device(): mate_places = lax.ppermute(for_mate, 'tile', mates)  2.46 us
    reshape x1, local copies, waits for them, and re-layouts, windows_of(): cube = bricks.reshape(count, EDGE, EDGE * EDGE)  2.31 us
    all_to_all x1, waiting for transfers between devices, on_device(): lax.all_to_all(found, 'tile', split_axis=0, concat_axis=0, tiled=True)  2.19 us
  transfers between devices with their start and end apart: 6, of which 3 were waited for; matrix products, arithmetic and copies ran while one was open for 12% of the time, Pallas kernels for 37%

profile of v16, /device:TPU:0, one launch (start us, length us, event | category | flops | bytes accessed | tf_op | source)
XLA Modules:
  0.0 46.6 jit_solution(14368612055301739343)
XLA Ops:
  0.7 2.2 %positions.1.place_ref = f32[8,120,128]{2,1,0:T(8,128)} custom-call(s32[3,320,128]{2,1,0:T(8,128)} %bitcast.19, f32[3,320,128]{2,1,0:T(8,128)} %bitcast.20), custom_call_target="tpu_custom_call" | custom-call | flops 122880 | bytes 1474560 | tf_op jit(solution)/shard_map/positions/pallas_call | solution.py:82
  2.9 6.3 %all-to-all-start = ((f32[8,120,128]{2,1,0:T(8,128)}), f32[8,120,128]{2,1,0:T(8,128)}, u32[]{:S(2)}, u32[]{:S(2)}) async-start(f32[8,120,128]{2,1,0:T(8,128)} %positions.1.place_ref), calls=%async_computation | async-start | bytes 983040 | tf_op jit(solution)/shard_map/all_to_all | solution.py:715
  9.2 0.6 %collective-permute-start.1 = (bf16[1,4,8,256]{3,1,2,0:T(4,128)(2,1)S(1)}, bf16[1,4,8,256]{3,1,2,0:T(4,128)(2,1)}, u32[]{:S(2)}, u32[]{:S(2)}) collective-permute-start(bf16[1,4,8,256]{3,1,2,0:T(4,128)(2,1)S(1)} %copy.17), channel_id=1, source_target_pairs={{0,1},{1,0},{2,3},{3,2},{4,5},{5,4},{6,7},{7,6},{8,9},{9,8},{10,11... | collective-permute-start | bytes 49160 | tf_op jit(solution)/shard_map/ppermute | solution.py:724
  9.8 1.2 %collective-permute-start.2 = (bf16[1,4,8,256]{3,1,2,0:T(4,128)(2,1)S(1)}, bf16[1,4,8,256]{3,1,2,0:T(4,128)(2,1)}, u32[]{:S(2)}, u32[]{:S(2)}) collective-permute-start(bf16[1,4,8,256]{3,1,2,0:T(4,128)(2,1)S(1)} %copy.17), channel_id=1, source_target_pairs={{1,2},{2,1},{3,4},{4,3},{5,6},{6,5},{9,10},{10,9},{11,12},{12,11},... | collective-permute-start | bytes 49160 | tf_op jit(solution)/shard_map/ppermute | solution.py:725
  11.0 0.8 %constant_dynamic-slice_fusion = f32[1,120,128]{2,1,0:T(8,128)S(1)} fusion(f32[8,120,128]{2,1,0:T(8,128)} %positions.1.place_ref, s32[]{:T(128)S(6)} %select_n.22), kind=kLoop, calls=%fused_computation.5 | loop fusion | bytes 122884 | tf_op jit(solution)/shard_map/dynamic_slice | solution.py:722
  11.9 2.5 %collective-permute-start = (f32[1,120,128]{2,1,0:T(8,128)S(1)}, f32[1,120,128]{2,1,0:T(8,128)S(1)}, u32[]{:S(2)}, u32[]{:S(2)}) collective-permute-start(f32[1,120,128]{2,1,0:T(8,128)S(1)} %constant_dynamic-slice_fusion), channel_id=1, source_target_pairs={{0,1},{1,0},{2,3},{3,2},{4,5},{5,4},{6,7},{7,6},{8,9},{9,8},{10,11... | collective-permute-start | bytes 184328 | tf_op jit(solution)/shard_map/ppermute | solution.py:723
  14.3 2.3 %reshape.15.cube_ref = bf16[16,34,1156]{2,1,0:T(8,128)(2,1)S(1)} reshape(bf16[16,39304]{1,0:T(8,128)(2,1)S(1)} %copy-done.10) | data formatting | bytes 2515456 | tf_op jit(solution)/shard_map/reshape | solution.py:166
  16.6 0.7 %pad.12.w_in = bf16[9,16,32]{2,1,0:T(8,128)(2,1)S(1)} pad(bf16[9,4,32]{2,1,0:T(4,128)(2,1)} %bitcast.21, bf16[]{:T(256)} %constant.26.clone.1), padding=0_0x0_12x0_0 | pad | bytes 11522 | tf_op jit(solution)/shard_map/jit(_pad)/pad | solution.py:729
  17.4 0.7 %pad.13.w_out = bf16[9,16,32]{2,1,0:T(8,128)(2,1)S(1)} pad(bf16[9,3,32]{2,1,0:T(4,128)(2,1)} %param.23, bf16[]{:T(256)} %constant.26.clone.1), padding=0_0x0_13x0_0 | pad | bytes 10946 | tf_op jit(solution)/shard_map/jit(_pad)/pad | solution.py:730
  18.1 0.1 pad_add_fusion.where_ref
  18.1 4.0 %brick_windows.1.brick_ref = bf16[17,208,256]{2,1,0:T(8,128)(2,1)S(1)} custom-call(s32[2]{0:T(128)S(1)} %pad_add_fusion.where_ref, s32[2,8]{1,0:T(2,128)S(1)} %bitcast.17, bf16[16,34,1156]{2,1,0:T(8,128)(2,1)S(1)} %reshape.15.cube_ref, f32[8,120,128]{2,1,0:T(8,128)S(1)} %copy-done, f32[1,120,128]{2,1,0:T(8,128)S(1)} %collective-permute-done.mate_place_ref), custom_call_target="tpu_custom_call" | custom-call | flops 905969664 | bytes 4194304 | tf_op jit(solution)/shard_map/brick_windows/pallas_call | solution.py:168
  22.2 1.2 %copy-done.1 = bf16[17,208,256]{2,1,0:T(8,128)(2,1)} copy-done((bf16[17,208,256]{2,1,0:T(8,128)(2,1)}, bf16[17,208,256]{2,1,0:T(8,128)(2,1)S(1)}, u32[]{:S(2)}) %copy-start.1) | copy-done | bytes 1810456
  23.4 0.6 %all-to-all-done.place_ref = f32[8,120,128]{2,1,0:T(8,128)} async-done(((f32[8,120,128]{2,1,0:T(8,128)}), f32[8,120,128]{2,1,0:T(8,128)}, u32[]{:S(2)}, u32[]{:S(2)}) %all-to-all-start) | async-done | bytes 491552 | tf_op jit(solution)/shard_map/all_to_all | solution.py:715
  24.0 7.7 %sample_values.1 = bf16[8,40,128]{2,1,0:T(8,128)(2,1)} custom-call(s32[2]{0:T(128)} %copy-done.4, s32[2,8]{1,0:T(2,128)} %bitcast.16, bf16[17,208,256]{2,1,0:T(8,128)(2,1)} %copy-done.1, f32[8,120,128]{2,1,0:T(8,128)} %all-to-all-done.place_ref), custom_call_target="tpu_custom_call" | custom-call | flops 4362076160 | bytes 3145728 | tf_op jit(solution)/shard_map/sample_values/pallas_call | solution.py:373
  31.6 3.4 %all-to-all-start.1 = ((bf16[8,40,128]{2,1,0:T(8,128)(2,1)}), bf16[8,40,128]{2,1,0:T(8,128)(2,1)S(1)}, u32[]{:S(2)}, u32[]{:S(2)}) async-start(bf16[8,40,128]{2,1,0:T(8,128)(2,1)} %sample_values.1), calls=%async_computation.1 | async-start | bytes 163840 | tf_op jit(solution)/shard_map/all_to_all | solution.py:736
  35.0 0.8 %select_bitcast_fusion.1 = (bf16[4,8,256]{2,0,1:T(4,128)(2,1)S(1)}, bf16[4,8,256]{2,0,1:T(4,128)(2,1)S(1)}, bf16[4,8,256]{2,0,1:T(4,128)(2,1)S(1)}) fusion(bf16[1,4,8,256]{3,1,2,0:T(4,128)(2,1)} %collective-permute-done.2, bf16[1,4,8,256]{3,1,2,0:T(4,128)(2,1)} %collective-permute-done.1, pred[]{:T(512)S(6)} %eq.5, bf16[1,4,8,256]{3,2,1,0:T(8,128)(2,1)S(1)} %copy-done.11), kind=kLoop, calls=%fused_computation.3 | loop fusion | flops 16384 | bytes 98305 | tf_op jit(solution)/shard_map/squeeze | solution.py:740
  35.9 1.7 %stem.1.second = bf16[20,32,256]{2,1,0:T(8,128)(2,1)S(1)} custom-call(s32[2]{0:T(128)S(1)} %copy-done.5, bf16[24,16,256]{2,1,0:T(8,128)(2,1)S(1)} %pad.14.x_ref, bf16[9,16,32]{2,1,0:T(8,128)(2,1)S(1)} %pad.12.w_in, bf16[9,32,32]{2,1,0:T(8,128)(2,1)S(1)} %copy-done.8), custom_call_target="tpu_custom_call" | custom-call | flops 1000000000 | bytes 1048576 | tf_op jit(solution)/shard_map/stem/pallas_call | solution.py:633
  37.6 1.3 %middle.1.third = bf16[8,112,128]{2,1,0:T(8,128)(2,1)S(1)} custom-call(s32[2]{0:T(128)S(1)} %copy-done.5, bf16[20,32,256]{2,1,0:T(8,128)(2,1)S(1)} %stem.1.second, bf16[9,32,112]{2,1,0:T(8,128)(2,1)S(1)} %bitcast.18), custom_call_target="tpu_custom_call" | custom-call | flops 500000000 | bytes 1048576 | tf_op jit(solution)/shard_map/middle/pallas_call | solution.py:651
  38.9 2.2 %all-to-all-done.1.value_ref = bf16[8,40,128]{2,1,0:T(8,128)(2,1)S(1)} async-done(((bf16[8,40,128]{2,1,0:T(8,128)(2,1)}), bf16[8,40,128]{2,1,0:T(8,128)(2,1)S(1)}, u32[]{:S(2)}, u32[]{:S(2)}) %all-to-all-start.1) | async-done | bytes 81952 | tf_op jit(solution)/shard_map/all_to_all | solution.py:736
  41.1 0.2 gbuffer.1
  41.3 1.5 %collective-permute-start.3 = (bf16[1,4,8,256]{3,2,1,0:T(8,128)(2,1)S(1)}, bf16[1,4,8,256]{3,2,1,0:T(8,128)(2,1)S(1)}, u32[]{:S(2)}, u32[]{:S(2)}) collective-permute-start(bf16[1,4,8,256]{3,2,1,0:T(8,128)(2,1)S(1)} %gbuffer.1), channel_id=1, source_target_pairs={{0,8},{8,16},{16,24},{24,0},{1,9},{9,17},{17,25},{25,1},{2,10},{10... | collective-permute-start | bytes 49160 | tf_op jit(solution)/shard_map/ppermute | solution.py:748
  42.8 2.9 %decoder.1 = bf16[1,3,8,256]{3,2,1,0:T(8,128)(2,1)} custom-call(s32[2]{0:T(128)S(1)} %copy-done.5, bf16[20,32,256]{2,1,0:T(8,128)(2,1)S(1)} %stem.1.second, bf16[8,112,128]{2,1,0:T(8,128)(2,1)S(1)} %middle.1.third, bf16[9,112,112]{2,1,0:T(8,128)(2,1)S(1)} %copy-done.6, bf16[9,32,144]{2,1,0:T(8,128)(2,1)S(1)} %copy-done.7, bf16[9,16,32]{2,1,0:T(8,128)(2,1)S(1)} %pad.13.w_out), custom_call_target="tpu_custom_call" | custom-call | flops 1500000000 | bytes 1048576 | tf_op jit(solution)/shard_map/decoder/pallas_call | solution.py:669
  45.7 0.3 collective-permute-done.3
  46.0 0.6 %copy.22 = bf16[1,4,8,256]{3,2,1,0:T(8,128)(2,1)} copy(bf16[1,4,8,256]{3,2,1,0:T(8,128)(2,1)S(1)} %collective-permute-done.3) | data formatting | bytes 32768
  (29 shorter events, 0.1 us)
Async XLA Ops:
  0.6 13.7 %copy-start.10 = (bf16[16,39304]{1,0:T(8,128)(2,1)S(1)}, bf16[16,39304]{1,0:T(8,128)(2,1)}, u32[]{:S(2)}) copy-start(bf16[16,39304]{1,0:T(8,128)(2,1)} %param.12) | copy-start | bytes 3773188
  0.6 8.6 %copy-start.11 = (bf16[1,4,8,256]{3,2,1,0:T(8,128)(2,1)S(1)}, bf16[1,4,8,256]{3,2,1,0:T(8,128)(2,1)}, u32[]{:S(2)}) copy-start(bf16[1,4,8,256]{3,2,1,0:T(8,128)(2,1)} %param.17) | copy-start | bytes 49156
  2.9 21.1 %all-to-all-start = ((f32[8,120,128]{2,1,0:T(8,128)}), f32[8,120,128]{2,1,0:T(8,128)}, u32[]{:S(2)}, u32[]{:S(2)}) async-start(f32[8,120,128]{2,1,0:T(8,128)} %positions.1.place_ref), calls=%async_computation | async-start | bytes 983040 | tf_op jit(solution)/shard_map/all_to_all | solution.py:715
  9.2 9.0 %copy-start = (f32[8,120,128]{2,1,0:T(8,128)S(1)}, f32[8,120,128]{2,1,0:T(8,128)}, u32[]{:S(2)}) copy-start(f32[8,120,128]{2,1,0:T(8,128)} %positions.1.place_ref) | copy-start | bytes 1474564
  9.2 8.9 %copy-start.3 = (s32[1,1,8,2]{2,3,1,0:T(2,128)S(1)}, s32[1,1,8,2]{2,3,1,0:T(2,128)}, u32[]{:S(2)}) copy-start(s32[1,1,8,2]{2,3,1,0:T(2,128)} %param.13) | copy-start | bytes 196
  9.2 22.4 %collective-permute-start.1 = (bf16[1,4,8,256]{3,1,2,0:T(4,128)(2,1)S(1)}, bf16[1,4,8,256]{3,1,2,0:T(4,128)(2,1)}, u32[]{:S(2)}, u32[]{:S(2)}) collective-permute-start(bf16[1,4,8,256]{3,1,2,0:T(4,128)(2,1)S(1)} %copy.17), channel_id=1, source_target_pairs={{0,1},{1,0},{2,3},{3,2},{4,5},{5,4},{6,7},{7,6},{8,9},{9,8},{10,11... | collective-permute-start | bytes 49160 | tf_op jit(solution)/shard_map/ppermute | solution.py:724
  9.8 21.8 %collective-permute-start.2 = (bf16[1,4,8,256]{3,1,2,0:T(4,128)(2,1)S(1)}, bf16[1,4,8,256]{3,1,2,0:T(4,128)(2,1)}, u32[]{:S(2)}, u32[]{:S(2)}) collective-permute-start(bf16[1,4,8,256]{3,1,2,0:T(4,128)(2,1)S(1)} %copy.17), channel_id=1, source_target_pairs={{1,2},{2,1},{3,4},{4,3},{5,6},{6,5},{9,10},{10,9},{11,12},{12,11},... | collective-permute-start | bytes 49160 | tf_op jit(solution)/shard_map/ppermute | solution.py:725
  11.9 6.3 %collective-permute-start = (f32[1,120,128]{2,1,0:T(8,128)S(1)}, f32[1,120,128]{2,1,0:T(8,128)S(1)}, u32[]{:S(2)}, u32[]{:S(2)}) collective-permute-start(f32[1,120,128]{2,1,0:T(8,128)S(1)} %constant_dynamic-slice_fusion), channel_id=1, source_target_pairs={{0,1},{1,0},{2,3},{3,2},{4,5},{5,4},{6,7},{7,6},{8,9},{9,8},{10,11... | collective-permute-start | bytes 184328 | tf_op jit(solution)/shard_map/ppermute | solution.py:723
  18.1 4.0 %copy-start.4 = (s32[2]{0:T(128)}, s32[2]{0:T(128)S(1)}, u32[]{:S(2)}) copy-start(s32[2]{0:T(128)S(1)} %pad_add_fusion.where_ref) | copy-start | bytes 28
  22.1 1.2 %copy-start.1 = (bf16[17,208,256]{2,1,0:T(8,128)(2,1)}, bf16[17,208,256]{2,1,0:T(8,128)(2,1)S(1)}, u32[]{:S(2)}) copy-start(bf16[17,208,256]{2,1,0:T(8,128)(2,1)S(1)} %brick_windows.1.brick_ref) | copy-start | bytes 5431300
  23.4 12.5 %copy-start.8 = (bf16[9,32,32]{2,1,0:T(8,128)(2,1)S(1)}, bf16[9,32,32]{2,1,0:T(8,128)(2,1)}, u32[]{:S(2)}) copy-start(bf16[9,32,32]{2,1,0:T(8,128)(2,1)} %w_mid.1) | copy-start | bytes 55300
  24.0 11.9 %copy-start.5 = (s32[2]{0:T(128)S(1)}, s32[2]{0:T(128)}, u32[]{:S(2)}) copy-start(s32[2]{0:T(128)} %copy-done.4) | copy-start | bytes 28
  31.6 9.4 %all-to-all-start.1 = ((bf16[8,40,128]{2,1,0:T(8,128)(2,1)}), bf16[8,40,128]{2,1,0:T(8,128)(2,1)S(1)}, u32[]{:S(2)}, u32[]{:S(2)}) async-start(bf16[8,40,128]{2,1,0:T(8,128)(2,1)} %sample_values.1), calls=%async_computation.1 | async-start | bytes 163840 | tf_op jit(solution)/shard_map/all_to_all | solution.py:736
  35.9 1.7 %copy-start.9 = (bf16[9,112,32]{1,2,0:T(8,128)(2,1)S(1)}, bf16[9,112,32]{1,2,0:T(8,128)(2,1)}, u32[]{:S(2)}) copy-start(bf16[9,112,32]{1,2,0:T(8,128)(2,1)} %param.20) | copy-start | bytes 193540
  37.6 3.5 %copy-start.2 = (s32[1,1,160,256]{3,2,1,0:T(8,128)S(1)}, s32[1,1,160,256]{3,2,1,0:T(8,128)}, u32[]{:S(2)}) copy-start(s32[1,1,160,256]{3,2,1,0:T(8,128)} %order_ref.1) | copy-start | bytes 491524
  37.6 5.2 %copy-start.6 = (bf16[9,112,112]{2,1,0:T(8,128)(2,1)S(1)}, bf16[9,112,112]{2,1,0:T(8,128)(2,1)}, u32[]{:S(2)}) copy-start(bf16[9,112,112]{2,1,0:T(8,128)(2,1)} %w_deep.1) | copy-start | bytes 677380
  37.6 5.2 %copy-start.7 = (bf16[9,32,144]{2,1,0:T(8,128)(2,1)S(1)}, bf16[9,32,144]{2,1,0:T(8,128)(2,1)}, u32[]{:S(2)}) copy-start(bf16[9,32,144]{2,1,0:T(8,128)(2,1)} %w_up.1) | copy-start | bytes 248836
  41.3 4.7 %collective-permute-start.3 = (bf16[1,4,8,256]{3,2,1,0:T(8,128)(2,1)S(1)}, bf16[1,4,8,256]{3,2,1,0:T(8,128)(2,1)S(1)}, u32[]{:S(2)}, u32[]{:S(2)}) collective-permute-start(bf16[1,4,8,256]{3,2,1,0:T(8,128)(2,1)S(1)} %gbuffer.1), channel_id=1, source_target_pairs={{0,8},{8,16},{16,24},{24,0},{1,9},{9,17},{17,25},{25,1},{2,10},{10... | collective-permute-start | bytes 49160 | tf_op jit(solution)/shard_map/ppermute | solution.py:748

commit v17 on v16

--- a/solution.py
+++ b/solution.py
@@ -490,6 +490,17 @@
     return jnp.concatenate([taps(weight_ref, tap) for tap in range(3)], axis=1)
 
 
+def beside_padded(weight_ref, spare):
+    few = weight_ref.shape[1]
+    spare[...] = jnp.zeros_like(spare)
+    for tap in range(3):
+        for column in range(3):
+            spare[tap, column * TAIL : column * TAIL + few, :] = weight_ref[
+                3 * tap + column
+            ].astype(F32)
+    return jnp.concatenate([spare[tap].astype(BF16) for tap in range(3)], axis=1)
+
+
 def sides(where_ref):
     above = jnp.where(where_ref[0] > 0, 1.0, 0.0)
     below = jnp.where(where_ref[0] < where_ref[1] - 1, 1.0, 0.0)
@@ -500,14 +511,23 @@
     return inside
 
 
-def turned(weight_ref):
-    _, chans, out_chans = weight_ref.shape
+def turned(weight_ref, spare=None):
+    _, few, out_chans = weight_ref.shape
     here = lax.broadcasted_iota(jnp.int32, (out_chans, out_chans), 0)
     there = lax.broadcasted_iota(jnp.int32, (out_chans, out_chans), 1)
     unit = jnp.where(here == there, 1.0, 0.0).astype(BF16)
+    if spare is not None:
+        spare[...] = jnp.zeros_like(spare)
     rows = []
     for column in range(3):
-        stack = jnp.concatenate([weight_ref[3 * tap + column] for tap in range(3)], axis=0)
+        if spare is None:
+            stack = jnp.concatenate([weight_ref[3 * tap + column] for tap in range(3)], axis=0)
+        else:
+            for tap in range(3):
+                spare[column, tap * TAIL : tap * TAIL + few, :] = weight_ref[
+                    3 * tap + column
+                ].astype(F32)
+            stack = spare[column].astype(BF16)
         rows.append(
             lax.dot_general(
                 unit, stack, (((1,), (1,)), ((), ())), preferred_element_type=F32
@@ -516,10 +536,17 @@
     return jnp.concatenate(rows, axis=0).astype(BF16)
 
 
-def stem_kernel(where_ref, x_ref, w_in, w_mid, second, first):
-    height = x_ref.shape[0] // 3
-    width = x_ref.shape[2]
+def stem_kernel(
+    where_ref, own_ref, near_ref, far_ref, w_in, w_mid, second, x_ref, first, spare
+):
+    height, chans, width = own_ref.shape
     inside = sides(where_ref)
+    first_core = lax.rem(where_ref[0], 2) == 0
+    near, far = near_ref[...].astype(F32), far_ref[...].astype(F32)
+    x_ref[...] = jnp.zeros_like(x_ref)
+    x_ref[:height, :chans, :] = jnp.where(first_core, far, near).astype(BF16)
+    x_ref[height : 2 * height, :chans, :] = own_ref[...]
+    x_ref[2 * height :, :chans, :] = jnp.where(first_core, near, far).astype(BF16)
 
     def full_layer(weight, source, target, low, high, unroll):
         chans = target.shape[1]
@@ -533,7 +560,7 @@
 
         lax.fori_loop(0, target.shape[0], step, 0, unroll=unroll)
 
-    full_layer(turned(w_in), x_ref, first, height - 1, 2 * height - 1, first.shape[0])
+    full_layer(turned(w_in, spare), x_ref, first, height - 1, 2 * height - 1, first.shape[0])
     full_layer(beside(w_mid), first, second, height - 2, 2 * height - 2, second.shape[0])
 
 
@@ -574,7 +601,7 @@
 
 
 def decoder_kernel(
-    where_ref, second, third, w_deep, w_up, w_out, out_ref, fourth, joined, fifth, final
+    where_ref, second, third, w_deep, w_up, w_out, out_ref, fourth, joined, fifth, final, spare
 ):
     height = out_ref.shape[2]
     half_height = height // 2
@@ -616,32 +643,35 @@
     lax.fori_loop(0, fifth.shape[0], up_step, 0, unroll=fifth.shape[0])
 
     colours = out_ref.shape[1]
-    weight_out = beside(w_out)
+    weight_out = beside_padded(w_out, spare)
     for row in range(height):
         lines = fifth[row : row + 3].reshape(3 * chans, width)
         total = jnp.dot(weight_out, lines, preferred_element_type=F32)
-        line = across(total, w_out.shape[1], width)
+        line = across(total, TAIL, width)
         for colour in range(colours):
             final[colour, row : row + 1, :] = line[colour : colour + 1, :]
     out_ref[0] = final[...].astype(BF16)
 
 
-def stem(where, field, w_in, w_mid):
-    height = field.shape[0] // 3
-    width = field.shape[2]
+def stem(where, own, near, far, w_in, w_mid):
+    height, _, width = own.shape
     one = w_mid.shape[1]
     return pl.pallas_call(
         stem_kernel,
         out_shape=jax.ShapeDtypeStruct((3 * height - 4, one, width), BF16),
-        in_specs=[smem()] + [vmem()] * 3,
+        in_specs=[smem()] + [vmem()] * 5,
         out_specs=vmem(),
-        scratch_shapes=[pltpu.VMEM((3 * height - 2, one, width), BF16)],
+        scratch_shapes=[
+            pltpu.VMEM((3 * height, TAIL, width), BF16),
+            pltpu.VMEM((3 * height - 2, one, width), BF16),
+            pltpu.VMEM((3, 3 * TAIL, one), F32),
+        ],
         compiler_params=params(16),
         cost_estimate=pl.CostEstimate(
             flops=1_000_000_000, bytes_accessed=MIB, transcendentals=300_000
         ),
         name="stem",
-    )(where, field, w_in, w_mid)
+    )(where, own, near, far, w_in, w_mid)
 
 
 def middle(where, second, w_down):
@@ -676,6 +706,7 @@
             pltpu.VMEM((height + 4, one + two, width), BF16),
             pltpu.VMEM((height + 2, one, width), BF16),
             pltpu.VMEM((colours, height, width), F32),
+            pltpu.VMEM((3, 3 * TAIL, one), F32),
         ],
         compiler_params=params(16),
         cost_estimate=pl.CostEstimate(
@@ -721,25 +752,17 @@
     ]
     for_mate = lax.dynamic_slice_in_dim(places, mate_of(tile), 1, 0)
     mate_places = lax.ppermute(for_mate, "tile", mates)
-    near = lax.ppermute(pending, "tile", mates)
-    far = lax.ppermute(pending, "tile", across_chips)
+    rows = pending[0].transpose(1, 0, 2)
+    near = lax.ppermute(rows, "tile", mates)
+    far = lax.ppermute(rows, "tile", across_chips)
     picks = sends[0, 0].T
     colours = w_out.shape[1]
-    w_in = w_in.transpose(0, 2, 1)
-    w_in = jnp.pad(w_in, ((0, 0), (0, 16 - w_in.shape[1]), (0, 0)))
-    w_out = jnp.pad(w_out, ((0, 0), (0, 16 - colours), (0, 0)))
     windows = windows_of(where, picks, bricks, places, mate_places)
-    arrived, w_in, w_out = lax.optimization_barrier((arrived, w_in, w_out))
     found = sample_values(where, picks, windows, arrived)
 
-    found, near, far, pending = lax.optimization_barrier((found, near, far, pending))
+    found, rows, near, far = lax.optimization_barrier((found, rows, near, far))
     values = lax.all_to_all(found, "tile", split_axis=0, concat_axis=0, tiled=True)
-    first_core = tile % 2 == 0
-    over = jnp.where(first_core, far, near)
-    under = jnp.where(first_core, near, far)
-    field = jnp.concatenate([over[0], pending[0], under[0]], axis=1).transpose(1, 0, 2)
-    field = jnp.pad(field, ((0, 0), (0, 16 - field.shape[1]), (0, 0)))
-    second = stem(where, field, w_in, w_mid)
+    second = stem(where, rows, near, far, w_in.transpose(0, 2, 1), w_mid)
     third = middle(where, second, w_down.transpose(0, 2, 1))
     values, third = lax.optimization_barrier((values, third))
     rendered = gbuffer(trim(values), sample_order, height, width)

time: 47.2 us -> 47 us (level)
  waiting for transfers between devices: 3.04 us -> 4.64 us
  local copies, waits for them, and re-layouts: 6.48 us -> 5.67 us
  other arithmetic: 0.87 us -> 0.08 us
    pad x3 -> x0, local copies, waits for them, and re-layouts: 1.45 us -> none  [the longest x1 0.71 us: on_device(): w_in = jnp.pad(w_in, ((0, 0), (0, 16 - w_in.shape[1]), (0, 0)))]
    all_to_all x1, waiting for transfers between devices: 0.57 us -> 1.38 us  [on_device(): lax.all_to_all(places, 'tile', split_axis=0, concat_axis=0, tiled=True)]
    all_to_all x1, waiting for transfers between devices: 2.19 us -> 2.99 us  [on_device(): lax.all_to_all(found, 'tile', split_axis=0, concat_axis=0, tiled=True)]
    squeeze x1 -> x0, other arithmetic: 0.76 us -> none  [on_device(): over[0]]
    dynamic_slice x1, local copies, waits for them, and re-layouts: 0.83 us -> 1.45 us  [on_device(): for_mate = lax.dynamic_slice_in_dim(places, mate_of(tile), 1, 0)]
    ppermute x2, starting transfers between devices: 1.8 us -> 1.21 us  [the longest x1 0.65 us: on_device(): far = lax.ppermute(rows, 'tile', across_chips)]
    ppermute x1, starting transfers between devices: 2.46 us -> 3.03 us  [on_device(): mate_places = lax.ppermute(for_mate, 'tile', mates)]
    unnamed x25 -> x29, local copies, waits for them, and re-layouts: 1.89 us -> 1.9 us
  transfers between devices with their start and end apart: 6 -> 6, of which waited for: 3 -> 3; matrix products, arithmetic and copies ran while one was open for 12% -> 8% of each run, Pallas kernels for 37% -> 37%
where the time goes in v17:
time: 47 us; the launch traced here: 46.6 us
  Pallas kernels  19.9 us (42%)
  starting transfers between devices  15.5 us (33%)
  local copies, waits for them, and re-layouts  5.67 us (12%)
  waiting for transfers between devices  4.64 us (10%)
  between operations  0.87 us (2%)
    pallas_call x1, Pallas kernels, sample_values(): pl.pallas_call(samples_kernel, out_shape=jax.ShapeDtypeStruct((owners, ro...  7.66 us
    all_to_all x1, starting transfers between devices, on_device(): lax.all_to_all(places, 'tile', split_axis=0, concat_axis=0, tiled=True)  6.34 us
    pallas_call x1, Pallas kernels, windows_of(): pl.pallas_call(windows_kernel, out_shape=jax.ShapeDtypeStruct((count + 1,...  3.97 us
    all_to_all x1, starting transfers between devices, on_device(): lax.all_to_all(found, 'tile', split_axis=0, concat_axis=0, tiled=True)  3.37 us
    ppermute x1, starting transfers between devices, on_device(): mate_places = lax.ppermute(for_mate, 'tile', mates)  3.03 us
    all_to_all x1, waiting for transfers between devices, on_device(): lax.all_to_all(found, 'tile', split_axis=0, concat_axis=0, tiled=True)  2.99 us
    pallas_call x1, Pallas kernels, decoder(): pl.pallas_call(decoder_kernel, out_shape=jax.ShapeDtypeStruct((1, colours...  2.88 us
    reshape x1, local copies, waits for them, and re-layouts, windows_of(): cube = bricks.reshape(count, EDGE, EDGE * EDGE)  2.31 us
  transfers between devices with their start and end apart: 6, of which 3 were waited for; matrix products, arithmetic and copies ran while one was open for 8% of the time, Pallas kernels for 37%

profile of v17, /device:TPU:0, one launch (start us, length us, event | category | flops | bytes accessed | tf_op | source)
XLA Modules:
  0.0 46.6 jit_solution(12524483204146308359)
XLA Ops:
  0.7 2.2 %positions.1.place_ref = f32[8,120,128]{2,1,0:T(8,128)} custom-call(s32[3,320,128]{2,1,0:T(8,128)} %bitcast.20, f32[3,320,128]{2,1,0:T(8,128)} %bitcast.21), custom_call_target="tpu_custom_call" | custom-call | flops 122880 | bytes 1474560 | tf_op jit(solution)/shard_map/positions/pallas_call | solution.py:82
  2.9 6.3 %all-to-all-start = ((f32[8,120,128]{2,1,0:T(8,128)}), f32[8,120,128]{2,1,0:T(8,128)}, u32[]{:S(2)}, u32[]{:S(2)}) async-start(f32[8,120,128]{2,1,0:T(8,128)} %positions.1.place_ref), calls=%async_computation | async-start | bytes 983040 | tf_op jit(solution)/shard_map/all_to_all | solution.py:746
  9.2 0.0 copy-start.3
  9.2 0.6 %collective-permute-start.1 = (bf16[8,4,256]{2,1,0:T(4,128)(2,1)S(1)}, bf16[8,4,256]{2,1,0:T(4,128)(2,1)S(1)}, u32[]{:S(2)}, u32[]{:S(2)}) collective-permute-start(bf16[8,4,256]{2,1,0:T(4,128)(2,1)S(1)} %bitcast.13), channel_id=1, source_target_pairs={{0,1},{1,0},{2,3},{3,2},{4,5},{5,4},{6,7},{7,6},{8,9},{9,8},{10,11... | collective-permute-start | bytes 49160 | tf_op jit(solution)/shard_map/ppermute | solution.py:756
  9.8 0.7 %collective-permute-start.2 = (bf16[8,4,256]{2,1,0:T(4,128)(2,1)S(1)}, bf16[8,4,256]{2,1,0:T(4,128)(2,1)S(1)}, u32[]{:S(2)}, u32[]{:S(2)}) collective-permute-start(bf16[8,4,256]{2,1,0:T(4,128)(2,1)S(1)} %bitcast.14), channel_id=1, source_target_pairs={{1,2},{2,1},{3,4},{4,3},{5,6},{6,5},{9,10},{10,9},{11,12},{12,11},... | collective-permute-start | bytes 49160 | tf_op jit(solution)/shard_map/ppermute | solution.py:757
  10.5 1.5 %constant_dynamic-slice_fusion = f32[1,120,128]{2,1,0:T(8,128)} fusion(f32[8,120,128]{2,1,0:T(8,128)} %positions.1.place_ref, s32[]{:T(128)S(6)} %select_n.3), kind=kLoop, calls=%fused_computation.2 | loop fusion | bytes 122884 | tf_op jit(solution)/shard_map/dynamic_slice | solution.py:753
  11.9 3.0 %collective-permute-start = (f32[1,120,128]{2,1,0:T(8,128)}, f32[1,120,128]{2,1,0:T(8,128)S(1)}, u32[]{:S(2)}, u32[]{:S(2)}) collective-permute-start(f32[1,120,128]{2,1,0:T(8,128)} %constant_dynamic-slice_fusion), channel_id=1, source_target_pairs={{0,1},{1,0},{2,3},{3,2},{4,5},{5,4},{6,7},{7,6},{8,9},{9,8},{10,11... | collective-permute-start | bytes 184328 | tf_op jit(solution)/shard_map/ppermute | solution.py:754
  15.0 2.3 %reshape.15.cube_ref = bf16[16,34,1156]{2,1,0:T(8,128)(2,1)S(1)} reshape(bf16[16,39304]{1,0:T(8,128)(2,1)S(1)} %copy-done.12) | data formatting | bytes 2515456 | tf_op jit(solution)/shard_map/reshape | solution.py:166
  17.3 0.1 pad_add_fusion.where_ref
  17.4 4.0 %brick_windows.1.brick_ref = bf16[17,208,256]{2,1,0:T(8,128)(2,1)S(1)} custom-call(s32[2]{0:T(128)S(1)} %pad_add_fusion.where_ref, s32[2,8]{1,0:T(2,128)S(1)} %bitcast.17, bf16[16,34,1156]{2,1,0:T(8,128)(2,1)S(1)} %reshape.15.cube_ref, f32[8,120,128]{2,1,0:T(8,128)S(1)} %copy-done, f32[1,120,128]{2,1,0:T(8,128)S(1)} %collective-permute-done.mate_place_ref), custom_call_target="tpu_custom_call" | custom-call | flops 905969664 | bytes 4194304 | tf_op jit(solution)/shard_map/brick_windows/pallas_call | solution.py:168
  21.4 1.2 %copy-done.1 = bf16[17,208,256]{2,1,0:T(8,128)(2,1)} copy-done((bf16[17,208,256]{2,1,0:T(8,128)(2,1)}, bf16[17,208,256]{2,1,0:T(8,128)(2,1)S(1)}, u32[]{:S(2)}) %copy-start.1) | copy-done | bytes 1810456
  22.6 1.4 %all-to-all-done.place_ref = f32[8,120,128]{2,1,0:T(8,128)} async-done(((f32[8,120,128]{2,1,0:T(8,128)}), f32[8,120,128]{2,1,0:T(8,128)}, u32[]{:S(2)}, u32[]{:S(2)}) %all-to-all-start) | async-done | bytes 491552 | tf_op jit(solution)/shard_map/all_to_all | solution.py:746
  24.0 7.7 %sample_values.1 = bf16[8,40,128]{2,1,0:T(8,128)(2,1)} custom-call(s32[2]{0:T(128)} %copy-done.4, s32[2,8]{1,0:T(2,128)} %bitcast.16, bf16[17,208,256]{2,1,0:T(8,128)(2,1)} %copy-done.1, f32[8,120,128]{2,1,0:T(8,128)} %all-to-all-done.place_ref), custom_call_target="tpu_custom_call" | custom-call | flops 4362076160 | bytes 3145728 | tf_op jit(solution)/shard_map/sample_values/pallas_call | solution.py:373
  31.7 3.4 %all-to-all-start.1 = ((bf16[8,40,128]{2,1,0:T(8,128)(2,1)}), bf16[8,40,128]{2,1,0:T(8,128)(2,1)S(1)}, u32[]{:S(2)}, u32[]{:S(2)}) async-start(bf16[8,40,128]{2,1,0:T(8,128)(2,1)} %sample_values.1), calls=%async_computation.1 | async-start | bytes 163840 | tf_op jit(solution)/shard_map/all_to_all | solution.py:764
  35.1 0.0 copy-start.9
  35.1 1.7 %stem.1.second = bf16[20,32,256]{2,1,0:T(8,128)(2,1)S(1)} custom-call(s32[2]{0:T(128)S(1)} %copy-done.5, bf16[8,4,256]{2,1,0:T(4,128)(2,1)S(1)} %bitcast.15, bf16[8,4,256]{2,1,0:T(4,128)(2,1)S(1)} %collective-permute-done.1.near_ref, bf16[8,4,256]{2,1,0:T(4,128)(2,1)S(1)} %collective-permute-done.2.far_ref, bf16[9,4,32]{2,1,0:T(4,128)(2,1)S(1)} %bitcast.19, ...), custom_call_target="tpu_custom_call" | custom-call | flops 1000000000 | bytes 1048576 | tf_op jit(solution)/shard_map/stem/pallas_call | solution.py:659
  36.8 0.0 copy-start.2
  36.8 1.3 %middle.1.third = bf16[8,112,128]{2,1,0:T(8,128)(2,1)S(1)} custom-call(s32[2]{0:T(128)S(1)} %copy-done.5, bf16[20,32,256]{2,1,0:T(8,128)(2,1)S(1)} %stem.1.second, bf16[9,32,112]{2,1,0:T(8,128)(2,1)S(1)} %bitcast.18), custom_call_target="tpu_custom_call" | custom-call | flops 500000000 | bytes 1048576 | tf_op jit(solution)/shard_map/middle/pallas_call | solution.py:681
  38.1 3.0 %all-to-all-done.1.value_ref = bf16[8,40,128]{2,1,0:T(8,128)(2,1)S(1)} async-done(((bf16[8,40,128]{2,1,0:T(8,128)(2,1)}), bf16[8,40,128]{2,1,0:T(8,128)(2,1)S(1)}, u32[]{:S(2)}, u32[]{:S(2)}) %all-to-all-start.1) | async-done | bytes 81952 | tf_op jit(solution)/shard_map/all_to_all | solution.py:764
  41.1 0.2 gbuffer.1
  41.3 1.5 %collective-permute-start.3 = (bf16[1,4,8,256]{3,2,1,0:T(8,128)(2,1)S(1)}, bf16[1,4,8,256]{3,2,1,0:T(8,128)(2,1)S(1)}, u32[]{:S(2)}, u32[]{:S(2)}) collective-permute-start(bf16[1,4,8,256]{3,2,1,0:T(8,128)(2,1)S(1)} %gbuffer.1), channel_id=1, source_target_pairs={{0,8},{8,16},{16,24},{24,0},{1,9},{9,17},{17,25},{25,1},{2,10},{10... | collective-permute-start | bytes 49160 | tf_op jit(solution)/shard_map/ppermute | solution.py:771
  42.8 2.9 %decoder.1 = bf16[1,3,8,256]{3,2,1,0:T(8,128)(2,1)} custom-call(s32[2]{0:T(128)S(1)} %copy-done.5, bf16[20,32,256]{2,1,0:T(8,128)(2,1)S(1)} %stem.1.second, bf16[8,112,128]{2,1,0:T(8,128)(2,1)S(1)} %middle.1.third, bf16[9,112,112]{2,1,0:T(8,128)(2,1)S(1)} %copy-done.6, bf16[9,32,144]{2,1,0:T(8,128)(2,1)S(1)} %copy-done.7, bf16[9,3,32]{2,1,0:T(4,128)(2,1)S(1)} %copy-done.11), custom_call_target="tpu_custom_call" | custom-call | flops 1500000000 | bytes 1048576 | tf_op jit(solution)/shard_map/decoder/pallas_call | solution.py:699
  45.7 0.3 collective-permute-done.3
  46.0 0.6 %copy.19 = bf16[1,4,8,256]{3,2,1,0:T(8,128)(2,1)} copy(bf16[1,4,8,256]{3,2,1,0:T(8,128)(2,1)S(1)} %collective-permute-done.3) | data formatting | bytes 32768
  (28 shorter events, 0.1 us)
Async XLA Ops:
  0.6 14.3 %copy-start.12 = (bf16[16,39304]{1,0:T(8,128)(2,1)S(1)}, bf16[16,39304]{1,0:T(8,128)(2,1)}, u32[]{:S(2)}) copy-start(bf16[16,39304]{1,0:T(8,128)(2,1)} %param.12) | copy-start | bytes 3773188
  0.6 8.6 %copy-start.13 = (bf16[1,4,8,256]{3,2,1,0:T(8,128)(2,1)S(1)}, bf16[1,4,8,256]{3,2,1,0:T(8,128)(2,1)}, u32[]{:S(2)}) copy-start(bf16[1,4,8,256]{3,2,1,0:T(8,128)(2,1)} %param.17) | copy-start | bytes 49156
  2.9 21.1 %all-to-all-start = ((f32[8,120,128]{2,1,0:T(8,128)}), f32[8,120,128]{2,1,0:T(8,128)}, u32[]{:S(2)}, u32[]{:S(2)}) async-start(f32[8,120,128]{2,1,0:T(8,128)} %positions.1.place_ref), calls=%async_computation | async-start | bytes 983040 | tf_op jit(solution)/shard_map/all_to_all | solution.py:746
  9.2 8.1 %copy-start = (f32[8,120,128]{2,1,0:T(8,128)S(1)}, f32[8,120,128]{2,1,0:T(8,128)}, u32[]{:S(2)}) copy-start(f32[8,120,128]{2,1,0:T(8,128)} %positions.1.place_ref) | copy-start | bytes 1474564
  9.2 8.1 %copy-start.3 = (s32[1,1,8,2]{2,3,1,0:T(2,128)S(1)}, s32[1,1,8,2]{2,3,1,0:T(2,128)}, u32[]{:S(2)}) copy-start(s32[1,1,8,2]{2,3,1,0:T(2,128)} %param.13) | copy-start | bytes 196
  9.2 22.4 %collective-permute-start.1 = (bf16[8,4,256]{2,1,0:T(4,128)(2,1)S(1)}, bf16[8,4,256]{2,1,0:T(4,128)(2,1)S(1)}, u32[]{:S(2)}, u32[]{:S(2)}) collective-permute-start(bf16[8,4,256]{2,1,0:T(4,128)(2,1)S(1)} %bitcast.13), channel_id=1, source_target_pairs={{0,1},{1,0},{2,3},{3,2},{4,5},{5,4},{6,7},{7,6},{8,9},{9,8},{10,11... | collective-permute-start | bytes 49160 | tf_op jit(solution)/shard_map/ppermute | solution.py:756
  9.8 21.9 %collective-permute-start.2 = (bf16[8,4,256]{2,1,0:T(4,128)(2,1)S(1)}, bf16[8,4,256]{2,1,0:T(4,128)(2,1)S(1)}, u32[]{:S(2)}, u32[]{:S(2)}) collective-permute-start(bf16[8,4,256]{2,1,0:T(4,128)(2,1)S(1)} %bitcast.14), channel_id=1, source_target_pairs={{1,2},{2,1},{3,4},{4,3},{5,6},{6,5},{9,10},{10,9},{11,12},{12,11},... | collective-permute-start | bytes 49160 | tf_op jit(solution)/shard_map/ppermute | solution.py:757
  11.9 5.4 %collective-permute-start = (f32[1,120,128]{2,1,0:T(8,128)}, f32[1,120,128]{2,1,0:T(8,128)S(1)}, u32[]{:S(2)}, u32[]{:S(2)}) collective-permute-start(f32[1,120,128]{2,1,0:T(8,128)} %constant_dynamic-slice_fusion), channel_id=1, source_target_pairs={{0,1},{1,0},{2,3},{3,2},{4,5},{5,4},{6,7},{7,6},{8,9},{9,8},{10,11... | collective-permute-start | bytes 184328 | tf_op jit(solution)/shard_map/ppermute | solution.py:754
  17.3 4.0 %copy-start.4 = (s32[2]{0:T(128)}, s32[2]{0:T(128)S(1)}, u32[]{:S(2)}) copy-start(s32[2]{0:T(128)S(1)} %pad_add_fusion.where_ref) | copy-start | bytes 28
  21.3 1.2 %copy-start.1 = (bf16[17,208,256]{2,1,0:T(8,128)(2,1)}, bf16[17,208,256]{2,1,0:T(8,128)(2,1)S(1)}, u32[]{:S(2)}) copy-start(bf16[17,208,256]{2,1,0:T(8,128)(2,1)S(1)} %brick_windows.1.brick_ref) | copy-start | bytes 5431300
  22.6 12.5 %copy-start.8 = (bf16[9,32,32]{2,1,0:T(8,128)(2,1)S(1)}, bf16[9,32,32]{2,1,0:T(8,128)(2,1)}, u32[]{:S(2)}) copy-start(bf16[9,32,32]{2,1,0:T(8,128)(2,1)} %w_mid.1) | copy-start | bytes 55300
  22.6 12.5 %copy-start.10 = (bf16[9,32,4]{1,2,0:T(4,128)(2,1)S(1)}, bf16[9,32,4]{1,2,0:T(4,128)(2,1)}, u32[]{:S(2)}) copy-start(bf16[9,32,4]{1,2,0:T(4,128)(2,1)} %param.18) | copy-start | bytes 6916
  24.0 11.1 %copy-start.5 = (s32[2]{0:T(128)S(1)}, s32[2]{0:T(128)}, u32[]{:S(2)}) copy-start(s32[2]{0:T(128)} %copy-done.4) | copy-start | bytes 28
  31.7 9.4 %all-to-all-start.1 = ((bf16[8,40,128]{2,1,0:T(8,128)(2,1)}), bf16[8,40,128]{2,1,0:T(8,128)(2,1)S(1)}, u32[]{:S(2)}, u32[]{:S(2)}) async-start(bf16[8,40,128]{2,1,0:T(8,128)(2,1)} %sample_values.1), calls=%async_computation.1 | async-start | bytes 163840 | tf_op jit(solution)/shard_map/all_to_all | solution.py:764
  35.1 1.8 %copy-start.9 = (bf16[9,112,32]{1,2,0:T(8,128)(2,1)S(1)}, bf16[9,112,32]{1,2,0:T(8,128)(2,1)}, u32[]{:S(2)}) copy-start(bf16[9,112,32]{1,2,0:T(8,128)(2,1)} %param.20) | copy-start | bytes 193540
  36.8 4.3 %copy-start.2 = (s32[1,1,160,256]{3,2,1,0:T(8,128)S(1)}, s32[1,1,160,256]{3,2,1,0:T(8,128)}, u32[]{:S(2)}) copy-start(s32[1,1,160,256]{3,2,1,0:T(8,128)} %order_ref.1) | copy-start | bytes 491524
  36.8 6.1 %copy-start.6 = (bf16[9,112,112]{2,1,0:T(8,128)(2,1)S(1)}, bf16[9,112,112]{2,1,0:T(8,128)(2,1)}, u32[]{:S(2)}) copy-start(bf16[9,112,112]{2,1,0:T(8,128)(2,1)} %w_deep.1) | copy-start | bytes 677380
  36.8 6.1 %copy-start.7 = (bf16[9,32,144]{2,1,0:T(8,128)(2,1)S(1)}, bf16[9,32,144]{2,1,0:T(8,128)(2,1)}, u32[]{:S(2)}) copy-start(bf16[9,32,144]{2,1,0:T(8,128)(2,1)} %w_up.1) | copy-start | bytes 248836
  36.8 6.0 %copy-start.11 = (bf16[9,3,32]{2,1,0:T(4,128)(2,1)S(1)}, bf16[9,3,32]{2,1,0:T(4,128)(2,1)}, u32[]{:S(2)}) copy-start(bf16[9,3,32]{2,1,0:T(4,128)(2,1)} %w_out.1) | copy-start | bytes 5188
  41.3 4.7 %collective-permute-start.3 = (bf16[1,4,8,256]{3,2,1,0:T(8,128)(2,1)S(1)}, bf16[1,4,8,256]{3,2,1,0:T(8,128)(2,1)S(1)}, u32[]{:S(2)}, u32[]{:S(2)}) collective-permute-start(bf16[1,4,8,256]{3,2,1,0:T(8,128)(2,1)S(1)} %gbuffer.1), channel_id=1, source_target_pairs={{0,8},{8,16},{16,24},{24,0},{1,9},{9,17},{17,25},{25,1},{2,10},{10... | collective-permute-start | bytes 49160 | tf_op jit(solution)/shard_map/ppermute | solution.py:771

commit v18 on v17

--- a/solution.py
+++ b/solution.py
@@ -59,12 +59,16 @@
             found.at[place], out_ref.at[place], departures.at[axis, part]
         )
 
-    for piece in pieces:
+    ahead = 3
+    for piece in pieces[:ahead]:
         for copy in reads(*piece):
             copy.start()
-    for axis, part in pieces:
+    for number, (axis, part) in enumerate(pieces):
         for copy in reads(axis, part):
             copy.wait()
+        for piece in pieces[number + ahead : number + ahead + 1]:
+            for copy in reads(*piece):
+                copy.start()
         span = slice(part * share * lines, (part + 1) * share * lines)
         place = cells[axis, span].astype(F32) + fracs[axis, span]
         found[part * share : (part + 1) * share, axis * lines : (axis + 1) * lines, :] = (
@@ -88,8 +92,8 @@
             pltpu.VMEM(cells.shape, jnp.int32),
             pltpu.VMEM(fracs.shape, F32),
             pltpu.VMEM(shape, F32),
-            pltpu.SemaphoreType.DMA((3, 4, 2)),
-            pltpu.SemaphoreType.DMA((3, 4)),
+            pltpu.SemaphoreType.DMA((3, 2, 2)),
+            pltpu.SemaphoreType.DMA((3, 2)),
         ],
         compiler_params=params(60),
         cost_estimate=pl.CostEstimate(
@@ -117,7 +121,7 @@
         copy.start()
     count = cube_ref.shape[0]
     plane = EDGE * EDGE
-    wide[...] = jnp.zeros_like(wide)
+    wide[:, :, plane // LANES * LANES :] = jnp.zeros((count, wide.shape[1], LANES), BF16)
     wide[:, :EDGE, :plane] = cube_ref[...]
     column = lax.broadcasted_iota(jnp.int32, (1, KDIM), 1)
     main = (column // MAIN) * EDGE + column % MAIN
@@ -321,6 +325,23 @@
         held = turn % 2
         for copy in fetches(turn, members):
             copy.wait()
+
+        if members == 2:
+
+            @pl.when(turn + 1 < pairs)
+            def _():
+                start(turn + 1, 2)
+
+            if rest:
+
+                @pl.when(turn + 1 == pairs)
+                def _():
+                    start(pairs, 1)
+
+            @pl.when(turn == 0)
+            def _():
+                own_values.start()
+
         for member in range(members):
             for piece in range(cap):
                 slot_sums(
@@ -338,26 +359,17 @@
     def one_pair(turn, carry):
         work(turn, 2)
 
-        @pl.when(turn + 2 < pairs)
-        def _():
-            start(turn + 2, 2)
-
-        if rest:
-
-            @pl.when(turn + 2 == pairs)
-            def _():
-                start(pairs, 1)
-
         return carry
 
-    for turn in range(min(2, pairs)):
-        start(turn, 2)
-    if rest and pairs < 2:
-        start(pairs, 1)
-    own_values.start()
+    if pairs > 0:
+        start(0, 2)
+    elif rest:
+        start(0, 1)
     lax.fori_loop(0, pairs, one_pair, 0)
     if rest:
         work(pairs, 1)
+    if pairs == 0:
+        own_values.start()
     own_values.wait()
     height = whole_tiles(lines)
     for i, renderer in enumerate((tile, mate_of(tile))):

time: 47 us -> 47.9 us (1.019)
  Pallas kernels: 19.9 us -> 20.6 us
    pallas_call x1, Pallas kernels: 2.2 us -> 3.03 us  [positions(): pl.pallas_call(positions_kernel, out_shape=jax.ShapeDtypeStruct(shape, F3...]
where the time goes in v18:
time: 47.9 us; the launch traced here: 47.4 us
  Pallas kernels  20.6 us (43%)
  starting transfers between devices  15.5 us (32%)
  local copies, waits for them, and re-layouts  5.67 us (12%)
  waiting for transfers between devices  4.69 us (10%)
  between operations  0.87 us (2%)
    pallas_call x1, Pallas kernels, sample_values(): pl.pallas_call(samples_kernel, out_shape=jax.ShapeDtypeStruct((owners, ro...  7.66 us
    all_to_all x1, starting transfers between devices, on_device(): lax.all_to_all(places, 'tile', split_axis=0, concat_axis=0, tiled=True)  6.34 us
    pallas_call x1, Pallas kernels, windows_of(): pl.pallas_call(windows_kernel, out_shape=jax.ShapeDtypeStruct((count + 1,...  3.93 us
    all_to_all x1, starting transfers between devices, on_device(): lax.all_to_all(found, 'tile', split_axis=0, concat_axis=0, tiled=True)  3.37 us
    pallas_call x1, Pallas kernels, positions(): pl.pallas_call(positions_kernel, out_shape=jax.ShapeDtypeStruct(shape, F3...  3.03 us
    ppermute x1, starting transfers between devices, on_device(): mate_places = lax.ppermute(for_mate, 'tile', mates)  3.03 us
    all_to_all x1, waiting for transfers between devices, on_device(): lax.all_to_all(found, 'tile', split_axis=0, concat_axis=0, tiled=True)  3 us
    pallas_call x1, Pallas kernels, decoder(): pl.pallas_call(decoder_kernel, out_shape=jax.ShapeDtypeStruct((1, colours...  2.88 us
  transfers between devices with their start and end apart: 6, of which 3 were waited for; matrix products, arithmetic and copies ran while one was open for 8% of the time, Pallas kernels for 37%

profile of v18, /device:TPU:0, one launch (start us, length us, event | category | flops | bytes accessed | tf_op | source)
XLA Modules:
  0.0 47.4 jit_solution(4254862004881436952)
XLA Ops:
  0.7 3.0 %positions.1.place_ref = f32[8,120,128]{2,1,0:T(8,128)} custom-call(s32[3,320,128]{2,1,0:T(8,128)} %bitcast.20, f32[3,320,128]{2,1,0:T(8,128)} %bitcast.21), custom_call_target="tpu_custom_call" | custom-call | flops 122880 | bytes 1474560 | tf_op jit(solution)/shard_map/positions/pallas_call | solution.py:86
  3.7 6.3 %all-to-all-start = ((f32[8,120,128]{2,1,0:T(8,128)}), f32[8,120,128]{2,1,0:T(8,128)}, u32[]{:S(2)}, u32[]{:S(2)}) async-start(f32[8,120,128]{2,1,0:T(8,128)} %positions.1.place_ref), calls=%async_computation | async-start | bytes 983040 | tf_op jit(solution)/shard_map/all_to_all | solution.py:758
  10.0 0.0 copy-start.3
  10.1 0.6 %collective-permute-start.1 = (bf16[8,4,256]{2,1,0:T(4,128)(2,1)S(1)}, bf16[8,4,256]{2,1,0:T(4,128)(2,1)S(1)}, u32[]{:S(2)}, u32[]{:S(2)}) collective-permute-start(bf16[8,4,256]{2,1,0:T(4,128)(2,1)S(1)} %bitcast.13), channel_id=1, source_target_pairs={{0,1},{1,0},{2,3},{3,2},{4,5},{5,4},{6,7},{7,6},{8,9},{9,8},{10,11... | collective-permute-start | bytes 49160 | tf_op jit(solution)/shard_map/ppermute | solution.py:768
  10.6 0.7 %collective-permute-start.2 = (bf16[8,4,256]{2,1,0:T(4,128)(2,1)S(1)}, bf16[8,4,256]{2,1,0:T(4,128)(2,1)S(1)}, u32[]{:S(2)}, u32[]{:S(2)}) collective-permute-start(bf16[8,4,256]{2,1,0:T(4,128)(2,1)S(1)} %bitcast.14), channel_id=1, source_target_pairs={{1,2},{2,1},{3,4},{4,3},{5,6},{6,5},{9,10},{10,9},{11,12},{12,11},... | collective-permute-start | bytes 49160 | tf_op jit(solution)/shard_map/ppermute | solution.py:769
  11.3 1.5 %constant_dynamic-slice_fusion = f32[1,120,128]{2,1,0:T(8,128)} fusion(f32[8,120,128]{2,1,0:T(8,128)} %positions.1.place_ref, s32[]{:T(128)S(6)} %select_n.3), kind=kLoop, calls=%fused_computation.2 | loop fusion | bytes 122884 | tf_op jit(solution)/shard_map/dynamic_slice | solution.py:765
  12.8 3.0 %collective-permute-start = (f32[1,120,128]{2,1,0:T(8,128)}, f32[1,120,128]{2,1,0:T(8,128)S(1)}, u32[]{:S(2)}, u32[]{:S(2)}) collective-permute-start(f32[1,120,128]{2,1,0:T(8,128)} %constant_dynamic-slice_fusion), channel_id=1, source_target_pairs={{0,1},{1,0},{2,3},{3,2},{4,5},{5,4},{6,7},{7,6},{8,9},{9,8},{10,11... | collective-permute-start | bytes 184328 | tf_op jit(solution)/shard_map/ppermute | solution.py:766
  15.8 2.3 %reshape.15.cube_ref = bf16[16,34,1156]{2,1,0:T(8,128)(2,1)S(1)} reshape(bf16[16,39304]{1,0:T(8,128)(2,1)S(1)} %copy-done.12) | data formatting | bytes 2515456 | tf_op jit(solution)/shard_map/reshape | solution.py:170
  18.1 0.1 pad_add_fusion.where_ref
  18.2 3.9 %brick_windows.1.brick_ref = bf16[17,208,256]{2,1,0:T(8,128)(2,1)S(1)} custom-call(s32[2]{0:T(128)S(1)} %pad_add_fusion.where_ref, s32[2,8]{1,0:T(2,128)S(1)} %bitcast.17, bf16[16,34,1156]{2,1,0:T(8,128)(2,1)S(1)} %reshape.15.cube_ref, f32[8,120,128]{2,1,0:T(8,128)S(1)} %copy-done, f32[1,120,128]{2,1,0:T(8,128)S(1)} %collective-permute-done.mate_place_ref), custom_call_target="tpu_custom_call" | custom-call | flops 905969664 | bytes 4194304 | tf_op jit(solution)/shard_map/brick_windows/pallas_call | solution.py:172
  22.1 1.2 %copy-done.1 = bf16[17,208,256]{2,1,0:T(8,128)(2,1)} copy-done((bf16[17,208,256]{2,1,0:T(8,128)(2,1)}, bf16[17,208,256]{2,1,0:T(8,128)(2,1)S(1)}, u32[]{:S(2)}) %copy-start.1) | copy-done | bytes 1810456
  23.4 1.4 %all-to-all-done.place_ref = f32[8,120,128]{2,1,0:T(8,128)} async-done(((f32[8,120,128]{2,1,0:T(8,128)}), f32[8,120,128]{2,1,0:T(8,128)}, u32[]{:S(2)}, u32[]{:S(2)}) %all-to-all-start) | async-done | bytes 491552 | tf_op jit(solution)/shard_map/all_to_all | solution.py:758
  24.8 7.7 %sample_values.1 = bf16[8,40,128]{2,1,0:T(8,128)(2,1)} custom-call(s32[2]{0:T(128)} %copy-done.4, s32[2,8]{1,0:T(2,128)} %bitcast.16, bf16[17,208,256]{2,1,0:T(8,128)(2,1)} %copy-done.1, f32[8,120,128]{2,1,0:T(8,128)} %all-to-all-done.place_ref), custom_call_target="tpu_custom_call" | custom-call | flops 4362076160 | bytes 3145728 | tf_op jit(solution)/shard_map/sample_values/pallas_call | solution.py:385
  32.5 3.4 %all-to-all-start.1 = ((bf16[8,40,128]{2,1,0:T(8,128)(2,1)}), bf16[8,40,128]{2,1,0:T(8,128)(2,1)S(1)}, u32[]{:S(2)}, u32[]{:S(2)}) async-start(bf16[8,40,128]{2,1,0:T(8,128)(2,1)} %sample_values.1), calls=%async_computation.1 | async-start | bytes 163840 | tf_op jit(solution)/shard_map/all_to_all | solution.py:776
  35.9 0.0 copy-start.9
  35.9 1.7 %stem.1.second = bf16[20,32,256]{2,1,0:T(8,128)(2,1)S(1)} custom-call(s32[2]{0:T(128)S(1)} %copy-done.5, bf16[8,4,256]{2,1,0:T(4,128)(2,1)S(1)} %bitcast.15, bf16[8,4,256]{2,1,0:T(4,128)(2,1)S(1)} %collective-permute-done.1.near_ref, bf16[8,4,256]{2,1,0:T(4,128)(2,1)S(1)} %collective-permute-done.2.far_ref, bf16[9,4,32]{2,1,0:T(4,128)(2,1)S(1)} %bitcast.19, ...), custom_call_target="tpu_custom_call" | custom-call | flops 1000000000 | bytes 1048576 | tf_op jit(solution)/shard_map/stem/pallas_call | solution.py:671
  37.6 0.0 copy-start.2
  37.7 1.3 %middle.1.third = bf16[8,112,128]{2,1,0:T(8,128)(2,1)S(1)} custom-call(s32[2]{0:T(128)S(1)} %copy-done.5, bf16[20,32,256]{2,1,0:T(8,128)(2,1)S(1)} %stem.1.second, bf16[9,32,112]{2,1,0:T(8,128)(2,1)S(1)} %bitcast.18), custom_call_target="tpu_custom_call" | custom-call | flops 500000000 | bytes 1048576 | tf_op jit(solution)/shard_map/middle/pallas_call | solution.py:693
  38.9 3.0 %all-to-all-done.1.value_ref = bf16[8,40,128]{2,1,0:T(8,128)(2,1)S(1)} async-done(((bf16[8,40,128]{2,1,0:T(8,128)(2,1)}), bf16[8,40,128]{2,1,0:T(8,128)(2,1)S(1)}, u32[]{:S(2)}, u32[]{:S(2)}) %all-to-all-start.1) | async-done | bytes 81952 | tf_op jit(solution)/shard_map/all_to_all | solution.py:776
  41.9 0.2 gbuffer.1
  42.1 1.5 %collective-permute-start.3 = (bf16[1,4,8,256]{3,2,1,0:T(8,128)(2,1)S(1)}, bf16[1,4,8,256]{3,2,1,0:T(8,128)(2,1)S(1)}, u32[]{:S(2)}, u32[]{:S(2)}) collective-permute-start(bf16[1,4,8,256]{3,2,1,0:T(8,128)(2,1)S(1)} %gbuffer.1), channel_id=1, source_target_pairs={{0,8},{8,16},{16,24},{24,0},{1,9},{9,17},{17,25},{25,1},{2,10},{10... | collective-permute-start | bytes 49160 | tf_op jit(solution)/shard_map/ppermute | solution.py:783
  43.7 2.9 %decoder.1 = bf16[1,3,8,256]{3,2,1,0:T(8,128)(2,1)} custom-call(s32[2]{0:T(128)S(1)} %copy-done.5, bf16[20,32,256]{2,1,0:T(8,128)(2,1)S(1)} %stem.1.second, bf16[8,112,128]{2,1,0:T(8,128)(2,1)S(1)} %middle.1.third, bf16[9,112,112]{2,1,0:T(8,128)(2,1)S(1)} %copy-done.6, bf16[9,32,144]{2,1,0:T(8,128)(2,1)S(1)} %copy-done.7, bf16[9,3,32]{2,1,0:T(4,128)(2,1)S(1)} %copy-done.11), custom_call_target="tpu_custom_call" | custom-call | flops 1500000000 | bytes 1048576 | tf_op jit(solution)/shard_map/decoder/pallas_call | solution.py:711
  46.5 0.3 collective-permute-done.3
  46.8 0.6 %copy.19 = bf16[1,4,8,256]{3,2,1,0:T(8,128)(2,1)} copy(bf16[1,4,8,256]{3,2,1,0:T(8,128)(2,1)S(1)} %collective-permute-done.3) | data formatting | bytes 32768
  (28 shorter events, 0.1 us)
Async XLA Ops:
  0.6 15.2 %copy-start.12 = (bf16[16,39304]{1,0:T(8,128)(2,1)S(1)}, bf16[16,39304]{1,0:T(8,128)(2,1)}, u32[]{:S(2)}) copy-start(bf16[16,39304]{1,0:T(8,128)(2,1)} %param.12) | copy-start | bytes 3773188
  0.6 9.4 %copy-start.13 = (bf16[1,4,8,256]{3,2,1,0:T(8,128)(2,1)S(1)}, bf16[1,4,8,256]{3,2,1,0:T(8,128)(2,1)}, u32[]{:S(2)}) copy-start(bf16[1,4,8,256]{3,2,1,0:T(8,128)(2,1)} %param.17) | copy-start | bytes 49156
  3.7 21.1 %all-to-all-start = ((f32[8,120,128]{2,1,0:T(8,128)}), f32[8,120,128]{2,1,0:T(8,128)}, u32[]{:S(2)}, u32[]{:S(2)}) async-start(f32[8,120,128]{2,1,0:T(8,128)} %positions.1.place_ref), calls=%async_computation | async-start | bytes 983040 | tf_op jit(solution)/shard_map/all_to_all | solution.py:758
  10.0 8.1 %copy-start = (f32[8,120,128]{2,1,0:T(8,128)S(1)}, f32[8,120,128]{2,1,0:T(8,128)}, u32[]{:S(2)}) copy-start(f32[8,120,128]{2,1,0:T(8,128)} %positions.1.place_ref) | copy-start | bytes 1474564
  10.0 8.1 %copy-start.3 = (s32[1,1,8,2]{2,3,1,0:T(2,128)S(1)}, s32[1,1,8,2]{2,3,1,0:T(2,128)}, u32[]{:S(2)}) copy-start(s32[1,1,8,2]{2,3,1,0:T(2,128)} %param.13) | copy-start | bytes 196
  10.1 22.4 %collective-permute-start.1 = (bf16[8,4,256]{2,1,0:T(4,128)(2,1)S(1)}, bf16[8,4,256]{2,1,0:T(4,128)(2,1)S(1)}, u32[]{:S(2)}, u32[]{:S(2)}) collective-permute-start(bf16[8,4,256]{2,1,0:T(4,128)(2,1)S(1)} %bitcast.13), channel_id=1, source_target_pairs={{0,1},{1,0},{2,3},{3,2},{4,5},{5,4},{6,7},{7,6},{8,9},{9,8},{10,11... | collective-permute-start | bytes 49160 | tf_op jit(solution)/shard_map/ppermute | solution.py:768
  10.6 21.9 %collective-permute-start.2 = (bf16[8,4,256]{2,1,0:T(4,128)(2,1)S(1)}, bf16[8,4,256]{2,1,0:T(4,128)(2,1)S(1)}, u32[]{:S(2)}, u32[]{:S(2)}) collective-permute-start(bf16[8,4,256]{2,1,0:T(4,128)(2,1)S(1)} %bitcast.14), channel_id=1, source_target_pairs={{1,2},{2,1},{3,4},{4,3},{5,6},{6,5},{9,10},{10,9},{11,12},{12,11},... | collective-permute-start | bytes 49160 | tf_op jit(solution)/shard_map/ppermute | solution.py:769
  12.8 5.4 %collective-permute-start = (f32[1,120,128]{2,1,0:T(8,128)}, f32[1,120,128]{2,1,0:T(8,128)S(1)}, u32[]{:S(2)}, u32[]{:S(2)}) collective-permute-start(f32[1,120,128]{2,1,0:T(8,128)} %constant_dynamic-slice_fusion), channel_id=1, source_target_pairs={{0,1},{1,0},{2,3},{3,2},{4,5},{5,4},{6,7},{7,6},{8,9},{9,8},{10,11... | collective-permute-start | bytes 184328 | tf_op jit(solution)/shard_map/ppermute | solution.py:766
  18.2 3.9 %copy-start.4 = (s32[2]{0:T(128)}, s32[2]{0:T(128)S(1)}, u32[]{:S(2)}) copy-start(s32[2]{0:T(128)S(1)} %pad_add_fusion.where_ref) | copy-start | bytes 28
  22.1 1.2 %copy-start.1 = (bf16[17,208,256]{2,1,0:T(8,128)(2,1)}, bf16[17,208,256]{2,1,0:T(8,128)(2,1)S(1)}, u32[]{:S(2)}) copy-start(bf16[17,208,256]{2,1,0:T(8,128)(2,1)S(1)} %brick_windows.1.brick_ref) | copy-start | bytes 5431300
  23.4 12.5 %copy-start.8 = (bf16[9,32,32]{2,1,0:T(8,128)(2,1)S(1)}, bf16[9,32,32]{2,1,0:T(8,128)(2,1)}, u32[]{:S(2)}) copy-start(bf16[9,32,32]{2,1,0:T(8,128)(2,1)} %w_mid.1) | copy-start | bytes 55300
  23.4 12.5 %copy-start.10 = (bf16[9,32,4]{1,2,0:T(4,128)(2,1)S(1)}, bf16[9,32,4]{1,2,0:T(4,128)(2,1)}, u32[]{:S(2)}) copy-start(bf16[9,32,4]{1,2,0:T(4,128)(2,1)} %param.18) | copy-start | bytes 6916
  24.8 11.1 %copy-start.5 = (s32[2]{0:T(128)S(1)}, s32[2]{0:T(128)}, u32[]{:S(2)}) copy-start(s32[2]{0:T(128)} %copy-done.4) | copy-start | bytes 28
  32.5 9.4 %all-to-all-start.1 = ((bf16[8,40,128]{2,1,0:T(8,128)(2,1)}), bf16[8,40,128]{2,1,0:T(8,128)(2,1)S(1)}, u32[]{:S(2)}, u32[]{:S(2)}) async-start(bf16[8,40,128]{2,1,0:T(8,128)(2,1)} %sample_values.1), calls=%async_computation.1 | async-start | bytes 163840 | tf_op jit(solution)/shard_map/all_to_all | solution.py:776
  35.9 1.8 %copy-start.9 = (bf16[9,112,32]{1,2,0:T(8,128)(2,1)S(1)}, bf16[9,112,32]{1,2,0:T(8,128)(2,1)}, u32[]{:S(2)}) copy-start(bf16[9,112,32]{1,2,0:T(8,128)(2,1)} %param.20) | copy-start | bytes 193540
  37.6 4.3 %copy-start.2 = (s32[1,1,160,256]{3,2,1,0:T(8,128)S(1)}, s32[1,1,160,256]{3,2,1,0:T(8,128)}, u32[]{:S(2)}) copy-start(s32[1,1,160,256]{3,2,1,0:T(8,128)} %order_ref.1) | copy-start | bytes 491524
  37.6 6.1 %copy-start.6 = (bf16[9,112,112]{2,1,0:T(8,128)(2,1)S(1)}, bf16[9,112,112]{2,1,0:T(8,128)(2,1)}, u32[]{:S(2)}) copy-start(bf16[9,112,112]{2,1,0:T(8,128)(2,1)} %w_deep.1) | copy-start | bytes 677380
  37.6 6.0 %copy-start.7 = (bf16[9,32,144]{2,1,0:T(8,128)(2,1)S(1)}, bf16[9,32,144]{2,1,0:T(8,128)(2,1)}, u32[]{:S(2)}) copy-start(bf16[9,32,144]{2,1,0:T(8,128)(2,1)} %w_up.1) | copy-start | bytes 248836
  37.6 6.0 %copy-start.11 = (bf16[9,3,32]{2,1,0:T(4,128)(2,1)S(1)}, bf16[9,3,32]{2,1,0:T(4,128)(2,1)}, u32[]{:S(2)}) copy-start(bf16[9,3,32]{2,1,0:T(4,128)(2,1)} %w_out.1) | copy-start | bytes 5188
  42.1 4.7 %collective-permute-start.3 = (bf16[1,4,8,256]{3,2,1,0:T(8,128)(2,1)S(1)}, bf16[1,4,8,256]{3,2,1,0:T(8,128)(2,1)S(1)}, u32[]{:S(2)}, u32[]{:S(2)}) collective-permute-start(bf16[1,4,8,256]{3,2,1,0:T(8,128)(2,1)S(1)} %gbuffer.1), channel_id=1, source_target_pairs={{0,8},{8,16},{16,24},{24,0},{1,9},{9,17},{17,25},{25,1},{2,10},{10... | collective-permute-start | bytes 49160 | tf_op jit(solution)/shard_map/ppermute | solution.py:783

commit v19 on v18

--- a/solution.py
+++ b/solution.py
@@ -59,16 +59,12 @@
             found.at[place], out_ref.at[place], departures.at[axis, part]
         )
 
-    ahead = 3
-    for piece in pieces[:ahead]:
+    for piece in pieces:
         for copy in reads(*piece):
             copy.start()
-    for number, (axis, part) in enumerate(pieces):
+    for axis, part in pieces:
         for copy in reads(axis, part):
             copy.wait()
-        for piece in pieces[number + ahead : number + ahead + 1]:
-            for copy in reads(*piece):
-                copy.start()
         span = slice(part * share * lines, (part + 1) * share * lines)
         place = cells[axis, span].astype(F32) + fracs[axis, span]
         found[part * share : (part + 1) * share, axis * lines : (axis + 1) * lines, :] = (
@@ -92,8 +88,8 @@
             pltpu.VMEM(cells.shape, jnp.int32),
             pltpu.VMEM(fracs.shape, F32),
             pltpu.VMEM(shape, F32),
-            pltpu.SemaphoreType.DMA((3, 2, 2)),
-            pltpu.SemaphoreType.DMA((3, 2)),
+            pltpu.SemaphoreType.DMA((3, 4, 2)),
+            pltpu.SemaphoreType.DMA((3, 4)),
         ],
         compiler_params=params(60),
         cost_estimate=pl.CostEstimate(
@@ -327,20 +323,10 @@
             copy.wait()
 
         if members == 2:
-
-            @pl.when(turn + 1 < pairs)
-            def _():
-                start(turn + 1, 2)
-
+            pl.when(turn + 1 < pairs)(lambda: start(turn + 1, 2))
             if rest:
-
-                @pl.when(turn + 1 == pairs)
-                def _():
-                    start(pairs, 1)
-
-            @pl.when(turn == 0)
-            def _():
-                own_values.start()
+                pl.when(turn + 1 == pairs)(lambda: start(pairs, 1))
+            pl.when(turn == 0)(own_values.start)
 
         for member in range(members):
             for piece in range(cap):
@@ -358,14 +344,17 @@
 
     def one_pair(turn, carry):
         work(turn, 2)
-
         return carry
 
     if pairs > 0:
         start(0, 2)
     elif rest:
         start(0, 1)
-    lax.fori_loop(0, pairs, one_pair, 0)
+    if pairs <= 4:
+        for turn in range(pairs):
+            work(turn, 2)
+    else:
+        lax.fori_loop(0, pairs, one_pair, 0)
     if rest:
         work(pairs, 1)
     if pairs == 0:

time: 47.9 us -> 47 us (0.981)
  Pallas kernels: 20.6 us -> 19.8 us
    pallas_call x1, Pallas kernels: 3.03 us -> 2.2 us  [positions(): pl.pallas_call(positions_kernel, out_shape=jax.ShapeDtypeStruct(shape, F3...]
where the time goes in v19:
time: 47 us; the launch traced here: 46.6 us
  Pallas kernels  19.8 us (42%)
  starting transfers between devices  15.5 us (33%)
  local copies, waits for them, and re-layouts  5.67 us (12%)
  waiting for transfers between devices  4.67 us (10%)
  between operations  0.87 us (2%)
    pallas_call x1, Pallas kernels, sample_values(): pl.pallas_call(samples_kernel, out_shape=jax.ShapeDtypeStruct((owners, ro...  7.64 us
    all_to_all x1, starting transfers between devices, on_device(): lax.all_to_all(places, 'tile', split_axis=0, concat_axis=0, tiled=True)  6.34 us
    pallas_call x1, Pallas kernels, windows_of(): pl.pallas_call(windows_kernel, out_shape=jax.ShapeDtypeStruct((count + 1,...  3.94 us
    all_to_all x1, starting transfers between devices, on_device(): lax.all_to_all(found, 'tile', split_axis=0, concat_axis=0, tiled=True)  3.37 us
    ppermute x1, starting transfers between devices, on_device(): mate_places = lax.ppermute(for_mate, 'tile', mates)  3.03 us
    all_to_all x1, waiting for transfers between devices, on_device(): lax.all_to_all(found, 'tile', split_axis=0, concat_axis=0, tiled=True)  3 us
    pallas_call x1, Pallas kernels, decoder(): pl.pallas_call(decoder_kernel, out_shape=jax.ShapeDtypeStruct((1, colours...  2.88 us
    reshape x1, local copies, waits for them, and re-layouts, windows_of(): cube = bricks.reshape(count, EDGE, EDGE * EDGE)  2.31 us
  transfers between devices with their start and end apart: 6, of which 3 were waited for; matrix products, arithmetic and copies ran while one was open for 8% of the time, Pallas kernels for 37%

profile of v19, /device:TPU:0, one launch (start us, length us, event | category | flops | bytes accessed | tf_op | source)
XLA Modules:
  0.0 46.6 jit_solution(12975254399476107794)
XLA Ops:
  0.7 2.2 %positions.1.place_ref = f32[8,120,128]{2,1,0:T(8,128)} custom-call(s32[3,320,128]{2,1,0:T(8,128)} %bitcast.20, f32[3,320,128]{2,1,0:T(8,128)} %bitcast.21), custom_call_target="tpu_custom_call" | custom-call | flops 122880 | bytes 1474560 | tf_op jit(solution)/shard_map/positions/pallas_call | solution.py:82
  2.9 6.3 %all-to-all-start = ((f32[8,120,128]{2,1,0:T(8,128)}), f32[8,120,128]{2,1,0:T(8,128)}, u32[]{:S(2)}, u32[]{:S(2)}) async-start(f32[8,120,128]{2,1,0:T(8,128)} %positions.1.place_ref), calls=%async_computation | async-start | bytes 983040 | tf_op jit(solution)/shard_map/all_to_all | solution.py:747
  9.2 0.0 copy-start.3
  9.2 0.6 %collective-permute-start.1 = (bf16[8,4,256]{2,1,0:T(4,128)(2,1)S(1)}, bf16[8,4,256]{2,1,0:T(4,128)(2,1)S(1)}, u32[]{:S(2)}, u32[]{:S(2)}) collective-permute-start(bf16[8,4,256]{2,1,0:T(4,128)(2,1)S(1)} %bitcast.13), channel_id=1, source_target_pairs={{0,1},{1,0},{2,3},{3,2},{4,5},{5,4},{6,7},{7,6},{8,9},{9,8},{10,11... | collective-permute-start | bytes 49160 | tf_op jit(solution)/shard_map/ppermute | solution.py:757
  9.8 0.7 %collective-permute-start.2 = (bf16[8,4,256]{2,1,0:T(4,128)(2,1)S(1)}, bf16[8,4,256]{2,1,0:T(4,128)(2,1)S(1)}, u32[]{:S(2)}, u32[]{:S(2)}) collective-permute-start(bf16[8,4,256]{2,1,0:T(4,128)(2,1)S(1)} %bitcast.14), channel_id=1, source_target_pairs={{1,2},{2,1},{3,4},{4,3},{5,6},{6,5},{9,10},{10,9},{11,12},{12,11},... | collective-permute-start | bytes 49160 | tf_op jit(solution)/shard_map/ppermute | solution.py:758
  10.5 1.5 %constant_dynamic-slice_fusion = f32[1,120,128]{2,1,0:T(8,128)} fusion(f32[8,120,128]{2,1,0:T(8,128)} %positions.1.place_ref, s32[]{:T(128)S(6)} %select_n.3), kind=kLoop, calls=%fused_computation.2 | loop fusion | bytes 122884 | tf_op jit(solution)/shard_map/dynamic_slice | solution.py:754
  11.9 3.0 %collective-permute-start = (f32[1,120,128]{2,1,0:T(8,128)}, f32[1,120,128]{2,1,0:T(8,128)S(1)}, u32[]{:S(2)}, u32[]{:S(2)}) collective-permute-start(f32[1,120,128]{2,1,0:T(8,128)} %constant_dynamic-slice_fusion), channel_id=1, source_target_pairs={{0,1},{1,0},{2,3},{3,2},{4,5},{5,4},{6,7},{7,6},{8,9},{9,8},{10,11... | collective-permute-start | bytes 184328 | tf_op jit(solution)/shard_map/ppermute | solution.py:755
  15.0 2.3 %reshape.15.cube_ref = bf16[16,34,1156]{2,1,0:T(8,128)(2,1)S(1)} reshape(bf16[16,39304]{1,0:T(8,128)(2,1)S(1)} %copy-done.12) | data formatting | bytes 2515456 | tf_op jit(solution)/shard_map/reshape | solution.py:166
  17.3 0.1 pad_add_fusion.where_ref
  17.4 3.9 %brick_windows.1.brick_ref = bf16[17,208,256]{2,1,0:T(8,128)(2,1)S(1)} custom-call(s32[2]{0:T(128)S(1)} %pad_add_fusion.where_ref, s32[2,8]{1,0:T(2,128)S(1)} %bitcast.17, bf16[16,34,1156]{2,1,0:T(8,128)(2,1)S(1)} %reshape.15.cube_ref, f32[8,120,128]{2,1,0:T(8,128)S(1)} %copy-done, f32[1,120,128]{2,1,0:T(8,128)S(1)} %collective-permute-done.mate_place_ref), custom_call_target="tpu_custom_call" | custom-call | flops 905969664 | bytes 4194304 | tf_op jit(solution)/shard_map/brick_windows/pallas_call | solution.py:168
  21.3 1.2 %copy-done.1 = bf16[17,208,256]{2,1,0:T(8,128)(2,1)} copy-done((bf16[17,208,256]{2,1,0:T(8,128)(2,1)}, bf16[17,208,256]{2,1,0:T(8,128)(2,1)S(1)}, u32[]{:S(2)}) %copy-start.1) | copy-done | bytes 1810456
  22.6 1.4 %all-to-all-done.place_ref = f32[8,120,128]{2,1,0:T(8,128)} async-done(((f32[8,120,128]{2,1,0:T(8,128)}), f32[8,120,128]{2,1,0:T(8,128)}, u32[]{:S(2)}, u32[]{:S(2)}) %all-to-all-start) | async-done | bytes 491552 | tf_op jit(solution)/shard_map/all_to_all | solution.py:747
  24.0 7.6 %sample_values.1 = bf16[8,40,128]{2,1,0:T(8,128)(2,1)} custom-call(s32[2]{0:T(128)} %copy-done.4, s32[2,8]{1,0:T(2,128)} %bitcast.16, bf16[17,208,256]{2,1,0:T(8,128)(2,1)} %copy-done.1, f32[8,120,128]{2,1,0:T(8,128)} %all-to-all-done.place_ref), custom_call_target="tpu_custom_call" | custom-call | flops 4362076160 | bytes 3145728 | tf_op jit(solution)/shard_map/sample_values/pallas_call | solution.py:374
  31.6 3.4 %all-to-all-start.1 = ((bf16[8,40,128]{2,1,0:T(8,128)(2,1)}), bf16[8,40,128]{2,1,0:T(8,128)(2,1)S(1)}, u32[]{:S(2)}, u32[]{:S(2)}) async-start(bf16[8,40,128]{2,1,0:T(8,128)(2,1)} %sample_values.1), calls=%async_computation.1 | async-start | bytes 163840 | tf_op jit(solution)/shard_map/all_to_all | solution.py:765
  35.1 1.7 %stem.1.second = bf16[20,32,256]{2,1,0:T(8,128)(2,1)S(1)} custom-call(s32[2]{0:T(128)S(1)} %copy-done.5, bf16[8,4,256]{2,1,0:T(4,128)(2,1)S(1)} %bitcast.15, bf16[8,4,256]{2,1,0:T(4,128)(2,1)S(1)} %collective-permute-done.1.near_ref, bf16[8,4,256]{2,1,0:T(4,128)(2,1)S(1)} %collective-permute-done.2.far_ref, bf16[9,4,32]{2,1,0:T(4,128)(2,1)S(1)} %bitcast.19, ...), custom_call_target="tpu_custom_call" | custom-call | flops 1000000000 | bytes 1048576 | tf_op jit(solution)/shard_map/stem/pallas_call | solution.py:660
  36.8 0.0 copy-start.6
  36.8 0.0 copy-start.7
  36.8 1.3 %middle.1.third = bf16[8,112,128]{2,1,0:T(8,128)(2,1)S(1)} custom-call(s32[2]{0:T(128)S(1)} %copy-done.5, bf16[20,32,256]{2,1,0:T(8,128)(2,1)S(1)} %stem.1.second, bf16[9,32,112]{2,1,0:T(8,128)(2,1)S(1)} %bitcast.18), custom_call_target="tpu_custom_call" | custom-call | flops 500000000 | bytes 1048576 | tf_op jit(solution)/shard_map/middle/pallas_call | solution.py:682
  38.1 3.0 %all-to-all-done.1.value_ref = bf16[8,40,128]{2,1,0:T(8,128)(2,1)S(1)} async-done(((bf16[8,40,128]{2,1,0:T(8,128)(2,1)}), bf16[8,40,128]{2,1,0:T(8,128)(2,1)S(1)}, u32[]{:S(2)}, u32[]{:S(2)}) %all-to-all-start.1) | async-done | bytes 81952 | tf_op jit(solution)/shard_map/all_to_all | solution.py:765
  41.1 0.2 gbuffer.1
  41.3 1.5 %collective-permute-start.3 = (bf16[1,4,8,256]{3,2,1,0:T(8,128)(2,1)S(1)}, bf16[1,4,8,256]{3,2,1,0:T(8,128)(2,1)S(1)}, u32[]{:S(2)}, u32[]{:S(2)}) collective-permute-start(bf16[1,4,8,256]{3,2,1,0:T(8,128)(2,1)S(1)} %gbuffer.1), channel_id=1, source_target_pairs={{0,8},{8,16},{16,24},{24,0},{1,9},{9,17},{17,25},{25,1},{2,10},{10... | collective-permute-start | bytes 49160 | tf_op jit(solution)/shard_map/ppermute | solution.py:772
  42.8 2.9 %decoder.1 = bf16[1,3,8,256]{3,2,1,0:T(8,128)(2,1)} custom-call(s32[2]{0:T(128)S(1)} %copy-done.5, bf16[20,32,256]{2,1,0:T(8,128)(2,1)S(1)} %stem.1.second, bf16[8,112,128]{2,1,0:T(8,128)(2,1)S(1)} %middle.1.third, bf16[9,112,112]{2,1,0:T(8,128)(2,1)S(1)} %copy-done.6, bf16[9,32,144]{2,1,0:T(8,128)(2,1)S(1)} %copy-done.7, bf16[9,3,32]{2,1,0:T(4,128)(2,1)S(1)} %copy-done.11), custom_call_target="tpu_custom_call" | custom-call | flops 1500000000 | bytes 1048576 | tf_op jit(solution)/shard_map/decoder/pallas_call | solution.py:700
  45.7 0.3 collective-permute-done.3
  46.0 0.6 %copy.19 = bf16[1,4,8,256]{3,2,1,0:T(8,128)(2,1)} copy(bf16[1,4,8,256]{3,2,1,0:T(8,128)(2,1)S(1)} %collective-permute-done.3) | data formatting | bytes 32768
  (28 shorter events, 0.1 us)
Async XLA Ops:
  0.6 14.3 %copy-start.12 = (bf16[16,39304]{1,0:T(8,128)(2,1)S(1)}, bf16[16,39304]{1,0:T(8,128)(2,1)}, u32[]{:S(2)}) copy-start(bf16[16,39304]{1,0:T(8,128)(2,1)} %param.12) | copy-start | bytes 3773188
  0.6 8.6 %copy-start.13 = (bf16[1,4,8,256]{3,2,1,0:T(8,128)(2,1)S(1)}, bf16[1,4,8,256]{3,2,1,0:T(8,128)(2,1)}, u32[]{:S(2)}) copy-start(bf16[1,4,8,256]{3,2,1,0:T(8,128)(2,1)} %param.17) | copy-start | bytes 49156
  2.9 21.1 %all-to-all-start = ((f32[8,120,128]{2,1,0:T(8,128)}), f32[8,120,128]{2,1,0:T(8,128)}, u32[]{:S(2)}, u32[]{:S(2)}) async-start(f32[8,120,128]{2,1,0:T(8,128)} %positions.1.place_ref), calls=%async_computation | async-start | bytes 983040 | tf_op jit(solution)/shard_map/all_to_all | solution.py:747
  9.2 8.1 %copy-start = (f32[8,120,128]{2,1,0:T(8,128)S(1)}, f32[8,120,128]{2,1,0:T(8,128)}, u32[]{:S(2)}) copy-start(f32[8,120,128]{2,1,0:T(8,128)} %positions.1.place_ref) | copy-start | bytes 1474564
  9.2 8.1 %copy-start.3 = (s32[1,1,8,2]{2,3,1,0:T(2,128)S(1)}, s32[1,1,8,2]{2,3,1,0:T(2,128)}, u32[]{:S(2)}) copy-start(s32[1,1,8,2]{2,3,1,0:T(2,128)} %param.13) | copy-start | bytes 196
  9.2 22.4 %collective-permute-start.1 = (bf16[8,4,256]{2,1,0:T(4,128)(2,1)S(1)}, bf16[8,4,256]{2,1,0:T(4,128)(2,1)S(1)}, u32[]{:S(2)}, u32[]{:S(2)}) collective-permute-start(bf16[8,4,256]{2,1,0:T(4,128)(2,1)S(1)} %bitcast.13), channel_id=1, source_target_pairs={{0,1},{1,0},{2,3},{3,2},{4,5},{5,4},{6,7},{7,6},{8,9},{9,8},{10,11... | collective-permute-start | bytes 49160 | tf_op jit(solution)/shard_map/ppermute | solution.py:757
  9.8 21.8 %collective-permute-start.2 = (bf16[8,4,256]{2,1,0:T(4,128)(2,1)S(1)}, bf16[8,4,256]{2,1,0:T(4,128)(2,1)S(1)}, u32[]{:S(2)}, u32[]{:S(2)}) collective-permute-start(bf16[8,4,256]{2,1,0:T(4,128)(2,1)S(1)} %bitcast.14), channel_id=1, source_target_pairs={{1,2},{2,1},{3,4},{4,3},{5,6},{6,5},{9,10},{10,9},{11,12},{12,11},... | collective-permute-start | bytes 49160 | tf_op jit(solution)/shard_map/ppermute | solution.py:758
  11.9 5.4 %collective-permute-start = (f32[1,120,128]{2,1,0:T(8,128)}, f32[1,120,128]{2,1,0:T(8,128)S(1)}, u32[]{:S(2)}, u32[]{:S(2)}) collective-permute-start(f32[1,120,128]{2,1,0:T(8,128)} %constant_dynamic-slice_fusion), channel_id=1, source_target_pairs={{0,1},{1,0},{2,3},{3,2},{4,5},{5,4},{6,7},{7,6},{8,9},{9,8},{10,11... | collective-permute-start | bytes 184328 | tf_op jit(solution)/shard_map/ppermute | solution.py:755
  17.3 4.0 %copy-start.4 = (s32[2]{0:T(128)}, s32[2]{0:T(128)S(1)}, u32[]{:S(2)}) copy-start(s32[2]{0:T(128)S(1)} %pad_add_fusion.where_ref) | copy-start | bytes 28
  21.3 1.2 %copy-start.1 = (bf16[17,208,256]{2,1,0:T(8,128)(2,1)}, bf16[17,208,256]{2,1,0:T(8,128)(2,1)S(1)}, u32[]{:S(2)}) copy-start(bf16[17,208,256]{2,1,0:T(8,128)(2,1)S(1)} %brick_windows.1.brick_ref) | copy-start | bytes 5431300
  22.6 12.5 %copy-start.8 = (bf16[9,32,32]{2,1,0:T(8,128)(2,1)S(1)}, bf16[9,32,32]{2,1,0:T(8,128)(2,1)}, u32[]{:S(2)}) copy-start(bf16[9,32,32]{2,1,0:T(8,128)(2,1)} %w_mid.1) | copy-start | bytes 55300
  22.6 12.5 %copy-start.10 = (bf16[9,32,4]{1,2,0:T(4,128)(2,1)S(1)}, bf16[9,32,4]{1,2,0:T(4,128)(2,1)}, u32[]{:S(2)}) copy-start(bf16[9,32,4]{1,2,0:T(4,128)(2,1)} %param.18) | copy-start | bytes 6916
  24.0 11.1 %copy-start.5 = (s32[2]{0:T(128)S(1)}, s32[2]{0:T(128)}, u32[]{:S(2)}) copy-start(s32[2]{0:T(128)} %copy-done.4) | copy-start | bytes 28
  31.6 9.4 %all-to-all-start.1 = ((bf16[8,40,128]{2,1,0:T(8,128)(2,1)}), bf16[8,40,128]{2,1,0:T(8,128)(2,1)S(1)}, u32[]{:S(2)}, u32[]{:S(2)}) async-start(bf16[8,40,128]{2,1,0:T(8,128)(2,1)} %sample_values.1), calls=%async_computation.1 | async-start | bytes 163840 | tf_op jit(solution)/shard_map/all_to_all | solution.py:765
  35.0 1.8 %copy-start.9 = (bf16[9,112,32]{1,2,0:T(8,128)(2,1)S(1)}, bf16[9,112,32]{1,2,0:T(8,128)(2,1)}, u32[]{:S(2)}) copy-start(bf16[9,112,32]{1,2,0:T(8,128)(2,1)} %param.20) | copy-start | bytes 193540
  36.8 4.3 %copy-start.2 = (s32[1,1,160,256]{3,2,1,0:T(8,128)S(1)}, s32[1,1,160,256]{3,2,1,0:T(8,128)}, u32[]{:S(2)}) copy-start(s32[1,1,160,256]{3,2,1,0:T(8,128)} %order_ref.1) | copy-start | bytes 491524
  36.8 6.1 %copy-start.6 = (bf16[9,112,112]{2,1,0:T(8,128)(2,1)S(1)}, bf16[9,112,112]{2,1,0:T(8,128)(2,1)}, u32[]{:S(2)}) copy-start(bf16[9,112,112]{2,1,0:T(8,128)(2,1)} %w_deep.1) | copy-start | bytes 677380
  36.8 6.1 %copy-start.7 = (bf16[9,32,144]{2,1,0:T(8,128)(2,1)S(1)}, bf16[9,32,144]{2,1,0:T(8,128)(2,1)}, u32[]{:S(2)}) copy-start(bf16[9,32,144]{2,1,0:T(8,128)(2,1)} %w_up.1) | copy-start | bytes 248836
  36.8 6.0 %copy-start.11 = (bf16[9,3,32]{2,1,0:T(4,128)(2,1)S(1)}, bf16[9,3,32]{2,1,0:T(4,128)(2,1)}, u32[]{:S(2)}) copy-start(bf16[9,3,32]{2,1,0:T(4,128)(2,1)} %w_out.1) | copy-start | bytes 5188
  41.3 4.7 %collective-permute-start.3 = (bf16[1,4,8,256]{3,2,1,0:T(8,128)(2,1)S(1)}, bf16[1,4,8,256]{3,2,1,0:T(8,128)(2,1)S(1)}, u32[]{:S(2)}, u32[]{:S(2)}) collective-permute-start(bf16[1,4,8,256]{3,2,1,0:T(8,128)(2,1)S(1)} %gbuffer.1), channel_id=1, source_target_pairs={{0,8},{8,16},{16,24},{24,0},{1,9},{9,17},{17,25},{25,1},{2,10},{10... | collective-permute-start | bytes 49160 | tf_op jit(solution)/shard_map/ppermute | solution.py:772

commit v20 on v19

--- a/solution.py
+++ b/solution.py
@@ -200,13 +200,14 @@
 
     cell_y = jnp.floor(py)
     frac_y = py - cell_y
-    lower, low_share, high_share = tile(cell_y), tile(1.0 - frac_y), tile(frac_y)
+    lower, upper = tile(cell_y), tile(cell_y + 1.0)
+    low_share, high_share = tile(1.0 - frac_y), tile(frac_y)
     nothing = jnp.zeros((TAIL, width), BF16)
     weight_y = []
     for start in range(0, MAIN, TAIL):
-        offset = places[start : start + TAIL] - lower
+        here = places[start : start + TAIL]
         weight_y.append(
-            jnp.where(offset == 0, low_share, jnp.where(offset == 1, high_share, nothing))
+            jnp.where(here == lower, low_share, jnp.where(here == upper, high_share, nothing))
         )
     window = jnp.floor(px * (1.0 / STRIDE))
     weight_x = hat(eight - (px - STRIDE * window))
@@ -238,18 +239,20 @@
 
 def slot_sums(brick, places, sums, first, blocks):
     lines = places.shape[0] // 3
-    for step in range(blocks):
+    together = 2 if blocks % 2 == 0 else 1
+    halves = 2 * together
+    for step in range(0, blocks, together):
         row = first + 2 * step
 
         def line(axis):
-            both = [
+            parts = [
                 jnp.broadcast_to(places[pl.ds(axis * lines + row + half, 1), :], (8, LANES))
-                for half in range(2)
+                for half in range(halves)
             ]
-            return jnp.concatenate(both, axis=1)
+            return jnp.concatenate(parts, axis=1)
 
         total = blend(brick, line(0), line(1), line(2))
-        for half in range(2):
+        for half in range(halves):
             sums[pl.ds(pl.multiple_of(8 * (row + half), 8), 8), :] = total[
                 :, half * LANES : (half + 1) * LANES
             ]
@@ -350,11 +353,7 @@
         start(0, 2)
     elif rest:
         start(0, 1)
-    if pairs <= 4:
-        for turn in range(pairs):
-            work(turn, 2)
-    else:
-        lax.fori_loop(0, pairs, one_pair, 0)
+    lax.fori_loop(0, pairs, one_pair, 0)
     if rest:
         work(pairs, 1)
     if pairs == 0:

time: 47 us -> 47 us (level)
  no operation moved by 1% of the time
where the time goes in v20:
time: 47 us; the launch traced here: 46.6 us
  Pallas kernels  19.8 us (42%)
  starting transfers between devices  15.5 us (33%)
  local copies, waits for them, and re-layouts  5.67 us (12%)
  waiting for transfers between devices  4.68 us (10%)
  between operations  0.87 us (2%)
    pallas_call x1, Pallas kernels, sample_values(): pl.pallas_call(samples_kernel, out_shape=jax.ShapeDtypeStruct((owners, ro...  7.64 us
    all_to_all x1, starting transfers between devices, on_device(): lax.all_to_all(places, 'tile', split_axis=0, concat_axis=0, tiled=True)  6.34 us
    pallas_call x1, Pallas kernels, windows_of(): pl.pallas_call(windows_kernel, out_shape=jax.ShapeDtypeStruct((count + 1,...  3.93 us
    all_to_all x1, starting transfers between devices, on_device(): lax.all_to_all(found, 'tile', split_axis=0, concat_axis=0, tiled=True)  3.37 us
    ppermute x1, starting transfers between devices, on_device(): mate_places = lax.ppermute(for_mate, 'tile', mates)  3.03 us
    all_to_all x1, waiting for transfers between devices, on_device(): lax.all_to_all(found, 'tile', split_axis=0, concat_axis=0, tiled=True)  3 us
    pallas_call x1, Pallas kernels, decoder(): pl.pallas_call(decoder_kernel, out_shape=jax.ShapeDtypeStruct((1, colours...  2.88 us
    reshape x1, local copies, waits for them, and re-layouts, windows_of(): cube = bricks.reshape(count, EDGE, EDGE * EDGE)  2.31 us
  transfers between devices with their start and end apart: 6, of which 3 were waited for; matrix products, arithmetic and copies ran while one was open for 8% of the time, Pallas kernels for 37%

profile of v20, /device:TPU:0, one launch (start us, length us, event | category | flops | bytes accessed | tf_op | source)
XLA Modules:
  0.0 46.6 jit_solution(9652065971318890981)
XLA Ops:
  0.7 2.2 %positions.1.place_ref = f32[8,120,128]{2,1,0:T(8,128)} custom-call(s32[3,320,128]{2,1,0:T(8,128)} %bitcast.20, f32[3,320,128]{2,1,0:T(8,128)} %bitcast.21), custom_call_target="tpu_custom_call" | custom-call | flops 122880 | bytes 1474560 | tf_op jit(solution)/shard_map/positions/pallas_call | solution.py:82
  2.9 6.3 %all-to-all-start = ((f32[8,120,128]{2,1,0:T(8,128)}), f32[8,120,128]{2,1,0:T(8,128)}, u32[]{:S(2)}, u32[]{:S(2)}) async-start(f32[8,120,128]{2,1,0:T(8,128)} %positions.1.place_ref), calls=%async_computation | async-start | bytes 983040 | tf_op jit(solution)/shard_map/all_to_all | solution.py:746
  9.2 0.0 copy-start.3
  9.2 0.6 %collective-permute-start.1 = (bf16[8,4,256]{2,1,0:T(4,128)(2,1)S(1)}, bf16[8,4,256]{2,1,0:T(4,128)(2,1)S(1)}, u32[]{:S(2)}, u32[]{:S(2)}) collective-permute-start(bf16[8,4,256]{2,1,0:T(4,128)(2,1)S(1)} %bitcast.13), channel_id=1, source_target_pairs={{0,1},{1,0},{2,3},{3,2},{4,5},{5,4},{6,7},{7,6},{8,9},{9,8},{10,11... | collective-permute-start | bytes 49160 | tf_op jit(solution)/shard_map/ppermute | solution.py:756
  9.8 0.7 %collective-permute-start.2 = (bf16[8,4,256]{2,1,0:T(4,128)(2,1)S(1)}, bf16[8,4,256]{2,1,0:T(4,128)(2,1)S(1)}, u32[]{:S(2)}, u32[]{:S(2)}) collective-permute-start(bf16[8,4,256]{2,1,0:T(4,128)(2,1)S(1)} %bitcast.14), channel_id=1, source_target_pairs={{1,2},{2,1},{3,4},{4,3},{5,6},{6,5},{9,10},{10,9},{11,12},{12,11},... | collective-permute-start | bytes 49160 | tf_op jit(solution)/shard_map/ppermute | solution.py:757
  10.5 1.5 %constant_dynamic-slice_fusion = f32[1,120,128]{2,1,0:T(8,128)} fusion(f32[8,120,128]{2,1,0:T(8,128)} %positions.1.place_ref, s32[]{:T(128)S(6)} %select_n.3), kind=kLoop, calls=%fused_computation.2 | loop fusion | bytes 122884 | tf_op jit(solution)/shard_map/dynamic_slice | solution.py:753
  11.9 3.0 %collective-permute-start = (f32[1,120,128]{2,1,0:T(8,128)}, f32[1,120,128]{2,1,0:T(8,128)S(1)}, u32[]{:S(2)}, u32[]{:S(2)}) collective-permute-start(f32[1,120,128]{2,1,0:T(8,128)} %constant_dynamic-slice_fusion), channel_id=1, source_target_pairs={{0,1},{1,0},{2,3},{3,2},{4,5},{5,4},{6,7},{7,6},{8,9},{9,8},{10,11... | collective-permute-start | bytes 184328 | tf_op jit(solution)/shard_map/ppermute | solution.py:754
  15.0 2.3 %reshape.15.cube_ref = bf16[16,34,1156]{2,1,0:T(8,128)(2,1)S(1)} reshape(bf16[16,39304]{1,0:T(8,128)(2,1)S(1)} %copy-done.12) | data formatting | bytes 2515456 | tf_op jit(solution)/shard_map/reshape | solution.py:166
  17.3 0.1 pad_add_fusion.where_ref
  17.4 3.9 %brick_windows.1.brick_ref = bf16[17,208,256]{2,1,0:T(8,128)(2,1)S(1)} custom-call(s32[2]{0:T(128)S(1)} %pad_add_fusion.where_ref, s32[2,8]{1,0:T(2,128)S(1)} %bitcast.17, bf16[16,34,1156]{2,1,0:T(8,128)(2,1)S(1)} %reshape.15.cube_ref, f32[8,120,128]{2,1,0:T(8,128)S(1)} %copy-done, f32[1,120,128]{2,1,0:T(8,128)S(1)} %collective-permute-done.mate_place_ref), custom_call_target="tpu_custom_call" | custom-call | flops 905969664 | bytes 4194304 | tf_op jit(solution)/shard_map/brick_windows/pallas_call | solution.py:168
  21.3 1.2 %copy-done.1 = bf16[17,208,256]{2,1,0:T(8,128)(2,1)} copy-done((bf16[17,208,256]{2,1,0:T(8,128)(2,1)}, bf16[17,208,256]{2,1,0:T(8,128)(2,1)S(1)}, u32[]{:S(2)}) %copy-start.1) | copy-done | bytes 1810456
  22.6 1.4 %all-to-all-done.place_ref = f32[8,120,128]{2,1,0:T(8,128)} async-done(((f32[8,120,128]{2,1,0:T(8,128)}), f32[8,120,128]{2,1,0:T(8,128)}, u32[]{:S(2)}, u32[]{:S(2)}) %all-to-all-start) | async-done | bytes 491552 | tf_op jit(solution)/shard_map/all_to_all | solution.py:746
  24.0 7.6 %sample_values.1 = bf16[8,40,128]{2,1,0:T(8,128)(2,1)} custom-call(s32[2]{0:T(128)} %copy-done.4, s32[2,8]{1,0:T(2,128)} %bitcast.16, bf16[17,208,256]{2,1,0:T(8,128)(2,1)} %copy-done.1, f32[8,120,128]{2,1,0:T(8,128)} %all-to-all-done.place_ref), custom_call_target="tpu_custom_call" | custom-call | flops 4362076160 | bytes 3145728 | tf_op jit(solution)/shard_map/sample_values/pallas_call | solution.py:373
  31.6 3.4 %all-to-all-start.1 = ((bf16[8,40,128]{2,1,0:T(8,128)(2,1)}), bf16[8,40,128]{2,1,0:T(8,128)(2,1)S(1)}, u32[]{:S(2)}, u32[]{:S(2)}) async-start(bf16[8,40,128]{2,1,0:T(8,128)(2,1)} %sample_values.1), calls=%async_computation.1 | async-start | bytes 163840 | tf_op jit(solution)/shard_map/all_to_all | solution.py:764
  35.1 1.7 %stem.1.second = bf16[20,32,256]{2,1,0:T(8,128)(2,1)S(1)} custom-call(s32[2]{0:T(128)S(1)} %copy-done.5, bf16[8,4,256]{2,1,0:T(4,128)(2,1)S(1)} %bitcast.15, bf16[8,4,256]{2,1,0:T(4,128)(2,1)S(1)} %collective-permute-done.1.near_ref, bf16[8,4,256]{2,1,0:T(4,128)(2,1)S(1)} %collective-permute-done.2.far_ref, bf16[9,4,32]{2,1,0:T(4,128)(2,1)S(1)} %bitcast.19, ...), custom_call_target="tpu_custom_call" | custom-call | flops 1000000000 | bytes 1048576 | tf_op jit(solution)/shard_map/stem/pallas_call | solution.py:659
  36.8 0.0 copy-start.6
  36.8 0.0 copy-start.7
  36.8 1.3 %middle.1.third = bf16[8,112,128]{2,1,0:T(8,128)(2,1)S(1)} custom-call(s32[2]{0:T(128)S(1)} %copy-done.5, bf16[20,32,256]{2,1,0:T(8,128)(2,1)S(1)} %stem.1.second, bf16[9,32,112]{2,1,0:T(8,128)(2,1)S(1)} %bitcast.18), custom_call_target="tpu_custom_call" | custom-call | flops 500000000 | bytes 1048576 | tf_op jit(solution)/shard_map/middle/pallas_call | solution.py:681
  38.1 3.0 %all-to-all-done.1.value_ref = bf16[8,40,128]{2,1,0:T(8,128)(2,1)S(1)} async-done(((bf16[8,40,128]{2,1,0:T(8,128)(2,1)}), bf16[8,40,128]{2,1,0:T(8,128)(2,1)S(1)}, u32[]{:S(2)}, u32[]{:S(2)}) %all-to-all-start.1) | async-done | bytes 81952 | tf_op jit(solution)/shard_map/all_to_all | solution.py:764
  41.1 0.2 gbuffer.1
  41.3 1.5 %collective-permute-start.3 = (bf16[1,4,8,256]{3,2,1,0:T(8,128)(2,1)S(1)}, bf16[1,4,8,256]{3,2,1,0:T(8,128)(2,1)S(1)}, u32[]{:S(2)}, u32[]{:S(2)}) collective-permute-start(bf16[1,4,8,256]{3,2,1,0:T(8,128)(2,1)S(1)} %gbuffer.1), channel_id=1, source_target_pairs={{0,8},{8,16},{16,24},{24,0},{1,9},{9,17},{17,25},{25,1},{2,10},{10... | collective-permute-start | bytes 49160 | tf_op jit(solution)/shard_map/ppermute | solution.py:771
  42.8 2.9 %decoder.1 = bf16[1,3,8,256]{3,2,1,0:T(8,128)(2,1)} custom-call(s32[2]{0:T(128)S(1)} %copy-done.5, bf16[20,32,256]{2,1,0:T(8,128)(2,1)S(1)} %stem.1.second, bf16[8,112,128]{2,1,0:T(8,128)(2,1)S(1)} %middle.1.third, bf16[9,112,112]{2,1,0:T(8,128)(2,1)S(1)} %copy-done.6, bf16[9,32,144]{2,1,0:T(8,128)(2,1)S(1)} %copy-done.7, bf16[9,3,32]{2,1,0:T(4,128)(2,1)S(1)} %copy-done.11), custom_call_target="tpu_custom_call" | custom-call | flops 1500000000 | bytes 1048576 | tf_op jit(solution)/shard_map/decoder/pallas_call | solution.py:699
  45.7 0.3 collective-permute-done.3
  46.0 0.6 %copy.19 = bf16[1,4,8,256]{3,2,1,0:T(8,128)(2,1)} copy(bf16[1,4,8,256]{3,2,1,0:T(8,128)(2,1)S(1)} %collective-permute-done.3) | data formatting | bytes 32768
  (28 shorter events, 0.1 us)
Async XLA Ops:
  0.6 14.3 %copy-start.12 = (bf16[16,39304]{1,0:T(8,128)(2,1)S(1)}, bf16[16,39304]{1,0:T(8,128)(2,1)}, u32[]{:S(2)}) copy-start(bf16[16,39304]{1,0:T(8,128)(2,1)} %param.12) | copy-start | bytes 3773188
  0.6 8.6 %copy-start.13 = (bf16[1,4,8,256]{3,2,1,0:T(8,128)(2,1)S(1)}, bf16[1,4,8,256]{3,2,1,0:T(8,128)(2,1)}, u32[]{:S(2)}) copy-start(bf16[1,4,8,256]{3,2,1,0:T(8,128)(2,1)} %param.17) | copy-start | bytes 49156
  2.9 21.1 %all-to-all-start = ((f32[8,120,128]{2,1,0:T(8,128)}), f32[8,120,128]{2,1,0:T(8,128)}, u32[]{:S(2)}, u32[]{:S(2)}) async-start(f32[8,120,128]{2,1,0:T(8,128)} %positions.1.place_ref), calls=%async_computation | async-start | bytes 983040 | tf_op jit(solution)/shard_map/all_to_all | solution.py:746
  9.2 8.1 %copy-start = (f32[8,120,128]{2,1,0:T(8,128)S(1)}, f32[8,120,128]{2,1,0:T(8,128)}, u32[]{:S(2)}) copy-start(f32[8,120,128]{2,1,0:T(8,128)} %positions.1.place_ref) | copy-start | bytes 1474564
  9.2 8.1 %copy-start.3 = (s32[1,1,8,2]{2,3,1,0:T(2,128)S(1)}, s32[1,1,8,2]{2,3,1,0:T(2,128)}, u32[]{:S(2)}) copy-start(s32[1,1,8,2]{2,3,1,0:T(2,128)} %param.13) | copy-start | bytes 196
  9.2 22.4 %collective-permute-start.1 = (bf16[8,4,256]{2,1,0:T(4,128)(2,1)S(1)}, bf16[8,4,256]{2,1,0:T(4,128)(2,1)S(1)}, u32[]{:S(2)}, u32[]{:S(2)}) collective-permute-start(bf16[8,4,256]{2,1,0:T(4,128)(2,1)S(1)} %bitcast.13), channel_id=1, source_target_pairs={{0,1},{1,0},{2,3},{3,2},{4,5},{5,4},{6,7},{7,6},{8,9},{9,8},{10,11... | collective-permute-start | bytes 49160 | tf_op jit(solution)/shard_map/ppermute | solution.py:756
  9.8 21.8 %collective-permute-start.2 = (bf16[8,4,256]{2,1,0:T(4,128)(2,1)S(1)}, bf16[8,4,256]{2,1,0:T(4,128)(2,1)S(1)}, u32[]{:S(2)}, u32[]{:S(2)}) collective-permute-start(bf16[8,4,256]{2,1,0:T(4,128)(2,1)S(1)} %bitcast.14), channel_id=1, source_target_pairs={{1,2},{2,1},{3,4},{4,3},{5,6},{6,5},{9,10},{10,9},{11,12},{12,11},... | collective-permute-start | bytes 49160 | tf_op jit(solution)/shard_map/ppermute | solution.py:757
  11.9 5.4 %collective-permute-start = (f32[1,120,128]{2,1,0:T(8,128)}, f32[1,120,128]{2,1,0:T(8,128)S(1)}, u32[]{:S(2)}, u32[]{:S(2)}) collective-permute-start(f32[1,120,128]{2,1,0:T(8,128)} %constant_dynamic-slice_fusion), channel_id=1, source_target_pairs={{0,1},{1,0},{2,3},{3,2},{4,5},{5,4},{6,7},{7,6},{8,9},{9,8},{10,11... | collective-permute-start | bytes 184328 | tf_op jit(solution)/shard_map/ppermute | solution.py:754
  17.3 4.0 %copy-start.4 = (s32[2]{0:T(128)}, s32[2]{0:T(128)S(1)}, u32[]{:S(2)}) copy-start(s32[2]{0:T(128)S(1)} %pad_add_fusion.where_ref) | copy-start | bytes 28
  21.3 1.2 %copy-start.1 = (bf16[17,208,256]{2,1,0:T(8,128)(2,1)}, bf16[17,208,256]{2,1,0:T(8,128)(2,1)S(1)}, u32[]{:S(2)}) copy-start(bf16[17,208,256]{2,1,0:T(8,128)(2,1)S(1)} %brick_windows.1.brick_ref) | copy-start | bytes 5431300
  22.5 12.5 %copy-start.8 = (bf16[9,32,32]{2,1,0:T(8,128)(2,1)S(1)}, bf16[9,32,32]{2,1,0:T(8,128)(2,1)}, u32[]{:S(2)}) copy-start(bf16[9,32,32]{2,1,0:T(8,128)(2,1)} %w_mid.1) | copy-start | bytes 55300
  22.5 12.5 %copy-start.10 = (bf16[9,32,4]{1,2,0:T(4,128)(2,1)S(1)}, bf16[9,32,4]{1,2,0:T(4,128)(2,1)}, u32[]{:S(2)}) copy-start(bf16[9,32,4]{1,2,0:T(4,128)(2,1)} %param.18) | copy-start | bytes 6916
  24.0 11.1 %copy-start.5 = (s32[2]{0:T(128)S(1)}, s32[2]{0:T(128)}, u32[]{:S(2)}) copy-start(s32[2]{0:T(128)} %copy-done.4) | copy-start | bytes 28
  31.6 9.4 %all-to-all-start.1 = ((bf16[8,40,128]{2,1,0:T(8,128)(2,1)}), bf16[8,40,128]{2,1,0:T(8,128)(2,1)S(1)}, u32[]{:S(2)}, u32[]{:S(2)}) async-start(bf16[8,40,128]{2,1,0:T(8,128)(2,1)} %sample_values.1), calls=%async_computation.1 | async-start | bytes 163840 | tf_op jit(solution)/shard_map/all_to_all | solution.py:764
  35.0 1.8 %copy-start.9 = (bf16[9,112,32]{1,2,0:T(8,128)(2,1)S(1)}, bf16[9,112,32]{1,2,0:T(8,128)(2,1)}, u32[]{:S(2)}) copy-start(bf16[9,112,32]{1,2,0:T(8,128)(2,1)} %param.20) | copy-start | bytes 193540
  36.7 4.3 %copy-start.2 = (s32[1,1,160,256]{3,2,1,0:T(8,128)S(1)}, s32[1,1,160,256]{3,2,1,0:T(8,128)}, u32[]{:S(2)}) copy-start(s32[1,1,160,256]{3,2,1,0:T(8,128)} %order_ref.1) | copy-start | bytes 491524
  36.8 6.1 %copy-start.6 = (bf16[9,112,112]{2,1,0:T(8,128)(2,1)S(1)}, bf16[9,112,112]{2,1,0:T(8,128)(2,1)}, u32[]{:S(2)}) copy-start(bf16[9,112,112]{2,1,0:T(8,128)(2,1)} %w_deep.1) | copy-start | bytes 677380
  36.8 6.1 %copy-start.7 = (bf16[9,32,144]{2,1,0:T(8,128)(2,1)S(1)}, bf16[9,32,144]{2,1,0:T(8,128)(2,1)}, u32[]{:S(2)}) copy-start(bf16[9,32,144]{2,1,0:T(8,128)(2,1)} %w_up.1) | copy-start | bytes 248836
  36.8 6.0 %copy-start.11 = (bf16[9,3,32]{2,1,0:T(4,128)(2,1)S(1)}, bf16[9,3,32]{2,1,0:T(4,128)(2,1)}, u32[]{:S(2)}) copy-start(bf16[9,3,32]{2,1,0:T(4,128)(2,1)} %w_out.1) | copy-start | bytes 5188
  41.3 4.7 %collective-permute-start.3 = (bf16[1,4,8,256]{3,2,1,0:T(8,128)(2,1)S(1)}, bf16[1,4,8,256]{3,2,1,0:T(8,128)(2,1)S(1)}, u32[]{:S(2)}, u32[]{:S(2)}) collective-permute-start(bf16[1,4,8,256]{3,2,1,0:T(8,128)(2,1)S(1)} %gbuffer.1), channel_id=1, source_target_pairs={{0,8},{8,16},{16,24},{24,0},{1,9},{9,17},{17,25},{25,1},{2,10},{10... | collective-permute-start | bytes 49160 | tf_op jit(solution)/shard_map/ppermute | solution.py:771

commit v21 on v20

--- a/solution.py
+++ b/solution.py
@@ -60,8 +60,8 @@
         )
 
     for piece in pieces:
-        for copy in reads(*piece):
-            copy.start()
+        for number, copy in enumerate(reads(*piece)):
+            copy.start(priority=number)
     for axis, part in pieces:
         for copy in reads(axis, part):
             copy.wait()
@@ -317,8 +317,8 @@
         return copies
 
     def start(turn, members):
-        for copy in fetches(turn, members):
-            copy.start()
+        for number, copy in enumerate(fetches(turn, members)):
+            copy.start(priority=number % 2)
 
     def work(turn, members):
         held = turn % 2

time: 47 us -> 47.1 us (level)
  no operation moved by 1% of the time
where the time goes in v21:
time: 47.1 us; the launch traced here: 46.6 us
  Pallas kernels  19.9 us (42%)
  starting transfers between devices  15.5 us (33%)
  local copies, waits for them, and re-layouts  5.67 us (12%)
  waiting for transfers between devices  4.7 us (10%)
  between operations  0.87 us (2%)
    pallas_call x1, Pallas kernels, sample_values(): pl.pallas_call(samples_kernel, out_shape=jax.ShapeDtypeStruct((owners, ro...  7.63 us
    all_to_all x1, starting transfers between devices, on_device(): lax.all_to_all(places, 'tile', split_axis=0, concat_axis=0, tiled=True)  6.34 us
    pallas_call x1, Pallas kernels, windows_of(): pl.pallas_call(windows_kernel, out_shape=jax.ShapeDtypeStruct((count + 1,...  3.92 us
    all_to_all x1, starting transfers between devices, on_device(): lax.all_to_all(found, 'tile', split_axis=0, concat_axis=0, tiled=True)  3.37 us
    ppermute x1, starting transfers between devices, on_device(): mate_places = lax.ppermute(for_mate, 'tile', mates)  3.03 us
    all_to_all x1, waiting for transfers between devices, on_device(): lax.all_to_all(found, 'tile', split_axis=0, concat_axis=0, tiled=True)  3 us
    pallas_call x1, Pallas kernels, decoder(): pl.pallas_call(decoder_kernel, out_shape=jax.ShapeDtypeStruct((1, colours...  2.88 us
    reshape x1, local copies, waits for them, and re-layouts, windows_of(): cube = bricks.reshape(count, EDGE, EDGE * EDGE)  2.31 us
  transfers between devices with their start and end apart: 6, of which 3 were waited for; matrix products, arithmetic and copies ran while one was open for 8% of the time, Pallas kernels for 37%

profile of v21, /device:TPU:0, one launch (start us, length us, event | category | flops | bytes accessed | tf_op | source)
XLA Modules:
  0.0 46.6 jit_solution(8955817011445190926)
XLA Ops:
  0.7 2.3 %positions.1.place_ref = f32[8,120,128]{2,1,0:T(8,128)} custom-call(s32[3,320,128]{2,1,0:T(8,128)} %bitcast.20, f32[3,320,128]{2,1,0:T(8,128)} %bitcast.21), custom_call_target="tpu_custom_call" | custom-call | flops 122880 | bytes 1474560 | tf_op jit(solution)/shard_map/positions/pallas_call | solution.py:82
  3.0 6.3 %all-to-all-start = ((f32[8,120,128]{2,1,0:T(8,128)}), f32[8,120,128]{2,1,0:T(8,128)}, u32[]{:S(2)}, u32[]{:S(2)}) async-start(f32[8,120,128]{2,1,0:T(8,128)} %positions.1.place_ref), calls=%async_computation | async-start | bytes 983040 | tf_op jit(solution)/shard_map/all_to_all | solution.py:746
  9.3 0.0 copy-start.3
  9.3 0.6 %collective-permute-start.1 = (bf16[8,4,256]{2,1,0:T(4,128)(2,1)S(1)}, bf16[8,4,256]{2,1,0:T(4,128)(2,1)S(1)}, u32[]{:S(2)}, u32[]{:S(2)}) collective-permute-start(bf16[8,4,256]{2,1,0:T(4,128)(2,1)S(1)} %bitcast.13), channel_id=1, source_target_pairs={{0,1},{1,0},{2,3},{3,2},{4,5},{5,4},{6,7},{7,6},{8,9},{9,8},{10,11... | collective-permute-start | bytes 49160 | tf_op jit(solution)/shard_map/ppermute | solution.py:756
  9.9 0.7 %collective-permute-start.2 = (bf16[8,4,256]{2,1,0:T(4,128)(2,1)S(1)}, bf16[8,4,256]{2,1,0:T(4,128)(2,1)S(1)}, u32[]{:S(2)}, u32[]{:S(2)}) collective-permute-start(bf16[8,4,256]{2,1,0:T(4,128)(2,1)S(1)} %bitcast.14), channel_id=1, source_target_pairs={{1,2},{2,1},{3,4},{4,3},{5,6},{6,5},{9,10},{10,9},{11,12},{12,11},... | collective-permute-start | bytes 49160 | tf_op jit(solution)/shard_map/ppermute | solution.py:757
  10.6 1.5 %constant_dynamic-slice_fusion = f32[1,120,128]{2,1,0:T(8,128)} fusion(f32[8,120,128]{2,1,0:T(8,128)} %positions.1.place_ref, s32[]{:T(128)S(6)} %select_n.3), kind=kLoop, calls=%fused_computation.2 | loop fusion | bytes 122884 | tf_op jit(solution)/shard_map/dynamic_slice | solution.py:753
  12.0 3.0 %collective-permute-start = (f32[1,120,128]{2,1,0:T(8,128)}, f32[1,120,128]{2,1,0:T(8,128)S(1)}, u32[]{:S(2)}, u32[]{:S(2)}) collective-permute-start(f32[1,120,128]{2,1,0:T(8,128)} %constant_dynamic-slice_fusion), channel_id=1, source_target_pairs={{0,1},{1,0},{2,3},{3,2},{4,5},{5,4},{6,7},{7,6},{8,9},{9,8},{10,11... | collective-permute-start | bytes 184328 | tf_op jit(solution)/shard_map/ppermute | solution.py:754
  15.0 2.3 %reshape.15.cube_ref = bf16[16,34,1156]{2,1,0:T(8,128)(2,1)S(1)} reshape(bf16[16,39304]{1,0:T(8,128)(2,1)S(1)} %copy-done.12) | data formatting | bytes 2515456 | tf_op jit(solution)/shard_map/reshape | solution.py:166
  17.4 0.1 pad_add_fusion.where_ref
  17.4 3.9 %brick_windows.1.brick_ref = bf16[17,208,256]{2,1,0:T(8,128)(2,1)S(1)} custom-call(s32[2]{0:T(128)S(1)} %pad_add_fusion.where_ref, s32[2,8]{1,0:T(2,128)S(1)} %bitcast.17, bf16[16,34,1156]{2,1,0:T(8,128)(2,1)S(1)} %reshape.15.cube_ref, f32[8,120,128]{2,1,0:T(8,128)S(1)} %copy-done, f32[1,120,128]{2,1,0:T(8,128)S(1)} %collective-permute-done.mate_place_ref), custom_call_target="tpu_custom_call" | custom-call | flops 905969664 | bytes 4194304 | tf_op jit(solution)/shard_map/brick_windows/pallas_call | solution.py:168
  21.4 1.2 %copy-done.1 = bf16[17,208,256]{2,1,0:T(8,128)(2,1)} copy-done((bf16[17,208,256]{2,1,0:T(8,128)(2,1)}, bf16[17,208,256]{2,1,0:T(8,128)(2,1)S(1)}, u32[]{:S(2)}) %copy-start.1) | copy-done | bytes 1810456
  22.6 1.4 %all-to-all-done.place_ref = f32[8,120,128]{2,1,0:T(8,128)} async-done(((f32[8,120,128]{2,1,0:T(8,128)}), f32[8,120,128]{2,1,0:T(8,128)}, u32[]{:S(2)}, u32[]{:S(2)}) %all-to-all-start) | async-done | bytes 491552 | tf_op jit(solution)/shard_map/all_to_all | solution.py:746
  24.1 7.6 %sample_values.1 = bf16[8,40,128]{2,1,0:T(8,128)(2,1)} custom-call(s32[2]{0:T(128)} %copy-done.4, s32[2,8]{1,0:T(2,128)} %bitcast.16, bf16[17,208,256]{2,1,0:T(8,128)(2,1)} %copy-done.1, f32[8,120,128]{2,1,0:T(8,128)} %all-to-all-done.place_ref), custom_call_target="tpu_custom_call" | custom-call | flops 4362076160 | bytes 3145728 | tf_op jit(solution)/shard_map/sample_values/pallas_call | solution.py:373
  31.7 3.4 %all-to-all-start.1 = ((bf16[8,40,128]{2,1,0:T(8,128)(2,1)}), bf16[8,40,128]{2,1,0:T(8,128)(2,1)S(1)}, u32[]{:S(2)}, u32[]{:S(2)}) async-start(bf16[8,40,128]{2,1,0:T(8,128)(2,1)} %sample_values.1), calls=%async_computation.1 | async-start | bytes 163840 | tf_op jit(solution)/shard_map/all_to_all | solution.py:764
  35.1 1.7 %stem.1.second = bf16[20,32,256]{2,1,0:T(8,128)(2,1)S(1)} custom-call(s32[2]{0:T(128)S(1)} %copy-done.5, bf16[8,4,256]{2,1,0:T(4,128)(2,1)S(1)} %bitcast.15, bf16[8,4,256]{2,1,0:T(4,128)(2,1)S(1)} %collective-permute-done.1.near_ref, bf16[8,4,256]{2,1,0:T(4,128)(2,1)S(1)} %collective-permute-done.2.far_ref, bf16[9,4,32]{2,1,0:T(4,128)(2,1)S(1)} %bitcast.19, ...), custom_call_target="tpu_custom_call" | custom-call | flops 1000000000 | bytes 1048576 | tf_op jit(solution)/shard_map/stem/pallas_call | solution.py:659
  36.8 0.0 copy-start.2
  36.9 0.0 copy-start.7
  36.9 1.3 %middle.1.third = bf16[8,112,128]{2,1,0:T(8,128)(2,1)S(1)} custom-call(s32[2]{0:T(128)S(1)} %copy-done.5, bf16[20,32,256]{2,1,0:T(8,128)(2,1)S(1)} %stem.1.second, bf16[9,32,112]{2,1,0:T(8,128)(2,1)S(1)} %bitcast.18), custom_call_target="tpu_custom_call" | custom-call | flops 500000000 | bytes 1048576 | tf_op jit(solution)/shard_map/middle/pallas_call | solution.py:681
  38.1 3.0 %all-to-all-done.1.value_ref = bf16[8,40,128]{2,1,0:T(8,128)(2,1)S(1)} async-done(((bf16[8,40,128]{2,1,0:T(8,128)(2,1)}), bf16[8,40,128]{2,1,0:T(8,128)(2,1)S(1)}, u32[]{:S(2)}, u32[]{:S(2)}) %all-to-all-start.1) | async-done | bytes 81952 | tf_op jit(solution)/shard_map/all_to_all | solution.py:764
  41.2 0.2 gbuffer.1
  41.4 1.5 %collective-permute-start.3 = (bf16[1,4,8,256]{3,2,1,0:T(8,128)(2,1)S(1)}, bf16[1,4,8,256]{3,2,1,0:T(8,128)(2,1)S(1)}, u32[]{:S(2)}, u32[]{:S(2)}) collective-permute-start(bf16[1,4,8,256]{3,2,1,0:T(8,128)(2,1)S(1)} %gbuffer.1), channel_id=1, source_target_pairs={{0,8},{8,16},{16,24},{24,0},{1,9},{9,17},{17,25},{25,1},{2,10},{10... | collective-permute-start | bytes 49160 | tf_op jit(solution)/shard_map/ppermute | solution.py:771
  42.9 2.9 %decoder.1 = bf16[1,3,8,256]{3,2,1,0:T(8,128)(2,1)} custom-call(s32[2]{0:T(128)S(1)} %copy-done.5, bf16[20,32,256]{2,1,0:T(8,128)(2,1)S(1)} %stem.1.second, bf16[8,112,128]{2,1,0:T(8,128)(2,1)S(1)} %middle.1.third, bf16[9,112,112]{2,1,0:T(8,128)(2,1)S(1)} %copy-done.6, bf16[9,32,144]{2,1,0:T(8,128)(2,1)S(1)} %copy-done.7, bf16[9,3,32]{2,1,0:T(4,128)(2,1)S(1)} %copy-done.11), custom_call_target="tpu_custom_call" | custom-call | flops 1500000000 | bytes 1048576 | tf_op jit(solution)/shard_map/decoder/pallas_call | solution.py:699
  45.8 0.3 collective-permute-done.3
  46.0 0.6 %copy.19 = bf16[1,4,8,256]{3,2,1,0:T(8,128)(2,1)} copy(bf16[1,4,8,256]{3,2,1,0:T(8,128)(2,1)S(1)} %collective-permute-done.3) | data formatting | bytes 32768
  (28 shorter events, 0.1 us)
Async XLA Ops:
  0.6 14.4 %copy-start.12 = (bf16[16,39304]{1,0:T(8,128)(2,1)S(1)}, bf16[16,39304]{1,0:T(8,128)(2,1)}, u32[]{:S(2)}) copy-start(bf16[16,39304]{1,0:T(8,128)(2,1)} %param.12) | copy-start | bytes 3773188
  0.6 8.7 %copy-start.13 = (bf16[1,4,8,256]{3,2,1,0:T(8,128)(2,1)S(1)}, bf16[1,4,8,256]{3,2,1,0:T(8,128)(2,1)}, u32[]{:S(2)}) copy-start(bf16[1,4,8,256]{3,2,1,0:T(8,128)(2,1)} %param.17) | copy-start | bytes 49156
  3.0 21.1 %all-to-all-start = ((f32[8,120,128]{2,1,0:T(8,128)}), f32[8,120,128]{2,1,0:T(8,128)}, u32[]{:S(2)}, u32[]{:S(2)}) async-start(f32[8,120,128]{2,1,0:T(8,128)} %positions.1.place_ref), calls=%async_computation | async-start | bytes 983040 | tf_op jit(solution)/shard_map/all_to_all | solution.py:746
  9.3 8.1 %copy-start = (f32[8,120,128]{2,1,0:T(8,128)S(1)}, f32[8,120,128]{2,1,0:T(8,128)}, u32[]{:S(2)}) copy-start(f32[8,120,128]{2,1,0:T(8,128)} %positions.1.place_ref) | copy-start | bytes 1474564
  9.3 8.1 %copy-start.3 = (s32[1,1,8,2]{2,3,1,0:T(2,128)S(1)}, s32[1,1,8,2]{2,3,1,0:T(2,128)}, u32[]{:S(2)}) copy-start(s32[1,1,8,2]{2,3,1,0:T(2,128)} %param.13) | copy-start | bytes 196
  9.3 22.4 %collective-permute-start.1 = (bf16[8,4,256]{2,1,0:T(4,128)(2,1)S(1)}, bf16[8,4,256]{2,1,0:T(4,128)(2,1)S(1)}, u32[]{:S(2)}, u32[]{:S(2)}) collective-permute-start(bf16[8,4,256]{2,1,0:T(4,128)(2,1)S(1)} %bitcast.13), channel_id=1, source_target_pairs={{0,1},{1,0},{2,3},{3,2},{4,5},{5,4},{6,7},{7,6},{8,9},{9,8},{10,11... | collective-permute-start | bytes 49160 | tf_op jit(solution)/shard_map/ppermute | solution.py:756
  9.9 21.8 %collective-permute-start.2 = (bf16[8,4,256]{2,1,0:T(4,128)(2,1)S(1)}, bf16[8,4,256]{2,1,0:T(4,128)(2,1)S(1)}, u32[]{:S(2)}, u32[]{:S(2)}) collective-permute-start(bf16[8,4,256]{2,1,0:T(4,128)(2,1)S(1)} %bitcast.14), channel_id=1, source_target_pairs={{1,2},{2,1},{3,4},{4,3},{5,6},{6,5},{9,10},{10,9},{11,12},{12,11},... | collective-permute-start | bytes 49160 | tf_op jit(solution)/shard_map/ppermute | solution.py:757
  12.0 5.4 %collective-permute-start = (f32[1,120,128]{2,1,0:T(8,128)}, f32[1,120,128]{2,1,0:T(8,128)S(1)}, u32[]{:S(2)}, u32[]{:S(2)}) collective-permute-start(f32[1,120,128]{2,1,0:T(8,128)} %constant_dynamic-slice_fusion), channel_id=1, source_target_pairs={{0,1},{1,0},{2,3},{3,2},{4,5},{5,4},{6,7},{7,6},{8,9},{9,8},{10,11... | collective-permute-start | bytes 184328 | tf_op jit(solution)/shard_map/ppermute | solution.py:754
  17.4 3.9 %copy-start.4 = (s32[2]{0:T(128)}, s32[2]{0:T(128)S(1)}, u32[]{:S(2)}) copy-start(s32[2]{0:T(128)S(1)} %pad_add_fusion.where_ref) | copy-start | bytes 28
  21.4 1.2 %copy-start.1 = (bf16[17,208,256]{2,1,0:T(8,128)(2,1)}, bf16[17,208,256]{2,1,0:T(8,128)(2,1)S(1)}, u32[]{:S(2)}) copy-start(bf16[17,208,256]{2,1,0:T(8,128)(2,1)S(1)} %brick_windows.1.brick_ref) | copy-start | bytes 5431300
  22.6 12.5 %copy-start.8 = (bf16[9,32,32]{2,1,0:T(8,128)(2,1)S(1)}, bf16[9,32,32]{2,1,0:T(8,128)(2,1)}, u32[]{:S(2)}) copy-start(bf16[9,32,32]{2,1,0:T(8,128)(2,1)} %w_mid.1) | copy-start | bytes 55300
  22.6 12.5 %copy-start.10 = (bf16[9,32,4]{1,2,0:T(4,128)(2,1)S(1)}, bf16[9,32,4]{1,2,0:T(4,128)(2,1)}, u32[]{:S(2)}) copy-start(bf16[9,32,4]{1,2,0:T(4,128)(2,1)} %param.18) | copy-start | bytes 6916
  24.1 11.1 %copy-start.5 = (s32[2]{0:T(128)S(1)}, s32[2]{0:T(128)}, u32[]{:S(2)}) copy-start(s32[2]{0:T(128)} %copy-done.4) | copy-start | bytes 28
  31.7 9.4 %all-to-all-start.1 = ((bf16[8,40,128]{2,1,0:T(8,128)(2,1)}), bf16[8,40,128]{2,1,0:T(8,128)(2,1)S(1)}, u32[]{:S(2)}, u32[]{:S(2)}) async-start(bf16[8,40,128]{2,1,0:T(8,128)(2,1)} %sample_values.1), calls=%async_computation.1 | async-start | bytes 163840 | tf_op jit(solution)/shard_map/all_to_all | solution.py:764
  35.1 1.8 %copy-start.9 = (bf16[9,112,32]{1,2,0:T(8,128)(2,1)S(1)}, bf16[9,112,32]{1,2,0:T(8,128)(2,1)}, u32[]{:S(2)}) copy-start(bf16[9,112,32]{1,2,0:T(8,128)(2,1)} %param.20) | copy-start | bytes 193540
  36.8 4.3 %copy-start.2 = (s32[1,1,160,256]{3,2,1,0:T(8,128)S(1)}, s32[1,1,160,256]{3,2,1,0:T(8,128)}, u32[]{:S(2)}) copy-start(s32[1,1,160,256]{3,2,1,0:T(8,128)} %order_ref.1) | copy-start | bytes 491524
  36.8 6.1 %copy-start.6 = (bf16[9,112,112]{2,1,0:T(8,128)(2,1)S(1)}, bf16[9,112,112]{2,1,0:T(8,128)(2,1)}, u32[]{:S(2)}) copy-start(bf16[9,112,112]{2,1,0:T(8,128)(2,1)} %w_deep.1) | copy-start | bytes 677380
  36.9 6.0 %copy-start.7 = (bf16[9,32,144]{2,1,0:T(8,128)(2,1)S(1)}, bf16[9,32,144]{2,1,0:T(8,128)(2,1)}, u32[]{:S(2)}) copy-start(bf16[9,32,144]{2,1,0:T(8,128)(2,1)} %w_up.1) | copy-start | bytes 248836
  36.9 6.0 %copy-start.11 = (bf16[9,3,32]{2,1,0:T(4,128)(2,1)S(1)}, bf16[9,3,32]{2,1,0:T(4,128)(2,1)}, u32[]{:S(2)}) copy-start(bf16[9,3,32]{2,1,0:T(4,128)(2,1)} %w_out.1) | copy-start | bytes 5188
  41.4 4.7 %collective-permute-start.3 = (bf16[1,4,8,256]{3,2,1,0:T(8,128)(2,1)S(1)}, bf16[1,4,8,256]{3,2,1,0:T(8,128)(2,1)S(1)}, u32[]{:S(2)}, u32[]{:S(2)}) collective-permute-start(bf16[1,4,8,256]{3,2,1,0:T(8,128)(2,1)S(1)} %gbuffer.1), channel_id=1, source_target_pairs={{0,8},{8,16},{16,24},{24,0},{1,9},{9,17},{17,25},{25,1},{2,10},{10... | collective-permute-start | bytes 49160 | tf_op jit(solution)/shard_map/ppermute | solution.py:771

commit v22 on v20

--- a/solution.py
+++ b/solution.py
@@ -210,10 +210,16 @@
             jnp.where(here == lower, low_share, jnp.where(here == upper, high_share, nothing))
         )
     window = jnp.floor(px * (1.0 / STRIDE))
-    weight_x = hat(eight - (px - STRIDE * window))
+    local_x = jnp.maximum(px - STRIDE * window, 0.0)
+    weight_x = hat(eight - local_x)
     parts = []
+    cell_x = jnp.floor(local_x)
+    frac_x = local_x - cell_x
+    place_x, low_x, high_x = tile(cell_x), tile(1.0 - frac_x), tile(frac_x)
+    hits = [place_x == i for i in range(STRIDE + 1)]
     for i in range(STRIDE + 1):
-        share = tile(jnp.broadcast_to(weight_x[i : i + 1], (8, width)))
+        share = nothing if i == 0 else jnp.where(hits[i - 1], high_x, nothing)
+        share = jnp.where(hits[i], low_x, share)
         parts += [share * part for part in weight_y]
     tail = [weight_x * hat(MAIN - py), weight_x * jnp.maximum(py - MAIN, 0.0)]
     parts.append(jnp.concatenate(tail, axis=0).astype(BF16))

time: 47 us -> 47.7 us (1.015)
  Pallas kernels: 19.8 us -> 20.8 us
    pallas_call x1, Pallas kernels: 7.64 us -> 8.36 us  [sample_values(): pl.pallas_call(samples_kernel, out_shape=jax.ShapeDtypeStruct((owners, ro...]
  transfers between devices with their start and end apart: 6 -> 6, of which waited for: 3 -> 3; matrix products, arithmetic and copies ran while one was open for 8% -> 8% of each run, Pallas kernels for 37% -> 39%
where the time goes in v22:
time: 47.7 us; the launch traced here: 47.3 us
  Pallas kernels  20.8 us (44%)
  starting transfers between devices  15.5 us (32%)
  local copies, waits for them, and re-layouts  5.67 us (12%)
  waiting for transfers between devices  4.44 us (9%)
  between operations  0.87 us (2%)
    pallas_call x1, Pallas kernels, sample_values(): pl.pallas_call(samples_kernel, out_shape=jax.ShapeDtypeStruct((owners, ro...  8.36 us
    all_to_all x1, starting transfers between devices, on_device(): lax.all_to_all(places, 'tile', split_axis=0, concat_axis=0, tiled=True)  6.34 us
    pallas_call x1, Pallas kernels, windows_of(): pl.pallas_call(windows_kernel, out_shape=jax.ShapeDtypeStruct((count + 1,...  4.18 us
    all_to_all x1, starting transfers between devices, on_device(): lax.all_to_all(found, 'tile', split_axis=0, concat_axis=0, tiled=True)  3.37 us
    ppermute x1, starting transfers between devices, on_device(): mate_places = lax.ppermute(for_mate, 'tile', mates)  3.03 us
    all_to_all x1, waiting for transfers between devices, on_device(): lax.all_to_all(found, 'tile', split_axis=0, concat_axis=0, tiled=True)  3 us
    pallas_call x1, Pallas kernels, decoder(): pl.pallas_call(decoder_kernel, out_shape=jax.ShapeDtypeStruct((1, colours...  2.88 us
    reshape x1, local copies, waits for them, and re-layouts, windows_of(): cube = bricks.reshape(count, EDGE, EDGE * EDGE)  2.31 us
  transfers between devices with their start and end apart: 6, of which 3 were waited for; matrix products, arithmetic and copies ran while one was open for 8% of the time, Pallas kernels for 39%

profile of v22, /device:TPU:0, one launch (start us, length us, event | category | flops | bytes accessed | tf_op | source)
XLA Modules:
  0.0 47.3 jit_solution(12729433401936159155)
XLA Ops:
  0.7 2.2 %positions.1.place_ref = f32[8,120,128]{2,1,0:T(8,128)} custom-call(s32[3,320,128]{2,1,0:T(8,128)} %bitcast.20, f32[3,320,128]{2,1,0:T(8,128)} %bitcast.21), custom_call_target="tpu_custom_call" | custom-call | flops 122880 | bytes 1474560 | tf_op jit(solution)/shard_map/positions/pallas_call | solution.py:82
  2.9 6.3 %all-to-all-start = ((f32[8,120,128]{2,1,0:T(8,128)}), f32[8,120,128]{2,1,0:T(8,128)}, u32[]{:S(2)}, u32[]{:S(2)}) async-start(f32[8,120,128]{2,1,0:T(8,128)} %positions.1.place_ref), calls=%async_computation | async-start | bytes 983040 | tf_op jit(solution)/shard_map/all_to_all | solution.py:752
  9.2 0.0 copy-start.3
  9.2 0.6 %collective-permute-start.1 = (bf16[8,4,256]{2,1,0:T(4,128)(2,1)S(1)}, bf16[8,4,256]{2,1,0:T(4,128)(2,1)S(1)}, u32[]{:S(2)}, u32[]{:S(2)}) collective-permute-start(bf16[8,4,256]{2,1,0:T(4,128)(2,1)S(1)} %bitcast.13), channel_id=1, source_target_pairs={{0,1},{1,0},{2,3},{3,2},{4,5},{5,4},{6,7},{7,6},{8,9},{9,8},{10,11... | collective-permute-start | bytes 49160 | tf_op jit(solution)/shard_map/ppermute | solution.py:762
  9.8 0.7 %collective-permute-start.2 = (bf16[8,4,256]{2,1,0:T(4,128)(2,1)S(1)}, bf16[8,4,256]{2,1,0:T(4,128)(2,1)S(1)}, u32[]{:S(2)}, u32[]{:S(2)}) collective-permute-start(bf16[8,4,256]{2,1,0:T(4,128)(2,1)S(1)} %bitcast.14), channel_id=1, source_target_pairs={{1,2},{2,1},{3,4},{4,3},{5,6},{6,5},{9,10},{10,9},{11,12},{12,11},... | collective-permute-start | bytes 49160 | tf_op jit(solution)/shard_map/ppermute | solution.py:763
  10.5 1.5 %constant_dynamic-slice_fusion = f32[1,120,128]{2,1,0:T(8,128)} fusion(f32[8,120,128]{2,1,0:T(8,128)} %positions.1.place_ref, s32[]{:T(128)S(6)} %select_n.3), kind=kLoop, calls=%fused_computation.2 | loop fusion | bytes 122884 | tf_op jit(solution)/shard_map/dynamic_slice | solution.py:759
  11.9 3.0 %collective-permute-start = (f32[1,120,128]{2,1,0:T(8,128)}, f32[1,120,128]{2,1,0:T(8,128)S(1)}, u32[]{:S(2)}, u32[]{:S(2)}) collective-permute-start(f32[1,120,128]{2,1,0:T(8,128)} %constant_dynamic-slice_fusion), channel_id=1, source_target_pairs={{0,1},{1,0},{2,3},{3,2},{4,5},{5,4},{6,7},{7,6},{8,9},{9,8},{10,11... | collective-permute-start | bytes 184328 | tf_op jit(solution)/shard_map/ppermute | solution.py:760
  15.0 2.3 %reshape.15.cube_ref = bf16[16,34,1156]{2,1,0:T(8,128)(2,1)S(1)} reshape(bf16[16,39304]{1,0:T(8,128)(2,1)S(1)} %copy-done.12) | data formatting | bytes 2515456 | tf_op jit(solution)/shard_map/reshape | solution.py:166
  17.3 0.1 pad_add_fusion.where_ref
  17.4 4.2 %brick_windows.1.brick_ref = bf16[17,208,256]{2,1,0:T(8,128)(2,1)S(1)} custom-call(s32[2]{0:T(128)S(1)} %pad_add_fusion.where_ref, s32[2,8]{1,0:T(2,128)S(1)} %bitcast.17, bf16[16,34,1156]{2,1,0:T(8,128)(2,1)S(1)} %reshape.15.cube_ref, f32[8,120,128]{2,1,0:T(8,128)S(1)} %copy-done, f32[1,120,128]{2,1,0:T(8,128)S(1)} %collective-permute-done.mate_place_ref), custom_call_target="tpu_custom_call" | custom-call | flops 905969664 | bytes 4194304 | tf_op jit(solution)/shard_map/brick_windows/pallas_call | solution.py:168
  21.6 1.2 %copy-done.1 = bf16[17,208,256]{2,1,0:T(8,128)(2,1)} copy-done((bf16[17,208,256]{2,1,0:T(8,128)(2,1)}, bf16[17,208,256]{2,1,0:T(8,128)(2,1)S(1)}, u32[]{:S(2)}) %copy-start.1) | copy-done | bytes 1810456
  22.8 1.2 %all-to-all-done.place_ref = f32[8,120,128]{2,1,0:T(8,128)} async-done(((f32[8,120,128]{2,1,0:T(8,128)}), f32[8,120,128]{2,1,0:T(8,128)}, u32[]{:S(2)}, u32[]{:S(2)}) %all-to-all-start) | async-done | bytes 491552 | tf_op jit(solution)/shard_map/all_to_all | solution.py:752
  24.0 8.4 %sample_values.1 = bf16[8,40,128]{2,1,0:T(8,128)(2,1)} custom-call(s32[2]{0:T(128)} %copy-done.4, s32[2,8]{1,0:T(2,128)} %bitcast.16, bf16[17,208,256]{2,1,0:T(8,128)(2,1)} %copy-done.1, f32[8,120,128]{2,1,0:T(8,128)} %all-to-all-done.place_ref), custom_call_target="tpu_custom_call" | custom-call | flops 4362076160 | bytes 3145728 | tf_op jit(solution)/shard_map/sample_values/pallas_call | solution.py:379
  32.4 3.4 %all-to-all-start.1 = ((bf16[8,40,128]{2,1,0:T(8,128)(2,1)}), bf16[8,40,128]{2,1,0:T(8,128)(2,1)S(1)}, u32[]{:S(2)}, u32[]{:S(2)}) async-start(bf16[8,40,128]{2,1,0:T(8,128)(2,1)} %sample_values.1), calls=%async_computation.1 | async-start | bytes 163840 | tf_op jit(solution)/shard_map/all_to_all | solution.py:770
  35.8 0.0 copy-start.9
  35.8 1.7 %stem.1.second = bf16[20,32,256]{2,1,0:T(8,128)(2,1)S(1)} custom-call(s32[2]{0:T(128)S(1)} %copy-done.5, bf16[8,4,256]{2,1,0:T(4,128)(2,1)S(1)} %bitcast.15, bf16[8,4,256]{2,1,0:T(4,128)(2,1)S(1)} %collective-permute-done.1.near_ref, bf16[8,4,256]{2,1,0:T(4,128)(2,1)S(1)} %collective-permute-done.2.far_ref, bf16[9,4,32]{2,1,0:T(4,128)(2,1)S(1)} %bitcast.19, ...), custom_call_target="tpu_custom_call" | custom-call | flops 1000000000 | bytes 1048576 | tf_op jit(solution)/shard_map/stem/pallas_call | solution.py:665
  37.5 0.0 copy-start.6
  37.5 1.3 %middle.1.third = bf16[8,112,128]{2,1,0:T(8,128)(2,1)S(1)} custom-call(s32[2]{0:T(128)S(1)} %copy-done.5, bf16[20,32,256]{2,1,0:T(8,128)(2,1)S(1)} %stem.1.second, bf16[9,32,112]{2,1,0:T(8,128)(2,1)S(1)} %bitcast.18), custom_call_target="tpu_custom_call" | custom-call | flops 500000000 | bytes 1048576 | tf_op jit(solution)/shard_map/middle/pallas_call | solution.py:687
  38.8 3.0 %all-to-all-done.1.value_ref = bf16[8,40,128]{2,1,0:T(8,128)(2,1)S(1)} async-done(((bf16[8,40,128]{2,1,0:T(8,128)(2,1)}), bf16[8,40,128]{2,1,0:T(8,128)(2,1)S(1)}, u32[]{:S(2)}, u32[]{:S(2)}) %all-to-all-start.1) | async-done | bytes 81952 | tf_op jit(solution)/shard_map/all_to_all | solution.py:770
  41.8 0.2 gbuffer.1
  42.0 1.5 %collective-permute-start.3 = (bf16[1,4,8,256]{3,2,1,0:T(8,128)(2,1)S(1)}, bf16[1,4,8,256]{3,2,1,0:T(8,128)(2,1)S(1)}, u32[]{:S(2)}, u32[]{:S(2)}) collective-permute-start(bf16[1,4,8,256]{3,2,1,0:T(8,128)(2,1)S(1)} %gbuffer.1), channel_id=1, source_target_pairs={{0,8},{8,16},{16,24},{24,0},{1,9},{9,17},{17,25},{25,1},{2,10},{10... | collective-permute-start | bytes 49160 | tf_op jit(solution)/shard_map/ppermute | solution.py:777
  43.5 2.9 %decoder.1 = bf16[1,3,8,256]{3,2,1,0:T(8,128)(2,1)} custom-call(s32[2]{0:T(128)S(1)} %copy-done.5, bf16[20,32,256]{2,1,0:T(8,128)(2,1)S(1)} %stem.1.second, bf16[8,112,128]{2,1,0:T(8,128)(2,1)S(1)} %middle.1.third, bf16[9,112,112]{2,1,0:T(8,128)(2,1)S(1)} %copy-done.6, bf16[9,32,144]{2,1,0:T(8,128)(2,1)S(1)} %copy-done.7, bf16[9,3,32]{2,1,0:T(4,128)(2,1)S(1)} %copy-done.11), custom_call_target="tpu_custom_call" | custom-call | flops 1500000000 | bytes 1048576 | tf_op jit(solution)/shard_map/decoder/pallas_call | solution.py:705
  46.4 0.3 collective-permute-done.3
  46.7 0.6 %copy.19 = bf16[1,4,8,256]{3,2,1,0:T(8,128)(2,1)} copy(bf16[1,4,8,256]{3,2,1,0:T(8,128)(2,1)S(1)} %collective-permute-done.3) | data formatting | bytes 32768
  (28 shorter events, 0.1 us)
Async XLA Ops:
  0.6 14.3 %copy-start.12 = (bf16[16,39304]{1,0:T(8,128)(2,1)S(1)}, bf16[16,39304]{1,0:T(8,128)(2,1)}, u32[]{:S(2)}) copy-start(bf16[16,39304]{1,0:T(8,128)(2,1)} %param.12) | copy-start | bytes 3773188
  0.6 8.6 %copy-start.13 = (bf16[1,4,8,256]{3,2,1,0:T(8,128)(2,1)S(1)}, bf16[1,4,8,256]{3,2,1,0:T(8,128)(2,1)}, u32[]{:S(2)}) copy-start(bf16[1,4,8,256]{3,2,1,0:T(8,128)(2,1)} %param.17) | copy-start | bytes 49156
  2.9 21.1 %all-to-all-start = ((f32[8,120,128]{2,1,0:T(8,128)}), f32[8,120,128]{2,1,0:T(8,128)}, u32[]{:S(2)}, u32[]{:S(2)}) async-start(f32[8,120,128]{2,1,0:T(8,128)} %positions.1.place_ref), calls=%async_computation | async-start | bytes 983040 | tf_op jit(solution)/shard_map/all_to_all | solution.py:752
  9.2 8.1 %copy-start = (f32[8,120,128]{2,1,0:T(8,128)S(1)}, f32[8,120,128]{2,1,0:T(8,128)}, u32[]{:S(2)}) copy-start(f32[8,120,128]{2,1,0:T(8,128)} %positions.1.place_ref) | copy-start | bytes 1474564
  9.2 8.1 %copy-start.3 = (s32[1,1,8,2]{2,3,1,0:T(2,128)S(1)}, s32[1,1,8,2]{2,3,1,0:T(2,128)}, u32[]{:S(2)}) copy-start(s32[1,1,8,2]{2,3,1,0:T(2,128)} %param.13) | copy-start | bytes 196
  9.2 23.1 %collective-permute-start.1 = (bf16[8,4,256]{2,1,0:T(4,128)(2,1)S(1)}, bf16[8,4,256]{2,1,0:T(4,128)(2,1)S(1)}, u32[]{:S(2)}, u32[]{:S(2)}) collective-permute-start(bf16[8,4,256]{2,1,0:T(4,128)(2,1)S(1)} %bitcast.13), channel_id=1, source_target_pairs={{0,1},{1,0},{2,3},{3,2},{4,5},{5,4},{6,7},{7,6},{8,9},{9,8},{10,11... | collective-permute-start | bytes 49160 | tf_op jit(solution)/shard_map/ppermute | solution.py:762
  9.8 22.6 %collective-permute-start.2 = (bf16[8,4,256]{2,1,0:T(4,128)(2,1)S(1)}, bf16[8,4,256]{2,1,0:T(4,128)(2,1)S(1)}, u32[]{:S(2)}, u32[]{:S(2)}) collective-permute-start(bf16[8,4,256]{2,1,0:T(4,128)(2,1)S(1)} %bitcast.14), channel_id=1, source_target_pairs={{1,2},{2,1},{3,4},{4,3},{5,6},{6,5},{9,10},{10,9},{11,12},{12,11},... | collective-permute-start | bytes 49160 | tf_op jit(solution)/shard_map/ppermute | solution.py:763
  11.9 5.4 %collective-permute-start = (f32[1,120,128]{2,1,0:T(8,128)}, f32[1,120,128]{2,1,0:T(8,128)S(1)}, u32[]{:S(2)}, u32[]{:S(2)}) collective-permute-start(f32[1,120,128]{2,1,0:T(8,128)} %constant_dynamic-slice_fusion), channel_id=1, source_target_pairs={{0,1},{1,0},{2,3},{3,2},{4,5},{5,4},{6,7},{7,6},{8,9},{9,8},{10,11... | collective-permute-start | bytes 184328 | tf_op jit(solution)/shard_map/ppermute | solution.py:760
  17.3 4.2 %copy-start.4 = (s32[2]{0:T(128)}, s32[2]{0:T(128)S(1)}, u32[]{:S(2)}) copy-start(s32[2]{0:T(128)S(1)} %pad_add_fusion.where_ref) | copy-start | bytes 28
  21.6 1.2 %copy-start.1 = (bf16[17,208,256]{2,1,0:T(8,128)(2,1)}, bf16[17,208,256]{2,1,0:T(8,128)(2,1)S(1)}, u32[]{:S(2)}) copy-start(bf16[17,208,256]{2,1,0:T(8,128)(2,1)S(1)} %brick_windows.1.brick_ref) | copy-start | bytes 5431300
  22.8 12.9 %copy-start.8 = (bf16[9,32,32]{2,1,0:T(8,128)(2,1)S(1)}, bf16[9,32,32]{2,1,0:T(8,128)(2,1)}, u32[]{:S(2)}) copy-start(bf16[9,32,32]{2,1,0:T(8,128)(2,1)} %w_mid.1) | copy-start | bytes 55300
  22.8 13.0 %copy-start.10 = (bf16[9,32,4]{1,2,0:T(4,128)(2,1)S(1)}, bf16[9,32,4]{1,2,0:T(4,128)(2,1)}, u32[]{:S(2)}) copy-start(bf16[9,32,4]{1,2,0:T(4,128)(2,1)} %param.18) | copy-start | bytes 6916
  24.0 11.8 %copy-start.5 = (s32[2]{0:T(128)S(1)}, s32[2]{0:T(128)}, u32[]{:S(2)}) copy-start(s32[2]{0:T(128)} %copy-done.4) | copy-start | bytes 28
  32.4 9.4 %all-to-all-start.1 = ((bf16[8,40,128]{2,1,0:T(8,128)(2,1)}), bf16[8,40,128]{2,1,0:T(8,128)(2,1)S(1)}, u32[]{:S(2)}, u32[]{:S(2)}) async-start(bf16[8,40,128]{2,1,0:T(8,128)(2,1)} %sample_values.1), calls=%async_computation.1 | async-start | bytes 163840 | tf_op jit(solution)/shard_map/all_to_all | solution.py:770
  35.8 1.8 %copy-start.9 = (bf16[9,112,32]{1,2,0:T(8,128)(2,1)S(1)}, bf16[9,112,32]{1,2,0:T(8,128)(2,1)}, u32[]{:S(2)}) copy-start(bf16[9,112,32]{1,2,0:T(8,128)(2,1)} %param.20) | copy-start | bytes 193540
  37.5 4.3 %copy-start.2 = (s32[1,1,160,256]{3,2,1,0:T(8,128)S(1)}, s32[1,1,160,256]{3,2,1,0:T(8,128)}, u32[]{:S(2)}) copy-start(s32[1,1,160,256]{3,2,1,0:T(8,128)} %order_ref.1) | copy-start | bytes 491524
  37.5 6.1 %copy-start.6 = (bf16[9,112,112]{2,1,0:T(8,128)(2,1)S(1)}, bf16[9,112,112]{2,1,0:T(8,128)(2,1)}, u32[]{:S(2)}) copy-start(bf16[9,112,112]{2,1,0:T(8,128)(2,1)} %w_deep.1) | copy-start | bytes 677380
  37.5 6.0 %copy-start.7 = (bf16[9,32,144]{2,1,0:T(8,128)(2,1)S(1)}, bf16[9,32,144]{2,1,0:T(8,128)(2,1)}, u32[]{:S(2)}) copy-start(bf16[9,32,144]{2,1,0:T(8,128)(2,1)} %w_up.1) | copy-start | bytes 248836
  37.5 6.0 %copy-start.11 = (bf16[9,3,32]{2,1,0:T(4,128)(2,1)S(1)}, bf16[9,3,32]{2,1,0:T(4,128)(2,1)}, u32[]{:S(2)}) copy-start(bf16[9,3,32]{2,1,0:T(4,128)(2,1)} %w_out.1) | copy-start | bytes 5188
  42.0 4.7 %collective-permute-start.3 = (bf16[1,4,8,256]{3,2,1,0:T(8,128)(2,1)S(1)}, bf16[1,4,8,256]{3,2,1,0:T(8,128)(2,1)S(1)}, u32[]{:S(2)}, u32[]{:S(2)}) collective-permute-start(bf16[1,4,8,256]{3,2,1,0:T(8,128)(2,1)S(1)} %gbuffer.1), channel_id=1, source_target_pairs={{0,8},{8,16},{16,24},{24,0},{1,9},{9,17},{17,25},{25,1},{2,10},{10... | collective-permute-start | bytes 49160 | tf_op jit(solution)/shard_map/ppermute | solution.py:777

commit v23 on v20

--- a/solution.py
+++ b/solution.py
@@ -200,14 +200,13 @@
 
     cell_y = jnp.floor(py)
     frac_y = py - cell_y
-    lower, upper = tile(cell_y), tile(cell_y + 1.0)
-    low_share, high_share = tile(1.0 - frac_y), tile(frac_y)
+    lower, high_share = tile(cell_y), tile(frac_y)
     nothing = jnp.zeros((TAIL, width), BF16)
     weight_y = []
     for start in range(0, MAIN, TAIL):
         here = places[start : start + TAIL]
         weight_y.append(
-            jnp.where(here == lower, low_share, jnp.where(here == upper, high_share, nothing))
+            jnp.maximum(1.0 - jnp.abs((here - lower) - high_share), nothing)
         )
     window = jnp.floor(px * (1.0 / STRIDE))
     weight_x = hat(eight - (px - STRIDE * window))

time: 47 us -> 47 us (level)
  no operation moved by 1% of the time
where the time goes in v23:
time: 47 us; the launch traced here: 46.6 us
  Pallas kernels  19.8 us (42%)
  starting transfers between devices  15.5 us (33%)
  local copies, waits for them, and re-layouts  5.67 us (12%)
  waiting for transfers between devices  4.7 us (10%)
  between operations  0.87 us (2%)
    pallas_call x1, Pallas kernels, sample_values(): pl.pallas_call(samples_kernel, out_shape=jax.ShapeDtypeStruct((owners, ro...  7.64 us
    all_to_all x1, starting transfers between devices, on_device(): lax.all_to_all(places, 'tile', split_axis=0, concat_axis=0, tiled=True)  6.34 us
    pallas_call x1, Pallas kernels, windows_of(): pl.pallas_call(windows_kernel, out_shape=jax.ShapeDtypeStruct((count + 1,...  3.92 us
    all_to_all x1, starting transfers between devices, on_device(): lax.all_to_all(found, 'tile', split_axis=0, concat_axis=0, tiled=True)  3.37 us
    ppermute x1, starting transfers between devices, on_device(): mate_places = lax.ppermute(for_mate, 'tile', mates)  3.03 us
    all_to_all x1, waiting for transfers between devices, on_device(): lax.all_to_all(found, 'tile', split_axis=0, concat_axis=0, tiled=True)  3 us
    pallas_call x1, Pallas kernels, decoder(): pl.pallas_call(decoder_kernel, out_shape=jax.ShapeDtypeStruct((1, colours...  2.88 us
    reshape x1, local copies, waits for them, and re-layouts, windows_of(): cube = bricks.reshape(count, EDGE, EDGE * EDGE)  2.31 us
  transfers between devices with their start and end apart: 6, of which 3 were waited for; matrix products, arithmetic and copies ran while one was open for 8% of the time, Pallas kernels for 37%

profile of v23, /device:TPU:0, one launch (start us, length us, event | category | flops | bytes accessed | tf_op | source)
XLA Modules:
  0.0 46.6 jit_solution(15127615429319663583)
XLA Ops:
  0.7 2.2 %positions.1.place_ref = f32[8,120,128]{2,1,0:T(8,128)} custom-call(s32[3,320,128]{2,1,0:T(8,128)} %bitcast.20, f32[3,320,128]{2,1,0:T(8,128)} %bitcast.21), custom_call_target="tpu_custom_call" | custom-call | flops 122880 | bytes 1474560 | tf_op jit(solution)/shard_map/positions/pallas_call | solution.py:82
  2.9 6.3 %all-to-all-start = ((f32[8,120,128]{2,1,0:T(8,128)}), f32[8,120,128]{2,1,0:T(8,128)}, u32[]{:S(2)}, u32[]{:S(2)}) async-start(f32[8,120,128]{2,1,0:T(8,128)} %positions.1.place_ref), calls=%async_computation | async-start | bytes 983040 | tf_op jit(solution)/shard_map/all_to_all | solution.py:745
  9.2 0.0 copy-start.3
  9.2 0.6 %collective-permute-start.1 = (bf16[8,4,256]{2,1,0:T(4,128)(2,1)S(1)}, bf16[8,4,256]{2,1,0:T(4,128)(2,1)S(1)}, u32[]{:S(2)}, u32[]{:S(2)}) collective-permute-start(bf16[8,4,256]{2,1,0:T(4,128)(2,1)S(1)} %bitcast.13), channel_id=1, source_target_pairs={{0,1},{1,0},{2,3},{3,2},{4,5},{5,4},{6,7},{7,6},{8,9},{9,8},{10,11... | collective-permute-start | bytes 49160 | tf_op jit(solution)/shard_map/ppermute | solution.py:755
  9.8 0.7 %collective-permute-start.2 = (bf16[8,4,256]{2,1,0:T(4,128)(2,1)S(1)}, bf16[8,4,256]{2,1,0:T(4,128)(2,1)S(1)}, u32[]{:S(2)}, u32[]{:S(2)}) collective-permute-start(bf16[8,4,256]{2,1,0:T(4,128)(2,1)S(1)} %bitcast.14), channel_id=1, source_target_pairs={{1,2},{2,1},{3,4},{4,3},{5,6},{6,5},{9,10},{10,9},{11,12},{12,11},... | collective-permute-start | bytes 49160 | tf_op jit(solution)/shard_map/ppermute | solution.py:756
  10.5 1.5 %constant_dynamic-slice_fusion = f32[1,120,128]{2,1,0:T(8,128)} fusion(f32[8,120,128]{2,1,0:T(8,128)} %positions.1.place_ref, s32[]{:T(128)S(6)} %select_n.3), kind=kLoop, calls=%fused_computation.2 | loop fusion | bytes 122884 | tf_op jit(solution)/shard_map/dynamic_slice | solution.py:752
  11.9 3.0 %collective-permute-start = (f32[1,120,128]{2,1,0:T(8,128)}, f32[1,120,128]{2,1,0:T(8,128)S(1)}, u32[]{:S(2)}, u32[]{:S(2)}) collective-permute-start(f32[1,120,128]{2,1,0:T(8,128)} %constant_dynamic-slice_fusion), channel_id=1, source_target_pairs={{0,1},{1,0},{2,3},{3,2},{4,5},{5,4},{6,7},{7,6},{8,9},{9,8},{10,11... | collective-permute-start | bytes 184328 | tf_op jit(solution)/shard_map/ppermute | solution.py:753
  15.0 2.3 %reshape.15.cube_ref = bf16[16,34,1156]{2,1,0:T(8,128)(2,1)S(1)} reshape(bf16[16,39304]{1,0:T(8,128)(2,1)S(1)} %copy-done.12) | data formatting | bytes 2515456 | tf_op jit(solution)/shard_map/reshape | solution.py:166
  17.3 0.1 pad_add_fusion.where_ref
  17.4 3.9 %brick_windows.1.brick_ref = bf16[17,208,256]{2,1,0:T(8,128)(2,1)S(1)} custom-call(s32[2]{0:T(128)S(1)} %pad_add_fusion.where_ref, s32[2,8]{1,0:T(2,128)S(1)} %bitcast.17, bf16[16,34,1156]{2,1,0:T(8,128)(2,1)S(1)} %reshape.15.cube_ref, f32[8,120,128]{2,1,0:T(8,128)S(1)} %copy-done, f32[1,120,128]{2,1,0:T(8,128)S(1)} %collective-permute-done.mate_place_ref), custom_call_target="tpu_custom_call" | custom-call | flops 905969664 | bytes 4194304 | tf_op jit(solution)/shard_map/brick_windows/pallas_call | solution.py:168
  21.3 1.2 %copy-done.1 = bf16[17,208,256]{2,1,0:T(8,128)(2,1)} copy-done((bf16[17,208,256]{2,1,0:T(8,128)(2,1)}, bf16[17,208,256]{2,1,0:T(8,128)(2,1)S(1)}, u32[]{:S(2)}) %copy-start.1) | copy-done | bytes 1810456
  22.5 1.4 %all-to-all-done.place_ref = f32[8,120,128]{2,1,0:T(8,128)} async-done(((f32[8,120,128]{2,1,0:T(8,128)}), f32[8,120,128]{2,1,0:T(8,128)}, u32[]{:S(2)}, u32[]{:S(2)}) %all-to-all-start) | async-done | bytes 491552 | tf_op jit(solution)/shard_map/all_to_all | solution.py:745
  24.0 7.6 %sample_values.1 = bf16[8,40,128]{2,1,0:T(8,128)(2,1)} custom-call(s32[2]{0:T(128)} %copy-done.4, s32[2,8]{1,0:T(2,128)} %bitcast.16, bf16[17,208,256]{2,1,0:T(8,128)(2,1)} %copy-done.1, f32[8,120,128]{2,1,0:T(8,128)} %all-to-all-done.place_ref), custom_call_target="tpu_custom_call" | custom-call | flops 4362076160 | bytes 3145728 | tf_op jit(solution)/shard_map/sample_values/pallas_call | solution.py:372
  31.6 3.4 %all-to-all-start.1 = ((bf16[8,40,128]{2,1,0:T(8,128)(2,1)}), bf16[8,40,128]{2,1,0:T(8,128)(2,1)S(1)}, u32[]{:S(2)}, u32[]{:S(2)}) async-start(bf16[8,40,128]{2,1,0:T(8,128)(2,1)} %sample_values.1), calls=%async_computation.1 | async-start | bytes 163840 | tf_op jit(solution)/shard_map/all_to_all | solution.py:763
  35.0 0.0 copy-start.9
  35.1 1.7 %stem.1.second = bf16[20,32,256]{2,1,0:T(8,128)(2,1)S(1)} custom-call(s32[2]{0:T(128)S(1)} %copy-done.5, bf16[8,4,256]{2,1,0:T(4,128)(2,1)S(1)} %bitcast.15, bf16[8,4,256]{2,1,0:T(4,128)(2,1)S(1)} %collective-permute-done.1.near_ref, bf16[8,4,256]{2,1,0:T(4,128)(2,1)S(1)} %collective-permute-done.2.far_ref, bf16[9,4,32]{2,1,0:T(4,128)(2,1)S(1)} %bitcast.19, ...), custom_call_target="tpu_custom_call" | custom-call | flops 1000000000 | bytes 1048576 | tf_op jit(solution)/shard_map/stem/pallas_call | solution.py:658
  36.7 0.0 copy-start.2
  36.8 1.3 %middle.1.third = bf16[8,112,128]{2,1,0:T(8,128)(2,1)S(1)} custom-call(s32[2]{0:T(128)S(1)} %copy-done.5, bf16[20,32,256]{2,1,0:T(8,128)(2,1)S(1)} %stem.1.second, bf16[9,32,112]{2,1,0:T(8,128)(2,1)S(1)} %bitcast.18), custom_call_target="tpu_custom_call" | custom-call | flops 500000000 | bytes 1048576 | tf_op jit(solution)/shard_map/middle/pallas_call | solution.py:680
  38.1 3.0 %all-to-all-done.1.value_ref = bf16[8,40,128]{2,1,0:T(8,128)(2,1)S(1)} async-done(((bf16[8,40,128]{2,1,0:T(8,128)(2,1)}), bf16[8,40,128]{2,1,0:T(8,128)(2,1)S(1)}, u32[]{:S(2)}, u32[]{:S(2)}) %all-to-all-start.1) | async-done | bytes 81952 | tf_op jit(solution)/shard_map/all_to_all | solution.py:763
  41.1 0.2 gbuffer.1
  41.3 1.5 %collective-permute-start.3 = (bf16[1,4,8,256]{3,2,1,0:T(8,128)(2,1)S(1)}, bf16[1,4,8,256]{3,2,1,0:T(8,128)(2,1)S(1)}, u32[]{:S(2)}, u32[]{:S(2)}) collective-permute-start(bf16[1,4,8,256]{3,2,1,0:T(8,128)(2,1)S(1)} %gbuffer.1), channel_id=1, source_target_pairs={{0,8},{8,16},{16,24},{24,0},{1,9},{9,17},{17,25},{25,1},{2,10},{10... | collective-permute-start | bytes 49160 | tf_op jit(solution)/shard_map/ppermute | solution.py:770
  42.8 2.9 %decoder.1 = bf16[1,3,8,256]{3,2,1,0:T(8,128)(2,1)} custom-call(s32[2]{0:T(128)S(1)} %copy-done.5, bf16[20,32,256]{2,1,0:T(8,128)(2,1)S(1)} %stem.1.second, bf16[8,112,128]{2,1,0:T(8,128)(2,1)S(1)} %middle.1.third, bf16[9,112,112]{2,1,0:T(8,128)(2,1)S(1)} %copy-done.6, bf16[9,32,144]{2,1,0:T(8,128)(2,1)S(1)} %copy-done.7, bf16[9,3,32]{2,1,0:T(4,128)(2,1)S(1)} %copy-done.11), custom_call_target="tpu_custom_call" | custom-call | flops 1500000000 | bytes 1048576 | tf_op jit(solution)/shard_map/decoder/pallas_call | solution.py:698
  45.7 0.3 collective-permute-done.3
  46.0 0.6 %copy.19 = bf16[1,4,8,256]{3,2,1,0:T(8,128)(2,1)} copy(bf16[1,4,8,256]{3,2,1,0:T(8,128)(2,1)S(1)} %collective-permute-done.3) | data formatting | bytes 32768
  (28 shorter events, 0.1 us)
Async XLA Ops:
  0.6 14.3 %copy-start.12 = (bf16[16,39304]{1,0:T(8,128)(2,1)S(1)}, bf16[16,39304]{1,0:T(8,128)(2,1)}, u32[]{:S(2)}) copy-start(bf16[16,39304]{1,0:T(8,128)(2,1)} %param.12) | copy-start | bytes 3773188
  0.6 8.6 %copy-start.13 = (bf16[1,4,8,256]{3,2,1,0:T(8,128)(2,1)S(1)}, bf16[1,4,8,256]{3,2,1,0:T(8,128)(2,1)}, u32[]{:S(2)}) copy-start(bf16[1,4,8,256]{3,2,1,0:T(8,128)(2,1)} %param.17) | copy-start | bytes 49156
  2.9 21.1 %all-to-all-start = ((f32[8,120,128]{2,1,0:T(8,128)}), f32[8,120,128]{2,1,0:T(8,128)}, u32[]{:S(2)}, u32[]{:S(2)}) async-start(f32[8,120,128]{2,1,0:T(8,128)} %positions.1.place_ref), calls=%async_computation | async-start | bytes 983040 | tf_op jit(solution)/shard_map/all_to_all | solution.py:745
  9.2 8.1 %copy-start = (f32[8,120,128]{2,1,0:T(8,128)S(1)}, f32[8,120,128]{2,1,0:T(8,128)}, u32[]{:S(2)}) copy-start(f32[8,120,128]{2,1,0:T(8,128)} %positions.1.place_ref) | copy-start | bytes 1474564
  9.2 8.1 %copy-start.3 = (s32[1,1,8,2]{2,3,1,0:T(2,128)S(1)}, s32[1,1,8,2]{2,3,1,0:T(2,128)}, u32[]{:S(2)}) copy-start(s32[1,1,8,2]{2,3,1,0:T(2,128)} %param.13) | copy-start | bytes 196
  9.2 22.4 %collective-permute-start.1 = (bf16[8,4,256]{2,1,0:T(4,128)(2,1)S(1)}, bf16[8,4,256]{2,1,0:T(4,128)(2,1)S(1)}, u32[]{:S(2)}, u32[]{:S(2)}) collective-permute-start(bf16[8,4,256]{2,1,0:T(4,128)(2,1)S(1)} %bitcast.13), channel_id=1, source_target_pairs={{0,1},{1,0},{2,3},{3,2},{4,5},{5,4},{6,7},{7,6},{8,9},{9,8},{10,11... | collective-permute-start | bytes 49160 | tf_op jit(solution)/shard_map/ppermute | solution.py:755
  9.8 21.8 %collective-permute-start.2 = (bf16[8,4,256]{2,1,0:T(4,128)(2,1)S(1)}, bf16[8,4,256]{2,1,0:T(4,128)(2,1)S(1)}, u32[]{:S(2)}, u32[]{:S(2)}) collective-permute-start(bf16[8,4,256]{2,1,0:T(4,128)(2,1)S(1)} %bitcast.14), channel_id=1, source_target_pairs={{1,2},{2,1},{3,4},{4,3},{5,6},{6,5},{9,10},{10,9},{11,12},{12,11},... | collective-permute-start | bytes 49160 | tf_op jit(solution)/shard_map/ppermute | solution.py:756
  11.9 5.4 %collective-permute-start = (f32[1,120,128]{2,1,0:T(8,128)}, f32[1,120,128]{2,1,0:T(8,128)S(1)}, u32[]{:S(2)}, u32[]{:S(2)}) collective-permute-start(f32[1,120,128]{2,1,0:T(8,128)} %constant_dynamic-slice_fusion), channel_id=1, source_target_pairs={{0,1},{1,0},{2,3},{3,2},{4,5},{5,4},{6,7},{7,6},{8,9},{9,8},{10,11... | collective-permute-start | bytes 184328 | tf_op jit(solution)/shard_map/ppermute | solution.py:753
  17.3 3.9 %copy-start.4 = (s32[2]{0:T(128)}, s32[2]{0:T(128)S(1)}, u32[]{:S(2)}) copy-start(s32[2]{0:T(128)S(1)} %pad_add_fusion.where_ref) | copy-start | bytes 28
  21.3 1.2 %copy-start.1 = (bf16[17,208,256]{2,1,0:T(8,128)(2,1)}, bf16[17,208,256]{2,1,0:T(8,128)(2,1)S(1)}, u32[]{:S(2)}) copy-start(bf16[17,208,256]{2,1,0:T(8,128)(2,1)S(1)} %brick_windows.1.brick_ref) | copy-start | bytes 5431300
  22.5 12.5 %copy-start.8 = (bf16[9,32,32]{2,1,0:T(8,128)(2,1)S(1)}, bf16[9,32,32]{2,1,0:T(8,128)(2,1)}, u32[]{:S(2)}) copy-start(bf16[9,32,32]{2,1,0:T(8,128)(2,1)} %w_mid.1) | copy-start | bytes 55300
  22.5 12.5 %copy-start.10 = (bf16[9,32,4]{1,2,0:T(4,128)(2,1)S(1)}, bf16[9,32,4]{1,2,0:T(4,128)(2,1)}, u32[]{:S(2)}) copy-start(bf16[9,32,4]{1,2,0:T(4,128)(2,1)} %param.18) | copy-start | bytes 6916
  24.0 11.1 %copy-start.5 = (s32[2]{0:T(128)S(1)}, s32[2]{0:T(128)}, u32[]{:S(2)}) copy-start(s32[2]{0:T(128)} %copy-done.4) | copy-start | bytes 28
  31.6 9.4 %all-to-all-start.1 = ((bf16[8,40,128]{2,1,0:T(8,128)(2,1)}), bf16[8,40,128]{2,1,0:T(8,128)(2,1)S(1)}, u32[]{:S(2)}, u32[]{:S(2)}) async-start(bf16[8,40,128]{2,1,0:T(8,128)(2,1)} %sample_values.1), calls=%async_computation.1 | async-start | bytes 163840 | tf_op jit(solution)/shard_map/all_to_all | solution.py:763
  35.0 1.8 %copy-start.9 = (bf16[9,112,32]{1,2,0:T(8,128)(2,1)S(1)}, bf16[9,112,32]{1,2,0:T(8,128)(2,1)}, u32[]{:S(2)}) copy-start(bf16[9,112,32]{1,2,0:T(8,128)(2,1)} %param.20) | copy-start | bytes 193540
  36.7 4.3 %copy-start.2 = (s32[1,1,160,256]{3,2,1,0:T(8,128)S(1)}, s32[1,1,160,256]{3,2,1,0:T(8,128)}, u32[]{:S(2)}) copy-start(s32[1,1,160,256]{3,2,1,0:T(8,128)} %order_ref.1) | copy-start | bytes 491524
  36.8 6.1 %copy-start.6 = (bf16[9,112,112]{2,1,0:T(8,128)(2,1)S(1)}, bf16[9,112,112]{2,1,0:T(8,128)(2,1)}, u32[]{:S(2)}) copy-start(bf16[9,112,112]{2,1,0:T(8,128)(2,1)} %w_deep.1) | copy-start | bytes 677380
  36.8 6.1 %copy-start.7 = (bf16[9,32,144]{2,1,0:T(8,128)(2,1)S(1)}, bf16[9,32,144]{2,1,0:T(8,128)(2,1)}, u32[]{:S(2)}) copy-start(bf16[9,32,144]{2,1,0:T(8,128)(2,1)} %w_up.1) | copy-start | bytes 248836
  36.8 6.0 %copy-start.11 = (bf16[9,3,32]{2,1,0:T(4,128)(2,1)S(1)}, bf16[9,3,32]{2,1,0:T(4,128)(2,1)}, u32[]{:S(2)}) copy-start(bf16[9,3,32]{2,1,0:T(4,128)(2,1)} %w_out.1) | copy-start | bytes 5188
  41.3 4.7 %collective-permute-start.3 = (bf16[1,4,8,256]{3,2,1,0:T(8,128)(2,1)S(1)}, bf16[1,4,8,256]{3,2,1,0:T(8,128)(2,1)S(1)}, u32[]{:S(2)}, u32[]{:S(2)}) collective-permute-start(bf16[1,4,8,256]{3,2,1,0:T(8,128)(2,1)S(1)} %gbuffer.1), channel_id=1, source_target_pairs={{0,8},{8,16},{16,24},{24,0},{1,9},{9,17},{17,25},{25,1},{2,10},{10... | collective-permute-start | bytes 49160 | tf_op jit(solution)/shard_map/ppermute | solution.py:770
